TPU v7x, 32 devices: a whole 2x2x4 slice. The times are simulated.
32 devices in a mesh: section: 4 (over y, x), seq: 4 (over z), rep: 2 (over core).
Axes of the slice: x: 2, y: 2, z: 4, core: 2. Of those that a mesh axis runs over, the one named last changes fastest.
Arguments:
- char_queries: bfloat16 [2, 4, 1024, 2048], P('rep', 'section', 'seq'), may hold values from -34 to 34
- char_keys: bfloat16 [2, 4, 1024, 2048], P('rep', 'section', 'seq'), may hold values from -6 to 6
- char_values: bfloat16 [2, 4, 1024, 2048], P('rep', 'section', 'seq'), may hold values from -48 to 48
- doc_starts: int32 [2, 4, 8], P('rep', 'section'), may hold values from 0 to 1023, as said below
- key_weight: bfloat16 [4, 2048, 1024], P('section'), may hold values from -0.125 to 0.125
- norm_gain: float32 [4, 2048], P('section'), may hold values from 0.25 to 1.75
- stashed: bfloat16 [2, 4, 2, 256, 2048], P('rep', 'section', None, 'seq'), may hold values from -48 to 48
- cotangent: bfloat16 [2, 4, 256, 1024], P('rep', 'section', 'seq'), may hold values from -6 to 6
- plan_slot: int32 [2, 4], P('rep', 'section'), may hold values from 0 to 1
Outputs:
- mol_keys: bfloat16 [2, 4, 256, 1024], P('rep', 'section', 'seq')
- upstream_grad: bfloat16 [2, 4, 256, 2048], P('rep', 'section', 'seq')
- gain_update: float32 [4, 2048], P('section')
Inputs may be any that keep to these rules, and one draw needn't show every extreme that they name: `doc_starts`: each row of offsets rises strictly, begins with 0 and ends with 1023.
All inputs are finite; a program needn't handle non-finite values.
Results may differ from a plain program's by a relative error of at most 0.012.
Values may be sent and summed in bfloat16 or wider, within the bound.
No kernel may reach another device: no remote copies, remote signals or barrier semaphores. Data moves between devices by JAX's collectives and lax.ppermute only.
A program may use at most 64 MiB of HBM per device.

v0:
```python
import math

import jax
import jax.numpy as jnp
from jax import lax
from jax.sharding import PartitionSpec as P

HEADS = 32
HEAD_DIM = 64
POOL = 4
WINDOW = 128


EPS_NORM = 1e-05
EPS_STEP = 1e-06


def from_behind(value, axis, steps):
    count = lax.axis_size(axis)
    first, last = (max(0, -steps), min(count, count - steps))
    return lax.ppermute(value, axis, [(source, source + steps) for source in range(first, last)])


def passed_along(block, axis, distance):
    devices = range(lax.axis_size(axis))
    route = [((i - distance) % len(devices), i) for i in devices]
    return lax.ppermute(block, axis, route)


def doc_index(positions, offsets):
    return jnp.sum((offsets[None, :] <= positions[:, None]).astype(jnp.int32), axis=1)


def attend(queries, keys_all, values_all, query_pos, key_pos, offsets):
    row_count = queries.shape[0]
    key_count = keys_all.shape[0]
    width = queries.shape[1]
    query_doc = doc_index(query_pos, offsets)
    key_doc = doc_index(key_pos, offsets)
    allowed = (
        (key_doc[None, :] == query_doc[:, None])
        & (key_pos[None, :] <= query_pos[:, None])
        & (key_pos[None, :] > query_pos[:, None] - WINDOW)
    )
    head_group = min(HEADS, 8)
    group_count = HEADS // head_group
    group_width = head_group * HEAD_DIM

    def one_group(group_index):
        group_start = group_index * group_width
        group_queries = lax.dynamic_slice_in_dim(queries, group_start, group_width, 1).reshape(
            row_count, head_group, HEAD_DIM
        )
        group_keys = lax.dynamic_slice_in_dim(keys_all, group_start, group_width, 1).reshape(
            key_count, head_group, HEAD_DIM
        )
        group_values = lax.dynamic_slice_in_dim(values_all, group_start, group_width, 1).reshape(
            key_count, head_group, HEAD_DIM
        )
        scores = jnp.einsum(
            "qhd,khd->hqk", group_queries, group_keys, preferred_element_type=jnp.float32
        ) * (1.0 / math.sqrt(HEAD_DIM))
        scores = jnp.where(allowed[None, :, :], scores, -1e30)
        row_max = jnp.max(scores, axis=2, keepdims=True)
        weights = jnp.exp(scores - row_max)
        row_total = jnp.sum(weights, axis=2, keepdims=True)
        rounded = weights.astype(jnp.bfloat16)
        mixed_heads = jnp.einsum(
            "hqk,khd->qhd", rounded, group_values, preferred_element_type=jnp.float32
        )
        return (
            (mixed_heads / jnp.transpose(row_total, (1, 0, 2)))
            .reshape(row_count, group_width)
            .astype(jnp.bfloat16)
        )

    groups = lax.map(one_group, jnp.arange(group_count, dtype=jnp.int32))
    return jnp.transpose(groups, (1, 0, 2)).reshape(row_count, width)


def shorten(rows_in):
    return jnp.mean(rows_in.astype(jnp.float32).reshape(-1, POOL, rows_in.shape[1]), axis=1).astype(
        jnp.bfloat16
    )


def local(
    char_queries,
    char_keys,
    char_values,
    doc_starts,
    key_weight,
    norm_gain,
    stashed,
    cotangent,
    plan_slot,
):
    queries = char_queries[0, 0]
    own_keys = char_keys[0, 0]
    own_values = char_values[0, 0]
    offsets = doc_starts[0, 0]
    row_count = queries.shape[0]
    first_pos = lax.axis_index("seq") * row_count
    query_pos = first_pos + jnp.arange(row_count, dtype=jnp.int32)
    far_keys, far_values = from_behind((own_keys, own_values), "seq", 1)
    far_pos = first_pos - row_count + jnp.arange(row_count, dtype=jnp.int32)
    keys_all = jnp.concatenate([far_keys, own_keys], axis=0)
    values_all = jnp.concatenate([far_values, own_values], axis=0)
    key_pos = jnp.concatenate([far_pos, query_pos], axis=0)
    attended = attend(queries, keys_all, values_all, query_pos, key_pos, offsets)
    arrived = shorten(passed_along(attended, "section", 1))
    projection = key_weight[0]
    gain_row = norm_gain[0]
    as_float = arrived.astype(jnp.float32)
    inv_norm = lax.rsqrt(jnp.mean(as_float * as_float, axis=1, keepdims=True) + EPS_NORM)
    normed = (as_float * inv_norm * gain_row).astype(jnp.bfloat16)
    mol_rows = jnp.dot(normed, projection, preferred_element_type=jnp.float32).astype(jnp.bfloat16)
    held_rows = lax.dynamic_index_in_dim(stashed[0, 0], plan_slot[0, 0], 0, keepdims=False).astype(
        jnp.float32
    )
    back_grad = lax.dot_general(
        cotangent[0, 0], projection, (((1,), (1,)), ((), ())), preferred_element_type=jnp.float32
    )
    inv_rms = lax.rsqrt(jnp.mean(held_rows * held_rows, axis=1, keepdims=True) + EPS_NORM)
    whitened = held_rows * inv_rms
    gain_term = jnp.sum(back_grad * whitened, axis=0)
    summed = lax.psum(gain_term, ("seq", "rep"))
    update = summed / jnp.sqrt(jnp.mean(summed * summed) + EPS_STEP)
    scaled = back_grad * gain_row
    dinput = (
        inv_rms * (scaled - whitened * jnp.mean(scaled * whitened, axis=1, keepdims=True))
    ).astype(jnp.bfloat16)
    upstream = passed_along(dinput, "section", -1)
    return (mol_rows[None, None], upstream[None, None], update[None])


def solution(mesh):
    in_specs = (
        P("rep", "section", "seq", None),
        P("rep", "section", "seq", None),
        P("rep", "section", "seq", None),
        P("rep", "section", None),
        P("section", None, None),
        P("section", None),
        P("rep", "section", None, "seq", None),
        P("rep", "section", "seq", None),
        P("rep", "section"),
    )
    out_specs = (
        P("rep", "section", "seq", None),
        P("rep", "section", "seq", None),
        P("section", None),
    )
    return jax.shard_map(local, mesh=mesh, in_specs=in_specs, out_specs=out_specs, check_vma=False)
```

profile of v0, /device:TPU:0, one launch (start us, length us, event | category | flops | bytes accessed | tf_op | source)
XLA Modules:
  0.0 122.2 jit_solution(2761936365151108832)
XLA Ops:
  0.7 1.5 %copy.19 = bf16[1,1,256,2048]{2,3,1,0:T(8,128)(2,1)S(1)} copy(bf16[1,1,256,2048]{3,2,1,0:T(8,128)(2,1)} %param.13) | data formatting | bytes 2097152 | tf_op args[2]
  2.2 6.0 %collective-permute-start = (bf16[256,2048]{0,1:T(8,128)(2,1)S(1)}, bf16[256,2048]{0,1:T(8,128)(2,1)}, u32[]{:S(2)}, u32[]{:S(2)}) collective-permute-start(bf16[256,2048]{0,1:T(8,128)(2,1)S(1)} %bitcast.82), channel_id=1, source_target_pairs={{0,2},{2,4},{4,6},{1,3},{3,5},{5,7},{8,10},{10,12},{12,14},{9,11},... | collective-permute-start | bytes 3145736 | tf_op jit(solution)/shard_map/ppermute | solution.py:21
  8.2 2.3 %copy.21 = bf16[1,1,256,2048]{2,3,1,0:T(8,128)(2,1)} copy(bf16[1,1,256,2048]{3,2,1,0:T(8,128)(2,1)} %param.12) | data formatting | bytes 2097152 | tf_op args[1]
  10.5 3.4 %collective-permute-start.1 = (bf16[256,2048]{0,1:T(8,128)(2,1)}, bf16[256,2048]{0,1:T(8,128)(2,1)}, u32[]{:S(2)}, u32[]{:S(2)}) collective-permute-start(bf16[256,2048]{0,1:T(8,128)(2,1)} %bitcast.2), channel_id=1, source_target_pairs={{0,2},{2,4},{4,6},{1,3},{3,5},{5,7},{8,10},{10,12},{12,14},{9,11},... | collective-permute-start | bytes 3145736 | tf_op jit(solution)/shard_map/ppermute | solution.py:21
  13.9 1.5 %copy.20 = bf16[1,1,256,2048]{2,3,1,0:T(8,128)(2,1)S(1)} copy(bf16[1,1,256,2048]{3,2,1,0:T(8,128)(2,1)} %param.11) | data formatting | bytes 2097152 | tf_op args[0]
  16.4 14.3 %collective-permute-done = bf16[256,2048]{0,1:T(8,128)(2,1)} collective-permute-done((bf16[256,2048]{0,1:T(8,128)(2,1)S(1)}, bf16[256,2048]{0,1:T(8,128)(2,1)}, u32[]{:S(2)}, u32[]{:S(2)}) %collective-permute-start) | collective-permute-done | bytes 1048608 | tf_op jit(solution)/shard_map/ppermute | solution.py:21
  30.7 1.7 %pad_maximum_fusion = bf16[512,2048]{0,1:T(8,128)(2,1)S(1)} fusion(bf16[256,2048]{0,1:T(8,128)(2,1)} %bitcast.83, bf16[256,2048]{0,1:T(8,128)(2,1)} %collective-permute-done), kind=kLoop, calls=%fused_computation.22 | loop fusion | flops 4194304 | bytes 4194304 | tf_op jit(solution)/shard_map/concatenate | solution.py:108
  32.4 19.7 %collective-permute-done.1 = bf16[256,2048]{0,1:T(8,128)(2,1)} collective-permute-done((bf16[256,2048]{0,1:T(8,128)(2,1)}, bf16[256,2048]{0,1:T(8,128)(2,1)}, u32[]{:S(2)}, u32[]{:S(2)}) %collective-permute-start.1) | collective-permute-done | bytes 1048608 | tf_op jit(solution)/shard_map/ppermute | solution.py:21
  52.1 3.0 %pad_maximum_fusion.1 = bf16[512,2048]{0,1:T(8,128)(2,1)} fusion(bf16[256,2048]{0,1:T(8,128)(2,1)} %bitcast.2, bf16[256,2048]{0,1:T(8,128)(2,1)} %collective-permute-done.1), kind=kLoop, calls=%fused_computation.23 | loop fusion | flops 4194304 | bytes 4194304 | tf_op jit(solution)/shard_map/concatenate | solution.py:107
  55.2 27.2 %while.11 = (s32[]{:T(128)}, bf16[4,256,512]{1,2,0:T(8,128)(2,1)}, s32[4]{0:T(128)S(1)}, bf16[512,2048]{0,1:T(8,128)(2,1)S(1)}, bf16[256,2048]{0,1:T(8,128)(2,1)...) while((s32[]{:T(128)}, bf16[4,256,512]{1,2,0:T(8,128)(2,1)}, ...), condition=%wide.region_5.6_spmd.clone, body=%wide.region_2.5_spmd.clone.sunk | while | flops 280883200 | bytes 17874140 | solution.py:77
  55.2 0.6 dynamic_slice.34
  56.4 1.1 constant_dynamic-slice_fusion.5
  57.5 0.2 compare_and_fusion.2
  57.8 0.9 fusion.60
  58.7 1.3 %fusion.61 = f32[8,256]{1,0:T(8,128)S(1)} fusion(f32[8,256,512]{2,1,0:T(8,128)S(1)} %get-tuple-element.174, f32[8,256]{1,0:T(8,128)S(1)} %get-tuple-element.175, pred[256,512]{1,0:T(8,128)(4,1)S(1)} %compare_and_fusion.2), kind=kLoop, calls=%fused_computation.4.clone.1 | loop fusion | flops 4192256 | bytes 4341760 | tf_op jit(solution)/shard_map/while/body/eval_jaxpr/reduce_sum | solution.py:66
  60.0 1.2 fusion.62
  61.3 0.7 constant_dynamic-update-slice_fusion.2
  62.0 0.6 dynamic_slice.34
  63.2 1.1 constant_dynamic-slice_fusion.5
  64.4 0.2 compare_and_fusion.2
  64.6 0.9 fusion.60
  65.5 1.3 %fusion.61 = f32[8,256]{1,0:T(8,128)S(1)} fusion(f32[8,256,512]{2,1,0:T(8,128)S(1)} %get-tuple-element.174, f32[8,256]{1,0:T(8,128)S(1)} %get-tuple-element.175, pred[256,512]{1,0:T(8,128)(4,1)S(1)} %compare_and_fusion.2), kind=kLoop, calls=%fused_computation.4.clone.1 | loop fusion | flops 4192256 | bytes 4341760 | tf_op jit(solution)/shard_map/while/body/eval_jaxpr/reduce_sum | solution.py:66
  66.8 1.2 fusion.62
  68.1 0.7 constant_dynamic-update-slice_fusion.2
  68.8 0.6 dynamic_slice.34
  70.0 1.1 constant_dynamic-slice_fusion.5
  71.4 0.9 fusion.60
  72.3 1.3 %fusion.61 = f32[8,256]{1,0:T(8,128)S(1)} fusion(f32[8,256,512]{2,1,0:T(8,128)S(1)} %get-tuple-element.174, f32[8,256]{1,0:T(8,128)S(1)} %get-tuple-element.175, pred[256,512]{1,0:T(8,128)(4,1)S(1)} %compare_and_fusion.2), kind=kLoop, calls=%fused_computation.4.clone.1 | loop fusion | flops 4192256 | bytes 4341760 | tf_op jit(solution)/shard_map/while/body/eval_jaxpr/reduce_sum | solution.py:66
  73.6 1.2 fusion.62
  74.8 0.7 constant_dynamic-update-slice_fusion.2
  75.6 0.6 dynamic_slice.34
  76.8 1.1 constant_dynamic-slice_fusion.5
  78.2 0.9 fusion.60
  79.1 1.3 %fusion.61 = f32[8,256]{1,0:T(8,128)S(1)} fusion(f32[8,256,512]{2,1,0:T(8,128)S(1)} %get-tuple-element.174, f32[8,256]{1,0:T(8,128)S(1)} %get-tuple-element.175, pred[256,512]{1,0:T(8,128)(4,1)S(1)} %compare_and_fusion.2), kind=kLoop, calls=%fused_computation.4.clone.1 | loop fusion | flops 4192256 | bytes 4341760 | tf_op jit(solution)/shard_map/while/body/eval_jaxpr/reduce_sum | solution.py:66
  80.4 1.2 fusion.62
  81.6 0.7 constant_dynamic-update-slice_fusion.2
  82.4 1.5 %copy.22 = bf16[256,2048]{1,0:T(8,128)(2,1)S(1)} copy(bf16[256,2048]{0,1:T(8,128)(2,1)} %bitcast.84) | data formatting | bytes 2097152 | tf_op jit(solution)/shard_map/reshape | solution.py:78
  83.9 1.5 %collective-permute-start.2 = (bf16[256,2048]{1,0:T(8,128)(2,1)S(1)}, bf16[256,2048]{1,0:T(8,128)(2,1)}, u32[]{:S(2)}, u32[]{:S(2)}) collective-permute-start(bf16[256,2048]{1,0:T(8,128)(2,1)S(1)} %copy.22), channel_id=1, source_target_pairs={{24,0},{0,8},{8,16},{16,24},{25,1},{1,9},{9,17},{17,25},{26,2},{2,... | collective-permute-start | bytes 3145736 | tf_op jit(solution)/shard_map/ppermute | solution.py:27
  85.5 3.7 %fusion.39 = (f32[2048]{0:T(1024)S(1)}, f32[64]{0:T(128)S(1)}, f32[64,2048]{1,0:T(8,128)S(1)}) fusion(f32[64]{0:T(128)S(1)} %add_rsqrt_fusion, bf16[1,1,2,64,2048]{4,3,2,1,0:T(8,128)(2,1)} %param.17, s32[]{:T(128)S(6)} %select_n.13, f32[2048]{0:T(1024)S(1)} %bitcast.87, bf16[1,2048,1024]{2,1,0:T(8,128)(2,1)} %param.15, bf16[1,1,64,1024]{3,2,1,0:T(8,128)(2,1)S(1)} %copy-done), kind=kOutput, calls=%fused_computation.40 | convolution fusion | flops 269350848 | bytes 5128708 | tf_op jit(solution)/shard_map/dot_general | solution.py:121
  89.4 1.5 %collective-permute-start.3 = (bf16[64,2048]{1,0:T(8,128)(2,1)S(1)}, bf16[64,2048]{1,0:T(8,128)(2,1)S(1)}, u32[]{:S(2)}, u32[]{:S(2)}) collective-permute-start(bf16[64,2048]{1,0:T(8,128)(2,1)S(1)} %fusion.38), channel_id=1, source_target_pairs={{8,0},{16,8},{24,16},{0,24},{9,1},{17,9},{25,17},{1,25},{10,2},{18... | collective-permute-start | bytes 786440 | tf_op jit(solution)/shard_map/ppermute | solution.py:27
  90.9 16.4 %psum.7 = f32[2048]{0:T(1024)S(1)} all-reduce(f32[2048]{0:T(1024)S(1)} %get-tuple-element.70), channel_id=1, replica_groups=mesh['section'=4,'seq'=4,'rep'=2] {'seq','rep'}, use_global_device_ids=true, to_apply=%region_11.12 | all-reduce | flops 2048 | bytes 16384 | tf_op jit(solution)/shard_map/psum | solution.py:127
  107.3 0.6 multiply_reduce_fusion
  108.6 0.6 broadcast_divide_fusion
  109.2 5.4 %collective-permute-done.3 = bf16[64,2048]{1,0:T(8,128)(2,1)S(1)} collective-permute-done((bf16[64,2048]{1,0:T(8,128)(2,1)S(1)}, bf16[64,2048]{1,0:T(8,128)(2,1)S(1)}, u32[]{:S(2)}, u32[]{:S(2)}) %collective-permute-start.3) | collective-permute-done | bytes 262176 | tf_op jit(solution)/shard_map/ppermute | solution.py:27
  114.6 1.7 %reshape.81 = f32[64,4,2048]{2,1,0:T(4,128)S(1)} reshape(bf16[256,2048]{1,0:T(8,128)(2,1)} %collective-permute-done.2) | data formatting | bytes 3145728 | tf_op jit(solution)/shard_map/reshape | solution.py:82
  116.3 1.3 %reduce_sum.83 = f32[64,2048]{1,0:T(8,128)S(1)} reduce(f32[64,4,2048]{2,1,0:T(4,128)S(1)} %reshape.81, f32[]{:T(128)} %constant.54.clone.1), dimensions={1}, to_apply=%region_6.7 | reduce | flops 393216 | bytes 2621444 | tf_op jit(solution)/shard_map/reduce_sum | solution.py:82
  117.8 3.7 %fusion.26 = bf16[1,1,64,1024]{3,2,1,0:T(8,128)(2,1)} fusion(bf16[1,2048,1024]{2,1,0:T(8,128)(2,1)} %param.15, f32[2048]{0:T(1024)S(1)} %bitcast.89, f32[64]{0:T(128)S(1)} %add_rsqrt_fusion.1, f32[64,2048]{1,0:T(8,128)S(1)} %reduce_sum.83), kind=kOutput, calls=%fused_computation.25 | convolution fusion | flops 269287424 | bytes 4858112 | tf_op jit(solution)/shard_map/dot_general | solution.py:117
  121.5 0.7 copy.32
  (32 shorter events, 1.3 us)
Async XLA Ops:
  0.6 84.8 %copy-start = (bf16[1,1,64,1024]{3,2,1,0:T(8,128)(2,1)S(1)}, bf16[1,1,64,1024]{3,2,1,0:T(8,128)(2,1)}, u32[]{:S(2)}) copy-start(bf16[1,1,64,1024]{3,2,1,0:T(8,128)(2,1)} %param.18) | copy-start | bytes 393220
  0.6 15.4 %copy-start.2 = (bf16[1,1,2,64,2048]{4,3,2,1,0:T(8,128)(2,1)S(1)}, bf16[1,1,2,64,2048]{4,3,2,1,0:T(8,128)(2,1)}, u32[]{:S(2)}) copy-start(bf16[1,1,2,64,2048]{4,3,2,1,0:T(8,128)(2,1)} %param.17) | copy-start | bytes 1572868
  0.7 15.6 %copy-start.5 = (s32[1,1,8]{2,1,0:T(1,128)S(1)}, s32[1,1,8]{2,1,0:T(1,128)}, u32[]{:S(2)}) copy-start(s32[1,1,8]{2,1,0:T(1,128)} %param.14) | copy-start | bytes 100
  2.2 14.2 %copy-start.1 = (bf16[1,1,256,2048]{2,3,1,0:T(8,128)(2,1)}, bf16[1,1,256,2048]{2,3,1,0:T(8,128)(2,1)S(1)}, u32[]{:S(2)}) copy-start(bf16[1,1,256,2048]{2,3,1,0:T(8,128)(2,1)S(1)} %copy.19) | copy-start | bytes 3145732
  2.2 28.5 %collective-permute-start = (bf16[256,2048]{0,1:T(8,128)(2,1)S(1)}, bf16[256,2048]{0,1:T(8,128)(2,1)}, u32[]{:S(2)}, u32[]{:S(2)}) collective-permute-start(bf16[256,2048]{0,1:T(8,128)(2,1)S(1)} %bitcast.82), channel_id=1, source_target_pairs={{0,2},{2,4},{4,6},{1,3},{3,5},{5,7},{8,10},{10,12},{12,14},{9,11},... | collective-permute-start | bytes 3145736 | tf_op jit(solution)/shard_map/ppermute | solution.py:21
  10.5 41.7 %collective-permute-start.1 = (bf16[256,2048]{0,1:T(8,128)(2,1)}, bf16[256,2048]{0,1:T(8,128)(2,1)}, u32[]{:S(2)}, u32[]{:S(2)}) collective-permute-start(bf16[256,2048]{0,1:T(8,128)(2,1)} %bitcast.2), channel_id=1, source_target_pairs={{0,2},{2,4},{4,6},{1,3},{3,5},{5,7},{8,10},{10,12},{12,14},{9,11},... | collective-permute-start | bytes 3145736 | tf_op jit(solution)/shard_map/ppermute | solution.py:21
  55.2 30.3 %copy-start.4 = (f32[1,2048]{1,0:T(1,128)S(1)}, f32[1,2048]{1,0:T(1,128)}, u32[]{:S(2)}) copy-start(f32[1,2048]{1,0:T(1,128)} %param.16) | copy-start | bytes 24580
  82.4 6.9 %copy-start.3 = (bf16[1,1,2,64,2048]{4,3,2,1,0:T(8,128)(2,1)S(1)}, bf16[1,1,2,64,2048]{4,3,2,1,0:T(8,128)(2,1)}, u32[]{:S(2)}) copy-start(bf16[1,1,2,64,2048]{4,3,2,1,0:T(8,128)(2,1)} %param.17) | copy-start | bytes 1572868
  83.9 30.7 %collective-permute-start.2 = (bf16[256,2048]{1,0:T(8,128)(2,1)S(1)}, bf16[256,2048]{1,0:T(8,128)(2,1)}, u32[]{:S(2)}, u32[]{:S(2)}) collective-permute-start(bf16[256,2048]{1,0:T(8,128)(2,1)S(1)} %copy.22), channel_id=1, source_target_pairs={{24,0},{0,8},{8,16},{16,24},{25,1},{1,9},{9,17},{17,25},{26,2},{2,... | collective-permute-start | bytes 3145736 | tf_op jit(solution)/shard_map/ppermute | solution.py:27
  89.4 25.2 %collective-permute-start.3 = (bf16[64,2048]{1,0:T(8,128)(2,1)S(1)}, bf16[64,2048]{1,0:T(8,128)(2,1)S(1)}, u32[]{:S(2)}, u32[]{:S(2)}) collective-permute-start(bf16[64,2048]{1,0:T(8,128)(2,1)S(1)} %fusion.38), channel_id=1, source_target_pairs={{8,0},{16,8},{24,16},{0,24},{9,1},{17,9},{25,17},{1,25},{10,2},{18... | collective-permute-start | bytes 786440 | tf_op jit(solution)/shard_map/ppermute | solution.py:27
where the time goes:
time: 123 us; the launch traced here: 122 us
  waiting for transfers between devices  39.4 us (32%)
  local copies, waits for them, and re-layouts  19.1 us (16%)
  blocking collectives  16.4 us (13%)
  matrix products  16 us (13%)
  other arithmetic  14 us (11%)
  starting transfers between devices  12.4 us (10%)
  loops' own time  2.71 us (2%)
  between operations  2.14 us (2%)
    ppermute x2, waiting for transfers between devices, from_behind(): lax.ppermute(value, axis, [(source, source + steps) for source in range(f...  34 us
    psum x1, blocking collectives, local(): summed = lax.psum(gain_term, ('seq', 'rep'))  16.4 us
    ppermute x2, starting transfers between devices, from_behind(): lax.ppermute(value, axis, [(source, source + steps) for source in range(f...  9.4 us
    unnamed x16, local copies, waits for them, and re-layouts  6.03 us
    ppermute x2, waiting for transfers between devices, passed_along(): return lax.ppermute(block, axis, route)  5.39 us
    reduce_sum x4, other arithmetic, one_group(): row_total = jnp.sum(weights, axis=2, keepdims=True)  5.24 us
    dot_general x4, matrix products, one_group(): jnp.einsum('hqk,khd->qhd', rounded, group_values, preferred_element_type=...  4.86 us
    dynamic_slice x4, local copies, waits for them, and re-layouts, one_group(): lax.dynamic_slice_in_dim(keys_all, group_start, group_width, 1)  4.47 us
  transfers between devices with their start and end apart: 4, of which 3 were waited for; matrix products, arithmetic and copies ran while one was open for 9% of the time, Pallas kernels for 0%

commit v1 on v0

v1 whole, which is shorter than its diff:
```python
import functools
import math

import jax
import jax.numpy as jnp
from jax import lax
from jax.experimental import pallas as pl
from jax.experimental.pallas import tpu as pltpu
from jax.sharding import PartitionSpec as P

HEAD_DIM = 64
POOL = 4
WINDOW = 128
LANES = 128
EPS_NORM = 1e-05
EPS_STEP = 1e-06
MASKED = -1e30

NT = (((1,), (1,)), ((), ()))


def dot_nt(a, b):
    return lax.dot_general(a, b, NT, preferred_element_type=jnp.float32)


def dot_nn(a, b):
    return jnp.dot(a, b, preferred_element_type=jnp.float32)


def shifted(value, axis, steps):
    count = lax.axis_size(axis)
    first, last = max(0, -steps), min(count, count - steps)
    return lax.ppermute(value, axis, [(i, i + steps) for i in range(first, last)])


def passed_along(value, axis, steps):
    count = lax.axis_size(axis)
    return lax.ppermute(value, axis, [(i, (i + steps) % count) for i in range(count)])


def earliest_key(offsets_ref, query_pos):
    start = jnp.zeros_like(query_pos)
    for d in range(offsets_ref.shape[1]):
        offset = offsets_ref[0, d]
        start = jnp.where(query_pos >= offset, offset, start)
    return jnp.maximum(start, query_pos - (WINDOW - 1))


def mask_bias(offsets_ref, key_start, key_count, query_start, query_count):
    query_pos = query_start + lax.broadcasted_iota(jnp.int32, (1, query_count), 1)
    lowest = earliest_key(offsets_ref, query_pos)
    key_pos = key_start + lax.broadcasted_iota(jnp.int32, (key_count, query_count), 0)
    allowed = (key_pos >= lowest) & (key_pos <= query_pos)
    return jnp.where(allowed, 0.0, MASKED).astype(jnp.float32)


def split_heads(queries):
    rows = queries.shape[0]
    lane = lax.broadcasted_iota(jnp.int32, (rows, LANES), 1)
    scaled = queries.astype(jnp.float32) * (1.0 / math.sqrt(HEAD_DIM))
    first = jnp.where(lane < HEAD_DIM, scaled, 0.0)
    second = jnp.where(lane < HEAD_DIM, 0.0, scaled)
    return jnp.concatenate([first, second], axis=0).astype(jnp.bfloat16)


def pool_matrix(queries):
    molecule = lax.broadcasted_iota(jnp.int32, (queries // POOL, queries), 0)
    query = lax.broadcasted_iota(jnp.int32, (queries // POOL, queries), 1)
    return jnp.where(query // POOL == molecule, 1.0 / POOL, 0.0).astype(jnp.bfloat16)


def own_heads(mixed, scale):
    count = mixed.shape[1] // 2
    return jnp.concatenate(
        [
            mixed[:HEAD_DIM, :count] * scale[:, :count],
            mixed[HEAD_DIM:, count:] * scale[:, count:],
        ],
        axis=0,
    )


def twice(bias):
    return jnp.concatenate([bias, bias], axis=1)


def softmax_parts(scores):
    top = jnp.max(scores, axis=0, keepdims=True)
    weights = jnp.exp(scores - top)
    total = jnp.sum(weights, axis=0, keepdims=True)
    return top, weights.astype(jnp.bfloat16), total


def own_kernel(rows, offsets_ref, q_ref, k_ref, v_ref, late_ref, early_ref, lse_ref, bias0, bias1):
    half = rows // 2
    shard_start = lax.axis_index("seq") * rows

    @pl.when(pl.program_id(0) == 0)
    def _():
        bias0[...] = mask_bias(offsets_ref, shard_start, half, shard_start, half)
        bias1[...] = mask_bias(offsets_ref, shard_start, rows, shard_start + half, half)

    pooling = pool_matrix(half)
    for pair in range(q_ref.shape[1] // LANES):
        columns = pl.ds(pair * LANES, LANES)
        keys = k_ref[:, columns]
        values_t = jnp.transpose(v_ref[:, columns])
        scores = dot_nt(keys[:half], split_heads(q_ref[:half, columns])) + twice(bias0[...])
        top, weights, total = softmax_parts(scores)
        mixed = dot_nn(values_t[:, :half], weights)
        early_ref[columns, :] = own_heads(mixed, 1.0 / total).astype(jnp.bfloat16)
        lse = top + jnp.log(total)
        lse_ref[0:1, columns] = lse[:, :half]
        lse_ref[1:2, columns] = lse[:, half:]
        scores = dot_nt(keys, split_heads(q_ref[half:, columns])) + twice(bias1[...])
        _, weights, total = softmax_parts(scores)
        mixed = dot_nn(values_t, weights)
        attended = own_heads(mixed, 1.0 / total).astype(jnp.bfloat16)
        late_ref[:, columns] = dot_nt(pooling, attended).astype(jnp.bfloat16)


def halo_kernel(rows, offsets_ref, q_ref, k_ref, v_ref, lse_ref, out_ref, bias):
    half = rows // 2
    next_start = (lax.axis_index("seq") + 1) * rows

    @pl.when(pl.program_id(0) == 0)
    def _():
        bias[...] = mask_bias(offsets_ref, next_start - half, half, next_start, half)

    pooling = pool_matrix(half)
    molecules = half // POOL
    for pair in range(q_ref.shape[1] // LANES):
        columns = pl.ds(pair * LANES, LANES)
        scores = dot_nt(k_ref[:, columns], split_heads(q_ref[:, columns])) + twice(bias[...])
        lse = jnp.concatenate([lse_ref[0:1, columns], lse_ref[1:2, columns]], axis=1)
        top = jnp.maximum(jnp.max(scores, axis=0, keepdims=True), lse)
        weights = jnp.exp(scores - top)
        rest = jnp.exp(lse - top)
        inverse = 1.0 / (jnp.sum(weights, axis=0, keepdims=True) + rest)
        mixed = dot_nn(jnp.transpose(v_ref[:, columns]), weights.astype(jnp.bfloat16))
        part = own_heads(mixed, inverse).astype(jnp.bfloat16)
        pooled = dot_nt(pooling, part).astype(jnp.bfloat16)
        share = rest * inverse
        high = share.astype(jnp.bfloat16)
        low = (share - high.astype(jnp.float32)).astype(jnp.bfloat16)
        out_ref[:molecules, columns] = pooled
        out_ref[molecules:, columns] = jnp.concatenate(
            [
                high[:, :half].astype(jnp.float32),
                low[:, :half].astype(jnp.float32),
                high[:, half:].astype(jnp.float32),
                low[:, half:].astype(jnp.float32),
                jnp.zeros((12, LANES), jnp.float32),
            ],
            axis=0,
        ).astype(jnp.bfloat16)


def combine_kernel(early_ref, halo_ref, out_ref):
    half = early_ref.shape[1]
    molecules = half // POOL
    pooling = pool_matrix(half)
    first = lax.axis_index("seq") == 0
    for pair in range(out_ref.shape[1] // LANES):
        columns = pl.ds(pair * LANES, LANES)
        shares = halo_ref[molecules:, columns].astype(jnp.float32)
        share_a = jnp.where(first, 1.0, shares[0:1] + shares[1:2])
        share_b = jnp.where(first, 1.0, shares[2:3] + shares[3:4])
        early = early_ref[columns, :].astype(jnp.float32)
        scaled = jnp.concatenate([early[:HEAD_DIM] * share_a, early[HEAD_DIM:] * share_b], axis=0)
        pooled = dot_nt(pooling, scaled.astype(jnp.bfloat16))
        out_ref[:, columns] = (pooled + halo_ref[:molecules, columns].astype(jnp.float32)).astype(
            jnp.bfloat16
        )


def back_kernel(slot_ref, cotangent_ref, weight_ref, gain_ref, held_ref, dinput_ref, term_ref, grad, stats):
    step = pl.program_id(0)
    width = weight_ref.shape[0]
    columns = pl.ds(pl.multiple_of(step * width, width), width)

    @pl.when(step == 0)
    def _():
        held = held_ref[0].astype(jnp.float32)
        mean = jnp.sum(held * held, axis=1, keepdims=True) / held.shape[1]
        stats[0] = jnp.broadcast_to(lax.rsqrt(mean + EPS_NORM), stats.shape[1:])
        stats[1] = jnp.zeros(stats.shape[1:], jnp.float32)

    inv_rms = stats[0, :, 0:1]
    back = dot_nt(cotangent_ref[...], weight_ref[...])
    whitened = held_ref[0, :, columns].astype(jnp.float32) * inv_rms
    product = back * whitened
    term_ref[:, columns] = jnp.sum(product, axis=0, keepdims=True)
    gain = gain_ref[:, columns]
    stats[1] += jnp.broadcast_to(jnp.sum(product * gain, axis=1, keepdims=True), stats.shape[1:])
    grad[:, columns] = back * gain

    @pl.when(step == pl.num_programs(0) - 1)
    def _():
        mean = stats[1, :, 0:1] / grad.shape[1]
        held = held_ref[0].astype(jnp.float32)
        dinput_ref[...] = (inv_rms * (grad[...] - held * inv_rms * mean)).astype(jnp.bfloat16)


def project_kernel(early_ref, late_ref, gain_ref, weight_ref, terms_ref, out_ref, update_ref):
    features = gain_ref.shape[1]
    arrived = jnp.concatenate([early_ref[...], late_ref[...]], axis=0).astype(jnp.float32)
    mean = jnp.sum(arrived * arrived, axis=1, keepdims=True) / features
    normed = (arrived * lax.rsqrt(mean + EPS_NORM) * gain_ref[...]).astype(jnp.bfloat16)
    out_ref[...] = dot_nn(normed, weight_ref[...]).astype(jnp.bfloat16)
    total = jnp.sum(terms_ref[...], axis=0, keepdims=True)
    mean = jnp.sum(total * total, axis=1, keepdims=True) / features
    update_ref[...] = total / jnp.sqrt(mean + EPS_STEP)


def cost(flops, read, exps=0):
    return pl.CostEstimate(flops=flops, bytes_accessed=read, transcendentals=exps)


SMEM = pl.BlockSpec(memory_space=pltpu.SMEM)
VMEM = pl.BlockSpec(memory_space=pltpu.VMEM)


def attend_own(queries, keys, values, offsets, steps):
    rows, width = queries.shape
    half, block = rows // 2, width // steps
    shard = pl.BlockSpec((rows, block), lambda i: (0, i))
    return pl.pallas_call(
        functools.partial(own_kernel, rows),
        grid=(steps,),
        in_specs=[SMEM, shard, shard, shard],
        out_specs=[
            pl.BlockSpec((half // POOL, block), lambda i: (0, i)),
            pl.BlockSpec((block, half), lambda i: (i, 0)),
            pl.BlockSpec((2, block), lambda i: (0, i)),
        ],
        out_shape=[
            jax.ShapeDtypeStruct((half // POOL, width), jnp.bfloat16),
            jax.ShapeDtypeStruct((width, half), jnp.bfloat16),
            jax.ShapeDtypeStruct((2, width), jnp.float32),
        ],
        scratch_shapes=[
            pltpu.VMEM((half, half), jnp.float32),
            pltpu.VMEM((rows, half), jnp.float32),
        ],
        cost_estimate=cost(12 * half * half * width, 6 * rows * width, 3 * half * half * width // 64),
        compiler_params=pltpu.CompilerParams(vmem_limit_bytes=24 * 2**20),
        name="attend_own",
    )(offsets, queries, keys, values)


def attend_halo(queries, keys, values, lse, offsets, steps):
    half, width = queries.shape
    rows, block = 2 * half, width // steps
    shard = pl.BlockSpec((half, block), lambda i: (0, i))
    tail = pl.BlockSpec((half, block), lambda i: (1, i))
    return pl.pallas_call(
        functools.partial(halo_kernel, rows),
        grid=(steps,),
        in_specs=[SMEM, shard, tail, tail, pl.BlockSpec((2, block), lambda i: (0, i))],
        out_specs=pl.BlockSpec((half // POOL + 16, block), lambda i: (0, i)),
        out_shape=jax.ShapeDtypeStruct((half // POOL + 16, width), jnp.bfloat16),
        scratch_shapes=[pltpu.VMEM((half, half), jnp.float32)],
        cost_estimate=cost(4 * half * half * width, 6 * half * width, half * half * width // 64),
        compiler_params=pltpu.CompilerParams(vmem_limit_bytes=24 * 2**20),
        name="attend_halo",
    )(offsets, queries, keys, values, lse)


def combine(early, halo):
    width, half = early.shape
    return pl.pallas_call(
        combine_kernel,
        in_specs=[VMEM, VMEM],
        out_specs=VMEM,
        out_shape=jax.ShapeDtypeStruct((half // POOL, width), jnp.bfloat16),
        cost_estimate=cost(half * half * width, 2 * half * width),
        name="combine",
    )(early, halo)


def backward(slot, cotangent, weight, gain, stashed, steps):
    rows, depth = cotangent.shape
    width = weight.shape[0]
    return pl.pallas_call(
        back_kernel,
        grid_spec=pltpu.PrefetchScalarGridSpec(
            num_scalar_prefetch=1,
            grid=(steps,),
            in_specs=[
                pl.BlockSpec((rows, depth), lambda i, slot: (0, 0)),
                pl.BlockSpec((width // steps, depth), lambda i, slot: (i, 0)),
                pl.BlockSpec((1, width), lambda i, slot: (0, 0)),
                pl.BlockSpec((1, rows, width), lambda i, slot: (slot[0], 0, 0)),
            ],
            out_specs=[
                pl.BlockSpec((rows, width), lambda i, slot: (0, 0)),
                pl.BlockSpec((1, width), lambda i, slot: (0, 0)),
            ],
            scratch_shapes=[
                pltpu.VMEM((rows, width), jnp.float32),
                pltpu.VMEM((2, rows, LANES), jnp.float32),
            ],
        ),
        out_shape=[
            jax.ShapeDtypeStruct((rows, width), jnp.bfloat16),
            jax.ShapeDtypeStruct((1, width), jnp.float32),
        ],
        cost_estimate=cost(2 * rows * width * depth, 2 * width * depth),
        compiler_params=pltpu.CompilerParams(vmem_limit_bytes=24 * 2**20),
        name="backward",
    )(slot, cotangent, weight, gain, stashed)


def project(early, late, gain, weight, terms):
    rows = early.shape[0] + late.shape[0]
    width, depth = weight.shape
    return pl.pallas_call(
        project_kernel,
        in_specs=[VMEM] * 5,
        out_specs=[VMEM] * 2,
        out_shape=[
            jax.ShapeDtypeStruct((rows, depth), jnp.bfloat16),
            jax.ShapeDtypeStruct((1, width), jnp.float32),
        ],
        cost_estimate=cost(2 * rows * width * depth, 2 * width * depth),
        compiler_params=pltpu.CompilerParams(vmem_limit_bytes=24 * 2**20),
        name="project",
    )(early, late, gain, weight, terms)


def local(queries, keys, values, doc_starts, weight, gain, stashed, cotangent, slot):
    queries, keys, values, offsets = queries[0, 0], keys[0, 0], values[0, 0], doc_starts[0]
    half = queries.shape[0] // 2
    next_queries = shifted(queries[:half], "seq", -1)
    late, early, lse = attend_own(queries, keys, values, offsets, 4)
    next_lse = shifted(lse, "seq", -1)
    late_arrived = passed_along(late, "section", 1)
    dinput, term = backward(slot[0], cotangent[0, 0], weight[0], gain, stashed[0, 0], 4)
    upstream = passed_along(dinput, "section", -1)
    terms = lax.all_gather(term, ("rep", "seq"), axis=0, tiled=True)
    halo = shifted(attend_halo(next_queries, keys, values, next_lse, offsets, 2), "seq", 1)
    early_arrived = passed_along(combine(early, halo), "section", 1)
    mol_keys, update = project(early_arrived, late_arrived, gain, weight[0], terms)
    return mol_keys[None, None], upstream[None, None], update


def solution(mesh):
    in_specs = (
        P("rep", "section", "seq", None),
        P("rep", "section", "seq", None),
        P("rep", "section", "seq", None),
        P("rep", "section", None),
        P("section", None, None),
        P("section", None),
        P("rep", "section", None, "seq", None),
        P("rep", "section", "seq", None),
        P("rep", "section"),
    )
    out_specs = (
        P("rep", "section", "seq", None),
        P("rep", "section", "seq", None),
        P("section", None),
    )
    return jax.shard_map(local, mesh=mesh, in_specs=in_specs, out_specs=out_specs, check_vma=False)
```

time: 123 us -> 77.2 us (0.63)
  waiting for transfers between devices: 39.4 us -> 5.98 us
  Pallas kernels: 0 us -> 20.5 us
  matrix products: 16 us -> 0 us
  other arithmetic: 14 us -> 0 us
  blocking collectives: 16.4 us -> 23.8 us
  local copies, waits for them, and re-layouts: 19.1 us -> 13.5 us
  loops' own time: 2.71 us -> 0 us
    ppermute x4 -> x6, waiting for transfers between devices: 39.4 us -> 5.98 us  [the longest x3 5.97 us: shifted(): lax.ppermute(value, axis, [(i, i + steps) for i in range(first, last)])]
    all_gather x0 -> x1, blocking collectives: none -> 23.8 us  [local(): terms = lax.all_gather(term, ('rep', 'seq'), axis=0, tiled=True)]
    pallas_call x0 -> x5, Pallas kernels: none -> 20.5 us  [the longest x1 9.54 us: attend_own(): pl.pallas_call(functools.partial(own_kernel, rows), grid=(steps,), in_spe...]
    psum x1 -> x0, blocking collectives: 16.4 us -> none  [local(): summed = lax.psum(gain_term, ('seq', 'rep'))]
    dot_general x10 -> x0, matrix products: 16 us -> none  [the longest x4 4.86 us: one_group(): jnp.einsum('hqk,khd->qhd', rounded, group_values, preferred_element_type=...]
    reduce_sum x10 -> x0, other arithmetic: 7.65 us -> none  [the longest x4 5.24 us: one_group(): row_total = jnp.sum(weights, axis=2, keepdims=True)]
    dynamic_slice x12 -> x0, local copies, waits for them, and re-layouts: 6.91 us -> none  [the longest x4 4.47 us: one_group(): lax.dynamic_slice_in_dim(keys_all, group_start, group_width, 1)]
    unnamed x16 -> x28, local copies, waits for them, and re-layouts: 6.03 us -> 12.3 us
  transfers between devices with their start and end apart: 4 -> 6, of which waited for: 3 -> 1; matrix products, arithmetic and copies ran while one was open for 9% -> 0% of each run, Pallas kernels for 0% -> 18%
where the time goes in v1:
time: 77.2 us; the launch traced here: 76.7 us
  blocking collectives  23.8 us (31%)
  Pallas kernels  20.5 us (27%)
  local copies, waits for them, and re-layouts  13.5 us (17%)
  starting transfers between devices  11.5 us (15%)
  waiting for transfers between devices  5.98 us (8%)
  between operations  1.41 us (2%)
    all_gather x1, blocking collectives, local(): terms = lax.all_gather(term, ('rep', 'seq'), axis=0, tiled=True)  23.8 us
    unnamed x28, local copies, waits for them, and re-layouts  12.3 us
    pallas_call x1, Pallas kernels, attend_own(): pl.pallas_call(functools.partial(own_kernel, rows), grid=(steps,), in_spe...  9.54 us
    ppermute x3, starting transfers between devices, shifted(): lax.ppermute(value, axis, [(i, i + steps) for i in range(first, last)])  6.64 us
    ppermute x3, waiting for transfers between devices, shifted(): lax.ppermute(value, axis, [(i, i + steps) for i in range(first, last)])  5.97 us
    ppermute x3, starting transfers between devices, passed_along(): lax.ppermute(value, axis, [(i, (i + steps) % count) for i in range(count)])  4.91 us
    pallas_call x1, Pallas kernels, attend_halo(): pl.pallas_call(functools.partial(halo_kernel, rows), grid=(steps,), in_sp...  4.79 us
    pallas_call x1, Pallas kernels, backward(): pl.pallas_call(back_kernel, grid_spec=pltpu.PrefetchScalarGridSpec(num_sc...  2.41 us
  transfers between devices with their start and end apart: 6, of which 1 were waited for; matrix products, arithmetic and copies ran while one was open for 0% of the time, Pallas kernels for 18%

profile of v1, /device:TPU:0, one launch (start us, length us, event | category | flops | bytes accessed | tf_op | source)
XLA Modules:
  0.0 76.7 jit_solution(8533784812432225644)
XLA Ops:
  0.6 0.0 copy-start
  0.6 1.2 %slice_bitcast_fusion = bf16[128,2048]{1,0:T(8,128)(2,1)S(1)} fusion(bf16[1,1,256,2048]{3,2,1,0:T(8,128)(2,1)} %param.9), kind=kLoop, calls=%fused_computation | loop fusion | bytes 1048576 | tf_op jit(solution)/shard_map/slice | solution.py:335
  1.9 1.4 %collective-permute-start = (bf16[128,2048]{1,0:T(8,128)(2,1)S(1)}, bf16[128,2048]{1,0:T(8,128)(2,1)S(1)}, u32[]{:S(2)}, u32[]{:S(2)}) collective-permute-start(bf16[128,2048]{1,0:T(8,128)(2,1)S(1)} %slice_bitcast_fusion), channel_id=1, source_target_pairs={{2,0},{4,2},{6,4},{3,1},{5,3},{7,5},{10,8},{12,10},{14,12},{11,9},... | collective-permute-start | bytes 1572872 | tf_op jit(solution)/shard_map/ppermute | solution.py:33
  3.3 0.0 copy-start.2
  3.3 1.2 %copy-done.2 = bf16[1,1,256,2048]{3,2,1,0:T(8,128)(2,1)S(1)} copy-done((bf16[1,1,256,2048]{3,2,1,0:T(8,128)(2,1)S(1)}, bf16[1,1,256,2048]{3,2,1,0:T(8,128)(2,1)}, u32[]{:S(2)}) %copy-start.2) | copy-done | bytes 1048600
  4.5 0.0 copy-start.4
  4.5 1.2 %copy-done.4 = bf16[1,1,256,2048]{3,2,1,0:T(8,128)(2,1)S(1)} copy-done((bf16[1,1,256,2048]{3,2,1,0:T(8,128)(2,1)S(1)}, bf16[1,1,256,2048]{3,2,1,0:T(8,128)(2,1)}, u32[]{:S(2)}) %copy-start.4) | copy-done | bytes 1048600
  5.8 0.0 copy-start.6
  5.8 1.2 %copy-done.6 = bf16[1,1,256,2048]{3,2,1,0:T(8,128)(2,1)S(1)} copy-done((bf16[1,1,256,2048]{3,2,1,0:T(8,128)(2,1)S(1)}, bf16[1,1,256,2048]{3,2,1,0:T(8,128)(2,1)}, u32[]{:S(2)}) %copy-start.6) | copy-done | bytes 1048600
  7.0 0.0 copy-start.11
  7.0 0.7 copy-done.11
  7.6 0.0 copy-start.10
  7.6 9.5 %attend_own.1 = (bf16[32,2048]{1,0:T(8,128)(2,1)S(1)}, bf16[2048,128]{1,0:T(8,128)(2,1)S(1)}, f32[2,2048]{1,0:T(2,128)S(1)}) custom-call(s32[1,8]{1,0:T(1,128)S(1)} %bitcast.28, bf16[256,2048]{1,0:T(8,128)(2,1)S(1)} %bitcast.23, bf16[256,2048]{1,0:T(8,128)(2,1)S(1)} %bitcast.19, bf16[256,2048]{1,0:T(8,128)(2,1)S(1)} %bitcast.21), custom_call_target="tpu_custom_call" | custom-call | flops 402653184 | bytes 3145728 | tf_op jit(solution)/shard_map/attend_own/pallas_call | solution.py:228
  17.2 0.0 copy-start.8
  17.2 1.3 %collective-permute-start.1 = (f32[2,2048]{1,0:T(2,128)S(1)}, f32[2,2048]{1,0:T(2,128)S(1)}, u32[]{:S(2)}, u32[]{:S(2)}) collective-permute-start(f32[2,2048]{1,0:T(2,128)S(1)} %get-tuple-element.11), channel_id=1, source_target_pairs={{2,0},{4,2},{6,4},{3,1},{5,3},{7,5},{10,8},{12,10},{14,12},{11,9},... | collective-permute-start | bytes 49160 | tf_op jit(solution)/shard_map/ppermute | solution.py:33
  18.5 6.0 %collective-permute-done.1.lse_ref = f32[2,2048]{1,0:T(2,128)S(1)} collective-permute-done((f32[2,2048]{1,0:T(2,128)S(1)}, f32[2,2048]{1,0:T(2,128)S(1)}, u32[]{:S(2)}, u32[]{:S(2)}) %collective-permute-start.1) | collective-permute-done | bytes 16416 | tf_op jit(solution)/shard_map/ppermute | solution.py:33
  24.5 0.0 collective-permute-done.q_ref
  24.5 0.0 copy-start.3
  24.5 1.2 %copy-done.3 = bf16[1,1,256,2048]{3,2,1,0:T(8,128)(2,1)S(1)} copy-done((bf16[1,1,256,2048]{3,2,1,0:T(8,128)(2,1)S(1)}, bf16[1,1,256,2048]{3,2,1,0:T(8,128)(2,1)}, u32[]{:S(2)}) %copy-start.3) | copy-done | bytes 1048600
  25.7 0.0 copy-start.5
  25.7 1.2 %copy-done.5 = bf16[1,1,256,2048]{3,2,1,0:T(8,128)(2,1)S(1)} copy-done((bf16[1,1,256,2048]{3,2,1,0:T(8,128)(2,1)S(1)}, bf16[1,1,256,2048]{3,2,1,0:T(8,128)(2,1)}, u32[]{:S(2)}) %copy-start.5) | copy-done | bytes 1048600
  26.9 4.8 %attend_halo.1 = bf16[48,2048]{1,0:T(8,128)(2,1)S(1)} custom-call(s32[1,8]{1,0:T(1,128)S(1)} %bitcast.29, bf16[128,2048]{1,0:T(8,128)(2,1)S(1)} %collective-permute-done.q_ref, bf16[256,2048]{1,0:T(8,128)(2,1)S(1)} %bitcast.20, bf16[256,2048]{1,0:T(8,128)(2,1)S(1)} %bitcast.22, f32[2,2048]{1,0:T(2,128)S(1)} %collective-permute-done.1.lse_ref), custom_call_target="tpu_custom_call" | custom-call | flops 134217728 | bytes 1572864 | tf_op jit(solution)/shard_map/attend_halo/pallas_call | solution.py:257
  31.7 3.9 %collective-permute-start.2 = (bf16[48,2048]{1,0:T(8,128)(2,1)S(1)}, bf16[48,2048]{1,0:T(8,128)(2,1)S(1)}, u32[]{:S(2)}, u32[]{:S(2)}) collective-permute-start(bf16[48,2048]{1,0:T(8,128)(2,1)S(1)} %attend_halo.1), channel_id=1, source_target_pairs={{0,2},{2,4},{4,6},{1,3},{3,5},{5,7},{8,10},{10,12},{12,14},{9,11},... | collective-permute-start | bytes 589832 | tf_op jit(solution)/shard_map/ppermute | solution.py:33
  36.3 0.0 copy-done
  36.3 0.0 copy-done.10
  36.3 0.0 copy-start.7
  36.3 1.0 %copy-done.7 = bf16[1,1,2,64,2048]{4,3,2,1,0:T(8,128)(2,1)S(1)} copy-done((bf16[1,1,2,64,2048]{4,3,2,1,0:T(8,128)(2,1)S(1)}, bf16[1,1,2,64,2048]{4,3,2,1,0:T(8,128)(2,1)}, u32[]{:S(2)}) %copy-start.7) | copy-done | bytes 524312
  37.3 0.0 copy-start.9
  37.3 0.9 %copy-done.9 = bf16[1,1,64,1024]{3,2,1,0:T(8,128)(2,1)S(1)} copy-done((bf16[1,1,64,1024]{3,2,1,0:T(8,128)(2,1)S(1)}, bf16[1,1,64,1024]{3,2,1,0:T(8,128)(2,1)}, u32[]{:S(2)}) %copy-start.9) | copy-done | bytes 131096
  38.2 2.4 %backward.1 = (bf16[64,2048]{1,0:T(8,128)(2,1)S(1)}, f32[1,2048]{1,0:T(1,128)S(1)}) custom-call(s32[1]{0:T(128)} %bitcast.16.slot_ref, bf16[64,1024]{1,0:T(8,128)(2,1)S(1)} %bitcast.26, bf16[2048,1024]{1,0:T(8,128)(2,1)S(1)} %bitcast.17, f32[1,2048]{1,0:T(1,128)S(1)} %copy-done.10, bf16[2,64,2048]{2,1,0:T(8,128)(2,1)S(1)} %bitcast.24), custom_call_target="tpu_custom_call" | custom-call | flops 268435456 | bytes 4194304 | tf_op jit(solution)/shard_map/backward/pallas_call | solution.py:285
  40.7 0.0 copy-done.8
  40.7 2.9 %collective-permute-start.5 = (bf16[64,2048]{1,0:T(8,128)(2,1)S(1)}, bf16[64,2048]{1,0:T(8,128)(2,1)S(1)}, u32[]{:S(2)}, u32[]{:S(2)}) collective-permute-start(bf16[64,2048]{1,0:T(8,128)(2,1)S(1)} %get-tuple-element.15), channel_id=1, source_target_pairs={{0,24},{8,0},{16,8},{24,16},{1,25},{9,1},{17,9},{25,17},{2,26},{10... | collective-permute-start | bytes 786440 | tf_op jit(solution)/shard_map/ppermute | solution.py:38
  43.6 0.0 collective-permute-start.4
  43.6 0.0 collective-permute-done.2.halo_ref
  43.6 0.0 copy-start.12
  43.6 0.7 copy-done.12
  44.3 2.1 %combine.1 = bf16[32,2048]{1,0:T(8,128)(2,1)} custom-call(bf16[2048,128]{1,0:T(8,128)(2,1)} %copy-done.8, bf16[48,2048]{1,0:T(8,128)(2,1)} %copy-done.12), custom_call_target="tpu_custom_call" | custom-call | flops 33554432 | bytes 524288 | tf_op jit(solution)/shard_map/combine/pallas_call | solution.py:272
  46.4 2.0 %collective-permute-start.3 = (bf16[32,2048]{1,0:T(8,128)(2,1)}, bf16[32,2048]{1,0:T(8,128)(2,1)S(1)}, u32[]{:S(2)}, u32[]{:S(2)}) collective-permute-start(bf16[32,2048]{1,0:T(8,128)(2,1)} %combine.1), channel_id=1, source_target_pairs={{0,8},{8,16},{16,24},{24,0},{1,9},{9,17},{17,25},{25,1},{2,10},{10... | collective-permute-start | bytes 393224 | tf_op jit(solution)/shard_map/ppermute | solution.py:38
  48.4 23.8 %all-gather = f32[8,1,2048]{2,1,0:T(1,128)S(1)} all-gather(f32[1,1,2048]{2,1,0:T(1,128)S(1)} %bitcast.27), channel_id=1, replica_groups=mesh['section'=4,'seq'=4,'rep'=2] {'rep','seq'}, dimensions={0}, use_global_device_ids=true | all-gather | bytes 73728 | tf_op jit(solution)/shard_map/all_gather | solution.py:341
  72.2 0.0 collective-permute-done.5
  72.2 0.0 collective-permute-done.4.late_ref
  72.2 0.0 collective-permute-done.3.early_ref
  72.2 0.0 copy-start.1
  72.3 2.2 %copy-done.1 = bf16[1,2048,1024]{2,1,0:T(8,128)(2,1)S(1)} copy-done((bf16[1,2048,1024]{2,1,0:T(8,128)(2,1)S(1)}, bf16[1,2048,1024]{2,1,0:T(8,128)(2,1)}, u32[]{:S(2)}) %copy-start.1) | copy-done | bytes 4194328
  74.4 1.6 %project.1 = (bf16[64,1024]{1,0:T(8,128)(2,1)}, f32[1,2048]{1,0:T(1,128)}) custom-call(bf16[32,2048]{1,0:T(8,128)(2,1)S(1)} %collective-permute-done.3.early_ref, bf16[32,2048]{1,0:T(8,128)(2,1)S(1)} %collective-permute-done.4.late_ref, f32[1,2048]{1,0:T(1,128)S(1)} %copy-done.10, bf16[2048,1024]{1,0:T(8,128)(2,1)S(1)} %bitcast.18, f32[8,2048]{1,0:T(8,128)S(1)} %bitcast.25), custom_call_target="tpu_custom_call" | custom-call | flops 268435456 | bytes 4194304 | tf_op jit(solution)/shard_map/project/pallas_call | solution.py:318
  76.0 0.7 copy.17
  (1 shorter events, 0.0 us)
Async XLA Ops:
  0.6 35.7 %copy-start = (bf16[1,2048,1024]{2,1,0:T(8,128)(2,1)S(1)}, bf16[1,2048,1024]{2,1,0:T(8,128)(2,1)}, u32[]{:S(2)}) copy-start(bf16[1,2048,1024]{2,1,0:T(8,128)(2,1)} %param.13) | copy-start | bytes 12582916
  1.9 22.6 %collective-permute-start = (bf16[128,2048]{1,0:T(8,128)(2,1)S(1)}, bf16[128,2048]{1,0:T(8,128)(2,1)S(1)}, u32[]{:S(2)}, u32[]{:S(2)}) collective-permute-start(bf16[128,2048]{1,0:T(8,128)(2,1)S(1)} %slice_bitcast_fusion), channel_id=1, source_target_pairs={{2,0},{4,2},{6,4},{3,1},{5,3},{7,5},{10,8},{12,10},{14,12},{11,9},... | collective-permute-start | bytes 1572872 | tf_op jit(solution)/shard_map/ppermute | solution.py:33
  3.3 1.2 %copy-start.2 = (bf16[1,1,256,2048]{3,2,1,0:T(8,128)(2,1)S(1)}, bf16[1,1,256,2048]{3,2,1,0:T(8,128)(2,1)}, u32[]{:S(2)}) copy-start(bf16[1,1,256,2048]{3,2,1,0:T(8,128)(2,1)} %param.10) | copy-start | bytes 3145732
  4.5 1.2 %copy-start.4 = (bf16[1,1,256,2048]{3,2,1,0:T(8,128)(2,1)S(1)}, bf16[1,1,256,2048]{3,2,1,0:T(8,128)(2,1)}, u32[]{:S(2)}) copy-start(bf16[1,1,256,2048]{3,2,1,0:T(8,128)(2,1)} %param.11) | copy-start | bytes 3145732
  5.8 1.2 %copy-start.6 = (bf16[1,1,256,2048]{3,2,1,0:T(8,128)(2,1)S(1)}, bf16[1,1,256,2048]{3,2,1,0:T(8,128)(2,1)}, u32[]{:S(2)}) copy-start(bf16[1,1,256,2048]{3,2,1,0:T(8,128)(2,1)} %param.9) | copy-start | bytes 3145732
  7.0 0.7 copy-start.11
  7.6 28.7 %copy-start.10 = (f32[1,2048]{1,0:T(1,128)S(1)}, f32[1,2048]{1,0:T(1,128)}, u32[]{:S(2)}) copy-start(f32[1,2048]{1,0:T(1,128)} %gain_ref.3) | copy-start | bytes 24580
  17.2 23.5 %copy-start.8 = (bf16[2048,128]{1,0:T(8,128)(2,1)}, bf16[2048,128]{1,0:T(8,128)(2,1)S(1)}, u32[]{:S(2)}) copy-start(bf16[2048,128]{1,0:T(8,128)(2,1)S(1)} %get-tuple-element.10.early_ref) | copy-start | bytes 1572868
  17.2 7.3 %collective-permute-start.1 = (f32[2,2048]{1,0:T(2,128)S(1)}, f32[2,2048]{1,0:T(2,128)S(1)}, u32[]{:S(2)}, u32[]{:S(2)}) collective-permute-start(f32[2,2048]{1,0:T(2,128)S(1)} %get-tuple-element.11), channel_id=1, source_target_pairs={{2,0},{4,2},{6,4},{3,1},{5,3},{7,5},{10,8},{12,10},{14,12},{11,9},... | collective-permute-start | bytes 49160 | tf_op jit(solution)/shard_map/ppermute | solution.py:33
  24.5 1.2 %copy-start.3 = (bf16[1,1,256,2048]{3,2,1,0:T(8,128)(2,1)S(1)}, bf16[1,1,256,2048]{3,2,1,0:T(8,128)(2,1)}, u32[]{:S(2)}) copy-start(bf16[1,1,256,2048]{3,2,1,0:T(8,128)(2,1)} %param.10) | copy-start | bytes 3145732
  25.7 1.2 %copy-start.5 = (bf16[1,1,256,2048]{3,2,1,0:T(8,128)(2,1)S(1)}, bf16[1,1,256,2048]{3,2,1,0:T(8,128)(2,1)}, u32[]{:S(2)}) copy-start(bf16[1,1,256,2048]{3,2,1,0:T(8,128)(2,1)} %param.11) | copy-start | bytes 3145732
  31.7 11.9 %collective-permute-start.2 = (bf16[48,2048]{1,0:T(8,128)(2,1)S(1)}, bf16[48,2048]{1,0:T(8,128)(2,1)S(1)}, u32[]{:S(2)}, u32[]{:S(2)}) collective-permute-start(bf16[48,2048]{1,0:T(8,128)(2,1)S(1)} %attend_halo.1), channel_id=1, source_target_pairs={{0,2},{2,4},{4,6},{1,3},{3,5},{5,7},{8,10},{10,12},{12,14},{9,11},... | collective-permute-start | bytes 589832 | tf_op jit(solution)/shard_map/ppermute | solution.py:33
  36.3 1.0 %copy-start.7 = (bf16[1,1,2,64,2048]{4,3,2,1,0:T(8,128)(2,1)S(1)}, bf16[1,1,2,64,2048]{4,3,2,1,0:T(8,128)(2,1)}, u32[]{:S(2)}) copy-start(bf16[1,1,2,64,2048]{4,3,2,1,0:T(8,128)(2,1)} %param.15) | copy-start | bytes 1572868
  37.3 0.9 %copy-start.9 = (bf16[1,1,64,1024]{3,2,1,0:T(8,128)(2,1)S(1)}, bf16[1,1,64,1024]{3,2,1,0:T(8,128)(2,1)}, u32[]{:S(2)}) copy-start(bf16[1,1,64,1024]{3,2,1,0:T(8,128)(2,1)} %param.16) | copy-start | bytes 393220
  40.7 31.5 %collective-permute-start.5 = (bf16[64,2048]{1,0:T(8,128)(2,1)S(1)}, bf16[64,2048]{1,0:T(8,128)(2,1)S(1)}, u32[]{:S(2)}, u32[]{:S(2)}) collective-permute-start(bf16[64,2048]{1,0:T(8,128)(2,1)S(1)} %get-tuple-element.15), channel_id=1, source_target_pairs={{0,24},{8,0},{16,8},{24,16},{1,25},{9,1},{17,9},{25,17},{2,26},{10... | collective-permute-start | bytes 786440 | tf_op jit(solution)/shard_map/ppermute | solution.py:38
  43.6 28.6 %collective-permute-start.4 = (bf16[32,2048]{1,0:T(8,128)(2,1)S(1)}, bf16[32,2048]{1,0:T(8,128)(2,1)S(1)}, u32[]{:S(2)}, u32[]{:S(2)}) collective-permute-start(bf16[32,2048]{1,0:T(8,128)(2,1)S(1)} %get-tuple-element.12), channel_id=1, source_target_pairs={{0,8},{8,16},{16,24},{24,0},{1,9},{9,17},{17,25},{25,1},{2,10},{10... | collective-permute-start | bytes 393224 | tf_op jit(solution)/shard_map/ppermute | solution.py:38
  43.6 0.7 copy-start.12
  46.4 25.8 %collective-permute-start.3 = (bf16[32,2048]{1,0:T(8,128)(2,1)}, bf16[32,2048]{1,0:T(8,128)(2,1)S(1)}, u32[]{:S(2)}, u32[]{:S(2)}) collective-permute-start(bf16[32,2048]{1,0:T(8,128)(2,1)} %combine.1), channel_id=1, source_target_pairs={{0,8},{8,16},{16,24},{24,0},{1,9},{9,17},{17,25},{25,1},{2,10},{10... | collective-permute-start | bytes 393224 | tf_op jit(solution)/shard_map/ppermute | solution.py:38
  72.2 2.2 %copy-start.1 = (bf16[1,2048,1024]{2,1,0:T(8,128)(2,1)S(1)}, bf16[1,2048,1024]{2,1,0:T(8,128)(2,1)}, u32[]{:S(2)}) copy-start(bf16[1,2048,1024]{2,1,0:T(8,128)(2,1)} %param.13) | copy-start | bytes 12582916

commit v2 on v1

v2 whole, which is shorter than its diff:
```python
import functools
import math

import jax
import jax.numpy as jnp
from jax import lax
from jax.experimental import pallas as pl
from jax.experimental.pallas import tpu as pltpu
from jax.sharding import PartitionSpec as P

HEAD_DIM = 64
POOL = 4
WINDOW = 128
LANES = 128
EPS_NORM = 1e-05
EPS_STEP = 1e-06
MASKED = -1e30
AHEAD = 2

NT = (((1,), (1,)), ((), ()))


def dot_nt(a, b):
    return lax.dot_general(a, b, NT, preferred_element_type=jnp.float32)


def dot_nn(a, b):
    return jnp.dot(a, b, preferred_element_type=jnp.float32)


def shifted(value, axis, steps):
    count = lax.axis_size(axis)
    first, last = max(0, -steps), min(count, count - steps)
    return lax.ppermute(value, axis, [(i, i + steps) for i in range(first, last)])


def passed_along(value, axis, steps):
    count = lax.axis_size(axis)
    return lax.ppermute(value, axis, [(i, (i + steps) % count) for i in range(count)])


def earliest_key(offsets_ref, query_pos):
    start = jnp.zeros_like(query_pos)
    for d in range(offsets_ref.shape[1]):
        offset = offsets_ref[0, d]
        start = jnp.where(query_pos >= offset, offset, start)
    return jnp.maximum(start, query_pos - (WINDOW - 1))


def mask_bias(offsets_ref, key_start, key_count, query_start, query_count):
    query_pos = query_start + lax.broadcasted_iota(jnp.int32, (1, query_count), 1)
    lowest = earliest_key(offsets_ref, query_pos)
    key_pos = key_start + lax.broadcasted_iota(jnp.int32, (key_count, query_count), 0)
    allowed = (key_pos >= lowest) & (key_pos <= query_pos)
    return jnp.where(allowed, 0.0, MASKED).astype(jnp.float32)


def split_heads(queries):
    lane = lax.broadcasted_iota(jnp.int32, (1, LANES), 1)
    scale = 1.0 / math.sqrt(HEAD_DIM)
    first = jnp.where(lane < HEAD_DIM, scale, 0.0).astype(jnp.bfloat16)
    second = jnp.where(lane < HEAD_DIM, 0.0, scale).astype(jnp.bfloat16)
    return jnp.concatenate([queries * first, queries * second], axis=0)


def pool_matrix(queries):
    molecule = lax.broadcasted_iota(jnp.int32, (queries // POOL, queries), 0)
    query = lax.broadcasted_iota(jnp.int32, (queries // POOL, queries), 1)
    return jnp.where(query // POOL == molecule, 1.0 / POOL, 0.0).astype(jnp.bfloat16)


def own_heads(mixed, scale):
    count = mixed.shape[1] // 2
    return jnp.concatenate(
        [
            mixed[:HEAD_DIM, :count] * scale[:, :count],
            mixed[HEAD_DIM:, count:] * scale[:, count:],
        ],
        axis=0,
    )


def twice(bias):
    return jnp.concatenate([bias, bias], axis=1)


def softmax_parts(scores):
    top = jnp.max(scores, axis=0, keepdims=True)
    weights = jnp.exp(scores - top)
    total = jnp.sum(weights, axis=0, keepdims=True)
    return top, weights.astype(jnp.bfloat16), total


def load(source, target, sem):
    copy = pltpu.make_async_copy(source, target, sem)
    copy.start()
    return copy


def own_kernel(
    rows, chunks, offsets_hbm, q_hbm, k_hbm, v_hbm, late_ref, early_ref, lse_ref,
    offsets_ref, q_ref, k_ref, v_ref, bias0, bias1, sems, offsets_sem,
):
    half = rows // 2
    block = q_ref.shape[1] // chunks
    offsets_copy = load(offsets_hbm, offsets_ref, offsets_sem)
    arrays = ((k_hbm, k_ref), (q_hbm, q_ref), (v_hbm, v_ref))
    for chunk in range(chunks):
        columns = pl.ds(chunk * block, block)
        for i, (source, target) in enumerate(arrays):
            load(source.at[:, columns], target.at[:, columns], sems.at[i, chunk])
    offsets_copy.wait()
    shard_start = lax.axis_index("seq") * rows
    bias0[...] = mask_bias(offsets_ref, shard_start, half, shard_start, half)
    bias1[...] = mask_bias(offsets_ref, shard_start, rows, shard_start + half, half)
    pooling = pool_matrix(half)

    @pl.loop(0, chunks)
    def _(chunk):
        begin = pl.multiple_of(chunk * block, block)
        whole = pl.ds(begin, block)
        for i, (source, target) in enumerate(arrays):
            pltpu.make_async_copy(source.at[:, whole], target.at[:, whole], sems.at[i, chunk]).wait()
        pairs = block // LANES

        def at(pair):
            return pl.ds(pl.multiple_of(begin + pair * LANES, LANES), LANES)

        def scores_of(pair):
            keys = k_ref[:, at(pair)]
            return (
                dot_nt(keys[:half], split_heads(q_ref[:half, at(pair)])),
                dot_nt(keys, split_heads(q_ref[half:, at(pair)])),
            )

        scores = {pair: scores_of(pair) for pair in range(min(AHEAD, pairs))}
        late = []
        for pair in range(pairs):
            if pair + AHEAD < pairs:
                scores[pair + AHEAD] = scores_of(pair + AHEAD)
            first, second = scores.pop(pair)
            values_t = jnp.transpose(v_ref[:, at(pair)])
            top, weights, total = softmax_parts(first + twice(bias0[...]))
            mixed = dot_nn(values_t[:, :half], weights)
            _, weights1, total1 = softmax_parts(second + twice(bias1[...]))
            mixed1 = dot_nn(values_t, weights1)
            early_ref[at(pair), :] = own_heads(mixed, 1.0 / total).astype(jnp.bfloat16)
            lse = top + jnp.log(total)
            lse_ref[0:1, at(pair)] = lse[:, :half]
            lse_ref[1:2, at(pair)] = lse[:, half:]
            late.append(own_heads(mixed1, 1.0 / total1).astype(jnp.bfloat16))
        late_ref[:, whole] = dot_nt(pooling, jnp.concatenate(late, axis=0)).astype(jnp.bfloat16)


def halo_kernel(
    rows, chunks, offsets_hbm, q_ref, k_hbm, v_hbm, lse_ref, term_ref, other_ref, *rest
):
    out_ref, sum_ref, offsets_ref, k_ref, v_ref, bias, sems, offsets_sem = rest[-8:]
    half = rows // 2
    block = q_ref.shape[1] // chunks
    offsets_copy = load(offsets_hbm, offsets_ref, offsets_sem)
    arrays = ((k_hbm, k_ref), (v_hbm, v_ref))
    copies = []
    for chunk in range(chunks):
        columns = pl.ds(chunk * block, block)
        for i, (source, target) in enumerate(arrays):
            tail = source.at[pl.ds(half, half), columns]
            copies.append(load(tail, target.at[:, columns], sems.at[i, chunk]))
    sum_ref[...] = term_ref[...] + other_ref[...]
    offsets_copy.wait()
    next_start = (lax.axis_index("seq") + 1) * rows
    bias[...] = mask_bias(offsets_ref, next_start - half, half, next_start, half)
    pooling = pool_matrix(half)
    molecules = half // POOL
    for copy in copies:
        copy.wait()
    pairs = q_ref.shape[1] // LANES

    def at(pair):
        return pl.ds(pair * LANES, LANES)

    def scores_of(pair):
        return dot_nt(k_ref[:, at(pair)], split_heads(q_ref[:, at(pair)]))

    scores = {pair: scores_of(pair) for pair in range(min(AHEAD, pairs))}
    parts = []
    for pair in range(pairs):
        if pair + AHEAD < pairs:
            scores[pair + AHEAD] = scores_of(pair + AHEAD)
        masked = scores.pop(pair) + twice(bias[...])
        lse = jnp.concatenate([lse_ref[0:1, at(pair)], lse_ref[1:2, at(pair)]], axis=1)
        top = jnp.maximum(jnp.max(masked, axis=0, keepdims=True), lse)
        weights = jnp.exp(masked - top)
        kept = jnp.exp(lse - top)
        inverse = 1.0 / (jnp.sum(weights, axis=0, keepdims=True) + kept)
        mixed = dot_nn(jnp.transpose(v_ref[:, at(pair)]), weights.astype(jnp.bfloat16))
        parts.append(own_heads(mixed, inverse).astype(jnp.bfloat16))
        share = kept * inverse
        high = share.astype(jnp.bfloat16).astype(jnp.float32)
        low = share - high
        out_ref[molecules:, at(pair)] = jnp.concatenate(
            [
                high[:, :half],
                low[:, :half],
                high[:, half:],
                low[:, half:],
                jnp.zeros((12, LANES), jnp.float32),
            ],
            axis=0,
        ).astype(jnp.bfloat16)
        if len(parts) == 4 or pair == pairs - 1:
            begin = (pair + 1 - len(parts)) * LANES
            pooled = dot_nt(pooling, jnp.concatenate(parts, axis=0)).astype(jnp.bfloat16)
            out_ref[:molecules, begin : (pair + 1) * LANES] = pooled
            parts = []


def combine_kernel(early_ref, halo_ref, term_ref, other_ref, out_ref, sum_ref):
    half = early_ref.shape[1]
    molecules = half // POOL
    pooling = pool_matrix(half)
    first = lax.axis_index("seq") == 0
    sum_ref[...] = term_ref[...] + other_ref[...]
    parts = []
    for pair in range(out_ref.shape[1] // LANES):
        columns = pl.ds(pair * LANES, LANES)
        shares = halo_ref[molecules:, columns].astype(jnp.float32)
        share_a = jnp.where(first, 1.0, shares[0:1] + shares[1:2])
        share_b = jnp.where(first, 1.0, shares[2:3] + shares[3:4])
        early = early_ref[columns, :].astype(jnp.float32)
        parts += [early[:HEAD_DIM] * share_a, early[HEAD_DIM:] * share_b]
        if len(parts) == 8:
            begin = (pair + 1) * LANES - 8 * HEAD_DIM
            columns = pl.ds(begin, 8 * HEAD_DIM)
            pooled = dot_nt(pooling, jnp.concatenate(parts, axis=0).astype(jnp.bfloat16))
            arrived = halo_ref[:molecules, columns].astype(jnp.float32)
            out_ref[:, columns] = (pooled + arrived).astype(jnp.bfloat16)
            parts = []


def back_kernel(
    slot_ref, cotangent_hbm, weight_ref, gain_ref, stashed_hbm, after_ref, dinput_ref, term_ref,
    cotangent_ref, held_ref, grad, sems,
):
    cotangent_copy = load(cotangent_hbm, cotangent_ref, sems.at[1])
    held_copy = load(stashed_hbm.at[slot_ref[0, 0]], held_ref, sems.at[0])
    cotangent_copy.wait()
    features = weight_ref.shape[0]
    block = 512
    for begin in range(0, features, block):
        columns = pl.ds(begin, block)
        grad[:, columns] = dot_nt(cotangent_ref[...], weight_ref[columns, :])
    held_copy.wait()
    held = held_ref[...].astype(jnp.float32)
    inv_rms = lax.rsqrt(jnp.sum(held * held, axis=1, keepdims=True) / features + EPS_NORM)
    along = jnp.zeros_like(inv_rms)
    for begin in range(0, features, block):
        columns = pl.ds(begin, block)
        product = grad[:, columns] * (held_ref[:, columns].astype(jnp.float32) * inv_rms)
        term_ref[:, columns] = jnp.sum(product, axis=0, keepdims=True)
        along += jnp.sum(product * gain_ref[:, columns], axis=1, keepdims=True)
    along = along / features
    for begin in range(0, features, block):
        columns = pl.ds(begin, block)
        whitened = held_ref[:, columns].astype(jnp.float32) * inv_rms
        scaled = grad[:, columns] * gain_ref[:, columns]
        dinput_ref[:, columns] = (inv_rms * (scaled - whitened * along)).astype(jnp.bfloat16)


def project_kernel(
    early_ref, late_ref, gain_ref, weight_ref, term_ref, other_ref, out_ref, update_ref
):
    features = gain_ref.shape[1]
    arrived = jnp.concatenate([early_ref[...], late_ref[...]], axis=0).astype(jnp.float32)
    mean = jnp.sum(arrived * arrived, axis=1, keepdims=True) / features
    normed = (arrived * lax.rsqrt(mean + EPS_NORM) * gain_ref[...]).astype(jnp.bfloat16)
    out_ref[...] = dot_nn(normed, weight_ref[...]).astype(jnp.bfloat16)
    total = term_ref[...] + other_ref[...]
    mean = jnp.sum(total * total, axis=1, keepdims=True) / features
    update_ref[...] = total / jnp.sqrt(mean + EPS_STEP)


def cost(flops, read, exps=0):
    return pl.CostEstimate(flops=flops, bytes_accessed=read, transcendentals=exps)


SMEM = pl.BlockSpec(memory_space=pltpu.SMEM)
HBM = pl.BlockSpec(memory_space=pltpu.HBM)
ANY = pl.BlockSpec(memory_space=pl.ANY)
VMEM = pl.BlockSpec(memory_space=pltpu.VMEM)


def in_hbm(*arrays):
    return [pltpu.with_memory_space_constraint(x, pltpu.HBM) for x in arrays]


def attend_own(queries, keys, values, offsets, chunks):
    rows, width = queries.shape
    half = rows // 2
    return pl.pallas_call(
        functools.partial(own_kernel, rows, chunks),
        in_specs=[HBM] * 4,
        out_specs=[VMEM] * 3,
        out_shape=[
            jax.ShapeDtypeStruct((half // POOL, width), jnp.bfloat16),
            jax.ShapeDtypeStruct((width, half), jnp.bfloat16),
            jax.ShapeDtypeStruct((2, width), jnp.float32),
        ],
        scratch_shapes=[
            pltpu.SMEM(offsets.shape, jnp.int32),
            pltpu.VMEM((rows, width), jnp.bfloat16),
            pltpu.VMEM((rows, width), jnp.bfloat16),
            pltpu.VMEM((rows, width), jnp.bfloat16),
            pltpu.VMEM((half, half), jnp.float32),
            pltpu.VMEM((rows, half), jnp.float32),
            pltpu.SemaphoreType.DMA((3, chunks)),
            pltpu.SemaphoreType.DMA,
        ],
        cost_estimate=cost(12 * half * half * width, 6 * rows * width, 3 * half * half * width // 64),
        compiler_params=pltpu.CompilerParams(vmem_limit_bytes=24 * 2**20),
        name="attend_own",
    )(*in_hbm(offsets, queries, keys, values))


def attend_halo(queries, keys, values, lse, offsets, term, other, after, chunks):
    half, width = queries.shape
    return pl.pallas_call(
        functools.partial(halo_kernel, 2 * half, chunks),
        in_specs=[HBM, VMEM, HBM, HBM, VMEM, VMEM, VMEM] + [ANY] * len(after),
        out_specs=[VMEM] * 2,
        out_shape=[
            jax.ShapeDtypeStruct((half // POOL + 16, width), jnp.bfloat16),
            jax.ShapeDtypeStruct(term.shape, term.dtype),
        ],
        scratch_shapes=[
            pltpu.SMEM(offsets.shape, jnp.int32),
            pltpu.VMEM((half, width), jnp.bfloat16),
            pltpu.VMEM((half, width), jnp.bfloat16),
            pltpu.VMEM((half, half), jnp.float32),
            pltpu.SemaphoreType.DMA((2, chunks)),
            pltpu.SemaphoreType.DMA,
        ],
        cost_estimate=cost(4 * half * half * width, 6 * half * width, half * half * width // 64),
        compiler_params=pltpu.CompilerParams(vmem_limit_bytes=24 * 2**20),
        name="attend_halo",
    )(*in_hbm(offsets), queries, *in_hbm(keys, values), lse, term, other, *after)


def combine(early, halo, term, other):
    width, half = early.shape
    return pl.pallas_call(
        combine_kernel,
        in_specs=[VMEM] * 4,
        out_specs=[VMEM] * 2,
        out_shape=[
            jax.ShapeDtypeStruct((half // POOL, width), jnp.bfloat16),
            jax.ShapeDtypeStruct(term.shape, term.dtype),
        ],
        cost_estimate=cost(half * half * width, 2 * half * width),
        compiler_params=pltpu.CompilerParams(vmem_limit_bytes=24 * 2**20),
        name="combine",
    )(early, halo, term, other)


def backward(slot, cotangent, weight, gain, stashed, after):
    rows, depth = cotangent.shape
    width = weight.shape[0]
    return pl.pallas_call(
        back_kernel,
        in_specs=[SMEM, HBM, VMEM, VMEM, HBM, ANY],
        out_specs=[VMEM] * 2,
        scratch_shapes=[
            pltpu.VMEM((rows, depth), jnp.bfloat16),
            pltpu.VMEM((rows, width), jnp.bfloat16),
            pltpu.VMEM((rows, width), jnp.float32),
            pltpu.SemaphoreType.DMA((2,)),
        ],
        out_shape=[
            jax.ShapeDtypeStruct((rows, width), jnp.bfloat16),
            jax.ShapeDtypeStruct((1, width), jnp.float32),
        ],
        cost_estimate=cost(2 * rows * width * depth, 2 * width * depth),
        compiler_params=pltpu.CompilerParams(vmem_limit_bytes=24 * 2**20),
        name="backward",
    )(slot, *in_hbm(cotangent), weight, gain, *in_hbm(stashed), after)


def project(early, late, gain, weight, term, other):
    rows = early.shape[0] + late.shape[0]
    width, depth = weight.shape
    return pl.pallas_call(
        project_kernel,
        in_specs=[VMEM] * 6,
        out_specs=[VMEM] * 2,
        out_shape=[
            jax.ShapeDtypeStruct((rows, depth), jnp.bfloat16),
            jax.ShapeDtypeStruct((1, width), jnp.float32),
        ],
        cost_estimate=cost(2 * rows * width * depth, 2 * width * depth),
        compiler_params=pltpu.CompilerParams(vmem_limit_bytes=24 * 2**20),
        name="project",
    )(early, late, gain, weight, term, other)


def swapped(value, axis, distance):
    return lax.ppermute(value, axis, [(i, i ^ distance) for i in range(lax.axis_size(axis))])


def sum_rounds():
    rounds = []
    for axis in ("rep", "seq"):
        count = lax.axis_size(axis)
        if count & (count - 1):
            return []
        rounds += [(axis, 1 << i) for i in range(count.bit_length() - 1)]
    return rounds if len(rounds) == 3 else []


def local(queries, keys, values, doc_starts, weight, gain, stashed, cotangent, slot):
    queries, keys, values, offsets = queries[0, 0], keys[0, 0], values[0, 0], doc_starts[0]
    half = queries.shape[0] // 2
    rounds = sum_rounds()

    def partner(term, index):
        return swapped(term, *rounds[index]) if rounds else jnp.zeros_like(term)

    next_queries = shifted(queries[:half], "seq", -1)
    late, early, lse = attend_own(queries, keys, values, offsets, 2)
    next_lse = shifted(lse, "seq", -1)
    late_arrived = passed_along(late, "section", 1)
    dinput, term = backward(slot, cotangent[0, 0], weight[0], gain, stashed[0, 0], lse)
    upstream = passed_along(dinput, "section", -1)
    term = term if rounds else lax.psum(term, ("rep", "seq"))
    halo, term = attend_halo(
        next_queries, keys, values, next_lse, offsets, term, partner(term, 0), (upstream, late_arrived), 4
    )
    halo = shifted(halo, "seq", 1)
    pooled, term = combine(early, halo, term, partner(term, 1))
    early_arrived = passed_along(pooled, "section", 1)
    mol_keys, update = project(early_arrived, late_arrived, gain, weight[0], term, partner(term, 2))
    return mol_keys[None, None], upstream[None, None], update


def solution(mesh):
    in_specs = (
        P("rep", "section", "seq", None),
        P("rep", "section", "seq", None),
        P("rep", "section", "seq", None),
        P("rep", "section", None),
        P("section", None, None),
        P("section", None),
        P("rep", "section", None, "seq", None),
        P("rep", "section", "seq", None),
        P("rep", "section"),
    )
    out_specs = (
        P("rep", "section", "seq", None),
        P("rep", "section", "seq", None),
        P("section", None),
    )
    return jax.shard_map(local, mesh=mesh, in_specs=in_specs, out_specs=out_specs, check_vma=False)
```

time: 77.2 us -> 48.5 us (0.63)
  blocking collectives: 23.8 us -> 0 us
  local copies, waits for them, and re-layouts: 13.5 us -> 1.94 us
  waiting for transfers between devices: 5.98 us -> 11.7 us
  starting transfers between devices: 11.5 us -> 17.1 us
  Pallas kernels: 20.5 us -> 16.2 us
    all_gather x1 -> x0, blocking collectives: 23.8 us -> none  [local(): terms = lax.all_gather(term, ('rep', 'seq'), axis=0, tiled=True)]
    unnamed x28 -> x5, local copies, waits for them, and re-layouts: 12.3 us -> 0.71 us
    ppermute x0 -> x3, waiting for transfers between devices: none -> 4.88 us  [swapped(): lax.ppermute(value, axis, [(i, i ^ distance) for i in range(lax.axis_size...]
    ppermute x0 -> x3, starting transfers between devices: none -> 4.63 us  [swapped(): lax.ppermute(value, axis, [(i, i ^ distance) for i in range(lax.axis_size...]
    pallas_call x5, Pallas kernels: 20.5 us -> 16.2 us  [the longest x1 7.61 us: attend_own(): pl.pallas_call(functools.partial(own_kernel, rows, chunks), in_specs=[HBM...]
    ppermute x3, waiting for transfers between devices: 0.01 us -> 3.11 us  [passed_along(): lax.ppermute(value, axis, [(i, (i + steps) % count) for i in range(count)])]
    ppermute x3, waiting for transfers between devices: 5.97 us -> 3.73 us  [shifted(): lax.ppermute(value, axis, [(i, i + steps) for i in range(first, last)])]
  transfers between devices with their start and end apart: 6 -> 9, of which waited for: 1 -> 5; matrix products, arithmetic and copies ran while one was open for 0% -> 0% of each run, Pallas kernels for 18% -> 21%
where the time goes in v2:
time: 48.5 us; the launch traced here: 48.3 us
  starting transfers between devices  17.1 us (35%)
  Pallas kernels  16.2 us (33%)
  waiting for transfers between devices  11.7 us (24%)
  local copies, waits for them, and re-layouts  1.94 us (4%)
  between operations  1.38 us (3%)
    pallas_call x1, Pallas kernels, attend_own(): pl.pallas_call(functools.partial(own_kernel, rows, chunks), in_specs=[HBM...  7.61 us
    ppermute x3, starting transfers between devices, shifted(): lax.ppermute(value, axis, [(i, i + steps) for i in range(first, last)])  6.99 us
    ppermute x3, starting transfers between devices, passed_along(): lax.ppermute(value, axis, [(i, (i + steps) % count) for i in range(count)])  5.46 us
    ppermute x3, waiting for transfers between devices, swapped(): lax.ppermute(value, axis, [(i, i ^ distance) for i in range(lax.axis_size...  4.88 us
    ppermute x3, starting transfers between devices, swapped(): lax.ppermute(value, axis, [(i, i ^ distance) for i in range(lax.axis_size...  4.63 us
    pallas_call x1, Pallas kernels, attend_halo(): pl.pallas_call(functools.partial(halo_kernel, 2 * half, chunks), in_specs...  4.03 us
    ppermute x3, waiting for transfers between devices, shifted(): lax.ppermute(value, axis, [(i, i + steps) for i in range(first, last)])  3.73 us
    ppermute x3, waiting for transfers between devices, passed_along(): lax.ppermute(value, axis, [(i, (i + steps) % count) for i in range(count)])  3.11 us
  transfers between devices with their start and end apart: 9, of which 5 were waited for; matrix products, arithmetic and copies ran while one was open for 0% of the time, Pallas kernels for 21%

profile of v2, /device:TPU:0, one launch (start us, length us, event | category | flops | bytes accessed | tf_op | source)
XLA Modules:
  0.0 48.3 jit_solution(2179081221700463110)
XLA Ops:
  0.6 0.0 copy-start.1
  0.6 0.0 copy-start
  0.7 1.2 %slice_bitcast_fusion = bf16[128,2048]{1,0:T(8,128)(2,1)S(1)} fusion(bf16[1,1,256,2048]{3,2,1,0:T(8,128)(2,1)} %param.9), kind=kLoop, calls=%fused_computation | loop fusion | bytes 1048576 | tf_op jit(solution)/shard_map/slice | solution.py:427
  1.9 1.4 %collective-permute-start = (bf16[128,2048]{1,0:T(8,128)(2,1)S(1)}, bf16[128,2048]{1,0:T(8,128)(2,1)S(1)}, u32[]{:S(2)}, u32[]{:S(2)}) collective-permute-start(bf16[128,2048]{1,0:T(8,128)(2,1)S(1)} %slice_bitcast_fusion), channel_id=1, source_target_pairs={{2,0},{4,2},{6,4},{3,1},{5,3},{7,5},{10,8},{12,10},{14,12},{11,9},... | collective-permute-start | bytes 1572872 | tf_op jit(solution)/shard_map/ppermute | solution.py:34
  4.0 7.6 %attend_own.1 = (bf16[32,2048]{1,0:T(8,128)(2,1)S(1)}, bf16[2048,128]{1,0:T(8,128)(2,1)S(1)}, f32[2,2048]{1,0:T(2,128)S(1)}) custom-call(s32[1,8]{1,0:T(1,128)} %bitcast.21, bf16[256,2048]{1,0:T(8,128)(2,1)} %bitcast.18, bf16[256,2048]{1,0:T(8,128)(2,1)} %bitcast.14, bf16[256,2048]{1,0:T(8,128)(2,1)} %bitcast.16), custom_call_target="tpu_custom_call" | custom-call | flops 402653184 | bytes 3145728 | tf_op jit(solution)/shard_map/attend_own/pallas_call | solution.py:300
  11.6 0.0 copy-done.1
  11.6 0.0 copy-done
  11.6 2.6 %backward.1 = (bf16[64,2048]{1,0:T(8,128)(2,1)S(1)}, f32[1,2048]{1,0:T(1,128)S(1)}) custom-call(s32[1,1]{1,0:T(1,128)S(6)} %copy.13.slot_ref, bf16[64,1024]{1,0:T(8,128)(2,1)} %bitcast.20, bf16[2048,1024]{1,0:T(8,128)(2,1)S(1)} %bitcast.11, f32[1,2048]{1,0:T(1,128)S(1)} %copy-done.1, bf16[2,64,2048]{2,1,0:T(8,128)(2,1)} %bitcast.19, ...), custom_call_target="tpu_custom_call" | custom-call | flops 268435456 | bytes 4194304 | tf_op jit(solution)/shard_map/backward/pallas_call | solution.py:368
  14.3 3.9 %collective-permute-start.3 = (bf16[64,2048]{1,0:T(8,128)(2,1)S(1)}, bf16[64,2048]{1,0:T(8,128)(2,1)S(1)}, u32[]{:S(2)}, u32[]{:S(2)}) collective-permute-start(bf16[64,2048]{1,0:T(8,128)(2,1)S(1)} %get-tuple-element.17), channel_id=1, source_target_pairs={{0,24},{8,0},{16,8},{24,16},{1,25},{9,1},{17,9},{25,17},{2,26},{10... | collective-permute-start | bytes 786440 | tf_op jit(solution)/shard_map/ppermute | solution.py:39
  18.2 0.0 collective-permute-start.4
  18.2 1.3 %collective-permute-start.1 = (f32[2,2048]{1,0:T(2,128)S(1)}, f32[2,2048]{1,0:T(2,128)S(1)}, u32[]{:S(2)}, u32[]{:S(2)}) collective-permute-start(f32[2,2048]{1,0:T(2,128)S(1)} %get-tuple-element.15.after_ref), channel_id=1, source_target_pairs={{2,0},{4,2},{6,4},{3,1},{5,3},{7,5},{10,8},{12,10},{14,12},{11,9},... | collective-permute-start | bytes 49160 | tf_op jit(solution)/shard_map/ppermute | solution.py:34
  19.5 0.1 collective-permute-start.2
  19.6 1.2 %collective-permute-done.2.other_ref = f32[1,2048]{1,0:T(1,128)S(1)} collective-permute-done((f32[1,2048]{1,0:T(1,128)S(1)}, f32[1,2048]{1,0:T(1,128)S(1)}, u32[]{:S(2)}, u32[]{:S(2)}) %collective-permute-start.2) | collective-permute-done | bytes 8224 | tf_op jit(solution)/shard_map/ppermute | solution.py:406
  20.7 3.7 %collective-permute-done.1.lse_ref = f32[2,2048]{1,0:T(2,128)S(1)} collective-permute-done((f32[2,2048]{1,0:T(2,128)S(1)}, f32[2,2048]{1,0:T(2,128)S(1)}, u32[]{:S(2)}, u32[]{:S(2)}) %collective-permute-start.1) | collective-permute-done | bytes 16416 | tf_op jit(solution)/shard_map/ppermute | solution.py:34
  24.5 3.1 %collective-permute-done.4.rest_1_.late_ref = bf16[32,2048]{1,0:T(8,128)(2,1)S(1)} collective-permute-done((bf16[32,2048]{1,0:T(8,128)(2,1)S(1)}, bf16[32,2048]{1,0:T(8,128)(2,1)S(1)}, u32[]{:S(2)}, u32[]{:S(2)}) %collective-permute-start.4) | collective-permute-done | bytes 131104 | tf_op jit(solution)/shard_map/ppermute | solution.py:39
  27.6 0.0 collective-permute-done.3.rest_0_
  27.6 0.0 collective-permute-done.q_ref
  27.6 4.0 %attend_halo.1 = (bf16[48,2048]{1,0:T(8,128)(2,1)S(1)}, f32[1,2048]{1,0:T(1,128)S(1)}) custom-call(s32[1,8]{1,0:T(1,128)} %bitcast.22, bf16[128,2048]{1,0:T(8,128)(2,1)S(1)} %collective-permute-done.q_ref, bf16[256,2048]{1,0:T(8,128)(2,1)} %bitcast.15, bf16[256,2048]{1,0:T(8,128)(2,1)} %bitcast.17, f32[2,2048]{1,0:T(2,128)S(1)} %collective-permute-done.1.lse_ref, ...), custom_call_target="tpu_custom_call" | custom-call | flops 134217728 | bytes 1572864 | tf_op jit(solution)/shard_map/attend_halo/pallas_call | solution.py:327
  31.6 4.3 %collective-permute-start.5 = (bf16[48,2048]{1,0:T(8,128)(2,1)S(1)}, bf16[48,2048]{1,0:T(8,128)(2,1)S(1)}, u32[]{:S(2)}, u32[]{:S(2)}) collective-permute-start(bf16[48,2048]{1,0:T(8,128)(2,1)S(1)} %get-tuple-element.19), channel_id=1, source_target_pairs={{0,2},{2,4},{4,6},{1,3},{3,5},{5,7},{8,10},{10,12},{12,14},{9,11},... | collective-permute-start | bytes 589832 | tf_op jit(solution)/shard_map/ppermute | solution.py:34
  35.9 1.6 %collective-permute-start.6 = (f32[1,2048]{1,0:T(1,128)S(1)}, f32[1,2048]{1,0:T(1,128)S(1)}, u32[]{:S(2)}, u32[]{:S(2)}) collective-permute-start(f32[1,2048]{1,0:T(1,128)S(1)} %get-tuple-element.20.term_ref), channel_id=1, source_target_pairs={{0,2},{2,0},{4,6},{6,4},{1,3},{3,1},{5,7},{7,5},{8,10},{10,8},{12,... | collective-permute-start | bytes 24584 | tf_op jit(solution)/shard_map/ppermute | solution.py:406
  37.5 2.1 %collective-permute-done.6.other_ref = f32[1,2048]{1,0:T(1,128)S(1)} collective-permute-done((f32[1,2048]{1,0:T(1,128)S(1)}, f32[1,2048]{1,0:T(1,128)S(1)}, u32[]{:S(2)}, u32[]{:S(2)}) %collective-permute-start.6) | collective-permute-done | bytes 8224 | tf_op jit(solution)/shard_map/ppermute | solution.py:406
  39.6 0.0 collective-permute-done.5.halo_ref
  39.6 0.3 combine.1
  39.9 1.5 %collective-permute-start.7 = (bf16[32,2048]{1,0:T(8,128)(2,1)S(1)}, bf16[32,2048]{1,0:T(8,128)(2,1)S(1)}, u32[]{:S(2)}, u32[]{:S(2)}) collective-permute-start(bf16[32,2048]{1,0:T(8,128)(2,1)S(1)} %get-tuple-element.21), channel_id=1, source_target_pairs={{0,8},{8,16},{16,24},{24,0},{1,9},{9,17},{17,25},{25,1},{2,10},{10... | collective-permute-start | bytes 393224 | tf_op jit(solution)/shard_map/ppermute | solution.py:39
  41.4 2.9 %collective-permute-start.8 = (f32[1,2048]{1,0:T(1,128)S(1)}, f32[1,2048]{1,0:T(1,128)S(1)}, u32[]{:S(2)}, u32[]{:S(2)}) collective-permute-start(f32[1,2048]{1,0:T(1,128)S(1)} %get-tuple-element.22.term_ref), channel_id=1, source_target_pairs={{0,4},{2,6},{4,0},{6,2},{1,5},{3,7},{5,1},{7,3},{8,12},{10,14},{12... | collective-permute-start | bytes 24584 | tf_op jit(solution)/shard_map/ppermute | solution.py:406
  44.4 1.6 %collective-permute-done.8.other_ref = f32[1,2048]{1,0:T(1,128)S(1)} collective-permute-done((f32[1,2048]{1,0:T(1,128)S(1)}, f32[1,2048]{1,0:T(1,128)S(1)}, u32[]{:S(2)}, u32[]{:S(2)}) %collective-permute-start.8) | collective-permute-done | bytes 8224 | tf_op jit(solution)/shard_map/ppermute | solution.py:406
  46.0 0.0 collective-permute-done.7.early_ref
  46.0 1.6 %project.1 = (bf16[64,1024]{1,0:T(8,128)(2,1)}, f32[1,2048]{1,0:T(1,128)}) custom-call(bf16[32,2048]{1,0:T(8,128)(2,1)S(1)} %collective-permute-done.7.early_ref, bf16[32,2048]{1,0:T(8,128)(2,1)S(1)} %collective-permute-done.4.rest_1_.late_ref, f32[1,2048]{1,0:T(1,128)S(1)} %copy-done.1, bf16[2048,1024]{1,0:T(8,128)(2,1)S(1)} %bitcast.12, ...), custom_call_target="tpu_custom_call" | custom-call | flops 268435456 | bytes 4194304 | tf_op jit(solution)/shard_map/project/pallas_call | solution.py:391
  47.6 0.7 %copy.14 = bf16[1,1,64,2048]{3,2,1,0:T(8,128)(2,1)} copy(bf16[1,1,64,2048]{3,2,1,0:T(8,128)(2,1)S(1)} %bitcast.13) | data formatting | bytes 524288
Async XLA Ops:
  0.6 11.0 %copy-start.1 = (f32[1,2048]{1,0:T(1,128)S(1)}, f32[1,2048]{1,0:T(1,128)}, u32[]{:S(2)}) copy-start(f32[1,2048]{1,0:T(1,128)} %gain_ref.3) | copy-start | bytes 24580
  0.6 11.0 %copy-start = (bf16[1,2048,1024]{2,1,0:T(8,128)(2,1)S(1)}, bf16[1,2048,1024]{2,1,0:T(8,128)(2,1)}, u32[]{:S(2)}) copy-start(bf16[1,2048,1024]{2,1,0:T(8,128)(2,1)} %param.13) | copy-start | bytes 12582916
  1.9 25.7 %collective-permute-start = (bf16[128,2048]{1,0:T(8,128)(2,1)S(1)}, bf16[128,2048]{1,0:T(8,128)(2,1)S(1)}, u32[]{:S(2)}, u32[]{:S(2)}) collective-permute-start(bf16[128,2048]{1,0:T(8,128)(2,1)S(1)} %slice_bitcast_fusion), channel_id=1, source_target_pairs={{2,0},{4,2},{6,4},{3,1},{5,3},{7,5},{10,8},{12,10},{14,12},{11,9},... | collective-permute-start | bytes 1572872 | tf_op jit(solution)/shard_map/ppermute | solution.py:34
  14.3 13.3 %collective-permute-start.3 = (bf16[64,2048]{1,0:T(8,128)(2,1)S(1)}, bf16[64,2048]{1,0:T(8,128)(2,1)S(1)}, u32[]{:S(2)}, u32[]{:S(2)}) collective-permute-start(bf16[64,2048]{1,0:T(8,128)(2,1)S(1)} %get-tuple-element.17), channel_id=1, source_target_pairs={{0,24},{8,0},{16,8},{24,16},{1,25},{9,1},{17,9},{25,17},{2,26},{10... | collective-permute-start | bytes 786440 | tf_op jit(solution)/shard_map/ppermute | solution.py:39
  18.2 9.4 %collective-permute-start.4 = (bf16[32,2048]{1,0:T(8,128)(2,1)S(1)}, bf16[32,2048]{1,0:T(8,128)(2,1)S(1)}, u32[]{:S(2)}, u32[]{:S(2)}) collective-permute-start(bf16[32,2048]{1,0:T(8,128)(2,1)S(1)} %get-tuple-element.18), channel_id=1, source_target_pairs={{0,8},{8,16},{16,24},{24,0},{1,9},{9,17},{17,25},{25,1},{2,10},{10... | collective-permute-start | bytes 393224 | tf_op jit(solution)/shard_map/ppermute | solution.py:39
  18.2 6.3 %collective-permute-start.1 = (f32[2,2048]{1,0:T(2,128)S(1)}, f32[2,2048]{1,0:T(2,128)S(1)}, u32[]{:S(2)}, u32[]{:S(2)}) collective-permute-start(f32[2,2048]{1,0:T(2,128)S(1)} %get-tuple-element.15.after_ref), channel_id=1, source_target_pairs={{2,0},{4,2},{6,4},{3,1},{5,3},{7,5},{10,8},{12,10},{14,12},{11,9},... | collective-permute-start | bytes 49160 | tf_op jit(solution)/shard_map/ppermute | solution.py:34
  19.5 1.2 %collective-permute-start.2 = (f32[1,2048]{1,0:T(1,128)S(1)}, f32[1,2048]{1,0:T(1,128)S(1)}, u32[]{:S(2)}, u32[]{:S(2)}) collective-permute-start(f32[1,2048]{1,0:T(1,128)S(1)} %get-tuple-element.16.term_ref), channel_id=1, source_target_pairs={{0,1},{1,0},{2,3},{3,2},{4,5},{5,4},{6,7},{7,6},{8,9},{9,8},{10,11... | collective-permute-start | bytes 24584 | tf_op jit(solution)/shard_map/ppermute | solution.py:406
  31.6 8.0 %collective-permute-start.5 = (bf16[48,2048]{1,0:T(8,128)(2,1)S(1)}, bf16[48,2048]{1,0:T(8,128)(2,1)S(1)}, u32[]{:S(2)}, u32[]{:S(2)}) collective-permute-start(bf16[48,2048]{1,0:T(8,128)(2,1)S(1)} %get-tuple-element.19), channel_id=1, source_target_pairs={{0,2},{2,4},{4,6},{1,3},{3,5},{5,7},{8,10},{10,12},{12,14},{9,11},... | collective-permute-start | bytes 589832 | tf_op jit(solution)/shard_map/ppermute | solution.py:34
  35.9 3.7 %collective-permute-start.6 = (f32[1,2048]{1,0:T(1,128)S(1)}, f32[1,2048]{1,0:T(1,128)S(1)}, u32[]{:S(2)}, u32[]{:S(2)}) collective-permute-start(f32[1,2048]{1,0:T(1,128)S(1)} %get-tuple-element.20.term_ref), channel_id=1, source_target_pairs={{0,2},{2,0},{4,6},{6,4},{1,3},{3,1},{5,7},{7,5},{8,10},{10,8},{12,... | collective-permute-start | bytes 24584 | tf_op jit(solution)/shard_map/ppermute | solution.py:406
  39.9 6.1 %collective-permute-start.7 = (bf16[32,2048]{1,0:T(8,128)(2,1)S(1)}, bf16[32,2048]{1,0:T(8,128)(2,1)S(1)}, u32[]{:S(2)}, u32[]{:S(2)}) collective-permute-start(bf16[32,2048]{1,0:T(8,128)(2,1)S(1)} %get-tuple-element.21), channel_id=1, source_target_pairs={{0,8},{8,16},{16,24},{24,0},{1,9},{9,17},{17,25},{25,1},{2,10},{10... | collective-permute-start | bytes 393224 | tf_op jit(solution)/shard_map/ppermute | solution.py:39
  41.4 4.6 %collective-permute-start.8 = (f32[1,2048]{1,0:T(1,128)S(1)}, f32[1,2048]{1,0:T(1,128)S(1)}, u32[]{:S(2)}, u32[]{:S(2)}) collective-permute-start(f32[1,2048]{1,0:T(1,128)S(1)} %get-tuple-element.22.term_ref), channel_id=1, source_target_pairs={{0,4},{2,6},{4,0},{6,2},{1,5},{3,7},{5,1},{7,3},{8,12},{10,14},{12... | collective-permute-start | bytes 24584 | tf_op jit(solution)/shard_map/ppermute | solution.py:406

commit v3 on v2

v3 whole, which is shorter than its diff:
```python
import functools
import math

import jax
import jax.numpy as jnp
from jax import lax
from jax.experimental import pallas as pl
from jax.experimental.pallas import tpu as pltpu
from jax.sharding import PartitionSpec as P

HEAD_DIM = 64
POOL = 4
WINDOW = 128
LANES = 128
EPS_NORM = 1e-05
EPS_STEP = 1e-06
MASKED = -1e30
AHEAD = 2

NT = (((1,), (1,)), ((), ()))


def dot_nt(a, b):
    return lax.dot_general(a, b, NT, preferred_element_type=jnp.float32)


def dot_nn(a, b):
    return jnp.dot(a, b, preferred_element_type=jnp.float32)


def shifted(value, axis, steps):
    count = lax.axis_size(axis)
    first, last = max(0, -steps), min(count, count - steps)
    return lax.ppermute(value, axis, [(i, i + steps) for i in range(first, last)])


def passed_along(value, axis, steps):
    count = lax.axis_size(axis)
    return lax.ppermute(value, axis, [(i, (i + steps) % count) for i in range(count)])


def earliest_key(offsets_ref, query_pos):
    start = jnp.zeros_like(query_pos)
    for d in range(offsets_ref.shape[1]):
        offset = offsets_ref[0, d]
        start = jnp.where(query_pos >= offset, offset, start)
    return jnp.maximum(start, query_pos - (WINDOW - 1))


def mask_bias(offsets_ref, key_start, key_count, query_start, query_count):
    query_pos = query_start + lax.broadcasted_iota(jnp.int32, (1, query_count), 1)
    lowest = earliest_key(offsets_ref, query_pos)
    key_pos = key_start + lax.broadcasted_iota(jnp.int32, (key_count, query_count), 0)
    allowed = (key_pos >= lowest) & (key_pos <= query_pos)
    return jnp.where(allowed, 0.0, MASKED).astype(jnp.float32)


def split_heads(queries):
    lane = lax.broadcasted_iota(jnp.int32, (1, LANES), 1)
    scale = 1.0 / math.sqrt(HEAD_DIM)
    first = jnp.where(lane < HEAD_DIM, scale, 0.0).astype(jnp.bfloat16)
    second = jnp.where(lane < HEAD_DIM, 0.0, scale).astype(jnp.bfloat16)
    return jnp.concatenate([queries * first, queries * second], axis=0)


def pool_matrix(queries):
    molecule = lax.broadcasted_iota(jnp.int32, (queries // POOL, queries), 0)
    query = lax.broadcasted_iota(jnp.int32, (queries // POOL, queries), 1)
    return jnp.where(query // POOL == molecule, 1.0 / POOL, 0.0).astype(jnp.bfloat16)


def own_heads(mixed, scale):
    count = mixed.shape[1] // 2
    return jnp.concatenate(
        [
            mixed[:HEAD_DIM, :count] * scale[:, :count],
            mixed[HEAD_DIM:, count:] * scale[:, count:],
        ],
        axis=0,
    )


def twice(bias):
    return jnp.concatenate([bias, bias], axis=1)


def load(source, target, sem):
    copy = pltpu.make_async_copy(source, target, sem)
    copy.start()
    return copy


def load_chunks(arrays, chunks, sems):
    block = arrays[0][1].shape[1] // chunks
    return [
        [
            load(source.at[:, pl.ds(chunk * block, block)], target.at[:, pl.ds(chunk * block, block)], sems.at[i, chunk])
            for i, (source, target) in enumerate(arrays)
        ]
        for chunk in range(chunks)
    ]


def at(pair):
    return pl.ds(pair * LANES, LANES)


def over_pairs(pairs, first, second, third, copies):
    ready, pending = {}, None
    per_chunk = pairs // len(copies)
    for step in range(pairs + AHEAD):
        if step < pairs:
            if step % per_chunk == 0:
                for copy in copies[step // per_chunk]:
                    copy.wait()
            ready[step] = first(step)
        pair = step - AHEAD
        if pair >= 0:
            result = second(pair, *ready.pop(pair))
            if pending is not None:
                third(pair - 1, *pending)
            pending = result
    third(pairs - 1, *pending)


def pool_into(pooling, out_ref, rows, parts, pair, last):
    if len(parts) == 4 or last:
        columns = pl.ds((pair + 1 - len(parts)) * LANES, len(parts) * LANES)
        pooled = dot_nt(pooling, jnp.concatenate(parts, axis=0))
        out_ref[pl.ds(0, rows), columns] = pooled.astype(jnp.bfloat16)
        parts.clear()


def three_terms(value):
    high = value.astype(jnp.bfloat16).astype(jnp.float32)
    middle = (value - high).astype(jnp.bfloat16).astype(jnp.float32)
    return [high, middle, value - high - middle]


def early_kernel(
    rows, chunks, offsets_hbm, q_hbm, k_hbm, v_hbm, sent_ref, early_ref,
    offsets_ref, k_ref, v_ref, bias, sems, offsets_sem,
):
    half = rows // 2
    head = pl.ds(0, half)
    offsets_copy = load(offsets_hbm, offsets_ref, offsets_sem)
    arrays = (
        (k_hbm.at[head], k_ref),
        (q_hbm.at[head], sent_ref.at[head]),
        (v_hbm.at[head], v_ref),
    )
    copies = load_chunks(arrays, chunks, sems)
    offsets_copy.wait()
    start = lax.axis_index("seq") * rows
    bias[...] = mask_bias(offsets_ref, start, half, start, half)

    def score(pair):
        return dot_nt(k_ref[:, at(pair)], split_heads(sent_ref[head, at(pair)])), jnp.transpose(
            v_ref[:, at(pair)]
        )

    def weigh(pair, scores, values_t):
        scores = scores + twice(bias[...])
        top = jnp.max(scores, axis=0, keepdims=True)
        weights = jnp.exp(scores - top)
        total = jnp.sum(weights, axis=0, keepdims=True)
        mixed = dot_nn(values_t, weights.astype(jnp.bfloat16))
        lse = top + jnp.log(total)
        terms = three_terms(lse[:, :half]) + three_terms(lse[:, half:])
        terms.append(jnp.zeros((10, LANES), jnp.float32))
        sent_ref[pl.ds(half, 16), at(pair)] = jnp.concatenate(terms, axis=0).astype(jnp.bfloat16)
        return mixed, 1.0 / total

    def finish(pair, mixed, inverse):
        early_ref[at(pair), :] = own_heads(mixed, inverse).astype(jnp.bfloat16)

    over_pairs(k_ref.shape[1] // LANES, score, weigh, finish, copies)


def late_kernel(
    rows, chunks, offsets_hbm, q_hbm, k_hbm, v_hbm, after_ref, late_ref,
    offsets_ref, q_ref, k_ref, v_ref, bias, own, other, sems, offsets_sem,
):
    half = rows // 2
    offsets_copy = load(offsets_hbm, offsets_ref, offsets_sem)
    arrays = ((k_hbm, k_ref), (q_hbm.at[pl.ds(half, half)], q_ref), (v_hbm, v_ref))
    copies = load_chunks(arrays, chunks, sems)
    offsets_copy.wait()
    start = lax.axis_index("seq") * rows
    key = lax.broadcasted_iota(jnp.int32, (half, half), 0)
    query = lax.broadcasted_iota(jnp.int32, (half, half), 1)
    lowest = earliest_key(
        offsets_ref, start + half + lax.broadcasted_iota(jnp.int32, (1, half), 1)
    )
    key_pos = start + key + jnp.where(key <= query, half, 0)
    bias[...] = jnp.where(key_pos >= lowest, 0.0, MASKED).astype(jnp.float32)
    own[...] = jnp.where(key <= query, 1.0, 0.0).astype(jnp.bfloat16)
    other[...] = jnp.where(key <= query, 0.0, 1.0).astype(jnp.bfloat16)
    pooling = pool_matrix(half)
    pairs = k_ref.shape[1] // LANES
    parts = []

    def score(pair):
        queries = split_heads(q_ref[:, at(pair)])
        return dot_nt(k_ref[:, at(pair)], queries), jnp.transpose(v_ref[:, at(pair)])

    def weigh(pair, scores, values_t):
        scores = jnp.where(twice(key <= query), scores[half:], scores[:half]) + twice(bias[...])
        top = jnp.max(scores, axis=0, keepdims=True)
        weights = jnp.exp(scores - top)
        total = jnp.sum(weights, axis=0, keepdims=True)
        weights = weights.astype(jnp.bfloat16)
        weights = jnp.concatenate([weights * twice(other[...]), weights * twice(own[...])], axis=0)
        return dot_nn(values_t, weights), 1.0 / total

    def finish(pair, mixed, inverse):
        parts.append(own_heads(mixed, inverse).astype(jnp.bfloat16))
        pool_into(pooling, late_ref, half // POOL, parts, pair, pair == pairs - 1)

    over_pairs(pairs, score, weigh, finish, copies)


def halo_kernel(rows, chunks, offsets_hbm, q_ref, k_hbm, v_hbm, *rest):
    out_ref, offsets_ref, k_ref, v_ref, bias, sems, offsets_sem = rest[-7:]
    half = rows // 2
    molecules = half // POOL
    offsets_copy = load(offsets_hbm, offsets_ref, offsets_sem)
    tail = pl.ds(half, half)
    copies = load_chunks(((k_hbm.at[tail], k_ref), (v_hbm.at[tail], v_ref)), chunks, sems)
    offsets_copy.wait()
    start = (lax.axis_index("seq") + 1) * rows
    bias[...] = mask_bias(offsets_ref, start - half, half, start, half)
    pooling = pool_matrix(half)
    pairs = k_ref.shape[1] // LANES
    parts = []

    def score(pair):
        queries = split_heads(q_ref[pl.ds(0, half), at(pair)])
        return dot_nt(k_ref[:, at(pair)], queries), jnp.transpose(v_ref[:, at(pair)])

    def weigh(pair, scores, values_t):
        terms = q_ref[pl.ds(half, 16), at(pair)].astype(jnp.float32)
        lse = jnp.concatenate(
            [terms[0:1] + terms[1:2] + terms[2:3], terms[3:4] + terms[4:5] + terms[5:6]], axis=1
        )
        scores = scores + twice(bias[...])
        top = jnp.maximum(jnp.max(scores, axis=0, keepdims=True), lse)
        weights = jnp.exp(scores - top)
        kept = jnp.exp(lse - top)
        inverse = 1.0 / (jnp.sum(weights, axis=0, keepdims=True) + kept)
        mixed = dot_nn(values_t, weights.astype(jnp.bfloat16))
        share = kept * inverse
        high = share.astype(jnp.bfloat16).astype(jnp.float32)
        low = share - high
        shares = [high[:, :half], low[:, :half], high[:, half:], low[:, half:]]
        shares.append(jnp.zeros((12, LANES), jnp.float32))
        out_ref[pl.ds(molecules, 16), at(pair)] = jnp.concatenate(shares, axis=0).astype(jnp.bfloat16)
        return mixed, inverse

    def finish(pair, mixed, inverse):
        parts.append(own_heads(mixed, inverse).astype(jnp.bfloat16))
        pool_into(pooling, out_ref, molecules, parts, pair, pair == pairs - 1)

    over_pairs(pairs, score, weigh, finish, copies)


def combine_kernel(early_ref, halo_ref, *rest):
    out_ref = rest[-1]
    half = early_ref.shape[1]
    molecules = half // POOL
    pooling = pool_matrix(half)
    first = lax.axis_index("seq") == 0
    parts = []
    for pair in range(out_ref.shape[1] // LANES):
        shares = halo_ref[molecules:, at(pair)].astype(jnp.float32)
        share_a = jnp.where(first, 1.0, shares[0:1] + shares[1:2])
        share_b = jnp.where(first, 1.0, shares[2:3] + shares[3:4])
        early = early_ref[at(pair), :].astype(jnp.float32)
        parts += [early[:HEAD_DIM] * share_a, early[HEAD_DIM:] * share_b]
        if len(parts) == 8:
            columns = pl.ds((pair - 3) * LANES, 4 * LANES)
            pooled = dot_nt(pooling, jnp.concatenate(parts, axis=0).astype(jnp.bfloat16))
            arrived = halo_ref[:molecules, columns].astype(jnp.float32)
            out_ref[:, columns] = (pooled + arrived).astype(jnp.bfloat16)
            parts = []


def back_kernel(
    slot_ref, cotangent_hbm, weight_ref, gain_ref, stashed_hbm, after_ref, dinput_ref, terms_ref,
    cotangent_ref, held_ref, grad, sems,
):
    cotangent_copy = load(cotangent_hbm, cotangent_ref, sems.at[1])
    held_copy = load(stashed_hbm.at[slot_ref[0, 0]], held_ref, sems.at[0])
    cotangent_copy.wait()
    features = weight_ref.shape[0]
    block = 512
    for begin in range(0, features, block):
        columns = pl.ds(begin, block)
        grad[:, columns] = dot_nt(cotangent_ref[...], weight_ref[columns, :])
    held_copy.wait()
    held = held_ref[...].astype(jnp.float32)
    inv_rms = lax.rsqrt(jnp.sum(held * held, axis=1, keepdims=True) / features + EPS_NORM)
    along = jnp.zeros_like(inv_rms)
    for begin in range(0, features, block):
        columns = pl.ds(begin, block)
        product = grad[:, columns] * (held_ref[:, columns].astype(jnp.float32) * inv_rms)
        total = jnp.sum(product, axis=0, keepdims=True)
        terms_ref[:, columns] = jnp.broadcast_to(total, (terms_ref.shape[0], block))
        along += jnp.sum(product * gain_ref[:, columns], axis=1, keepdims=True)
    along = along / features
    for begin in range(0, features, block):
        columns = pl.ds(begin, block)
        whitened = held_ref[:, columns].astype(jnp.float32) * inv_rms
        scaled = grad[:, columns] * gain_ref[:, columns]
        dinput_ref[:, columns] = (inv_rms * (scaled - whitened * along)).astype(jnp.bfloat16)


def project_kernel(
    early_ref, late_ref, gain_ref, weight_ref, terms_ref, out_ref, update_ref
):
    features = gain_ref.shape[1]
    arrived = jnp.concatenate([early_ref[...], late_ref[...]], axis=0).astype(jnp.float32)
    mean = jnp.sum(arrived * arrived, axis=1, keepdims=True) / features
    normed = (arrived * lax.rsqrt(mean + EPS_NORM) * gain_ref[...]).astype(jnp.bfloat16)
    out_ref[...] = dot_nn(normed, weight_ref[...]).astype(jnp.bfloat16)
    total = jnp.sum(terms_ref[...], axis=0, keepdims=True)
    mean = jnp.sum(total * total, axis=1, keepdims=True) / features
    update_ref[...] = total / jnp.sqrt(mean + EPS_STEP)


def cost(flops, read, exps=0):
    return pl.CostEstimate(flops=flops, bytes_accessed=read, transcendentals=exps)


SMEM = pl.BlockSpec(memory_space=pltpu.SMEM)
HBM = pl.BlockSpec(memory_space=pltpu.HBM)
ANY = pl.BlockSpec(memory_space=pl.ANY)
VMEM = pl.BlockSpec(memory_space=pltpu.VMEM)


def in_hbm(*arrays):
    return [pltpu.with_memory_space_constraint(x, pltpu.HBM) for x in arrays]


def params():
    return pltpu.CompilerParams(vmem_limit_bytes=24 * 2**20)


def attend_early(queries, keys, values, offsets, chunks):
    rows, width = queries.shape
    half = rows // 2
    return pl.pallas_call(
        functools.partial(early_kernel, rows, chunks),
        in_specs=[HBM] * 4,
        out_specs=[VMEM] * 2,
        out_shape=[
            jax.ShapeDtypeStruct((half + 16, width), jnp.bfloat16),
            jax.ShapeDtypeStruct((width, half), jnp.bfloat16),
        ],
        scratch_shapes=[
            pltpu.SMEM(offsets.shape, jnp.int32),
            pltpu.VMEM((half, width), jnp.bfloat16),
            pltpu.VMEM((half, width), jnp.bfloat16),
            pltpu.VMEM((half, half), jnp.float32),
            pltpu.SemaphoreType.DMA((3, chunks)),
            pltpu.SemaphoreType.DMA,
        ],
        cost_estimate=cost(4 * half * half * width, 6 * half * width, half * half * width // 64),
        compiler_params=params(),
        name="attend_early",
    )(*in_hbm(offsets, queries, keys, values))


def attend_late(queries, keys, values, offsets, after, chunks):
    rows, width = queries.shape
    half = rows // 2
    return pl.pallas_call(
        functools.partial(late_kernel, rows, chunks),
        in_specs=[HBM] * 4 + [ANY],
        out_specs=VMEM,
        out_shape=jax.ShapeDtypeStruct((half // POOL, width), jnp.bfloat16),
        scratch_shapes=[
            pltpu.SMEM(offsets.shape, jnp.int32),
            pltpu.VMEM((half, width), jnp.bfloat16),
            pltpu.VMEM((rows, width), jnp.bfloat16),
            pltpu.VMEM((rows, width), jnp.bfloat16),
            pltpu.VMEM((half, half), jnp.float32),
            pltpu.VMEM((half, half), jnp.bfloat16),
            pltpu.VMEM((half, half), jnp.bfloat16),
            pltpu.SemaphoreType.DMA((3, chunks)),
            pltpu.SemaphoreType.DMA,
        ],
        cost_estimate=cost(8 * half * half * width, 5 * rows * width, half * half * width // 64),
        compiler_params=params(),
        name="attend_late",
    )(*in_hbm(offsets, queries, keys, values), after)


def attend_halo(sent, keys, values, offsets, after, chunks):
    rows, width = keys.shape
    half = rows // 2
    return pl.pallas_call(
        functools.partial(halo_kernel, rows, chunks),
        in_specs=[HBM, VMEM, HBM, HBM] + [ANY] * len(after),
        out_specs=VMEM,
        out_shape=jax.ShapeDtypeStruct((half // POOL + 16, width), jnp.bfloat16),
        scratch_shapes=[
            pltpu.SMEM(offsets.shape, jnp.int32),
            pltpu.VMEM((half, width), jnp.bfloat16),
            pltpu.VMEM((half, width), jnp.bfloat16),
            pltpu.VMEM((half, half), jnp.float32),
            pltpu.SemaphoreType.DMA((2, chunks)),
            pltpu.SemaphoreType.DMA,
        ],
        cost_estimate=cost(4 * half * half * width, 6 * half * width, half * half * width // 64),
        compiler_params=params(),
        name="attend_halo",
    )(*in_hbm(offsets), sent, *in_hbm(keys, values), *after)


def combine(early, halo, after):
    width, half = early.shape
    return pl.pallas_call(
        combine_kernel,
        in_specs=[VMEM] * 2 + [ANY] * len(after),
        out_specs=VMEM,
        out_shape=jax.ShapeDtypeStruct((half // POOL, width), jnp.bfloat16),
        cost_estimate=cost(half * half * width, 2 * half * width),
        compiler_params=params(),
        name="combine",
    )(early, halo, *after)


def backward(slot, cotangent, weight, gain, stashed, copies, after):
    rows, depth = cotangent.shape
    width = weight.shape[0]
    return pl.pallas_call(
        back_kernel,
        in_specs=[SMEM, HBM, VMEM, VMEM, HBM, ANY],
        out_specs=[VMEM] * 2,
        scratch_shapes=[
            pltpu.VMEM((rows, depth), jnp.bfloat16),
            pltpu.VMEM((rows, width), jnp.bfloat16),
            pltpu.VMEM((rows, width), jnp.float32),
            pltpu.SemaphoreType.DMA((2,)),
        ],
        out_shape=[
            jax.ShapeDtypeStruct((rows, width), jnp.bfloat16),
            jax.ShapeDtypeStruct((copies, width), jnp.float32),
        ],
        cost_estimate=cost(2 * rows * width * depth, 2 * width * depth),
        compiler_params=params(),
        name="backward",
    )(slot, *in_hbm(cotangent), weight, gain, *in_hbm(stashed), after)


def project(early, late, gain, weight, terms):
    rows = early.shape[0] + late.shape[0]
    width, depth = weight.shape
    return pl.pallas_call(
        project_kernel,
        in_specs=[VMEM] * 5,
        out_specs=[VMEM] * 2,
        out_shape=[
            jax.ShapeDtypeStruct((rows, depth), jnp.bfloat16),
            jax.ShapeDtypeStruct((1, width), jnp.float32),
        ],
        cost_estimate=cost(2 * rows * width * depth, 2 * width * depth),
        compiler_params=params(),
        name="project",
    )(early, late, gain, weight, terms)


def local(queries, keys, values, doc_starts, weight, gain, stashed, cotangent, slot):
    queries, keys, values, offsets = queries[0, 0], keys[0, 0], values[0, 0], doc_starts[0]
    group = ("rep", "seq")
    sent, early = attend_early(queries, keys, values, offsets, 4)
    arrived = shifted(sent, "seq", -1)
    late = attend_late(queries, keys, values, offsets, early, 4)
    late_arrived = passed_along(late, "section", 1)
    copies = lax.axis_size(group)
    dinput, terms = backward(slot, cotangent[0, 0], weight[0], gain, stashed[0, 0], copies, late)
    upstream = passed_along(dinput, "section", -1)
    terms = lax.all_to_all(terms, group, 0, 0, tiled=True)
    halo = attend_halo(arrived, keys, values, offsets, (late_arrived,), 4)
    pooled = combine(early, shifted(halo, "seq", 1), (upstream, terms))
    early_arrived = passed_along(pooled, "section", 1)
    mol_keys, update = project(early_arrived, late_arrived, gain, weight[0], terms)
    return mol_keys[None, None], upstream[None, None], update


def solution(mesh):
    in_specs = (
        P("rep", "section", "seq", None),
        P("rep", "section", "seq", None),
        P("rep", "section", "seq", None),
        P("rep", "section", None),
        P("section", None, None),
        P("section", None),
        P("rep", "section", None, "seq", None),
        P("rep", "section", "seq", None),
        P("rep", "section"),
    )
    out_specs = (
        P("rep", "section", "seq", None),
        P("rep", "section", "seq", None),
        P("section", None),
    )
    return jax.shard_map(local, mesh=mesh, in_specs=in_specs, out_specs=out_specs, check_vma=False)
```

time: 48.5 us -> 48 us (0.990)
  blocking collectives: 0 us -> 8.64 us
  starting transfers between devices: 17.1 us -> 10.5 us
  local copies, waits for them, and re-layouts: 1.94 us -> 0.8 us
  waiting for transfers between devices: 11.7 us -> 10.7 us
  Pallas kernels: 16.2 us -> 15.7 us
    all_to_all x0 -> x1, blocking collectives: none -> 8.64 us  [local(): terms = lax.all_to_all(terms, group, 0, 0, tiled=True)]
    ppermute x3 -> x0, waiting for transfers between devices: 4.88 us -> none  [swapped(): lax.ppermute(value, axis, [(i, i ^ distance) for i in range(lax.axis_size...]
    ppermute x3 -> x0, starting transfers between devices: 4.63 us -> none  [swapped(): lax.ppermute(value, axis, [(i, i ^ distance) for i in range(lax.axis_size...]
    ppermute x3 -> x2, starting transfers between devices: 6.99 us -> 4.94 us  [shifted(): lax.ppermute(value, axis, [(i, i + steps) for i in range(first, last)])]
    ppermute x3, waiting for transfers between devices: 3.11 us -> 5.04 us  [passed_along(): lax.ppermute(value, axis, [(i, (i + steps) % count) for i in range(count)])]
    ppermute x3 -> x2, waiting for transfers between devices: 3.73 us -> 5.66 us  [shifted(): lax.ppermute(value, axis, [(i, i + steps) for i in range(first, last)])]
    slice x1 -> x0, local copies, waits for them, and re-layouts: 1.23 us -> none  [local(): next_queries = shifted(queries[:half], 'seq', -1)]
    pallas_call x4 -> x5, Pallas kernels: 13.5 us -> 13.1 us  [the longest x1 3.86 us: attend_halo(): pl.pallas_call(functools.partial(halo_kernel, rows, chunks), in_specs=[HB...]
  transfers between devices with their start and end apart: 9 -> 5, of which waited for: 5 -> 3; matrix products, arithmetic and copies ran while one was open for 0% -> 0% of each run, Pallas kernels for 21% -> 22%
where the time goes in v3:
time: 48 us; the launch traced here: 47.7 us
  Pallas kernels  15.7 us (33%)
  waiting for transfers between devices  10.7 us (22%)
  starting transfers between devices  10.5 us (22%)
  blocking collectives  8.64 us (18%)
  between operations  1.39 us (3%)
  local copies, waits for them, and re-layouts  0.8 us (2%)
    all_to_all x1, blocking collectives, local(): terms = lax.all_to_all(terms, group, 0, 0, tiled=True)  8.64 us
    ppermute x2, waiting for transfers between devices, shifted(): lax.ppermute(value, axis, [(i, i + steps) for i in range(first, last)])  5.66 us
    ppermute x3, starting transfers between devices, passed_along(): lax.ppermute(value, axis, [(i, (i + steps) % count) for i in range(count)])  5.54 us
    ppermute x3, waiting for transfers between devices, passed_along(): lax.ppermute(value, axis, [(i, (i + steps) % count) for i in range(count)])  5.04 us
    ppermute x2, starting transfers between devices, shifted(): lax.ppermute(value, axis, [(i, i + steps) for i in range(first, last)])  4.94 us
    pallas_call x1, Pallas kernels, attend_halo(): pl.pallas_call(functools.partial(halo_kernel, rows, chunks), in_specs=[HB...  3.86 us
    pallas_call x1, Pallas kernels, attend_late(): pl.pallas_call(functools.partial(late_kernel, rows, chunks), in_specs=[HB...  3.85 us
    pallas_call x1, Pallas kernels, attend_early(): pl.pallas_call(functools.partial(early_kernel, rows, chunks), in_specs=[H...  3.5 us
  transfers between devices with their start and end apart: 5, of which 3 were waited for; matrix products, arithmetic and copies ran while one was open for 0% of the time, Pallas kernels for 22%

profile of v3, /device:TPU:0, one launch (start us, length us, event | category | flops | bytes accessed | tf_op | source)
XLA Modules:
  0.0 47.7 jit_solution(8394200906629983363)
XLA Ops:
  0.6 0.0 copy-start
  0.6 0.0 copy-start.1
  0.7 3.5 %attend_early.1 = (bf16[144,2048]{1,0:T(8,128)(2,1)S(1)}, bf16[2048,128]{1,0:T(8,128)(2,1)S(1)}) custom-call(s32[1,8]{1,0:T(1,128)} %bitcast.29, bf16[256,2048]{1,0:T(8,128)(2,1)} %bitcast.25, bf16[256,2048]{1,0:T(8,128)(2,1)} %bitcast.19, bf16[256,2048]{1,0:T(8,128)(2,1)} %bitcast.22), custom_call_target="tpu_custom_call" | custom-call | flops 134217728 | bytes 1572864 | tf_op jit(solution)/shard_map/attend_early/pallas_call | solution.py:352
  4.2 1.3 %collective-permute-start = (bf16[144,2048]{1,0:T(8,128)(2,1)S(1)}, bf16[144,2048]{1,0:T(8,128)(2,1)S(1)}, u32[]{:S(2)}, u32[]{:S(2)}) collective-permute-start(bf16[144,2048]{1,0:T(8,128)(2,1)S(1)} %get-tuple-element.10), channel_id=1, source_target_pairs={{2,0},{4,2},{6,4},{3,1},{5,3},{7,5},{10,8},{12,10},{14,12},{11,9},... | collective-permute-start | bytes 1769480 | tf_op jit(solution)/shard_map/ppermute | solution.py:34
  5.5 3.8 %attend_late.1.after_ref = bf16[32,2048]{1,0:T(8,128)(2,1)S(1)} custom-call(s32[1,8]{1,0:T(1,128)} %bitcast.30, bf16[256,2048]{1,0:T(8,128)(2,1)} %bitcast.26, bf16[256,2048]{1,0:T(8,128)(2,1)} %bitcast.20, bf16[256,2048]{1,0:T(8,128)(2,1)} %bitcast.23, bf16[2048,128]{1,0:T(8,128)(2,1)S(1)} %get-tuple-element.9.after_ref.early_ref), custom_call_target="tpu_custom_call" | custom-call | flops 268435456 | bytes 2621440 | tf_op jit(solution)/shard_map/attend_late/pallas_call | solution.py:377
  9.3 3.0 %collective-permute-start.1 = (bf16[32,2048]{1,0:T(8,128)(2,1)S(1)}, bf16[32,2048]{1,0:T(8,128)(2,1)S(1)}, u32[]{:S(2)}, u32[]{:S(2)}) collective-permute-start(bf16[32,2048]{1,0:T(8,128)(2,1)S(1)} %attend_late.1.after_ref), channel_id=1, source_target_pairs={{0,8},{8,16},{16,24},{24,0},{1,9},{9,17},{17,25},{25,1},{2,10},{10... | collective-permute-start | bytes 393224 | tf_op jit(solution)/shard_map/ppermute | solution.py:39
  13.0 0.0 copy-done
  13.0 0.0 copy-done.1
  13.0 2.6 %backward.1 = (bf16[64,2048]{1,0:T(8,128)(2,1)S(1)}, f32[8,2048]{1,0:T(8,128)S(1)}) custom-call(s32[1,1]{1,0:T(1,128)S(6)} %copy.17.slot_ref, bf16[64,1024]{1,0:T(8,128)(2,1)} %bitcast.28, bf16[2048,1024]{1,0:T(8,128)(2,1)S(1)} %bitcast.13, f32[1,2048]{1,0:T(1,128)S(1)} %copy-done.1, bf16[2,64,2048]{2,1,0:T(8,128)(2,1)} %bitcast.27, ...), custom_call_target="tpu_custom_call" | custom-call | flops 268435456 | bytes 4194304 | tf_op jit(solution)/shard_map/backward/pallas_call | solution.py:437
  15.6 1.0 %collective-permute-start.3 = (bf16[64,2048]{1,0:T(8,128)(2,1)S(1)}, bf16[64,2048]{1,0:T(8,128)(2,1)S(1)}, u32[]{:S(2)}, u32[]{:S(2)}) collective-permute-start(bf16[64,2048]{1,0:T(8,128)(2,1)S(1)} %get-tuple-element.11), channel_id=1, source_target_pairs={{0,24},{8,0},{16,8},{24,16},{1,25},{9,1},{17,9},{25,17},{2,26},{10... | collective-permute-start | bytes 786440 | tf_op jit(solution)/shard_map/ppermute | solution.py:39
  16.6 0.1 collective-permute-done.1.rest_0_.late_ref
  16.8 5.7 %collective-permute-done.q_ref = bf16[144,2048]{1,0:T(8,128)(2,1)S(1)} collective-permute-done((bf16[144,2048]{1,0:T(8,128)(2,1)S(1)}, bf16[144,2048]{1,0:T(8,128)(2,1)S(1)}, u32[]{:S(2)}, u32[]{:S(2)}) %collective-permute-start) | collective-permute-done | bytes 589856 | tf_op jit(solution)/shard_map/ppermute | solution.py:34
  22.4 3.9 %attend_halo.1 = bf16[48,2048]{1,0:T(8,128)(2,1)S(1)} custom-call(s32[1,8]{1,0:T(1,128)} %bitcast.31, bf16[144,2048]{1,0:T(8,128)(2,1)S(1)} %collective-permute-done.q_ref, bf16[256,2048]{1,0:T(8,128)(2,1)} %bitcast.21, bf16[256,2048]{1,0:T(8,128)(2,1)} %bitcast.24, bf16[32,2048]{1,0:T(8,128)(2,1)S(1)} %collective-permute-done.1.rest_0_.late_ref), custom_call_target="tpu_custom_call" | custom-call | flops 134217728 | bytes 1572864 | tf_op jit(solution)/shard_map/attend_halo/pallas_call | solution.py:402
  26.3 3.6 %collective-permute-start.2 = (bf16[48,2048]{1,0:T(8,128)(2,1)S(1)}, bf16[48,2048]{1,0:T(8,128)(2,1)S(1)}, u32[]{:S(2)}, u32[]{:S(2)}) collective-permute-start(bf16[48,2048]{1,0:T(8,128)(2,1)S(1)} %attend_halo.1), channel_id=1, source_target_pairs={{0,2},{2,4},{4,6},{1,3},{3,5},{5,7},{8,10},{10,12},{12,14},{9,11},... | collective-permute-start | bytes 589832 | tf_op jit(solution)/shard_map/ppermute | solution.py:34
  29.9 0.1 copy.12
  30.0 8.6 %all_to_all.11 = f32[8,1,2048]{2,1,0:T(1,128)S(1)} all-to-all(f32[8,1,2048]{2,1,0:T(1,128)S(1)} %copy.12), channel_id=1, replica_groups=mesh['section'=4,'seq'=4,'rep'=2] {'rep','seq'}, dimensions={0} | all-to-all | bytes 131072 | tf_op jit(solution)/shard_map/all_to_all | solution.py:484
  38.7 0.0 collective-permute-done.3.rest_0_
  38.7 0.0 collective-permute-done.2.halo_ref
  38.7 0.3 combine.1
  39.0 1.5 %collective-permute-start.4 = (bf16[32,2048]{1,0:T(8,128)(2,1)S(1)}, bf16[32,2048]{1,0:T(8,128)(2,1)S(1)}, u32[]{:S(2)}, u32[]{:S(2)}) collective-permute-start(bf16[32,2048]{1,0:T(8,128)(2,1)S(1)} %combine.1), channel_id=1, source_target_pairs={{0,8},{8,16},{16,24},{24,0},{1,9},{9,17},{17,25},{25,1},{2,10},{10... | collective-permute-start | bytes 393224 | tf_op jit(solution)/shard_map/ppermute | solution.py:39
  40.5 4.9 %collective-permute-done.4.early_ref = bf16[32,2048]{1,0:T(8,128)(2,1)S(1)} collective-permute-done((bf16[32,2048]{1,0:T(8,128)(2,1)S(1)}, bf16[32,2048]{1,0:T(8,128)(2,1)S(1)}, u32[]{:S(2)}, u32[]{:S(2)}) %collective-permute-start.4) | collective-permute-done | bytes 131104 | tf_op jit(solution)/shard_map/ppermute | solution.py:39
  45.5 1.6 %project.1 = (bf16[64,1024]{1,0:T(8,128)(2,1)}, f32[1,2048]{1,0:T(1,128)}) custom-call(bf16[32,2048]{1,0:T(8,128)(2,1)S(1)} %collective-permute-done.4.early_ref, bf16[32,2048]{1,0:T(8,128)(2,1)S(1)} %collective-permute-done.1.rest_0_.late_ref, f32[1,2048]{1,0:T(1,128)S(1)} %copy-done.1, bf16[2048,1024]{1,0:T(8,128)(2,1)S(1)} %bitcast.14, f32[8,2048]{1,0:T(8,128)S(1)} %bitcast.17), custom_call_target="tpu_custom_call" | custom-call | flops 268435456 | bytes 4194304 | tf_op jit(solution)/shard_map/project/pallas_call | solution.py:460
  47.0 0.7 %copy.18 = bf16[1,1,64,2048]{3,2,1,0:T(8,128)(2,1)} copy(bf16[1,1,64,2048]{3,2,1,0:T(8,128)(2,1)S(1)} %bitcast.15) | data formatting | bytes 524288
  (1 shorter events, 0.0 us)
Async XLA Ops:
  0.6 12.3 %copy-start = (bf16[1,2048,1024]{2,1,0:T(8,128)(2,1)S(1)}, bf16[1,2048,1024]{2,1,0:T(8,128)(2,1)}, u32[]{:S(2)}) copy-start(bf16[1,2048,1024]{2,1,0:T(8,128)(2,1)} %param.13) | copy-start | bytes 12582916
  0.6 12.3 %copy-start.1 = (f32[1,2048]{1,0:T(1,128)S(1)}, f32[1,2048]{1,0:T(1,128)}, u32[]{:S(2)}) copy-start(f32[1,2048]{1,0:T(1,128)} %gain_ref.3) | copy-start | bytes 24580
  4.2 18.3 %collective-permute-start = (bf16[144,2048]{1,0:T(8,128)(2,1)S(1)}, bf16[144,2048]{1,0:T(8,128)(2,1)S(1)}, u32[]{:S(2)}, u32[]{:S(2)}) collective-permute-start(bf16[144,2048]{1,0:T(8,128)(2,1)S(1)} %get-tuple-element.10), channel_id=1, source_target_pairs={{2,0},{4,2},{6,4},{3,1},{5,3},{7,5},{10,8},{12,10},{14,12},{11,9},... | collective-permute-start | bytes 1769480 | tf_op jit(solution)/shard_map/ppermute | solution.py:34
  9.3 7.4 %collective-permute-start.1 = (bf16[32,2048]{1,0:T(8,128)(2,1)S(1)}, bf16[32,2048]{1,0:T(8,128)(2,1)S(1)}, u32[]{:S(2)}, u32[]{:S(2)}) collective-permute-start(bf16[32,2048]{1,0:T(8,128)(2,1)S(1)} %attend_late.1.after_ref), channel_id=1, source_target_pairs={{0,8},{8,16},{16,24},{24,0},{1,9},{9,17},{17,25},{25,1},{2,10},{10... | collective-permute-start | bytes 393224 | tf_op jit(solution)/shard_map/ppermute | solution.py:39
  15.6 23.1 %collective-permute-start.3 = (bf16[64,2048]{1,0:T(8,128)(2,1)S(1)}, bf16[64,2048]{1,0:T(8,128)(2,1)S(1)}, u32[]{:S(2)}, u32[]{:S(2)}) collective-permute-start(bf16[64,2048]{1,0:T(8,128)(2,1)S(1)} %get-tuple-element.11), channel_id=1, source_target_pairs={{0,24},{8,0},{16,8},{24,16},{1,25},{9,1},{17,9},{25,17},{2,26},{10... | collective-permute-start | bytes 786440 | tf_op jit(solution)/shard_map/ppermute | solution.py:39
  26.3 12.4 %collective-permute-start.2 = (bf16[48,2048]{1,0:T(8,128)(2,1)S(1)}, bf16[48,2048]{1,0:T(8,128)(2,1)S(1)}, u32[]{:S(2)}, u32[]{:S(2)}) collective-permute-start(bf16[48,2048]{1,0:T(8,128)(2,1)S(1)} %attend_halo.1), channel_id=1, source_target_pairs={{0,2},{2,4},{4,6},{1,3},{3,5},{5,7},{8,10},{10,12},{12,14},{9,11},... | collective-permute-start | bytes 589832 | tf_op jit(solution)/shard_map/ppermute | solution.py:34
  39.0 6.5 %collective-permute-start.4 = (bf16[32,2048]{1,0:T(8,128)(2,1)S(1)}, bf16[32,2048]{1,0:T(8,128)(2,1)S(1)}, u32[]{:S(2)}, u32[]{:S(2)}) collective-permute-start(bf16[32,2048]{1,0:T(8,128)(2,1)S(1)} %combine.1), channel_id=1, source_target_pairs={{0,8},{8,16},{16,24},{24,0},{1,9},{9,17},{17,25},{25,1},{2,10},{10... | collective-permute-start | bytes 393224 | tf_op jit(solution)/shard_map/ppermute | solution.py:39

commit v4 on v3

v4 whole, which is shorter than its diff:
```python
import functools
import math

import jax
import jax.numpy as jnp
from jax import lax
from jax.experimental import pallas as pl
from jax.experimental.pallas import tpu as pltpu
from jax.sharding import PartitionSpec as P

HEAD_DIM = 64
POOL = 4
WINDOW = 128
LANES = 128
EPS_NORM = 1e-05
EPS_STEP = 1e-06
MASKED = -1e30
LAGS = (0, 2, 3, 4)

NT = (((1,), (1,)), ((), ()))


def dot_nt(a, b):
    return lax.dot_general(a, b, NT, preferred_element_type=jnp.float32)


def dot_nn(a, b):
    return jnp.dot(a, b, preferred_element_type=jnp.float32)


def shifted(value, axis, steps):
    count = lax.axis_size(axis)
    first, last = max(0, -steps), min(count, count - steps)
    return lax.ppermute(value, axis, [(i, i + steps) for i in range(first, last)])


def passed_along(value, axis, steps):
    count = lax.axis_size(axis)
    return lax.ppermute(value, axis, [(i, (i + steps) % count) for i in range(count)])


def earliest_key(offsets_ref, query_pos):
    start = jnp.zeros_like(query_pos)
    for d in range(offsets_ref.shape[1]):
        offset = offsets_ref[0, d]
        start = jnp.where(query_pos >= offset, offset, start)
    return jnp.maximum(start, query_pos - (WINDOW - 1))


def mask_bias(offsets_ref, query_start, key_start, keep):
    key = lax.broadcasted_iota(jnp.int32, (WINDOW, 2 * WINDOW), 0)
    query = lax.broadcasted_iota(jnp.int32, (WINDOW, 2 * WINDOW), 1) % WINDOW
    lane = lax.broadcasted_iota(jnp.int32, (1, 2 * WINDOW), 1) % WINDOW
    lowest = earliest_key(offsets_ref, query_start + lane)
    allowed = (key_start + key >= lowest) & keep(key, query)
    return jnp.where(allowed, 0.0, MASKED).astype(jnp.float32)


def split_heads(queries):
    lane = lax.broadcasted_iota(jnp.int32, (1, LANES), 1)
    scale = 1.0 / math.sqrt(HEAD_DIM)
    first = jnp.where(lane < HEAD_DIM, scale, 0.0).astype(jnp.bfloat16)
    second = jnp.where(lane < HEAD_DIM, 0.0, scale).astype(jnp.bfloat16)
    return jnp.concatenate([queries * first, queries * second], axis=0)


def pool_matrix(queries):
    molecule = lax.broadcasted_iota(jnp.int32, (queries // POOL, queries), 0)
    query = lax.broadcasted_iota(jnp.int32, (queries // POOL, queries), 1)
    return jnp.where(query // POOL == molecule, 1.0 / POOL, 0.0).astype(jnp.bfloat16)


def own_heads(mixed, scale):
    count = mixed.shape[1] // 2
    return jnp.concatenate(
        [
            mixed[:HEAD_DIM, :count] * scale[:, :count],
            mixed[HEAD_DIM:LANES, count:] * scale[:, count:],
        ],
        axis=0,
    )


def load(source, target, sem):
    copy = pltpu.make_async_copy(source, target, sem)
    copy.start()
    return copy


def load_chunks(arrays, chunks, sems):
    block = arrays[0][1].shape[1] // chunks
    return [
        [
            load(source.at[:, pl.ds(chunk * block, block)], target.at[:, pl.ds(chunk * block, block)], sems.at[i, chunk])
            for i, (source, target) in enumerate(arrays)
        ]
        for chunk in range(chunks)
    ]


def at(pair):
    return pl.ds(pair * LANES, LANES)


def over_pairs(pairs, stages, lags, before):
    results = {}
    for step in range(pairs + lags[-1]):
        if step < pairs:
            before(step)
        for stage, lag in zip(stages, lags):
            pair = step - lag
            if 0 <= pair < pairs:
                results[pair] = stage(pair, *results.get(pair, ()))


def tops(scores):
    rows = scores.shape[0]
    while rows > 8:
        rows //= 2
        scores = jnp.maximum(scores[:rows], scores[rows:])
    return jnp.max(scores, axis=0, keepdims=True)


def with_ones(values_t):
    return jnp.concatenate([values_t, jnp.ones((16, values_t.shape[1]), jnp.bfloat16)], axis=0)


def pool_into(pooling, out_ref, rows, parts, pair, last):
    if len(parts) == 4 or last:
        columns = pl.ds((pair + 1 - len(parts)) * LANES, len(parts) * LANES)
        pooled = dot_nt(pooling, jnp.concatenate(parts, axis=0))
        out_ref[pl.ds(0, rows), columns] = pooled.astype(jnp.bfloat16)
        parts.clear()


def three_terms(value):
    high = value.astype(jnp.bfloat16).astype(jnp.float32)
    middle = (value - high).astype(jnp.bfloat16).astype(jnp.float32)
    return [high, middle, value - high - middle]


def early_kernel(
    rows, chunks, offsets_hbm, q_hbm, k_hbm, v_hbm,
    sent_ref, early_ref, q_late_ref, k_ref, v_ref, own_ref, other_ref, next_ref,
    offsets_ref, bias, sems, offsets_sem,
):
    half = rows // 2
    head, tail = pl.ds(0, half), pl.ds(half, half)
    offsets_copy = load(offsets_hbm, offsets_ref, offsets_sem.at[0])
    arrays = (
        (k_hbm.at[head], k_ref.at[head]),
        (q_hbm.at[head], sent_ref.at[head]),
        (v_hbm.at[head], v_ref.at[head]),
    )
    copies = load_chunks(arrays, chunks, sems)
    rest = [
        load(k_hbm.at[tail], k_ref.at[tail], offsets_sem.at[1]),
        load(v_hbm.at[tail], v_ref.at[tail], offsets_sem.at[2]),
        load(q_hbm.at[tail], q_late_ref, offsets_sem.at[3]),
    ]
    offsets_copy.wait()
    start = lax.axis_index("seq") * rows
    bias[...] = mask_bias(offsets_ref, start, start, lambda key, query: key <= query)
    pairs = k_ref.shape[1] // LANES

    def arrive(pair):
        per_chunk = pairs // chunks
        if pair % per_chunk == 0:
            for copy in copies[pair // per_chunk]:
                copy.wait()

    def score(pair):
        scores = dot_nt(k_ref[head, at(pair)], split_heads(sent_ref[head, at(pair)]))
        return scores, with_ones(jnp.transpose(v_ref[head, at(pair)]))

    def top(pair, scores, values_t):
        scores = scores + bias[...]
        return scores, tops(scores), values_t

    def weigh(pair, scores, top, values_t):
        return top, dot_nn(values_t, jnp.exp(scores - top).astype(jnp.bfloat16))

    def finish(pair, top, mixed):
        total = mixed[LANES : LANES + 1]
        early_ref[at(pair), :] = own_heads(mixed, 1.0 / total).astype(jnp.bfloat16)
        lse = top + jnp.log(total)
        terms = three_terms(lse[:, :half]) + three_terms(lse[:, half:])
        terms.append(jnp.zeros((10, LANES), jnp.float32))
        sent_ref[pl.ds(half, 16), at(pair)] = jnp.concatenate(terms, axis=0).astype(jnp.bfloat16)
        return ()

    over_pairs(pairs, (score, top, weigh, finish), LAGS, arrive)
    own_ref[...] = mask_bias(offsets_ref, start + half, start + half, lambda key, query: key <= query)
    other_ref[...] = mask_bias(offsets_ref, start + half, start, lambda key, query: key > query)
    next_ref[...] = mask_bias(offsets_ref, start + rows, start + half, lambda key, query: key > query)
    for copy in rest:
        copy.wait()


def late_kernel(q_ref, k_ref, v_ref, own_bias, other_bias, late_ref, own, other):
    half = q_ref.shape[0]
    key = lax.broadcasted_iota(jnp.int32, own.shape, 0)
    query = lax.broadcasted_iota(jnp.int32, own.shape, 1) % half
    own[...] = jnp.where(key <= query, 1.0, 0.0).astype(jnp.bfloat16)
    other[...] = jnp.where(key <= query, 0.0, 1.0).astype(jnp.bfloat16)
    pooling = pool_matrix(half)
    pairs = k_ref.shape[1] // LANES
    parts = []

    def score(pair):
        scores = dot_nt(k_ref[:, at(pair)], split_heads(q_ref[:, at(pair)]))
        return scores, with_ones(jnp.transpose(v_ref[:, at(pair)]))

    def top(pair, scores, values_t):
        scores = jnp.maximum(scores[:half] + other_bias[...], scores[half:] + own_bias[...])
        return scores, tops(scores), values_t

    def weigh(pair, scores, top, values_t):
        weights = jnp.exp(scores - top).astype(jnp.bfloat16)
        weights = jnp.concatenate([weights * other[...], weights * own[...]], axis=0)
        return (dot_nn(values_t, weights),)

    def finish(pair, mixed):
        inverse = 1.0 / mixed[LANES : LANES + 1]
        parts.append(own_heads(mixed, inverse).astype(jnp.bfloat16))
        pool_into(pooling, late_ref, half // POOL, parts, pair, pair == pairs - 1)
        return ()

    over_pairs(pairs, (score, top, weigh, finish), LAGS, lambda pair: None)


def halo_kernel(q_ref, k_ref, v_ref, bias, term_ref, other_ref, *rest):
    out_ref, sum_ref = rest[-2:]
    sum_ref[...] = term_ref[...] + other_ref[...]
    half = bias.shape[0]
    molecules = half // POOL
    tail = pl.ds(half, half)
    pooling = pool_matrix(half)
    pairs = k_ref.shape[1] // LANES
    parts = []

    def score(pair):
        queries = split_heads(q_ref[pl.ds(0, half), at(pair)])
        scores = dot_nt(k_ref[tail, at(pair)], queries)
        return scores, with_ones(jnp.transpose(v_ref[tail, at(pair)]))

    def top(pair, scores, values_t):
        terms = q_ref[pl.ds(half, 16), at(pair)].astype(jnp.float32)
        lse = jnp.concatenate(
            [terms[0:1] + terms[1:2] + terms[2:3], terms[3:4] + terms[4:5] + terms[5:6]], axis=1
        )
        scores = scores + bias[...]
        return scores, jnp.maximum(tops(scores), lse), lse, values_t

    def weigh(pair, scores, top, lse, values_t):
        mixed = dot_nn(values_t, jnp.exp(scores - top).astype(jnp.bfloat16))
        return mixed, jnp.exp(lse - top)

    def finish(pair, mixed, kept):
        inverse = 1.0 / (mixed[LANES : LANES + 1] + kept)
        parts.append(own_heads(mixed, inverse).astype(jnp.bfloat16))
        pool_into(pooling, out_ref, molecules, parts, pair, pair == pairs - 1)
        share = kept * inverse
        high = share.astype(jnp.bfloat16).astype(jnp.float32)
        low = share - high
        shares = [high[:, :half], low[:, :half], high[:, half:], low[:, half:]]
        shares.append(jnp.zeros((12, LANES), jnp.float32))
        out_ref[pl.ds(molecules, 16), at(pair)] = jnp.concatenate(shares, axis=0).astype(jnp.bfloat16)
        return ()

    over_pairs(pairs, (score, top, weigh, finish), LAGS, lambda pair: None)


def back_kernel(
    slot_ref, cotangent_hbm, weight_ref, gain_ref, stashed_hbm, after_ref, dinput_ref, term_ref,
    cotangent_ref, held_ref, grad, sems,
):
    cotangent_copy = load(cotangent_hbm, cotangent_ref, sems.at[1])
    held_copy = load(stashed_hbm.at[slot_ref[0, 0]], held_ref, sems.at[0])
    cotangent_copy.wait()
    features = weight_ref.shape[0]
    block = 512
    for begin in range(0, features, block):
        columns = pl.ds(begin, block)
        grad[:, columns] = dot_nt(cotangent_ref[...], weight_ref[columns, :])
    held_copy.wait()
    held = held_ref[...].astype(jnp.float32)
    inv_rms = lax.rsqrt(jnp.sum(held * held, axis=1, keepdims=True) / features + EPS_NORM)
    along = jnp.zeros_like(inv_rms)
    for begin in range(0, features, block):
        columns = pl.ds(begin, block)
        product = grad[:, columns] * (held_ref[:, columns].astype(jnp.float32) * inv_rms)
        term_ref[:, columns] = jnp.sum(product, axis=0, keepdims=True)
        along += jnp.sum(product * gain_ref[:, columns], axis=1, keepdims=True)
    along = along / features
    for begin in range(0, features, block):
        columns = pl.ds(begin, block)
        whitened = held_ref[:, columns].astype(jnp.float32) * inv_rms
        scaled = grad[:, columns] * gain_ref[:, columns]
        dinput_ref[:, columns] = (inv_rms * (scaled - whitened * along)).astype(jnp.bfloat16)


def project_kernel(
    early_ref, late_ref, halo_ref, gain_ref, weight_ref, term_ref, other_ref, upstream_hbm,
    out_ref, update_ref, passed_hbm, pooled, sem,
):
    passing = load(upstream_hbm, passed_hbm, sem)
    half = early_ref.shape[1]
    molecules = half // POOL
    pooling = pool_matrix(half)
    first = lax.axis_index("seq") == 0
    parts = []
    for pair in range(early_ref.shape[0] // LANES):
        shares = halo_ref[molecules:, at(pair)].astype(jnp.float32)
        share_a = jnp.where(first, 1.0, shares[0:1] + shares[1:2])
        share_b = jnp.where(first, 1.0, shares[2:3] + shares[3:4])
        early = early_ref[at(pair), :].astype(jnp.float32)
        parts += [early[:HEAD_DIM] * share_a, early[HEAD_DIM:] * share_b]
        if len(parts) == 8:
            columns = pl.ds((pair - 3) * LANES, 4 * LANES)
            mean = dot_nt(pooling, jnp.concatenate(parts, axis=0).astype(jnp.bfloat16))
            arrived = halo_ref[:molecules, columns].astype(jnp.float32)
            pooled[pl.ds(0, molecules), columns] = (mean + arrived).astype(jnp.bfloat16)
            parts = []
    pooled[pl.ds(molecules, molecules), :] = late_ref[...]
    features = gain_ref.shape[1]
    arrived = pooled[...].astype(jnp.float32)
    mean = jnp.sum(arrived * arrived, axis=1, keepdims=True) / features
    normed = (arrived * lax.rsqrt(mean + EPS_NORM) * gain_ref[...]).astype(jnp.bfloat16)
    out_ref[...] = dot_nn(normed, weight_ref[...]).astype(jnp.bfloat16)
    total = term_ref[...] + other_ref[...]
    mean = jnp.sum(total * total, axis=1, keepdims=True) / features
    update_ref[...] = total / jnp.sqrt(mean + EPS_STEP)
    passing.wait()


def cost(flops, read, exps=0):
    return pl.CostEstimate(flops=flops, bytes_accessed=read, transcendentals=exps)


SMEM = pl.BlockSpec(memory_space=pltpu.SMEM)
HBM = pl.BlockSpec(memory_space=pltpu.HBM)
ANY = pl.BlockSpec(memory_space=pl.ANY)
VMEM = pl.BlockSpec(memory_space=pltpu.VMEM)


def in_hbm(*arrays):
    return [pltpu.with_memory_space_constraint(x, pltpu.HBM) for x in arrays]


def params():
    return pltpu.CompilerParams(vmem_limit_bytes=24 * 2**20)


def attend_early(queries, keys, values, offsets, chunks):
    rows, width = queries.shape
    half = rows // 2
    masks = [jax.ShapeDtypeStruct((half, 2 * half), jnp.float32)] * 3
    return pl.pallas_call(
        functools.partial(early_kernel, rows, chunks),
        in_specs=[HBM] * 4,
        out_specs=[VMEM] * 8,
        out_shape=[
            jax.ShapeDtypeStruct((half + 16, width), jnp.bfloat16),
            jax.ShapeDtypeStruct((width, half), jnp.bfloat16),
            jax.ShapeDtypeStruct((half, width), jnp.bfloat16),
            jax.ShapeDtypeStruct((rows, width), jnp.bfloat16),
            jax.ShapeDtypeStruct((rows, width), jnp.bfloat16),
        ]
        + masks,
        scratch_shapes=[
            pltpu.SMEM(offsets.shape, jnp.int32),
            pltpu.VMEM((half, 2 * half), jnp.float32),
            pltpu.SemaphoreType.DMA((3, chunks)),
            pltpu.SemaphoreType.DMA((4,)),
        ],
        cost_estimate=cost(4 * half * half * width, 6 * rows * width, half * half * width // 64),
        compiler_params=params(),
        name="attend_early",
    )(*in_hbm(offsets, queries, keys, values))


def attend_late(queries, keys, values, own_bias, other_bias):
    half, width = queries.shape
    return pl.pallas_call(
        late_kernel,
        in_specs=[VMEM] * 5,
        out_specs=VMEM,
        out_shape=jax.ShapeDtypeStruct((half // POOL, width), jnp.bfloat16),
        scratch_shapes=[pltpu.VMEM((half, 2 * half), jnp.bfloat16)] * 2,
        cost_estimate=cost(8 * half * half * width, 10 * half * width, half * half * width // 64),
        compiler_params=params(),
        name="attend_late",
    )(queries, keys, values, own_bias, other_bias)


def attend_halo(sent, keys, values, bias, term, other, after):
    half, width = bias.shape[0], keys.shape[1]
    return pl.pallas_call(
        halo_kernel,
        in_specs=[VMEM] * 6 + [ANY] * len(after),
        out_specs=[VMEM] * 2,
        out_shape=[
            jax.ShapeDtypeStruct((half // POOL + 16, width), jnp.bfloat16),
            jax.ShapeDtypeStruct(term.shape, term.dtype),
        ],
        cost_estimate=cost(4 * half * half * width, 6 * half * width, half * half * width // 64),
        compiler_params=params(),
        name="attend_halo",
    )(sent, keys, values, bias, term, other, *after)


def backward(slot, cotangent, weight, gain, stashed, after):
    rows, depth = cotangent.shape
    width = weight.shape[0]
    return pl.pallas_call(
        back_kernel,
        in_specs=[SMEM, HBM, VMEM, VMEM, HBM, ANY],
        out_specs=[VMEM] * 2,
        scratch_shapes=[
            pltpu.VMEM((rows, depth), jnp.bfloat16),
            pltpu.VMEM((rows, width), jnp.bfloat16),
            pltpu.VMEM((rows, width), jnp.float32),
            pltpu.SemaphoreType.DMA((2,)),
        ],
        out_shape=[
            jax.ShapeDtypeStruct((rows, width), jnp.bfloat16),
            jax.ShapeDtypeStruct((1, width), jnp.float32),
        ],
        cost_estimate=cost(2 * rows * width * depth, 2 * width * depth),
        compiler_params=params(),
        name="backward",
    )(slot, *in_hbm(cotangent), weight, gain, *in_hbm(stashed), after)


def project(early, late, halo, gain, weight, term, other, upstream):
    rows = 2 * late.shape[0]
    width, depth = weight.shape
    return pl.pallas_call(
        project_kernel,
        in_specs=[VMEM] * 7 + [ANY],
        out_specs=[VMEM, VMEM, HBM],
        out_shape=[
            jax.ShapeDtypeStruct((rows, depth), jnp.bfloat16),
            jax.ShapeDtypeStruct((1, width), jnp.float32),
            jax.ShapeDtypeStruct(upstream.shape, upstream.dtype),
        ],
        scratch_shapes=[pltpu.VMEM((rows, width), jnp.bfloat16), pltpu.SemaphoreType.DMA],
        cost_estimate=cost(2 * rows * width * depth, 2 * width * depth),
        compiler_params=params(),
        name="project",
    )(early, late, halo, gain, weight, term, other, upstream)


def swapped(value, axis, distance):
    return lax.ppermute(value, axis, [(i, i ^ distance) for i in range(lax.axis_size(axis))])


def sum_rounds():
    rounds = []
    for axis in ("rep", "seq"):
        count = lax.axis_size(axis)
        if count & (count - 1):
            return []
        rounds += [(axis, 1 << i) for i in range(count.bit_length() - 1)]
    return rounds if len(rounds) == 3 else []


def onward(value):
    sections, shards = lax.axis_size("section"), lax.axis_size("seq")
    route = [
        (s * shards + k, (s + 1) % sections * shards + k + 1)
        for s in range(sections)
        for k in range(shards - 1)
    ]
    return lax.ppermute(value, ("section", "seq"), route)


def local(queries, keys, values, doc_starts, weight, gain, stashed, cotangent, slot):
    queries, keys, values, offsets = queries[0, 0], keys[0, 0], values[0, 0], doc_starts[0]
    rounds = sum_rounds()

    def partner(term, index):
        return swapped(term, *rounds[index]) if rounds else jnp.zeros_like(term)

    sent, early, q_late, keys, values, own_bias, other_bias, next_bias = attend_early(
        queries, keys, values, offsets, 4
    )
    arrived = shifted(sent, "seq", -1)
    early = passed_along(early, "section", 1)
    late = attend_late(q_late, keys, values, own_bias, other_bias)
    late_arrived = passed_along(late, "section", 1)
    dinput, term = backward(slot, cotangent[0, 0], weight[0], gain, stashed[0, 0], late)
    upstream = passed_along(dinput, "section", -1)
    term = term if rounds else lax.psum(term, ("rep", "seq"))
    halo, term = attend_halo(arrived, keys, values, next_bias, term, partner(term, 0), (late_arrived,))
    halo = onward(halo)
    term = term + partner(term, 1)
    mol_keys, update, upstream = project(
        early, late_arrived, halo, gain, weight[0], term, partner(term, 2), upstream
    )
    return mol_keys[None, None], upstream[None, None], update


def solution(mesh):
    in_specs = (
        P("rep", "section", "seq", None),
        P("rep", "section", "seq", None),
        P("rep", "section", "seq", None),
        P("rep", "section", None),
        P("section", None, None),
        P("section", None),
        P("rep", "section", None, "seq", None),
        P("rep", "section", "seq", None),
        P("rep", "section"),
    )
    out_specs = (
        P("rep", "section", "seq", None),
        P("rep", "section", "seq", None),
        P("section", None),
    )
    return jax.shard_map(local, mesh=mesh, in_specs=in_specs, out_specs=out_specs, check_vma=False)
```

time: 48 us -> 42.4 us (0.88)
  blocking collectives: 8.64 us -> 0 us
  starting transfers between devices: 10.5 us -> 16.7 us
  Pallas kernels: 15.7 us -> 11.6 us
  waiting for transfers between devices: 10.7 us -> 12.4 us
  local copies, waits for them, and re-layouts: 0.8 us -> 0.01 us
    ppermute x0 -> x4, starting transfers between devices: none -> 9.47 us  [the longest x1 5.15 us: onward(): return lax.ppermute(value, ('section', 'seq'), route)]
    all_to_all x1 -> x0, blocking collectives: 8.64 us -> none  [local(): terms = lax.all_to_all(terms, group, 0, 0, tiled=True)]
    ppermute x2 -> x1, waiting for transfers between devices: 5.66 us -> 0.01 us  [shifted(): lax.ppermute(value, axis, [(i, i + steps) for i in range(first, last)])]
    ppermute x0 -> x4, waiting for transfers between devices: none -> 5.18 us  [the longest x3 5.18 us: swapped(): lax.ppermute(value, axis, [(i, i ^ distance) for i in range(lax.axis_size...]
    pallas_call x4 -> x3, Pallas kernels: 9.59 us -> 5.44 us  [the longest x1 1.88 us: project(): pl.pallas_call(project_kernel, in_specs=[VMEM] * 7 + [ANY], out_specs=[VM...]
    ppermute x2 -> x1, starting transfers between devices: 4.94 us -> 1.29 us  [shifted(): lax.ppermute(value, axis, [(i, i + steps) for i in range(first, last)])]
    ppermute x3, waiting for transfers between devices: 5.04 us -> 7.26 us  [passed_along(): lax.ppermute(value, axis, [(i, (i + steps) % count) for i in range(count)])]
    unnamed x6 -> x4, local copies, waits for them, and re-layouts: 0.73 us -> 0.01 us
  transfers between devices with their start and end apart: 5 -> 8, of which waited for: 3 -> 4; matrix products, arithmetic and copies ran while one was open for 0% -> 0% of each run, Pallas kernels for 22% -> 15%
where the time goes in v4:
time: 42.4 us; the launch traced here: 42.2 us
  starting transfers between devices  16.7 us (39%)
  waiting for transfers between devices  12.4 us (29%)
  Pallas kernels  11.6 us (27%)
  between operations  1.36 us (3%)
    ppermute x3, waiting for transfers between devices, passed_along(): lax.ppermute(value, axis, [(i, (i + steps) % count) for i in range(count)])  7.26 us
    ppermute x3, starting transfers between devices, passed_along(): lax.ppermute(value, axis, [(i, (i + steps) % count) for i in range(count)])  5.99 us
    ppermute x3, waiting for transfers between devices, swapped(): lax.ppermute(value, axis, [(i, i ^ distance) for i in range(lax.axis_size...  5.18 us
    ppermute x1, starting transfers between devices, onward(): return lax.ppermute(value, ('section', 'seq'), route)  5.15 us
    ppermute x3, starting transfers between devices, swapped(): lax.ppermute(value, axis, [(i, i ^ distance) for i in range(lax.axis_size...  4.32 us
    pallas_call x1, Pallas kernels, attend_early(): pl.pallas_call(functools.partial(early_kernel, rows, chunks), in_specs=[H...  3.54 us
    pallas_call x1, Pallas kernels, backward(): pl.pallas_call(back_kernel, in_specs=[SMEM, HBM, VMEM, VMEM, HBM, ANY], o...  2.65 us
    pallas_call x1, Pallas kernels, project(): pl.pallas_call(project_kernel, in_specs=[VMEM] * 7 + [ANY], out_specs=[VM...  1.88 us
  transfers between devices with their start and end apart: 8, of which 4 were waited for; matrix products, arithmetic and copies ran while one was open for 0% of the time, Pallas kernels for 15%

profile of v4, /device:TPU:0, one launch (start us, length us, event | category | flops | bytes accessed | tf_op | source)
XLA Modules:
  0.0 42.2 jit_solution(15479596138353981592)
XLA Ops:
  0.6 0.0 copy-start.1
  0.6 0.0 copy-start
  0.7 3.5 %attend_early.1 = (bf16[144,2048]{1,0:T(8,128)(2,1)S(1)}, bf16[2048,128]{1,0:T(8,128)(2,1)S(1)}, bf16[128,2048]{1,0:T(8,128)(2,1)S(1)}, bf16[256,2048]{1,0:T(8,1...) custom-call(s32[1,8]{1,0:T(1,128)} %bitcast.16, ...), custom_call_target="tpu_custom_call" | custom-call | flops 134217728 | bytes 3145728 | tf_op jit(solution)/shard_map/attend_early/pallas_call | solution.py:359
  4.2 1.3 %collective-permute-start.2 = (bf16[144,2048]{1,0:T(8,128)(2,1)S(1)}, bf16[144,2048]{1,0:T(8,128)(2,1)S(1)}, u32[]{:S(2)}, u32[]{:S(2)}) collective-permute-start(bf16[144,2048]{1,0:T(8,128)(2,1)S(1)} %get-tuple-element.24), channel_id=1, source_target_pairs={{2,0},{4,2},{6,4},{3,1},{5,3},{7,5},{10,8},{12,10},{14,12},{11,9},... | collective-permute-start | bytes 1769480 | tf_op jit(solution)/shard_map/ppermute | solution.py:34
  5.5 3.0 %collective-permute-start = (bf16[2048,128]{1,0:T(8,128)(2,1)S(1)}, bf16[2048,128]{1,0:T(8,128)(2,1)S(1)}, u32[]{:S(2)}, u32[]{:S(2)}) collective-permute-start(bf16[2048,128]{1,0:T(8,128)(2,1)S(1)} %get-tuple-element.18), channel_id=1, source_target_pairs={{0,8},{8,16},{16,24},{24,0},{1,9},{9,17},{17,25},{25,1},{2,10},{10... | collective-permute-start | bytes 1572872 | tf_op jit(solution)/shard_map/ppermute | solution.py:39
  8.5 1.8 %attend_late.1.after_ref = bf16[32,2048]{1,0:T(8,128)(2,1)S(1)} custom-call(bf16[128,2048]{1,0:T(8,128)(2,1)S(1)} %get-tuple-element.19.q_ref, bf16[256,2048]{1,0:T(8,128)(2,1)S(1)} %get-tuple-element.20.k_ref, bf16[256,2048]{1,0:T(8,128)(2,1)S(1)} %get-tuple-element.21.v_ref, f32[128,256]{1,0:T(8,128)S(1)} %get-tuple-element.22.own_bias, ...), custom_call_target="tpu_custom_call" | custom-call | flops 268435456 | bytes 2621440 | tf_op jit(solution)/shard_map/attend_late/pallas_call | solution.py:385
  10.3 1.5 %collective-permute-start.1 = (bf16[32,2048]{1,0:T(8,128)(2,1)S(1)}, bf16[32,2048]{1,0:T(8,128)(2,1)S(1)}, u32[]{:S(2)}, u32[]{:S(2)}) collective-permute-start(bf16[32,2048]{1,0:T(8,128)(2,1)S(1)} %attend_late.1.after_ref), channel_id=1, source_target_pairs={{0,8},{8,16},{16,24},{24,0},{1,9},{9,17},{17,25},{25,1},{2,10},{10... | collective-permute-start | bytes 393224 | tf_op jit(solution)/shard_map/ppermute | solution.py:39
  12.4 0.0 copy-done.1
  12.4 0.0 copy-done
  12.4 2.6 %backward.1 = (bf16[64,2048]{1,0:T(8,128)(2,1)S(1)}, f32[1,2048]{1,0:T(1,128)S(1)}) custom-call(s32[1,1]{1,0:T(1,128)S(6)} %copy.12.slot_ref, bf16[64,1024]{1,0:T(8,128)(2,1)} %bitcast.15, bf16[2048,1024]{1,0:T(8,128)(2,1)S(1)} %bitcast.9, f32[1,2048]{1,0:T(1,128)S(1)} %copy-done.1, bf16[2,64,2048]{2,1,0:T(8,128)(2,1)} %bitcast.14, ...), custom_call_target="tpu_custom_call" | custom-call | flops 268435456 | bytes 4194304 | tf_op jit(solution)/shard_map/backward/pallas_call | solution.py:416
  15.1 1.5 %collective-permute-start.7 = (bf16[64,2048]{1,0:T(8,128)(2,1)S(1)}, bf16[64,2048]{1,0:T(8,128)(2,1)S(1)}, u32[]{:S(2)}, u32[]{:S(2)}) collective-permute-start(bf16[64,2048]{1,0:T(8,128)(2,1)S(1)} %get-tuple-element.29), channel_id=1, source_target_pairs={{0,24},{8,0},{16,8},{24,16},{1,25},{9,1},{17,9},{25,17},{2,26},{10... | collective-permute-start | bytes 786440 | tf_op jit(solution)/shard_map/ppermute | solution.py:39
  16.6 0.0 collective-permute-start.3
  16.6 1.2 %collective-permute-done.3.other_ref = f32[1,2048]{1,0:T(1,128)S(1)} collective-permute-done((f32[1,2048]{1,0:T(1,128)S(1)}, f32[1,2048]{1,0:T(1,128)S(1)}, u32[]{:S(2)}, u32[]{:S(2)}) %collective-permute-start.3) | collective-permute-done | bytes 8224 | tf_op jit(solution)/shard_map/ppermute | solution.py:456
  17.8 7.3 %collective-permute-done.1.rest_0_.late_ref = bf16[32,2048]{1,0:T(8,128)(2,1)S(1)} collective-permute-done((bf16[32,2048]{1,0:T(8,128)(2,1)S(1)}, bf16[32,2048]{1,0:T(8,128)(2,1)S(1)}, u32[]{:S(2)}, u32[]{:S(2)}) %collective-permute-start.1) | collective-permute-done | bytes 131104 | tf_op jit(solution)/shard_map/ppermute | solution.py:39
  25.0 0.0 collective-permute-done.2.q_ref
  25.0 1.8 %attend_halo.1 = (bf16[48,2048]{1,0:T(8,128)(2,1)S(1)}, f32[1,2048]{1,0:T(1,128)S(1)}) custom-call(bf16[144,2048]{1,0:T(8,128)(2,1)S(1)} %collective-permute-done.2.q_ref, bf16[256,2048]{1,0:T(8,128)(2,1)S(1)} %get-tuple-element.20.k_ref, bf16[256,2048]{1,0:T(8,128)(2,1)S(1)} %get-tuple-element.21.v_ref, f32[128,256]{1,0:T(8,128)S(1)} %get-tuple-element.25.bias, ...), custom_call_target="tpu_custom_call" | custom-call | flops 134217728 | bytes 1572864 | tf_op jit(solution)/shard_map/attend_halo/pallas_call | solution.py:399
  26.8 5.1 %collective-permute-start.4 = (bf16[48,2048]{1,0:T(8,128)(2,1)S(1)}, bf16[48,2048]{1,0:T(8,128)(2,1)S(1)}, u32[]{:S(2)}, u32[]{:S(2)}) collective-permute-start(bf16[48,2048]{1,0:T(8,128)(2,1)S(1)} %get-tuple-element.27), channel_id=1, source_target_pairs={{0,10},{2,12},{4,14},{8,18},{10,20},{12,22},{16,26},{18,28},{20,30... | collective-permute-start | bytes 589832 | tf_op jit(solution)/shard_map/ppermute | solution.py:476
  32.0 1.6 %collective-permute-start.5 = (f32[1,2048]{1,0:T(1,128)S(1)}, f32[1,2048]{1,0:T(1,128)S(1)}, u32[]{:S(2)}, u32[]{:S(2)}) collective-permute-start(f32[1,2048]{1,0:T(1,128)S(1)} %get-tuple-element.28), channel_id=1, source_target_pairs={{0,2},{2,0},{4,6},{6,4},{1,3},{3,1},{5,7},{7,5},{8,10},{10,8},{12,... | collective-permute-start | bytes 24584 | tf_op jit(solution)/shard_map/ppermute | solution.py:456
  33.6 2.1 %collective-permute-done.5 = f32[1,2048]{1,0:T(1,128)S(1)} collective-permute-done((f32[1,2048]{1,0:T(1,128)S(1)}, f32[1,2048]{1,0:T(1,128)S(1)}, u32[]{:S(2)}, u32[]{:S(2)}) %collective-permute-start.5) | collective-permute-done | bytes 8224 | tf_op jit(solution)/shard_map/ppermute | solution.py:456
  35.7 2.7 %collective-permute-start.6 = (f32[1,2048]{1,0:T(1,128)S(1)}, f32[1,2048]{1,0:T(1,128)S(1)}, u32[]{:S(2)}, u32[]{:S(2)}) collective-permute-start(f32[1,2048]{1,0:T(1,128)S(1)} %add.3.term_ref), channel_id=1, source_target_pairs={{0,4},{2,6},{4,0},{6,2},{1,5},{3,7},{5,1},{7,3},{8,12},{10,14},{12... | collective-permute-start | bytes 24584 | tf_op jit(solution)/shard_map/ppermute | solution.py:456
  38.4 0.0 collective-permute-done.7.upstream_hbm
  38.4 0.0 collective-permute-done.early_ref
  38.4 1.9 %collective-permute-done.6.other_ref = f32[1,2048]{1,0:T(1,128)S(1)} collective-permute-done((f32[1,2048]{1,0:T(1,128)S(1)}, f32[1,2048]{1,0:T(1,128)S(1)}, u32[]{:S(2)}, u32[]{:S(2)}) %collective-permute-start.6) | collective-permute-done | bytes 8224 | tf_op jit(solution)/shard_map/ppermute | solution.py:456
  40.3 0.0 collective-permute-done.4.halo_ref
  40.3 1.9 %project.1 = (bf16[64,1024]{1,0:T(8,128)(2,1)}, f32[1,2048]{1,0:T(1,128)}, bf16[64,2048]{1,0:T(8,128)(2,1)}) custom-call(bf16[2048,128]{1,0:T(8,128)(2,1)S(1)} %collective-permute-done.early_ref, bf16[32,2048]{1,0:T(8,128)(2,1)S(1)} %collective-permute-done.1.rest_0_.late_ref, bf16[48,2048]{1,0:T(8,128)(2,1)S(1)} %collective-permute-done.4.halo_ref, ...), custom_call_target="tpu_custom_call" | custom-call | flops 268435456 | bytes 4194304 | tf_op jit(solution)/shard_map/project/pallas_call | solution.py:439
  (1 shorter events, 0.0 us)
Async XLA Ops:
  0.6 11.8 %copy-start.1 = (f32[1,2048]{1,0:T(1,128)S(1)}, f32[1,2048]{1,0:T(1,128)}, u32[]{:S(2)}) copy-start(f32[1,2048]{1,0:T(1,128)} %gain_ref.3) | copy-start | bytes 24580
  0.6 11.8 %copy-start = (bf16[1,2048,1024]{2,1,0:T(8,128)(2,1)S(1)}, bf16[1,2048,1024]{2,1,0:T(8,128)(2,1)}, u32[]{:S(2)}) copy-start(bf16[1,2048,1024]{2,1,0:T(8,128)(2,1)} %param.13) | copy-start | bytes 12582916
  4.2 20.8 %collective-permute-start.2 = (bf16[144,2048]{1,0:T(8,128)(2,1)S(1)}, bf16[144,2048]{1,0:T(8,128)(2,1)S(1)}, u32[]{:S(2)}, u32[]{:S(2)}) collective-permute-start(bf16[144,2048]{1,0:T(8,128)(2,1)S(1)} %get-tuple-element.24), channel_id=1, source_target_pairs={{2,0},{4,2},{6,4},{3,1},{5,3},{7,5},{10,8},{12,10},{14,12},{11,9},... | collective-permute-start | bytes 1769480 | tf_op jit(solution)/shard_map/ppermute | solution.py:34
  5.5 32.9 %collective-permute-start = (bf16[2048,128]{1,0:T(8,128)(2,1)S(1)}, bf16[2048,128]{1,0:T(8,128)(2,1)S(1)}, u32[]{:S(2)}, u32[]{:S(2)}) collective-permute-start(bf16[2048,128]{1,0:T(8,128)(2,1)S(1)} %get-tuple-element.18), channel_id=1, source_target_pairs={{0,8},{8,16},{16,24},{24,0},{1,9},{9,17},{17,25},{25,1},{2,10},{10... | collective-permute-start | bytes 1572872 | tf_op jit(solution)/shard_map/ppermute | solution.py:39
  10.3 14.8 %collective-permute-start.1 = (bf16[32,2048]{1,0:T(8,128)(2,1)S(1)}, bf16[32,2048]{1,0:T(8,128)(2,1)S(1)}, u32[]{:S(2)}, u32[]{:S(2)}) collective-permute-start(bf16[32,2048]{1,0:T(8,128)(2,1)S(1)} %attend_late.1.after_ref), channel_id=1, source_target_pairs={{0,8},{8,16},{16,24},{24,0},{1,9},{9,17},{17,25},{25,1},{2,10},{10... | collective-permute-start | bytes 393224 | tf_op jit(solution)/shard_map/ppermute | solution.py:39
  15.1 23.3 %collective-permute-start.7 = (bf16[64,2048]{1,0:T(8,128)(2,1)S(1)}, bf16[64,2048]{1,0:T(8,128)(2,1)S(1)}, u32[]{:S(2)}, u32[]{:S(2)}) collective-permute-start(bf16[64,2048]{1,0:T(8,128)(2,1)S(1)} %get-tuple-element.29), channel_id=1, source_target_pairs={{0,24},{8,0},{16,8},{24,16},{1,25},{9,1},{17,9},{25,17},{2,26},{10... | collective-permute-start | bytes 786440 | tf_op jit(solution)/shard_map/ppermute | solution.py:39
  16.6 1.2 %collective-permute-start.3 = (f32[1,2048]{1,0:T(1,128)S(1)}, f32[1,2048]{1,0:T(1,128)S(1)}, u32[]{:S(2)}, u32[]{:S(2)}) collective-permute-start(f32[1,2048]{1,0:T(1,128)S(1)} %get-tuple-element.26.term_ref), channel_id=1, source_target_pairs={{0,1},{1,0},{2,3},{3,2},{4,5},{5,4},{6,7},{7,6},{8,9},{9,8},{10,11... | collective-permute-start | bytes 24584 | tf_op jit(solution)/shard_map/ppermute | solution.py:456
  26.8 13.5 %collective-permute-start.4 = (bf16[48,2048]{1,0:T(8,128)(2,1)S(1)}, bf16[48,2048]{1,0:T(8,128)(2,1)S(1)}, u32[]{:S(2)}, u32[]{:S(2)}) collective-permute-start(bf16[48,2048]{1,0:T(8,128)(2,1)S(1)} %get-tuple-element.27), channel_id=1, source_target_pairs={{0,10},{2,12},{4,14},{8,18},{10,20},{12,22},{16,26},{18,28},{20,30... | collective-permute-start | bytes 589832 | tf_op jit(solution)/shard_map/ppermute | solution.py:476
  32.0 3.7 %collective-permute-start.5 = (f32[1,2048]{1,0:T(1,128)S(1)}, f32[1,2048]{1,0:T(1,128)S(1)}, u32[]{:S(2)}, u32[]{:S(2)}) collective-permute-start(f32[1,2048]{1,0:T(1,128)S(1)} %get-tuple-element.28), channel_id=1, source_target_pairs={{0,2},{2,0},{4,6},{6,4},{1,3},{3,1},{5,7},{7,5},{8,10},{10,8},{12,... | collective-permute-start | bytes 24584 | tf_op jit(solution)/shard_map/ppermute | solution.py:456
  35.7 4.6 %collective-permute-start.6 = (f32[1,2048]{1,0:T(1,128)S(1)}, f32[1,2048]{1,0:T(1,128)S(1)}, u32[]{:S(2)}, u32[]{:S(2)}) collective-permute-start(f32[1,2048]{1,0:T(1,128)S(1)} %add.3.term_ref), channel_id=1, source_target_pairs={{0,4},{2,6},{4,0},{6,2},{1,5},{3,7},{5,1},{7,3},{8,12},{10,14},{12... | collective-permute-start | bytes 24584 | tf_op jit(solution)/shard_map/ppermute | solution.py:456

commit v5 on v4

--- a/solution.py
+++ b/solution.py
@@ -16,6 +16,7 @@
 EPS_STEP = 1e-06
 MASKED = -1e30
 LAGS = (0, 2, 3, 4)
+EXTRA = 8
 
 NT = (((1,), (1,)), ((), ()))
 
@@ -125,14 +126,6 @@
     return jnp.concatenate([values_t, jnp.ones((16, values_t.shape[1]), jnp.bfloat16)], axis=0)
 
 
-def pool_into(pooling, out_ref, rows, parts, pair, last):
-    if len(parts) == 4 or last:
-        columns = pl.ds((pair + 1 - len(parts)) * LANES, len(parts) * LANES)
-        pooled = dot_nt(pooling, jnp.concatenate(parts, axis=0))
-        out_ref[pl.ds(0, rows), columns] = pooled.astype(jnp.bfloat16)
-        parts.clear()
-
-
 def three_terms(value):
     high = value.astype(jnp.bfloat16).astype(jnp.float32)
     middle = (value - high).astype(jnp.bfloat16).astype(jnp.float32)
@@ -140,24 +133,18 @@
 
 
 def early_kernel(
-    rows, chunks, offsets_hbm, q_hbm, k_hbm, v_hbm,
-    sent_ref, early_ref, q_late_ref, k_ref, v_ref, own_ref, other_ref, next_ref,
-    offsets_ref, bias, sems, offsets_sem,
+    rows, chunks, offsets_hbm, q_hbm, k_hbm, v_hbm, sent_ref, early_ref,
+    offsets_ref, k_ref, v_ref, bias, sems, offsets_sem,
 ):
     half = rows // 2
-    head, tail = pl.ds(0, half), pl.ds(half, half)
-    offsets_copy = load(offsets_hbm, offsets_ref, offsets_sem.at[0])
+    head = pl.ds(0, half)
+    offsets_copy = load(offsets_hbm, offsets_ref, offsets_sem)
     arrays = (
-        (k_hbm.at[head], k_ref.at[head]),
+        (k_hbm.at[head], k_ref),
         (q_hbm.at[head], sent_ref.at[head]),
-        (v_hbm.at[head], v_ref.at[head]),
+        (v_hbm.at[head], v_ref),
     )
     copies = load_chunks(arrays, chunks, sems)
-    rest = [
-        load(k_hbm.at[tail], k_ref.at[tail], offsets_sem.at[1]),
-        load(v_hbm.at[tail], v_ref.at[tail], offsets_sem.at[2]),
-        load(q_hbm.at[tail], q_late_ref, offsets_sem.at[3]),
-    ]
     offsets_copy.wait()
     start = lax.axis_index("seq") * rows
     bias[...] = mask_bias(offsets_ref, start, start, lambda key, query: key <= query)
@@ -170,8 +157,8 @@
                 copy.wait()
 
     def score(pair):
-        scores = dot_nt(k_ref[head, at(pair)], split_heads(sent_ref[head, at(pair)]))
-        return scores, with_ones(jnp.transpose(v_ref[head, at(pair)]))
+        scores = dot_nt(k_ref[:, at(pair)], split_heads(sent_ref[head, at(pair)]))
+        return scores, with_ones(jnp.transpose(v_ref[:, at(pair)]))
 
     def top(pair, scores, values_t):
         scores = scores + bias[...]
@@ -185,31 +172,56 @@
         early_ref[at(pair), :] = own_heads(mixed, 1.0 / total).astype(jnp.bfloat16)
         lse = top + jnp.log(total)
         terms = three_terms(lse[:, :half]) + three_terms(lse[:, half:])
-        terms.append(jnp.zeros((10, LANES), jnp.float32))
-        sent_ref[pl.ds(half, 16), at(pair)] = jnp.concatenate(terms, axis=0).astype(jnp.bfloat16)
+        terms.append(jnp.zeros((EXTRA - 6, LANES), jnp.float32))
+        sent_ref[pl.ds(half, EXTRA), at(pair)] = jnp.concatenate(terms, axis=0).astype(jnp.bfloat16)
         return ()
 
     over_pairs(pairs, (score, top, weigh, finish), LAGS, arrive)
-    own_ref[...] = mask_bias(offsets_ref, start + half, start + half, lambda key, query: key <= query)
-    other_ref[...] = mask_bias(offsets_ref, start + half, start, lambda key, query: key > query)
-    next_ref[...] = mask_bias(offsets_ref, start + rows, start + half, lambda key, query: key > query)
-    for copy in rest:
-        copy.wait()
-
-
-def late_kernel(q_ref, k_ref, v_ref, own_bias, other_bias, late_ref, own, other):
-    half = q_ref.shape[0]
+
+
+def late_kernel(
+    rows, chunks, offsets_hbm, q_hbm, k_hbm, v_hbm, early_ref,
+    both_ref, k_tail_ref, v_tail_ref, next_ref,
+    offsets_ref, q_ref, k_ref, v_ref, own_bias, other_bias, own, other, sems, offsets_sem,
+):
+    half = rows // 2
+    head, tail = pl.ds(0, half), pl.ds(half, half)
+    offsets_copy = load(offsets_hbm, offsets_ref, offsets_sem)
+    arrays = (
+        (k_hbm.at[head], k_ref),
+        (k_hbm.at[tail], k_tail_ref),
+        (q_hbm.at[tail], q_ref),
+        (v_hbm.at[head], v_ref),
+        (v_hbm.at[tail], v_tail_ref),
+    )
+    copies = load_chunks(arrays, chunks, sems)
+    features = early_ref.shape[0]
+    both_ref[pl.ds(0, features), :] = early_ref[...]
     key = lax.broadcasted_iota(jnp.int32, own.shape, 0)
     query = lax.broadcasted_iota(jnp.int32, own.shape, 1) % half
     own[...] = jnp.where(key <= query, 1.0, 0.0).astype(jnp.bfloat16)
     other[...] = jnp.where(key <= query, 0.0, 1.0).astype(jnp.bfloat16)
     pooling = pool_matrix(half)
+    molecules = half // POOL
+    offsets_copy.wait()
+    start = lax.axis_index("seq") * rows
+    own_bias[...] = mask_bias(offsets_ref, start + half, start + half, lambda key, query: key <= query)
+    other_bias[...] = mask_bias(offsets_ref, start + half, start, lambda key, query: key > query)
+    next_ref[...] = mask_bias(offsets_ref, start + rows, start + half, lambda key, query: key > query)
     pairs = k_ref.shape[1] // LANES
     parts = []
 
+    def arrive(pair):
+        per_chunk = pairs // chunks
+        if pair % per_chunk == 0:
+            for copy in copies[pair // per_chunk]:
+                copy.wait()
+
     def score(pair):
-        scores = dot_nt(k_ref[:, at(pair)], split_heads(q_ref[:, at(pair)]))
-        return scores, with_ones(jnp.transpose(v_ref[:, at(pair)]))
+        queries = split_heads(q_ref[:, at(pair)])
+        values = jnp.concatenate([v_ref[:, at(pair)], v_tail_ref[:, at(pair)]], axis=0)
+        keys = jnp.concatenate([k_ref[:, at(pair)], k_tail_ref[:, at(pair)]], axis=0)
+        return dot_nt(keys, queries), with_ones(jnp.transpose(values))
 
     def top(pair, scores, values_t):
         scores = jnp.maximum(scores[:half] + other_bias[...], scores[half:] + own_bias[...])
@@ -223,29 +235,31 @@
     def finish(pair, mixed):
         inverse = 1.0 / mixed[LANES : LANES + 1]
         parts.append(own_heads(mixed, inverse).astype(jnp.bfloat16))
-        pool_into(pooling, late_ref, half // POOL, parts, pair, pair == pairs - 1)
+        if len(parts) == 4:
+            pooled = dot_nt(pooling, jnp.concatenate(parts, axis=0)).astype(jnp.bfloat16)
+            for i in range(4):
+                place = features + (pair - 3 + i) * molecules
+                both_ref[pl.ds(place, molecules), :] = pooled[:, i * LANES : (i + 1) * LANES]
+            parts.clear()
         return ()
 
-    over_pairs(pairs, (score, top, weigh, finish), LAGS, lambda pair: None)
-
-
-def halo_kernel(q_ref, k_ref, v_ref, bias, term_ref, other_ref, *rest):
-    out_ref, sum_ref = rest[-2:]
-    sum_ref[...] = term_ref[...] + other_ref[...]
+    over_pairs(pairs, (score, top, weigh, finish), LAGS, arrive)
+
+
+def halo_kernel(q_ref, k_ref, v_ref, bias, after_ref, out_ref):
     half = bias.shape[0]
     molecules = half // POOL
-    tail = pl.ds(half, half)
     pooling = pool_matrix(half)
     pairs = k_ref.shape[1] // LANES
     parts = []
 
     def score(pair):
         queries = split_heads(q_ref[pl.ds(0, half), at(pair)])
-        scores = dot_nt(k_ref[tail, at(pair)], queries)
-        return scores, with_ones(jnp.transpose(v_ref[tail, at(pair)]))
+        scores = dot_nt(k_ref[:, at(pair)], queries)
+        return scores, with_ones(jnp.transpose(v_ref[:, at(pair)]))
 
     def top(pair, scores, values_t):
-        terms = q_ref[pl.ds(half, 16), at(pair)].astype(jnp.float32)
+        terms = q_ref[pl.ds(half, EXTRA), at(pair)].astype(jnp.float32)
         lse = jnp.concatenate(
             [terms[0:1] + terms[1:2] + terms[2:3], terms[3:4] + terms[4:5] + terms[5:6]], axis=1
         )
@@ -259,13 +273,16 @@
     def finish(pair, mixed, kept):
         inverse = 1.0 / (mixed[LANES : LANES + 1] + kept)
         parts.append(own_heads(mixed, inverse).astype(jnp.bfloat16))
-        pool_into(pooling, out_ref, molecules, parts, pair, pair == pairs - 1)
+        if len(parts) == 4:
+            pooled = dot_nt(pooling, jnp.concatenate(parts, axis=0)).astype(jnp.bfloat16)
+            out_ref[pl.ds(0, molecules), pl.ds((pair - 3) * LANES, 4 * LANES)] = pooled
+            parts.clear()
         share = kept * inverse
         high = share.astype(jnp.bfloat16).astype(jnp.float32)
         low = share - high
         shares = [high[:, :half], low[:, :half], high[:, half:], low[:, half:]]
-        shares.append(jnp.zeros((12, LANES), jnp.float32))
-        out_ref[pl.ds(molecules, 16), at(pair)] = jnp.concatenate(shares, axis=0).astype(jnp.bfloat16)
+        shares.append(jnp.zeros((EXTRA - 4, LANES), jnp.float32))
+        out_ref[pl.ds(molecules, EXTRA), at(pair)] = jnp.concatenate(shares, axis=0).astype(jnp.bfloat16)
         return ()
 
     over_pairs(pairs, (score, top, weigh, finish), LAGS, lambda pair: None)
@@ -301,20 +318,23 @@
 
 
 def project_kernel(
-    early_ref, late_ref, halo_ref, gain_ref, weight_ref, term_ref, other_ref, upstream_hbm,
+    both_ref, halo_ref, gain_ref, weight_ref, term_ref, other_ref, upstream_hbm,
     out_ref, update_ref, passed_hbm, pooled, sem,
 ):
     passing = load(upstream_hbm, passed_hbm, sem)
-    half = early_ref.shape[1]
+    half = both_ref.shape[1]
+    features = gain_ref.shape[1]
     molecules = half // POOL
     pooling = pool_matrix(half)
     first = lax.axis_index("seq") == 0
     parts = []
-    for pair in range(early_ref.shape[0] // LANES):
+    for pair in range(features // LANES):
         shares = halo_ref[molecules:, at(pair)].astype(jnp.float32)
         share_a = jnp.where(first, 1.0, shares[0:1] + shares[1:2])
         share_b = jnp.where(first, 1.0, shares[2:3] + shares[3:4])
-        early = early_ref[at(pair), :].astype(jnp.float32)
+        early = both_ref[at(pair), :].astype(jnp.float32)
+        place = pl.ds(features + pair * molecules, molecules)
+        pooled[pl.ds(molecules, molecules), at(pair)] = both_ref[place, :]
         parts += [early[:HEAD_DIM] * share_a, early[HEAD_DIM:] * share_b]
         if len(parts) == 8:
             columns = pl.ds((pair - 3) * LANES, 4 * LANES)
@@ -322,8 +342,6 @@
             arrived = halo_ref[:molecules, columns].astype(jnp.float32)
             pooled[pl.ds(0, molecules), columns] = (mean + arrived).astype(jnp.bfloat16)
             parts = []
-    pooled[pl.ds(molecules, molecules), :] = late_ref[...]
-    features = gain_ref.shape[1]
     arrived = pooled[...].astype(jnp.float32)
     mean = jnp.sum(arrived * arrived, axis=1, keepdims=True) / features
     normed = (arrived * lax.rsqrt(mean + EPS_NORM) * gain_ref[...]).astype(jnp.bfloat16)
@@ -355,59 +373,70 @@
 def attend_early(queries, keys, values, offsets, chunks):
     rows, width = queries.shape
     half = rows // 2
-    masks = [jax.ShapeDtypeStruct((half, 2 * half), jnp.float32)] * 3
     return pl.pallas_call(
         functools.partial(early_kernel, rows, chunks),
         in_specs=[HBM] * 4,
-        out_specs=[VMEM] * 8,
+        out_specs=[VMEM] * 2,
         out_shape=[
-            jax.ShapeDtypeStruct((half + 16, width), jnp.bfloat16),
+            jax.ShapeDtypeStruct((half + EXTRA, width), jnp.bfloat16),
             jax.ShapeDtypeStruct((width, half), jnp.bfloat16),
-            jax.ShapeDtypeStruct((half, width), jnp.bfloat16),
-            jax.ShapeDtypeStruct((rows, width), jnp.bfloat16),
-            jax.ShapeDtypeStruct((rows, width), jnp.bfloat16),
-        ]
-        + masks,
+        ],
         scratch_shapes=[
             pltpu.SMEM(offsets.shape, jnp.int32),
+            pltpu.VMEM((half, width), jnp.bfloat16),
+            pltpu.VMEM((half, width), jnp.bfloat16),
             pltpu.VMEM((half, 2 * half), jnp.float32),
             pltpu.SemaphoreType.DMA((3, chunks)),
-            pltpu.SemaphoreType.DMA((4,)),
-        ],
-        cost_estimate=cost(4 * half * half * width, 6 * rows * width, half * half * width // 64),
+            pltpu.SemaphoreType.DMA,
+        ],
+        cost_estimate=cost(4 * half * half * width, 6 * half * width, half * half * width // 64),
         compiler_params=params(),
         name="attend_early",
     )(*in_hbm(offsets, queries, keys, values))
 
 
-def attend_late(queries, keys, values, own_bias, other_bias):
-    half, width = queries.shape
+def attend_late(queries, keys, values, offsets, early, chunks):
+    rows, width = queries.shape
+    half = rows // 2
     return pl.pallas_call(
-        late_kernel,
-        in_specs=[VMEM] * 5,
-        out_specs=VMEM,
-        out_shape=jax.ShapeDtypeStruct((half // POOL, width), jnp.bfloat16),
-        scratch_shapes=[pltpu.VMEM((half, 2 * half), jnp.bfloat16)] * 2,
+        functools.partial(late_kernel, rows, chunks),
+        in_specs=[HBM] * 4 + [VMEM],
+        out_specs=[VMEM] * 4,
+        out_shape=[
+            jax.ShapeDtypeStruct((width + width // POOL, half), jnp.bfloat16),
+            jax.ShapeDtypeStruct((half, width), jnp.bfloat16),
+            jax.ShapeDtypeStruct((half, width), jnp.bfloat16),
+            jax.ShapeDtypeStruct((half, 2 * half), jnp.float32),
+        ],
+        scratch_shapes=[
+            pltpu.SMEM(offsets.shape, jnp.int32),
+            pltpu.VMEM((half, width), jnp.bfloat16),
+            pltpu.VMEM((half, width), jnp.bfloat16),
+            pltpu.VMEM((half, width), jnp.bfloat16),
+            pltpu.VMEM((half, 2 * half), jnp.float32),
+            pltpu.VMEM((half, 2 * half), jnp.float32),
+            pltpu.VMEM((half, 2 * half), jnp.bfloat16),
+            pltpu.VMEM((half, 2 * half), jnp.bfloat16),
+            pltpu.SemaphoreType.DMA((5, chunks)),
+            pltpu.SemaphoreType.DMA,
+        ],
         cost_estimate=cost(8 * half * half * width, 10 * half * width, half * half * width // 64),
         compiler_params=params(),
         name="attend_late",
-    )(queries, keys, values, own_bias, other_bias)
-
-
-def attend_halo(sent, keys, values, bias, term, other, after):
-    half, width = bias.shape[0], keys.shape[1]
+    )(*in_hbm(offsets, queries, keys, values), early)
+
+
+def attend_halo(sent, keys, values, bias, after):
+    half, width = keys.shape
     return pl.pallas_call(
         halo_kernel,
-        in_specs=[VMEM] * 6 + [ANY] * len(after),
-        out_specs=[VMEM] * 2,
-        out_shape=[
-            jax.ShapeDtypeStruct((half // POOL + 16, width), jnp.bfloat16),
-            jax.ShapeDtypeStruct(term.shape, term.dtype),
-        ],
+        in_specs=[VMEM] * 4 + [ANY],
+        out_specs=VMEM,
+        out_shape=jax.ShapeDtypeStruct((half // POOL + EXTRA, width), jnp.bfloat16),
         cost_estimate=cost(4 * half * half * width, 6 * half * width, half * half * width // 64),
         compiler_params=params(),
         name="attend_halo",
-    )(sent, keys, values, bias, term, other, *after)
+    )(sent, keys, values, bias, after)
 
 
 def backward(slot, cotangent, weight, gain, stashed, after):
@@ -433,12 +462,12 @@
     )(slot, *in_hbm(cotangent), weight, gain, *in_hbm(stashed), after)
 
 
-def project(early, late, halo, gain, weight, term, other, upstream):
-    rows = 2 * late.shape[0]
+def project(both, halo, gain, weight, term, other, upstream):
+    rows = upstream.shape[0]
     width, depth = weight.shape
     return pl.pallas_call(
         project_kernel,
-        in_specs=[VMEM] * 7 + [ANY],
+        in_specs=[VMEM] * 6 + [ANY],
         out_specs=[VMEM, VMEM, HBM],
         out_shape=[
             jax.ShapeDtypeStruct((rows, depth), jnp.bfloat16),
@@ -449,7 +478,7 @@
         cost_estimate=cost(2 * rows * width * depth, 2 * width * depth),
         compiler_params=params(),
         name="project",
-    )(early, late, halo, gain, weight, term, other, upstream)
+    )(both, halo, gain, weight, term, other, upstream)
 
 
 def swapped(value, axis, distance):
@@ -483,21 +512,18 @@
     def partner(term, index):
         return swapped(term, *rounds[index]) if rounds else jnp.zeros_like(term)
 
-    sent, early, q_late, keys, values, own_bias, other_bias, next_bias = attend_early(
-        queries, keys, values, offsets, 4
-    )
+    sent, early = attend_early(queries, keys, values, offsets, 4)
     arrived = shifted(sent, "seq", -1)
-    early = passed_along(early, "section", 1)
-    late = attend_late(q_late, keys, values, own_bias, other_bias)
-    late_arrived = passed_along(late, "section", 1)
-    dinput, term = backward(slot, cotangent[0, 0], weight[0], gain, stashed[0, 0], late)
+    both, k_tail, v_tail, next_bias = attend_late(queries, keys, values, offsets, early, 4)
+    both_arrived = passed_along(both, "section", 1)
+    dinput, term = backward(slot, cotangent[0, 0], weight[0], gain, stashed[0, 0], both)
     upstream = passed_along(dinput, "section", -1)
     term = term if rounds else lax.psum(term, ("rep", "seq"))
-    halo, term = attend_halo(arrived, keys, values, next_bias, term, partner(term, 0), (late_arrived,))
-    halo = onward(halo)
+    term = term + partner(term, 0)
     term = term + partner(term, 1)
+    halo = onward(attend_halo(arrived, k_tail, v_tail, next_bias, term))
     mol_keys, update, upstream = project(
-        early, late_arrived, halo, gain, weight[0], term, partner(term, 2), upstream
+        both_arrived, halo, gain, weight[0], term, partner(term, 2), upstream
     )
     return mol_keys[None, None], upstream[None, None], update
 

time: 42.4 us -> 38.7 us (0.913)
  the two profiles are of different devices: /device:TPU:0 before, /device:TPU:24 now
where the time goes in v5:
time: 38.7 us; the launch traced here: 38.4 us
  waiting for transfers between devices  13.7 us (35%)
  Pallas kernels  13.5 us (35%)
  starting transfers between devices  9.84 us (25%)
  between operations  1.37 us (4%)
    ppermute x3, waiting for transfers between devices, swapped(): lax.ppermute(value, axis, [(i, i ^ distance) for i in range(lax.axis_size...  8.14 us
    ppermute x2, waiting for transfers between devices, passed_along(): lax.ppermute(value, axis, [(i, (i + steps) % count) for i in range(count)])  5.58 us
    pallas_call x1, Pallas kernels, attend_late(): pl.pallas_call(functools.partial(late_kernel, rows, chunks), in_specs=[HB...  3.67 us
    pallas_call x1, Pallas kernels, attend_early(): pl.pallas_call(functools.partial(early_kernel, rows, chunks), in_specs=[H...  3.49 us
    ppermute x3, starting transfers between devices, swapped(): lax.ppermute(value, axis, [(i, i ^ distance) for i in range(lax.axis_size...  3.11 us
    ppermute x2, starting transfers between devices, passed_along(): lax.ppermute(value, axis, [(i, (i + steps) % count) for i in range(count)])  3.03 us
    pallas_call x1, Pallas kernels, backward(): pl.pallas_call(back_kernel, in_specs=[SMEM, HBM, VMEM, VMEM, HBM, ANY], o...  2.65 us
    ppermute x1, starting transfers between devices, shifted(): lax.ppermute(value, axis, [(i, i + steps) for i in range(first, last)])  2.39 us
  transfers between devices with their start and end apart: 7, of which 4 were waited for; matrix products, arithmetic and copies ran while one was open for 0% of the time, Pallas kernels for 21%

profile of v5, /device:TPU:24, one launch (start us, length us, event | category | flops | bytes accessed | tf_op | source)
XLA Modules:
  0.0 38.4 jit_solution(2761587689208356166)
XLA Ops:
  0.6 0.0 copy-start.1
  0.6 0.0 copy-start
  0.7 3.5 %attend_early.1 = (bf16[136,2048]{1,0:T(8,128)(2,1)S(1)}, bf16[2048,128]{1,0:T(8,128)(2,1)S(1)}) custom-call(s32[1,8]{1,0:T(1,128)} %bitcast.19, bf16[256,2048]{1,0:T(8,128)(2,1)} %bitcast.11, bf16[256,2048]{1,0:T(8,128)(2,1)} %bitcast.13, bf16[256,2048]{1,0:T(8,128)(2,1)} %bitcast.15), custom_call_target="tpu_custom_call" | custom-call | flops 134217728 | bytes 1572864 | tf_op jit(solution)/shard_map/attend_early/pallas_call | solution.py:376
  4.1 2.4 %collective-permute-start.1 = (bf16[136,2048]{1,0:T(8,128)(2,1)S(1)}, bf16[136,2048]{1,0:T(8,128)(2,1)S(1)}, u32[]{:S(2)}, u32[]{:S(2)}) collective-permute-start(bf16[136,2048]{1,0:T(8,128)(2,1)S(1)} %get-tuple-element.16), channel_id=1, source_target_pairs={{2,0},{4,2},{6,4},{3,1},{5,3},{7,5},{10,8},{12,10},{14,12},{11,9},... | collective-permute-start | bytes 1671176 | tf_op jit(solution)/shard_map/ppermute | solution.py:35
  6.5 3.7 %attend_late.1 = (bf16[2560,128]{1,0:T(8,128)(2,1)S(1)}, bf16[128,2048]{1,0:T(8,128)(2,1)S(1)}, bf16[128,2048]{1,0:T(8,128)(2,1)S(1)}, f32[128,256]{1,0:T(8,128)S(1)}) custom-call(s32[1,8]{1,0:T(1,128)} %bitcast.20, bf16[256,2048]{1,0:T(8,128)(2,1)} %bitcast.12, bf16[256,2048]{1,0:T(8,128)(2,1)} %bitcast.14, bf16[256,2048]{1,0:T(8,128)(2,1)} %bitcast.16, ...), custom_call_target="tpu_custom_call" | custom-call | flops 268435456 | bytes 2621440 | tf_op jit(solution)/shard_map/attend_late/pallas_call | solution.py:401
  10.2 1.6 %collective-permute-start = (bf16[2560,128]{1,0:T(8,128)(2,1)S(1)}, bf16[2560,128]{1,0:T(8,128)(2,1)S(1)}, u32[]{:S(2)}, u32[]{:S(2)}) collective-permute-start(bf16[2560,128]{1,0:T(8,128)(2,1)S(1)} %get-tuple-element.15.after_ref), channel_id=1, source_target_pairs={{0,8},{8,16},{16,24},{24,0},{1,9},{9,17},{17,25},{25,1},{2,10},{10... | collective-permute-start | bytes 1966088 | tf_op jit(solution)/shard_map/ppermute | solution.py:40
  12.4 0.0 copy-done.1
  12.4 0.0 copy-done
  12.4 2.6 %backward.1 = (bf16[64,2048]{1,0:T(8,128)(2,1)S(1)}, f32[1,2048]{1,0:T(1,128)S(1)}) custom-call(s32[1,1]{1,0:T(1,128)S(6)} %copy.12.slot_ref, bf16[64,1024]{1,0:T(8,128)(2,1)} %bitcast.18, bf16[2048,1024]{1,0:T(8,128)(2,1)S(1)} %bitcast.9, f32[1,2048]{1,0:T(1,128)S(1)} %copy-done.1, bf16[2,64,2048]{2,1,0:T(8,128)(2,1)} %bitcast.17, ...), custom_call_target="tpu_custom_call" | custom-call | flops 268435456 | bytes 4194304 | tf_op jit(solution)/shard_map/backward/pallas_call | solution.py:445
  15.1 1.5 %collective-permute-start.6 = (bf16[64,2048]{1,0:T(8,128)(2,1)S(1)}, bf16[64,2048]{1,0:T(8,128)(2,1)S(1)}, u32[]{:S(2)}, u32[]{:S(2)}) collective-permute-start(bf16[64,2048]{1,0:T(8,128)(2,1)S(1)} %get-tuple-element.21), channel_id=1, source_target_pairs={{0,24},{8,0},{16,8},{24,16},{1,25},{9,1},{17,9},{25,17},{2,26},{10... | collective-permute-start | bytes 786440 | tf_op jit(solution)/shard_map/ppermute | solution.py:40
  16.6 0.0 collective-permute-start.2
  16.6 1.2 %collective-permute-done.2 = f32[1,2048]{1,0:T(1,128)S(1)} collective-permute-done((f32[1,2048]{1,0:T(1,128)S(1)}, f32[1,2048]{1,0:T(1,128)S(1)}, u32[]{:S(2)}, u32[]{:S(2)}) %collective-permute-start.2) | collective-permute-done | bytes 8224 | tf_op jit(solution)/shard_map/ppermute | solution.py:485
  17.8 0.5 %collective-permute-start.3 = (f32[1,2048]{1,0:T(1,128)S(1)}, f32[1,2048]{1,0:T(1,128)S(1)}, u32[]{:S(2)}, u32[]{:S(2)}) collective-permute-start(f32[1,2048]{1,0:T(1,128)S(1)} %add.6), channel_id=1, source_target_pairs={{0,2},{2,0},{4,6},{6,4},{1,3},{3,1},{5,7},{7,5},{8,10},{10,8},{12,... | collective-permute-start | bytes 24584 | tf_op jit(solution)/shard_map/ppermute | solution.py:485
  18.3 3.2 %collective-permute-done.3 = f32[1,2048]{1,0:T(1,128)S(1)} collective-permute-done((f32[1,2048]{1,0:T(1,128)S(1)}, f32[1,2048]{1,0:T(1,128)S(1)}, u32[]{:S(2)}, u32[]{:S(2)}) %collective-permute-start.3) | collective-permute-done | bytes 8224 | tf_op jit(solution)/shard_map/ppermute | solution.py:485
  21.5 0.0 collective-permute-done.1.q_ref
  21.5 1.8 %attend_halo.1 = bf16[40,2048]{1,0:T(8,128)(2,1)S(1)} custom-call(bf16[136,2048]{1,0:T(8,128)(2,1)S(1)} %collective-permute-done.1.q_ref, bf16[128,2048]{1,0:T(8,128)(2,1)S(1)} %get-tuple-element.17.k_ref, bf16[128,2048]{1,0:T(8,128)(2,1)S(1)} %get-tuple-element.18.v_ref, f32[128,256]{1,0:T(8,128)S(1)} %get-tuple-element.19.bias, ...), custom_call_target="tpu_custom_call" | custom-call | flops 134217728 | bytes 1572864 | tf_op jit(solution)/shard_map/attend_halo/pallas_call | solution.py:431
  23.3 1.3 %collective-permute-start.4 = (bf16[40,2048]{1,0:T(8,128)(2,1)S(1)}, bf16[40,2048]{1,0:T(8,128)(2,1)S(1)}, u32[]{:S(2)}, u32[]{:S(2)}) collective-permute-start(bf16[40,2048]{1,0:T(8,128)(2,1)S(1)} %attend_halo.1), channel_id=1, source_target_pairs={{0,10},{2,12},{4,14},{8,18},{10,20},{12,22},{16,26},{18,28},{20,30... | collective-permute-start | bytes 491528 | tf_op jit(solution)/shard_map/ppermute | solution.py:505
  24.6 2.6 %collective-permute-start.5 = (f32[1,2048]{1,0:T(1,128)S(1)}, f32[1,2048]{1,0:T(1,128)S(1)}, u32[]{:S(2)}, u32[]{:S(2)}) collective-permute-start(f32[1,2048]{1,0:T(1,128)S(1)} %add.7.after_ref.term_ref), channel_id=1, source_target_pairs={{0,4},{2,6},{4,0},{6,2},{1,5},{3,7},{5,1},{7,3},{8,12},{10,14},{12... | collective-permute-start | bytes 24584 | tf_op jit(solution)/shard_map/ppermute | solution.py:485
  27.2 3.7 %collective-permute-done.5.other_ref = f32[1,2048]{1,0:T(1,128)S(1)} collective-permute-done((f32[1,2048]{1,0:T(1,128)S(1)}, f32[1,2048]{1,0:T(1,128)S(1)}, u32[]{:S(2)}, u32[]{:S(2)}) %collective-permute-start.5) | collective-permute-done | bytes 8224 | tf_op jit(solution)/shard_map/ppermute | solution.py:485
  31.0 5.6 %collective-permute-done.6.upstream_hbm = bf16[64,2048]{1,0:T(8,128)(2,1)S(1)} collective-permute-done((bf16[64,2048]{1,0:T(8,128)(2,1)S(1)}, bf16[64,2048]{1,0:T(8,128)(2,1)S(1)}, u32[]{:S(2)}, u32[]{:S(2)}) %collective-permute-start.6) | collective-permute-done | bytes 262176 | tf_op jit(solution)/shard_map/ppermute | solution.py:40
  36.6 0.0 collective-permute-done.both_ref
  36.6 0.0 collective-permute-done.4.halo_ref
  36.6 1.9 %project.1 = (bf16[64,1024]{1,0:T(8,128)(2,1)}, f32[1,2048]{1,0:T(1,128)}, bf16[64,2048]{1,0:T(8,128)(2,1)}) custom-call(bf16[2560,128]{1,0:T(8,128)(2,1)S(1)} %collective-permute-done.both_ref, bf16[40,2048]{1,0:T(8,128)(2,1)S(1)} %collective-permute-done.4.halo_ref, f32[1,2048]{1,0:T(1,128)S(1)} %copy-done.1, bf16[2048,1024]{1,0:T(8,128)(2,1)S(1)} %bitcast.10, ...), custom_call_target="tpu_custom_call" | custom-call | flops 268435456 | bytes 4194304 | tf_op jit(solution)/shard_map/project/pallas_call | solution.py:468
  (2 shorter events, 0.0 us)
Async XLA Ops:
  0.6 11.8 %copy-start.1 = (f32[1,2048]{1,0:T(1,128)S(1)}, f32[1,2048]{1,0:T(1,128)}, u32[]{:S(2)}) copy-start(f32[1,2048]{1,0:T(1,128)} %gain_ref.3) | copy-start | bytes 24580
  0.6 11.8 %copy-start = (bf16[1,2048,1024]{2,1,0:T(8,128)(2,1)S(1)}, bf16[1,2048,1024]{2,1,0:T(8,128)(2,1)}, u32[]{:S(2)}) copy-start(bf16[1,2048,1024]{2,1,0:T(8,128)(2,1)} %param.13) | copy-start | bytes 12582916
  4.1 17.4 %collective-permute-start.1 = (bf16[136,2048]{1,0:T(8,128)(2,1)S(1)}, bf16[136,2048]{1,0:T(8,128)(2,1)S(1)}, u32[]{:S(2)}, u32[]{:S(2)}) collective-permute-start(bf16[136,2048]{1,0:T(8,128)(2,1)S(1)} %get-tuple-element.16), channel_id=1, source_target_pairs={{2,0},{4,2},{6,4},{3,1},{5,3},{7,5},{10,8},{12,10},{14,12},{11,9},... | collective-permute-start | bytes 1671176 | tf_op jit(solution)/shard_map/ppermute | solution.py:35
  10.2 26.3 %collective-permute-start = (bf16[2560,128]{1,0:T(8,128)(2,1)S(1)}, bf16[2560,128]{1,0:T(8,128)(2,1)S(1)}, u32[]{:S(2)}, u32[]{:S(2)}) collective-permute-start(bf16[2560,128]{1,0:T(8,128)(2,1)S(1)} %get-tuple-element.15.after_ref), channel_id=1, source_target_pairs={{0,8},{8,16},{16,24},{24,0},{1,9},{9,17},{17,25},{25,1},{2,10},{10... | collective-permute-start | bytes 1966088 | tf_op jit(solution)/shard_map/ppermute | solution.py:40
  15.1 21.5 %collective-permute-start.6 = (bf16[64,2048]{1,0:T(8,128)(2,1)S(1)}, bf16[64,2048]{1,0:T(8,128)(2,1)S(1)}, u32[]{:S(2)}, u32[]{:S(2)}) collective-permute-start(bf16[64,2048]{1,0:T(8,128)(2,1)S(1)} %get-tuple-element.21), channel_id=1, source_target_pairs={{0,24},{8,0},{16,8},{24,16},{1,25},{9,1},{17,9},{25,17},{2,26},{10... | collective-permute-start | bytes 786440 | tf_op jit(solution)/shard_map/ppermute | solution.py:40
  16.6 1.2 %collective-permute-start.2 = (f32[1,2048]{1,0:T(1,128)S(1)}, f32[1,2048]{1,0:T(1,128)S(1)}, u32[]{:S(2)}, u32[]{:S(2)}) collective-permute-start(f32[1,2048]{1,0:T(1,128)S(1)} %get-tuple-element.20), channel_id=1, source_target_pairs={{0,1},{1,0},{2,3},{3,2},{4,5},{5,4},{6,7},{7,6},{8,9},{9,8},{10,11... | collective-permute-start | bytes 24584 | tf_op jit(solution)/shard_map/ppermute | solution.py:485
  17.8 3.7 %collective-permute-start.3 = (f32[1,2048]{1,0:T(1,128)S(1)}, f32[1,2048]{1,0:T(1,128)S(1)}, u32[]{:S(2)}, u32[]{:S(2)}) collective-permute-start(f32[1,2048]{1,0:T(1,128)S(1)} %add.6), channel_id=1, source_target_pairs={{0,2},{2,0},{4,6},{6,4},{1,3},{3,1},{5,7},{7,5},{8,10},{10,8},{12,... | collective-permute-start | bytes 24584 | tf_op jit(solution)/shard_map/ppermute | solution.py:485
  23.3 13.3 %collective-permute-start.4 = (bf16[40,2048]{1,0:T(8,128)(2,1)S(1)}, bf16[40,2048]{1,0:T(8,128)(2,1)S(1)}, u32[]{:S(2)}, u32[]{:S(2)}) collective-permute-start(bf16[40,2048]{1,0:T(8,128)(2,1)S(1)} %attend_halo.1), channel_id=1, source_target_pairs={{0,10},{2,12},{4,14},{8,18},{10,20},{12,22},{16,26},{18,28},{20,30... | collective-permute-start | bytes 491528 | tf_op jit(solution)/shard_map/ppermute | solution.py:505
  24.6 6.4 %collective-permute-start.5 = (f32[1,2048]{1,0:T(1,128)S(1)}, f32[1,2048]{1,0:T(1,128)S(1)}, u32[]{:S(2)}, u32[]{:S(2)}) collective-permute-start(f32[1,2048]{1,0:T(1,128)S(1)} %add.7.after_ref.term_ref), channel_id=1, source_target_pairs={{0,4},{2,6},{4,0},{6,2},{1,5},{3,7},{5,1},{7,3},{8,12},{10,14},{12... | collective-permute-start | bytes 24584 | tf_op jit(solution)/shard_map/ppermute | solution.py:485

commit v6 on v4

--- a/solution.py
+++ b/solution.py
@@ -16,6 +16,7 @@
 EPS_STEP = 1e-06
 MASKED = -1e30
 LAGS = (0, 2, 3, 4)
+EXTRA = 8
 
 NT = (((1,), (1,)), ((), ()))
 
@@ -123,14 +124,6 @@
 
 def with_ones(values_t):
     return jnp.concatenate([values_t, jnp.ones((16, values_t.shape[1]), jnp.bfloat16)], axis=0)
-
-
-def pool_into(pooling, out_ref, rows, parts, pair, last):
-    if len(parts) == 4 or last:
-        columns = pl.ds((pair + 1 - len(parts)) * LANES, len(parts) * LANES)
-        pooled = dot_nt(pooling, jnp.concatenate(parts, axis=0))
-        out_ref[pl.ds(0, rows), columns] = pooled.astype(jnp.bfloat16)
-        parts.clear()
 
 
 def three_terms(value):
@@ -185,8 +178,8 @@
         early_ref[at(pair), :] = own_heads(mixed, 1.0 / total).astype(jnp.bfloat16)
         lse = top + jnp.log(total)
         terms = three_terms(lse[:, :half]) + three_terms(lse[:, half:])
-        terms.append(jnp.zeros((10, LANES), jnp.float32))
-        sent_ref[pl.ds(half, 16), at(pair)] = jnp.concatenate(terms, axis=0).astype(jnp.bfloat16)
+        terms.append(jnp.zeros((EXTRA - 6, LANES), jnp.float32))
+        sent_ref[pl.ds(half, EXTRA), at(pair)] = jnp.concatenate(terms, axis=0).astype(jnp.bfloat16)
         return ()
 
     over_pairs(pairs, (score, top, weigh, finish), LAGS, arrive)
@@ -197,7 +190,15 @@
         copy.wait()
 
 
-def late_kernel(q_ref, k_ref, v_ref, own_bias, other_bias, late_ref, own, other):
+def late_kernel(
+    q_ref, k_ref, v_ref, own_bias, other_bias, slot_ref, weight_hbm, cotangent_hbm, stashed_hbm,
+    late_ref, weight_ref, cotangent_ref, held_ref, own, other, sems,
+):
+    copies = [
+        load(cotangent_hbm, cotangent_ref, sems.at[0]),
+        load(stashed_hbm.at[slot_ref[0, 0]], held_ref, sems.at[1]),
+        load(weight_hbm, weight_ref, sems.at[2]),
+    ]
     half = q_ref.shape[0]
     key = lax.broadcasted_iota(jnp.int32, own.shape, 0)
     query = lax.broadcasted_iota(jnp.int32, own.shape, 1) % half
@@ -223,15 +224,18 @@
     def finish(pair, mixed):
         inverse = 1.0 / mixed[LANES : LANES + 1]
         parts.append(own_heads(mixed, inverse).astype(jnp.bfloat16))
-        pool_into(pooling, late_ref, half // POOL, parts, pair, pair == pairs - 1)
+        if len(parts) == 4:
+            pooled = dot_nt(pooling, jnp.concatenate(parts, axis=0)).astype(jnp.bfloat16)
+            late_ref[:, pl.ds((pair - 3) * LANES, 4 * LANES)] = pooled
+            parts.clear()
         return ()
 
     over_pairs(pairs, (score, top, weigh, finish), LAGS, lambda pair: None)
-
-
-def halo_kernel(q_ref, k_ref, v_ref, bias, term_ref, other_ref, *rest):
-    out_ref, sum_ref = rest[-2:]
-    sum_ref[...] = term_ref[...] + other_ref[...]
+    for copy in copies:
+        copy.wait()
+
+
+def halo_kernel(q_ref, k_ref, v_ref, bias, after_ref, out_ref):
     half = bias.shape[0]
     molecules = half // POOL
     tail = pl.ds(half, half)
@@ -245,7 +249,7 @@
         return scores, with_ones(jnp.transpose(v_ref[tail, at(pair)]))
 
     def top(pair, scores, values_t):
-        terms = q_ref[pl.ds(half, 16), at(pair)].astype(jnp.float32)
+        terms = q_ref[pl.ds(half, EXTRA), at(pair)].astype(jnp.float32)
         lse = jnp.concatenate(
             [terms[0:1] + terms[1:2] + terms[2:3], terms[3:4] + terms[4:5] + terms[5:6]], axis=1
         )
@@ -259,31 +263,27 @@
     def finish(pair, mixed, kept):
         inverse = 1.0 / (mixed[LANES : LANES + 1] + kept)
         parts.append(own_heads(mixed, inverse).astype(jnp.bfloat16))
-        pool_into(pooling, out_ref, molecules, parts, pair, pair == pairs - 1)
+        if len(parts) == 4:
+            pooled = dot_nt(pooling, jnp.concatenate(parts, axis=0)).astype(jnp.bfloat16)
+            out_ref[pl.ds(0, molecules), pl.ds((pair - 3) * LANES, 4 * LANES)] = pooled
+            parts.clear()
         share = kept * inverse
         high = share.astype(jnp.bfloat16).astype(jnp.float32)
         low = share - high
         shares = [high[:, :half], low[:, :half], high[:, half:], low[:, half:]]
-        shares.append(jnp.zeros((12, LANES), jnp.float32))
-        out_ref[pl.ds(molecules, 16), at(pair)] = jnp.concatenate(shares, axis=0).astype(jnp.bfloat16)
+        shares.append(jnp.zeros((EXTRA - 4, LANES), jnp.float32))
+        out_ref[pl.ds(molecules, EXTRA), at(pair)] = jnp.concatenate(shares, axis=0).astype(jnp.bfloat16)
         return ()
 
     over_pairs(pairs, (score, top, weigh, finish), LAGS, lambda pair: None)
 
 
-def back_kernel(
-    slot_ref, cotangent_hbm, weight_ref, gain_ref, stashed_hbm, after_ref, dinput_ref, term_ref,
-    cotangent_ref, held_ref, grad, sems,
-):
-    cotangent_copy = load(cotangent_hbm, cotangent_ref, sems.at[1])
-    held_copy = load(stashed_hbm.at[slot_ref[0, 0]], held_ref, sems.at[0])
-    cotangent_copy.wait()
+def back_kernel(cotangent_ref, weight_ref, gain_ref, held_ref, dinput_ref, term_ref, grad):
     features = weight_ref.shape[0]
     block = 512
     for begin in range(0, features, block):
         columns = pl.ds(begin, block)
         grad[:, columns] = dot_nt(cotangent_ref[...], weight_ref[columns, :])
-    held_copy.wait()
     held = held_ref[...].astype(jnp.float32)
     inv_rms = lax.rsqrt(jnp.sum(held * held, axis=1, keepdims=True) / features + EPS_NORM)
     along = jnp.zeros_like(inv_rms)
@@ -306,11 +306,12 @@
 ):
     passing = load(upstream_hbm, passed_hbm, sem)
     half = early_ref.shape[1]
+    features = gain_ref.shape[1]
     molecules = half // POOL
     pooling = pool_matrix(half)
     first = lax.axis_index("seq") == 0
     parts = []
-    for pair in range(early_ref.shape[0] // LANES):
+    for pair in range(features // LANES):
         shares = halo_ref[molecules:, at(pair)].astype(jnp.float32)
         share_a = jnp.where(first, 1.0, shares[0:1] + shares[1:2])
         share_b = jnp.where(first, 1.0, shares[2:3] + shares[3:4])
@@ -323,7 +324,6 @@
             pooled[pl.ds(0, molecules), columns] = (mean + arrived).astype(jnp.bfloat16)
             parts = []
     pooled[pl.ds(molecules, molecules), :] = late_ref[...]
-    features = gain_ref.shape[1]
     arrived = pooled[...].astype(jnp.float32)
     mean = jnp.sum(arrived * arrived, axis=1, keepdims=True) / features
     normed = (arrived * lax.rsqrt(mean + EPS_NORM) * gain_ref[...]).astype(jnp.bfloat16)
@@ -361,7 +361,7 @@
         in_specs=[HBM] * 4,
         out_specs=[VMEM] * 8,
         out_shape=[
-            jax.ShapeDtypeStruct((half + 16, width), jnp.bfloat16),
+            jax.ShapeDtypeStruct((half + EXTRA, width), jnp.bfloat16),
             jax.ShapeDtypeStruct((width, half), jnp.bfloat16),
             jax.ShapeDtypeStruct((half, width), jnp.bfloat16),
             jax.ShapeDtypeStruct((rows, width), jnp.bfloat16),
@@ -380,49 +380,50 @@
     )(*in_hbm(offsets, queries, keys, values))
 
 
-def attend_late(queries, keys, values, own_bias, other_bias):
+def attend_late(queries, keys, values, own_bias, other_bias, slot, weight, cotangent, stashed):
     half, width = queries.shape
     return pl.pallas_call(
         late_kernel,
-        in_specs=[VMEM] * 5,
-        out_specs=VMEM,
-        out_shape=jax.ShapeDtypeStruct((half // POOL, width), jnp.bfloat16),
-        scratch_shapes=[pltpu.VMEM((half, 2 * half), jnp.bfloat16)] * 2,
-        cost_estimate=cost(8 * half * half * width, 10 * half * width, half * half * width // 64),
+        in_specs=[VMEM] * 5 + [SMEM] + [HBM] * 3,
+        out_specs=[VMEM] * 4,
+        out_shape=[
+            jax.ShapeDtypeStruct((half // POOL, width), jnp.bfloat16),
+            jax.ShapeDtypeStruct(weight.shape, weight.dtype),
+            jax.ShapeDtypeStruct(cotangent.shape, cotangent.dtype),
+            jax.ShapeDtypeStruct(stashed.shape[1:], stashed.dtype),
+        ],
+        scratch_shapes=[
+            pltpu.VMEM((half, 2 * half), jnp.bfloat16),
+            pltpu.VMEM((half, 2 * half), jnp.bfloat16),
+            pltpu.SemaphoreType.DMA((3,)),
+        ],
+        cost_estimate=cost(8 * half * half * width, 30 * half * width, half * half * width // 64),
         compiler_params=params(),
         name="attend_late",
-    )(queries, keys, values, own_bias, other_bias)
-
-
-def attend_halo(sent, keys, values, bias, term, other, after):
+    )(queries, keys, values, own_bias, other_bias, slot, *in_hbm(weight, cotangent, stashed))
+
+
+def attend_halo(sent, keys, values, bias, after):
     half, width = bias.shape[0], keys.shape[1]
     return pl.pallas_call(
         halo_kernel,
-        in_specs=[VMEM] * 6 + [ANY] * len(after),
-        out_specs=[VMEM] * 2,
-        out_shape=[
-            jax.ShapeDtypeStruct((half // POOL + 16, width), jnp.bfloat16),
-            jax.ShapeDtypeStruct(term.shape, term.dtype),
-        ],
+        in_specs=[VMEM] * 4 + [ANY],
+        out_specs=VMEM,
+        out_shape=jax.ShapeDtypeStruct((half // POOL + EXTRA, width), jnp.bfloat16),
         cost_estimate=cost(4 * half * half * width, 6 * half * width, half * half * width // 64),
         compiler_params=params(),
         name="attend_halo",
-    )(sent, keys, values, bias, term, other, *after)
-
-
-def backward(slot, cotangent, weight, gain, stashed, after):
-    rows, depth = cotangent.shape
-    width = weight.shape[0]
+    )(sent, keys, values, bias, after)
+
+
+def backward(cotangent, weight, gain, held):
+    rows, width = held.shape
+    depth = weight.shape[1]
     return pl.pallas_call(
         back_kernel,
-        in_specs=[SMEM, HBM, VMEM, VMEM, HBM, ANY],
+        in_specs=[VMEM] * 4,
         out_specs=[VMEM] * 2,
-        scratch_shapes=[
-            pltpu.VMEM((rows, depth), jnp.bfloat16),
-            pltpu.VMEM((rows, width), jnp.bfloat16),
-            pltpu.VMEM((rows, width), jnp.float32),
-            pltpu.SemaphoreType.DMA((2,)),
-        ],
+        scratch_shapes=[pltpu.VMEM((rows, width), jnp.float32)],
         out_shape=[
             jax.ShapeDtypeStruct((rows, width), jnp.bfloat16),
             jax.ShapeDtypeStruct((1, width), jnp.float32),
@@ -430,11 +431,11 @@
         cost_estimate=cost(2 * rows * width * depth, 2 * width * depth),
         compiler_params=params(),
         name="backward",
-    )(slot, *in_hbm(cotangent), weight, gain, *in_hbm(stashed), after)
+    )(cotangent, weight, gain, held)
 
 
 def project(early, late, halo, gain, weight, term, other, upstream):
-    rows = 2 * late.shape[0]
+    rows = upstream.shape[0]
     width, depth = weight.shape
     return pl.pallas_call(
         project_kernel,
@@ -488,16 +489,18 @@
     )
     arrived = shifted(sent, "seq", -1)
     early = passed_along(early, "section", 1)
-    late = attend_late(q_late, keys, values, own_bias, other_bias)
-    late_arrived = passed_along(late, "section", 1)
-    dinput, term = backward(slot, cotangent[0, 0], weight[0], gain, stashed[0, 0], late)
+    late, weight, cotangent, held = attend_late(
+        q_late, keys, values, own_bias, other_bias, slot, weight[0], cotangent[0, 0], stashed[0, 0]
+    )
+    dinput, term = backward(cotangent, weight, gain, held)
     upstream = passed_along(dinput, "section", -1)
     term = term if rounds else lax.psum(term, ("rep", "seq"))
-    halo, term = attend_halo(arrived, keys, values, next_bias, term, partner(term, 0), (late_arrived,))
-    halo = onward(halo)
+    term = term + partner(term, 0)
     term = term + partner(term, 1)
+    late = passed_along(late, "section", 1)
+    halo = onward(attend_halo(arrived, keys, values, next_bias, term))
     mol_keys, update, upstream = project(
-        early, late_arrived, halo, gain, weight[0], term, partner(term, 2), upstream
+        early, late, halo, gain, weight, term, partner(term, 2), upstream
     )
     return mol_keys[None, None], upstream[None, None], update
 

time: 42.4 us -> 36.5 us (0.86)
  waiting for transfers between devices: 12.4 us -> 5.66 us
  Pallas kernels: 11.6 us -> 12.3 us
    ppermute x3, waiting for transfers between devices: 7.26 us -> 0.01 us  [passed_along(): lax.ppermute(value, axis, [(i, (i + steps) % count) for i in range(count)])]
    ppermute x3, starting transfers between devices: 4.32 us -> 5.35 us  [swapped(): lax.ppermute(value, axis, [(i, i ^ distance) for i in range(lax.axis_size...]
    pallas_call x3, Pallas kernels: 6.21 us -> 7.06 us  [the longest x1 3.74 us: attend_late(): pl.pallas_call(late_kernel, in_specs=[VMEM] * 5 + [SMEM] + [HBM] * 3, out...]
    ppermute x1, starting transfers between devices: 5.15 us -> 4.39 us  [onward(): return lax.ppermute(value, ('section', 'seq'), route)]
    ppermute x3, waiting for transfers between devices: 5.18 us -> 5.65 us  [swapped(): lax.ppermute(value, axis, [(i, i ^ distance) for i in range(lax.axis_size...]
  transfers between devices with their start and end apart: 8 -> 8, of which waited for: 4 -> 3; matrix products, arithmetic and copies ran while one was open for 0% -> 0% of each run, Pallas kernels for 15% -> 20%
where the time goes in v6:
time: 36.5 us; the launch traced here: 36 us
  starting transfers between devices  16.6 us (45%)
  Pallas kernels  12.3 us (34%)
  waiting for transfers between devices  5.66 us (16%)
  between operations  1.37 us (4%)
    ppermute x3, waiting for transfers between devices, swapped(): lax.ppermute(value, axis, [(i, i ^ distance) for i in range(lax.axis_size...  5.65 us
    ppermute x3, starting transfers between devices, passed_along(): lax.ppermute(value, axis, [(i, (i + steps) % count) for i in range(count)])  5.57 us
    ppermute x3, starting transfers between devices, swapped(): lax.ppermute(value, axis, [(i, i ^ distance) for i in range(lax.axis_size...  5.35 us
    ppermute x1, starting transfers between devices, onward(): return lax.ppermute(value, ('section', 'seq'), route)  4.39 us
    pallas_call x1, Pallas kernels, attend_late(): pl.pallas_call(late_kernel, in_specs=[VMEM] * 5 + [SMEM] + [HBM] * 3, out...  3.74 us
    pallas_call x1, Pallas kernels, attend_early(): pl.pallas_call(functools.partial(early_kernel, rows, chunks), in_specs=[H...  3.38 us
    pallas_call x1, Pallas kernels, project(): pl.pallas_call(project_kernel, in_specs=[VMEM] * 7 + [ANY], out_specs=[VM...  1.88 us
    pallas_call x1, Pallas kernels, attend_halo(): pl.pallas_call(halo_kernel, in_specs=[VMEM] * 4 + [ANY], out_specs=VMEM,...  1.78 us
  transfers between devices with their start and end apart: 8, of which 3 were waited for; matrix products, arithmetic and copies ran while one was open for 0% of the time, Pallas kernels for 20%

profile of v6, /device:TPU:0, one launch (start us, length us, event | category | flops | bytes accessed | tf_op | source)
XLA Modules:
  0.0 36.0 jit_solution(5546402569289480808)
XLA Ops:
  0.6 3.4 %attend_early.1 = (bf16[136,2048]{1,0:T(8,128)(2,1)S(1)}, bf16[2048,128]{1,0:T(8,128)(2,1)S(1)}, bf16[128,2048]{1,0:T(8,128)(2,1)S(1)}, bf16[256,2048]{1,0:T(8,1...) custom-call(s32[1,8]{1,0:T(1,128)} %bitcast.15, ...), custom_call_target="tpu_custom_call" | custom-call | flops 134217728 | bytes 3145728 | tf_op jit(solution)/shard_map/attend_early/pallas_call | solution.py:359
  4.0 0.0 copy-start
  4.0 1.3 %collective-permute-start.2 = (bf16[136,2048]{1,0:T(8,128)(2,1)S(1)}, bf16[136,2048]{1,0:T(8,128)(2,1)S(1)}, u32[]{:S(2)}, u32[]{:S(2)}) collective-permute-start(bf16[136,2048]{1,0:T(8,128)(2,1)S(1)} %get-tuple-element.27), channel_id=1, source_target_pairs={{2,0},{4,2},{6,4},{3,1},{5,3},{7,5},{10,8},{12,10},{14,12},{11,9},... | collective-permute-start | bytes 1671176 | tf_op jit(solution)/shard_map/ppermute | solution.py:35
  5.3 3.0 %collective-permute-start = (bf16[2048,128]{1,0:T(8,128)(2,1)S(1)}, bf16[2048,128]{1,0:T(8,128)(2,1)S(1)}, u32[]{:S(2)}, u32[]{:S(2)}) collective-permute-start(bf16[2048,128]{1,0:T(8,128)(2,1)S(1)} %get-tuple-element.20), channel_id=1, source_target_pairs={{0,8},{8,16},{16,24},{24,0},{1,9},{9,17},{17,25},{25,1},{2,10},{10... | collective-permute-start | bytes 1572872 | tf_op jit(solution)/shard_map/ppermute | solution.py:40
  9.0 3.7 %attend_late.1 = (bf16[32,2048]{1,0:T(8,128)(2,1)S(1)}, bf16[2048,1024]{1,0:T(8,128)(2,1)S(1)}, bf16[64,1024]{1,0:T(8,128)(2,1)S(1)}, bf16[64,2048]{1,0:T(8,128)(2,1)S(1)}) custom-call(bf16[128,2048]{1,0:T(8,128)(2,1)S(1)} %get-tuple-element.21.q_ref, bf16[256,2048]{1,0:T(8,128)(2,1)S(1)} %get-tuple-element.22.k_ref, ...), custom_call_target="tpu_custom_call" | custom-call | flops 268435456 | bytes 7864320 | tf_op jit(solution)/shard_map/attend_late/pallas_call | solution.py:385
  12.7 0.0 copy-done
  12.7 1.5 %backward.1 = (bf16[64,2048]{1,0:T(8,128)(2,1)S(1)}, f32[1,2048]{1,0:T(1,128)S(1)}) custom-call(bf16[64,1024]{1,0:T(8,128)(2,1)S(1)} %get-tuple-element.29.cotangent_ref, bf16[2048,1024]{1,0:T(8,128)(2,1)S(1)} %get-tuple-element.30.weight_ref, f32[1,2048]{1,0:T(1,128)S(1)} %copy-done, bf16[64,2048]{1,0:T(8,128)(2,1)S(1)} %get-tuple-element.31.held_ref), custom_call_target="tpu_custom_call" | custom-call | flops 268435456 | bytes 4194304 | tf_op jit(solution)/shard_map/backward/pallas_call | solution.py:422
  14.3 1.0 %collective-permute-start.7 = (bf16[64,2048]{1,0:T(8,128)(2,1)S(1)}, bf16[64,2048]{1,0:T(8,128)(2,1)S(1)}, u32[]{:S(2)}, u32[]{:S(2)}) collective-permute-start(bf16[64,2048]{1,0:T(8,128)(2,1)S(1)} %get-tuple-element.33), channel_id=1, source_target_pairs={{0,24},{8,0},{16,8},{24,16},{1,25},{9,1},{17,9},{25,17},{2,26},{10... | collective-permute-start | bytes 786440 | tf_op jit(solution)/shard_map/ppermute | solution.py:40
  15.3 0.0 collective-permute-start.3
  15.3 1.2 %collective-permute-done.3 = f32[1,2048]{1,0:T(1,128)S(1)} collective-permute-done((f32[1,2048]{1,0:T(1,128)S(1)}, f32[1,2048]{1,0:T(1,128)S(1)}, u32[]{:S(2)}, u32[]{:S(2)}) %collective-permute-start.3) | collective-permute-done | bytes 8224 | tf_op jit(solution)/shard_map/ppermute | solution.py:457
  16.5 2.7 %collective-permute-start.4 = (f32[1,2048]{1,0:T(1,128)S(1)}, f32[1,2048]{1,0:T(1,128)S(1)}, u32[]{:S(2)}, u32[]{:S(2)}) collective-permute-start(f32[1,2048]{1,0:T(1,128)S(1)} %add.6), channel_id=1, source_target_pairs={{0,2},{2,0},{4,6},{6,4},{1,3},{3,1},{5,7},{7,5},{8,10},{10,8},{12,... | collective-permute-start | bytes 24584 | tf_op jit(solution)/shard_map/ppermute | solution.py:457
  19.2 2.5 %collective-permute-done.4 = f32[1,2048]{1,0:T(1,128)S(1)} collective-permute-done((f32[1,2048]{1,0:T(1,128)S(1)}, f32[1,2048]{1,0:T(1,128)S(1)}, u32[]{:S(2)}, u32[]{:S(2)}) %collective-permute-start.4) | collective-permute-done | bytes 8224 | tf_op jit(solution)/shard_map/ppermute | solution.py:457
  21.8 0.0 collective-permute-done.2.q_ref
  21.8 1.8 %attend_halo.1 = bf16[40,2048]{1,0:T(8,128)(2,1)S(1)} custom-call(bf16[136,2048]{1,0:T(8,128)(2,1)S(1)} %collective-permute-done.2.q_ref, bf16[256,2048]{1,0:T(8,128)(2,1)S(1)} %get-tuple-element.22.k_ref, bf16[256,2048]{1,0:T(8,128)(2,1)S(1)} %get-tuple-element.23.v_ref, f32[128,256]{1,0:T(8,128)S(1)} %get-tuple-element.28.bias, ...), custom_call_target="tpu_custom_call" | custom-call | flops 134217728 | bytes 1572864 | tf_op jit(solution)/shard_map/attend_halo/pallas_call | solution.py:408
  23.6 4.4 %collective-permute-start.5 = (bf16[40,2048]{1,0:T(8,128)(2,1)S(1)}, bf16[40,2048]{1,0:T(8,128)(2,1)S(1)}, u32[]{:S(2)}, u32[]{:S(2)}) collective-permute-start(bf16[40,2048]{1,0:T(8,128)(2,1)S(1)} %attend_halo.1), channel_id=1, source_target_pairs={{0,10},{2,12},{4,14},{8,18},{10,20},{12,22},{16,26},{18,28},{20,30... | collective-permute-start | bytes 491528 | tf_op jit(solution)/shard_map/ppermute | solution.py:477
  28.0 1.6 %collective-permute-start.1 = (bf16[32,2048]{1,0:T(8,128)(2,1)S(1)}, bf16[32,2048]{1,0:T(8,128)(2,1)S(1)}, u32[]{:S(2)}, u32[]{:S(2)}) collective-permute-start(bf16[32,2048]{1,0:T(8,128)(2,1)S(1)} %get-tuple-element.26), channel_id=1, source_target_pairs={{0,8},{8,16},{16,24},{24,0},{1,9},{9,17},{17,25},{25,1},{2,10},{10... | collective-permute-start | bytes 393224 | tf_op jit(solution)/shard_map/ppermute | solution.py:40
  29.5 2.6 %collective-permute-start.6 = (f32[1,2048]{1,0:T(1,128)S(1)}, f32[1,2048]{1,0:T(1,128)S(1)}, u32[]{:S(2)}, u32[]{:S(2)}) collective-permute-start(f32[1,2048]{1,0:T(1,128)S(1)} %add.7.after_ref.term_ref), channel_id=1, source_target_pairs={{0,4},{2,6},{4,0},{6,2},{1,5},{3,7},{5,1},{7,3},{8,12},{10,14},{12... | collective-permute-start | bytes 24584 | tf_op jit(solution)/shard_map/ppermute | solution.py:457
  32.1 1.9 %collective-permute-done.6.other_ref = f32[1,2048]{1,0:T(1,128)S(1)} collective-permute-done((f32[1,2048]{1,0:T(1,128)S(1)}, f32[1,2048]{1,0:T(1,128)S(1)}, u32[]{:S(2)}, u32[]{:S(2)}) %collective-permute-start.6) | collective-permute-done | bytes 8224 | tf_op jit(solution)/shard_map/ppermute | solution.py:457
  34.1 0.0 collective-permute-done.1.late_ref
  34.1 0.0 collective-permute-done.7.upstream_hbm
  34.1 0.0 collective-permute-done.early_ref
  34.1 0.0 collective-permute-done.5.halo_ref
  34.1 1.9 %project.1 = (bf16[64,1024]{1,0:T(8,128)(2,1)}, f32[1,2048]{1,0:T(1,128)}, bf16[64,2048]{1,0:T(8,128)(2,1)}) custom-call(bf16[2048,128]{1,0:T(8,128)(2,1)S(1)} %collective-permute-done.early_ref, bf16[32,2048]{1,0:T(8,128)(2,1)S(1)} %collective-permute-done.1.late_ref, bf16[40,2048]{1,0:T(8,128)(2,1)S(1)} %collective-permute-done.5.halo_ref, ...), custom_call_target="tpu_custom_call" | custom-call | flops 268435456 | bytes 4194304 | tf_op jit(solution)/shard_map/project/pallas_call | solution.py:440
  (2 shorter events, 0.0 us)
Async XLA Ops:
  4.0 8.7 %copy-start = (f32[1,2048]{1,0:T(1,128)S(1)}, f32[1,2048]{1,0:T(1,128)}, u32[]{:S(2)}) copy-start(f32[1,2048]{1,0:T(1,128)} %gain_ref.3) | copy-start | bytes 24580
  4.0 17.7 %collective-permute-start.2 = (bf16[136,2048]{1,0:T(8,128)(2,1)S(1)}, bf16[136,2048]{1,0:T(8,128)(2,1)S(1)}, u32[]{:S(2)}, u32[]{:S(2)}) collective-permute-start(bf16[136,2048]{1,0:T(8,128)(2,1)S(1)} %get-tuple-element.27), channel_id=1, source_target_pairs={{2,0},{4,2},{6,4},{3,1},{5,3},{7,5},{10,8},{12,10},{14,12},{11,9},... | collective-permute-start | bytes 1671176 | tf_op jit(solution)/shard_map/ppermute | solution.py:35
  5.3 28.8 %collective-permute-start = (bf16[2048,128]{1,0:T(8,128)(2,1)S(1)}, bf16[2048,128]{1,0:T(8,128)(2,1)S(1)}, u32[]{:S(2)}, u32[]{:S(2)}) collective-permute-start(bf16[2048,128]{1,0:T(8,128)(2,1)S(1)} %get-tuple-element.20), channel_id=1, source_target_pairs={{0,8},{8,16},{16,24},{24,0},{1,9},{9,17},{17,25},{25,1},{2,10},{10... | collective-permute-start | bytes 1572872 | tf_op jit(solution)/shard_map/ppermute | solution.py:40
  14.3 19.8 %collective-permute-start.7 = (bf16[64,2048]{1,0:T(8,128)(2,1)S(1)}, bf16[64,2048]{1,0:T(8,128)(2,1)S(1)}, u32[]{:S(2)}, u32[]{:S(2)}) collective-permute-start(bf16[64,2048]{1,0:T(8,128)(2,1)S(1)} %get-tuple-element.33), channel_id=1, source_target_pairs={{0,24},{8,0},{16,8},{24,16},{1,25},{9,1},{17,9},{25,17},{2,26},{10... | collective-permute-start | bytes 786440 | tf_op jit(solution)/shard_map/ppermute | solution.py:40
  15.3 1.2 %collective-permute-start.3 = (f32[1,2048]{1,0:T(1,128)S(1)}, f32[1,2048]{1,0:T(1,128)S(1)}, u32[]{:S(2)}, u32[]{:S(2)}) collective-permute-start(f32[1,2048]{1,0:T(1,128)S(1)} %get-tuple-element.32), channel_id=1, source_target_pairs={{0,1},{1,0},{2,3},{3,2},{4,5},{5,4},{6,7},{7,6},{8,9},{9,8},{10,11... | collective-permute-start | bytes 24584 | tf_op jit(solution)/shard_map/ppermute | solution.py:457
  16.5 5.3 %collective-permute-start.4 = (f32[1,2048]{1,0:T(1,128)S(1)}, f32[1,2048]{1,0:T(1,128)S(1)}, u32[]{:S(2)}, u32[]{:S(2)}) collective-permute-start(f32[1,2048]{1,0:T(1,128)S(1)} %add.6), channel_id=1, source_target_pairs={{0,2},{2,0},{4,6},{6,4},{1,3},{3,1},{5,7},{7,5},{8,10},{10,8},{12,... | collective-permute-start | bytes 24584 | tf_op jit(solution)/shard_map/ppermute | solution.py:457
  23.6 10.5 %collective-permute-start.5 = (bf16[40,2048]{1,0:T(8,128)(2,1)S(1)}, bf16[40,2048]{1,0:T(8,128)(2,1)S(1)}, u32[]{:S(2)}, u32[]{:S(2)}) collective-permute-start(bf16[40,2048]{1,0:T(8,128)(2,1)S(1)} %attend_halo.1), channel_id=1, source_target_pairs={{0,10},{2,12},{4,14},{8,18},{10,20},{12,22},{16,26},{18,28},{20,30... | collective-permute-start | bytes 491528 | tf_op jit(solution)/shard_map/ppermute | solution.py:477
  28.0 6.1 %collective-permute-start.1 = (bf16[32,2048]{1,0:T(8,128)(2,1)S(1)}, bf16[32,2048]{1,0:T(8,128)(2,1)S(1)}, u32[]{:S(2)}, u32[]{:S(2)}) collective-permute-start(bf16[32,2048]{1,0:T(8,128)(2,1)S(1)} %get-tuple-element.26), channel_id=1, source_target_pairs={{0,8},{8,16},{16,24},{24,0},{1,9},{9,17},{17,25},{25,1},{2,10},{10... | collective-permute-start | bytes 393224 | tf_op jit(solution)/shard_map/ppermute | solution.py:40
  29.5 4.5 %collective-permute-start.6 = (f32[1,2048]{1,0:T(1,128)S(1)}, f32[1,2048]{1,0:T(1,128)S(1)}, u32[]{:S(2)}, u32[]{:S(2)}) collective-permute-start(f32[1,2048]{1,0:T(1,128)S(1)} %add.7.after_ref.term_ref), channel_id=1, source_target_pairs={{0,4},{2,6},{4,0},{6,2},{1,5},{3,7},{5,1},{7,3},{8,12},{10,14},{12... | collective-permute-start | bytes 24584 | tf_op jit(solution)/shard_map/ppermute | solution.py:457

commit v7 on v6

--- a/solution.py
+++ b/solution.py
@@ -133,8 +133,8 @@
 
 
 def early_kernel(
-    rows, chunks, offsets_hbm, q_hbm, k_hbm, v_hbm,
-    sent_ref, early_ref, q_late_ref, k_ref, v_ref, own_ref, other_ref, next_ref,
+    rows, chunks, offsets_hbm, q_hbm, k_hbm, v_hbm, cotangent_hbm, stashed_hbm,
+    sent_ref, early_ref, q_late_ref, k_ref, v_ref, own_ref, other_ref, next_ref, cotangent_ref, stashed_ref,
     offsets_ref, bias, sems, offsets_sem,
 ):
     half = rows // 2
@@ -150,10 +150,10 @@
         load(k_hbm.at[tail], k_ref.at[tail], offsets_sem.at[1]),
         load(v_hbm.at[tail], v_ref.at[tail], offsets_sem.at[2]),
         load(q_hbm.at[tail], q_late_ref, offsets_sem.at[3]),
+        load(cotangent_hbm, cotangent_ref, offsets_sem.at[4]),
+        load(stashed_hbm, stashed_ref, offsets_sem.at[5]),
     ]
-    offsets_copy.wait()
     start = lax.axis_index("seq") * rows
-    bias[...] = mask_bias(offsets_ref, start, start, lambda key, query: key <= query)
     pairs = k_ref.shape[1] // LANES
 
     def arrive(pair):
@@ -161,6 +161,9 @@
         if pair % per_chunk == 0:
             for copy in copies[pair // per_chunk]:
                 copy.wait()
+        if pair == 1:
+            offsets_copy.wait()
+            bias[...] = mask_bias(offsets_ref, start, start, lambda key, query: key <= query)
 
     def score(pair):
         scores = dot_nt(k_ref[head, at(pair)], split_heads(sent_ref[head, at(pair)]))
@@ -191,20 +194,17 @@
 
 
 def late_kernel(
-    q_ref, k_ref, v_ref, own_bias, other_bias, slot_ref, weight_hbm, cotangent_hbm, stashed_hbm,
-    late_ref, weight_ref, cotangent_ref, held_ref, own, other, sems,
+    q_ref, k_ref, v_ref, own_bias, other_bias, early_ref, both_ref, own, other
 ):
-    copies = [
-        load(cotangent_hbm, cotangent_ref, sems.at[0]),
-        load(stashed_hbm.at[slot_ref[0, 0]], held_ref, sems.at[1]),
-        load(weight_hbm, weight_ref, sems.at[2]),
-    ]
     half = q_ref.shape[0]
     key = lax.broadcasted_iota(jnp.int32, own.shape, 0)
     query = lax.broadcasted_iota(jnp.int32, own.shape, 1) % half
     own[...] = jnp.where(key <= query, 1.0, 0.0).astype(jnp.bfloat16)
     other[...] = jnp.where(key <= query, 0.0, 1.0).astype(jnp.bfloat16)
     pooling = pool_matrix(half)
+    molecules = half // POOL
+    features = early_ref.shape[0]
+    both_ref[pl.ds(0, features), :] = early_ref[...]
     pairs = k_ref.shape[1] // LANES
     parts = []
 
@@ -226,13 +226,13 @@
         parts.append(own_heads(mixed, inverse).astype(jnp.bfloat16))
         if len(parts) == 4:
             pooled = dot_nt(pooling, jnp.concatenate(parts, axis=0)).astype(jnp.bfloat16)
-            late_ref[:, pl.ds((pair - 3) * LANES, 4 * LANES)] = pooled
+            for i in range(4):
+                place = features + (pair - 3 + i) * molecules
+                both_ref[pl.ds(place, molecules), :] = pooled[:, i * LANES : (i + 1) * LANES]
             parts.clear()
         return ()
 
     over_pairs(pairs, (score, top, weigh, finish), LAGS, lambda pair: None)
-    for copy in copies:
-        copy.wait()
 
 
 def halo_kernel(q_ref, k_ref, v_ref, bias, after_ref, out_ref):
@@ -278,7 +278,13 @@
     over_pairs(pairs, (score, top, weigh, finish), LAGS, lambda pair: None)
 
 
-def back_kernel(cotangent_ref, weight_ref, gain_ref, held_ref, dinput_ref, term_ref, grad):
+def back_kernel(
+    slot_ref, cotangent_ref, weight_ref, gain_ref, stashed_ref, after_ref, dinput_ref, term_ref, grad, held_ref
+):
+    held = stashed_ref[0]
+    for i in range(1, stashed_ref.shape[0]):
+        held = jnp.where(slot_ref[0:1, 0:1] == i, stashed_ref[i].astype(jnp.float32), held.astype(jnp.float32))
+    held_ref[...] = held.astype(jnp.bfloat16)
     features = weight_ref.shape[0]
     block = 512
     for begin in range(0, features, block):
@@ -301,11 +307,11 @@
 
 
 def project_kernel(
-    early_ref, late_ref, halo_ref, gain_ref, weight_ref, term_ref, other_ref, upstream_hbm,
+    both_ref, halo_ref, gain_ref, weight_ref, term_ref, other_ref, upstream_hbm,
     out_ref, update_ref, passed_hbm, pooled, sem,
 ):
     passing = load(upstream_hbm, passed_hbm, sem)
-    half = early_ref.shape[1]
+    half = both_ref.shape[1]
     features = gain_ref.shape[1]
     molecules = half // POOL
     pooling = pool_matrix(half)
@@ -315,7 +321,9 @@
         shares = halo_ref[molecules:, at(pair)].astype(jnp.float32)
         share_a = jnp.where(first, 1.0, shares[0:1] + shares[1:2])
         share_b = jnp.where(first, 1.0, shares[2:3] + shares[3:4])
-        early = early_ref[at(pair), :].astype(jnp.float32)
+        early = both_ref[at(pair), :].astype(jnp.float32)
+        place = pl.ds(features + pair * molecules, molecules)
+        pooled[pl.ds(molecules, molecules), at(pair)] = both_ref[place, :]
         parts += [early[:HEAD_DIM] * share_a, early[HEAD_DIM:] * share_b]
         if len(parts) == 8:
             columns = pl.ds((pair - 3) * LANES, 4 * LANES)
@@ -323,7 +331,6 @@
             arrived = halo_ref[:molecules, columns].astype(jnp.float32)
             pooled[pl.ds(0, molecules), columns] = (mean + arrived).astype(jnp.bfloat16)
             parts = []
-    pooled[pl.ds(molecules, molecules), :] = late_ref[...]
     arrived = pooled[...].astype(jnp.float32)
     mean = jnp.sum(arrived * arrived, axis=1, keepdims=True) / features
     normed = (arrived * lax.rsqrt(mean + EPS_NORM) * gain_ref[...]).astype(jnp.bfloat16)
@@ -352,14 +359,14 @@
     return pltpu.CompilerParams(vmem_limit_bytes=24 * 2**20)
 
 
-def attend_early(queries, keys, values, offsets, chunks):
+def attend_early(queries, keys, values, offsets, cotangent, stashed, chunks):
     rows, width = queries.shape
     half = rows // 2
     masks = [jax.ShapeDtypeStruct((half, 2 * half), jnp.float32)] * 3
     return pl.pallas_call(
         functools.partial(early_kernel, rows, chunks),
-        in_specs=[HBM] * 4,
-        out_specs=[VMEM] * 8,
+        in_specs=[HBM] * 6,
+        out_specs=[VMEM] * 10,
         out_shape=[
             jax.ShapeDtypeStruct((half + EXTRA, width), jnp.bfloat16),
             jax.ShapeDtypeStruct((width, half), jnp.bfloat16),
@@ -367,40 +374,38 @@
             jax.ShapeDtypeStruct((rows, width), jnp.bfloat16),
             jax.ShapeDtypeStruct((rows, width), jnp.bfloat16),
         ]
-        + masks,
+        + masks
+        + [
+            jax.ShapeDtypeStruct(cotangent.shape, cotangent.dtype),
+            jax.ShapeDtypeStruct(stashed.shape, stashed.dtype),
+        ],
         scratch_shapes=[
             pltpu.SMEM(offsets.shape, jnp.int32),
             pltpu.VMEM((half, 2 * half), jnp.float32),
             pltpu.SemaphoreType.DMA((3, chunks)),
-            pltpu.SemaphoreType.DMA((4,)),
+            pltpu.SemaphoreType.DMA((6,)),
         ],
         cost_estimate=cost(4 * half * half * width, 6 * rows * width, half * half * width // 64),
         compiler_params=params(),
         name="attend_early",
-    )(*in_hbm(offsets, queries, keys, values))
-
-
-def attend_late(queries, keys, values, own_bias, other_bias, slot, weight, cotangent, stashed):
+    )(*in_hbm(offsets, queries, keys, values, cotangent, stashed))
+
+
+def attend_late(queries, keys, values, own_bias, other_bias, early):
     half, width = queries.shape
     return pl.pallas_call(
         late_kernel,
-        in_specs=[VMEM] * 5 + [SMEM] + [HBM] * 3,
-        out_specs=[VMEM] * 4,
-        out_shape=[
-            jax.ShapeDtypeStruct((half // POOL, width), jnp.bfloat16),
-            jax.ShapeDtypeStruct(weight.shape, weight.dtype),
-            jax.ShapeDtypeStruct(cotangent.shape, cotangent.dtype),
-            jax.ShapeDtypeStruct(stashed.shape[1:], stashed.dtype),
-        ],
+        in_specs=[VMEM] * 6,
+        out_specs=VMEM,
+        out_shape=jax.ShapeDtypeStruct((width + width // POOL, half), jnp.bfloat16),
         scratch_shapes=[
             pltpu.VMEM((half, 2 * half), jnp.bfloat16),
             pltpu.VMEM((half, 2 * half), jnp.bfloat16),
-            pltpu.SemaphoreType.DMA((3,)),
-        ],
-        cost_estimate=cost(8 * half * half * width, 30 * half * width, half * half * width // 64),
+        ],
+        cost_estimate=cost(8 * half * half * width, 10 * half * width, half * half * width // 64),
         compiler_params=params(),
         name="attend_late",
-    )(queries, keys, values, own_bias, other_bias, slot, *in_hbm(weight, cotangent, stashed))
+    )(queries, keys, values, own_bias, other_bias, early)
 
 
 def attend_halo(sent, keys, values, bias, after):
@@ -416,14 +421,17 @@
     )(sent, keys, values, bias, after)
 
 
-def backward(cotangent, weight, gain, held):
-    rows, width = held.shape
+def backward(slot, cotangent, weight, gain, stashed, after):
+    rows, width = stashed.shape[1:]
     depth = weight.shape[1]
     return pl.pallas_call(
         back_kernel,
-        in_specs=[VMEM] * 4,
+        in_specs=[VMEM] * 5 + [ANY],
         out_specs=[VMEM] * 2,
-        scratch_shapes=[pltpu.VMEM((rows, width), jnp.float32)],
+        scratch_shapes=[
+            pltpu.VMEM((rows, width), jnp.float32),
+            pltpu.VMEM((rows, width), jnp.bfloat16),
+        ],
         out_shape=[
             jax.ShapeDtypeStruct((rows, width), jnp.bfloat16),
             jax.ShapeDtypeStruct((1, width), jnp.float32),
@@ -431,15 +439,15 @@
         cost_estimate=cost(2 * rows * width * depth, 2 * width * depth),
         compiler_params=params(),
         name="backward",
-    )(cotangent, weight, gain, held)
-
-
-def project(early, late, halo, gain, weight, term, other, upstream):
+    )(slot, cotangent, weight, gain, stashed, after)
+
+
+def project(both, halo, gain, weight, term, other, upstream):
     rows = upstream.shape[0]
     width, depth = weight.shape
     return pl.pallas_call(
         project_kernel,
-        in_specs=[VMEM] * 7 + [ANY],
+        in_specs=[VMEM] * 6 + [ANY],
         out_specs=[VMEM, VMEM, HBM],
         out_shape=[
             jax.ShapeDtypeStruct((rows, depth), jnp.bfloat16),
@@ -450,7 +458,7 @@
         cost_estimate=cost(2 * rows * width * depth, 2 * width * depth),
         compiler_params=params(),
         name="project",
-    )(early, late, halo, gain, weight, term, other, upstream)
+    )(both, halo, gain, weight, term, other, upstream)
 
 
 def swapped(value, axis, distance):
@@ -459,7 +467,7 @@
 
 def sum_rounds():
     rounds = []
-    for axis in ("rep", "seq"):
+    for axis in ("seq", "rep"):
         count = lax.axis_size(axis)
         if count & (count - 1):
             return []
@@ -484,23 +492,21 @@
     def partner(term, index):
         return swapped(term, *rounds[index]) if rounds else jnp.zeros_like(term)
 
-    sent, early, q_late, keys, values, own_bias, other_bias, next_bias = attend_early(
-        queries, keys, values, offsets, 4
+    sent, early, q_late, keys, values, own_bias, other_bias, next_bias, cotangent, stashed = (
+        attend_early(queries, keys, values, offsets, cotangent[0, 0], stashed[0, 0], 4)
     )
     arrived = shifted(sent, "seq", -1)
-    early = passed_along(early, "section", 1)
-    late, weight, cotangent, held = attend_late(
-        q_late, keys, values, own_bias, other_bias, slot, weight[0], cotangent[0, 0], stashed[0, 0]
-    )
-    dinput, term = backward(cotangent, weight, gain, held)
+    both = attend_late(q_late, keys, values, own_bias, other_bias, early)
+    slot = jnp.broadcast_to(slot, (1, LANES))
+    dinput, term = backward(slot, cotangent, weight[0], gain, stashed, both)
+    both = passed_along(both, "section", 1)
     upstream = passed_along(dinput, "section", -1)
     term = term if rounds else lax.psum(term, ("rep", "seq"))
     term = term + partner(term, 0)
+    halo = onward(attend_halo(arrived, keys, values, next_bias, term))
     term = term + partner(term, 1)
-    late = passed_along(late, "section", 1)
-    halo = onward(attend_halo(arrived, keys, values, next_bias, term))
     mol_keys, update, upstream = project(
-        early, late, halo, gain, weight, term, partner(term, 2), upstream
+        both, halo, gain, weight[0], term, partner(term, 2), upstream
     )
     return mol_keys[None, None], upstream[None, None], update
 

time: 36.5 us -> 36.9 us (1.011)
  the two profiles are of different devices: /device:TPU:0 before, /device:TPU:26 now
where the time goes in v7:
time: 36.9 us; the launch traced here: 36.8 us
  waiting for transfers between devices  12.8 us (35%)
  starting transfers between devices  11.8 us (32%)
  Pallas kernels  10.8 us (29%)
  between operations  1.38 us (4%)
    ppermute x3, waiting for transfers between devices, swapped(): lax.ppermute(value, axis, [(i, i ^ distance) for i in range(lax.axis_size...  9.9 us
    ppermute x3, starting transfers between devices, swapped(): lax.ppermute(value, axis, [(i, i ^ distance) for i in range(lax.axis_size...  6.03 us
    pallas_call x1, Pallas kernels, attend_early(): pl.pallas_call(functools.partial(early_kernel, rows, chunks), in_specs=[H...  3.62 us
    ppermute x2, waiting for transfers between devices, passed_along(): lax.ppermute(value, axis, [(i, (i + steps) % count) for i in range(count)])  2.85 us
    ppermute x1, starting transfers between devices, shifted(): lax.ppermute(value, axis, [(i, i + steps) for i in range(first, last)])  2.39 us
    ppermute x2, starting transfers between devices, passed_along(): lax.ppermute(value, axis, [(i, (i + steps) % count) for i in range(count)])  2.09 us
    pallas_call x1, Pallas kernels, project(): pl.pallas_call(project_kernel, in_specs=[VMEM] * 6 + [ANY], out_specs=[VM...  1.89 us
    pallas_call x1, Pallas kernels, attend_late(): pl.pallas_call(late_kernel, in_specs=[VMEM] * 6, out_specs=VMEM, out_shap...  1.88 us
  transfers between devices with their start and end apart: 7, of which 4 were waited for; matrix products, arithmetic and copies ran while one was open for 0% of the time, Pallas kernels for 14%

profile of v7, /device:TPU:26, one launch (start us, length us, event | category | flops | bytes accessed | tf_op | source)
XLA Modules:
  0.0 36.8 jit_solution(1052177570455689549)
XLA Ops:
  0.6 0.0 copy-start
  0.6 0.0 copy-start.1
  0.7 3.6 %attend_early.1 = (bf16[136,2048]{1,0:T(8,128)(2,1)S(1)}, bf16[2048,128]{1,0:T(8,128)(2,1)S(1)}, bf16[128,2048]{1,0:T(8,128)(2,1)S(1)}, bf16[256,2048]{1,0:T(8,1...) custom-call(s32[1,8]{1,0:T(1,128)} %bitcast.18, ...), custom_call_target="tpu_custom_call" | custom-call | flops 134217728 | bytes 3145728 | tf_op jit(solution)/shard_map/attend_early/pallas_call | solution.py:366
  4.3 2.4 %collective-permute-start.1 = (bf16[136,2048]{1,0:T(8,128)(2,1)S(1)}, bf16[136,2048]{1,0:T(8,128)(2,1)S(1)}, u32[]{:S(2)}, u32[]{:S(2)}) collective-permute-start(bf16[136,2048]{1,0:T(8,128)(2,1)S(1)} %get-tuple-element.24), channel_id=1, source_target_pairs={{2,0},{4,2},{6,4},{3,1},{5,3},{7,5},{10,8},{12,10},{14,12},{11,9},... | collective-permute-start | bytes 1671176 | tf_op jit(solution)/shard_map/ppermute | solution.py:35
  6.7 1.9 %attend_late.1.after_ref = bf16[2560,128]{1,0:T(8,128)(2,1)S(1)} custom-call(bf16[128,2048]{1,0:T(8,128)(2,1)S(1)} %get-tuple-element.18.q_ref, bf16[256,2048]{1,0:T(8,128)(2,1)S(1)} %get-tuple-element.19.k_ref, bf16[256,2048]{1,0:T(8,128)(2,1)S(1)} %get-tuple-element.20.v_ref, f32[128,256]{1,0:T(8,128)S(1)} %get-tuple-element.21.own_bias, ...), custom_call_target="tpu_custom_call" | custom-call | flops 268435456 | bytes 2621440 | tf_op jit(solution)/shard_map/attend_late/pallas_call | solution.py:396
  8.6 1.5 %collective-permute-start = (bf16[2560,128]{1,0:T(8,128)(2,1)S(1)}, bf16[2560,128]{1,0:T(8,128)(2,1)S(1)}, u32[]{:S(2)}, u32[]{:S(2)}) collective-permute-start(bf16[2560,128]{1,0:T(8,128)(2,1)S(1)} %attend_late.1.after_ref), channel_id=1, source_target_pairs={{0,8},{8,16},{16,24},{24,0},{1,9},{9,17},{17,25},{25,1},{2,10},{10... | collective-permute-start | bytes 1966088 | tf_op jit(solution)/shard_map/ppermute | solution.py:40
  10.7 0.0 copy-done
  10.7 0.0 copy-done.1
  10.7 1.6 %backward.1 = (bf16[64,2048]{1,0:T(8,128)(2,1)S(1)}, f32[1,2048]{1,0:T(1,128)S(1)}) custom-call(s32[1,128]{1,0:T(1,128)S(1)} %broadcast_in_dim.14.slot_ref, bf16[64,1024]{1,0:T(8,128)(2,1)S(1)} %get-tuple-element.26.cotangent_ref, bf16[2048,1024]{1,0:T(8,128)(2,1)S(1)} %bitcast.11, f32[1,2048]{1,0:T(1,128)S(1)} %copy-done.1, ...), custom_call_target="tpu_custom_call" | custom-call | flops 268435456 | bytes 4194304 | tf_op jit(solution)/shard_map/backward/pallas_call | solution.py:427
  12.3 0.6 %collective-permute-start.6 = (bf16[64,2048]{1,0:T(8,128)(2,1)S(1)}, bf16[64,2048]{1,0:T(8,128)(2,1)S(1)}, u32[]{:S(2)}, u32[]{:S(2)}) collective-permute-start(bf16[64,2048]{1,0:T(8,128)(2,1)S(1)} %get-tuple-element.29), channel_id=1, source_target_pairs={{0,24},{8,0},{16,8},{24,16},{1,25},{9,1},{17,9},{25,17},{2,26},{10... | collective-permute-start | bytes 786440 | tf_op jit(solution)/shard_map/ppermute | solution.py:40
  12.9 0.4 %collective-permute-start.2 = (f32[1,2048]{1,0:T(1,128)S(1)}, f32[1,2048]{1,0:T(1,128)S(1)}, u32[]{:S(2)}, u32[]{:S(2)}) collective-permute-start(f32[1,2048]{1,0:T(1,128)S(1)} %get-tuple-element.28), channel_id=1, source_target_pairs={{0,2},{2,0},{4,6},{6,4},{1,3},{3,1},{5,7},{7,5},{8,10},{10,8},{12,... | collective-permute-start | bytes 24584 | tf_op jit(solution)/shard_map/ppermute | solution.py:465
  13.3 5.4 %collective-permute-done.2 = f32[1,2048]{1,0:T(1,128)S(1)} collective-permute-done((f32[1,2048]{1,0:T(1,128)S(1)}, f32[1,2048]{1,0:T(1,128)S(1)}, u32[]{:S(2)}, u32[]{:S(2)}) %collective-permute-start.2) | collective-permute-done | bytes 8224 | tf_op jit(solution)/shard_map/ppermute | solution.py:465
  18.7 0.0 collective-permute-done.1.q_ref
  18.7 1.8 %attend_halo.1 = bf16[40,2048]{1,0:T(8,128)(2,1)S(1)} custom-call(bf16[136,2048]{1,0:T(8,128)(2,1)S(1)} %collective-permute-done.1.q_ref, bf16[256,2048]{1,0:T(8,128)(2,1)S(1)} %get-tuple-element.19.k_ref, bf16[256,2048]{1,0:T(8,128)(2,1)S(1)} %get-tuple-element.20.v_ref, f32[128,256]{1,0:T(8,128)S(1)} %get-tuple-element.25.bias, f32[1,2048]{1,0:T(1,128)S(1)} %add.6.after_ref), custom_call_target="tpu_custom_call" | custom-call | flops 134217728 | bytes 1572864 | tf_op jit(solution)/shard_map/attend_halo/pallas_call | solution.py:413
  20.5 1.3 %collective-permute-start.3 = (bf16[40,2048]{1,0:T(8,128)(2,1)S(1)}, bf16[40,2048]{1,0:T(8,128)(2,1)S(1)}, u32[]{:S(2)}, u32[]{:S(2)}) collective-permute-start(bf16[40,2048]{1,0:T(8,128)(2,1)S(1)} %attend_halo.1), channel_id=1, source_target_pairs={{0,10},{2,12},{4,14},{8,18},{10,20},{12,22},{16,26},{18,28},{20,30... | collective-permute-start | bytes 491528 | tf_op jit(solution)/shard_map/ppermute | solution.py:485
  21.8 5.5 %collective-permute-start.4 = (f32[1,2048]{1,0:T(1,128)S(1)}, f32[1,2048]{1,0:T(1,128)S(1)}, u32[]{:S(2)}, u32[]{:S(2)}) collective-permute-start(f32[1,2048]{1,0:T(1,128)S(1)} %add.6.after_ref), channel_id=1, source_target_pairs={{0,4},{2,6},{4,0},{6,2},{1,5},{3,7},{5,1},{7,3},{8,12},{10,14},{12... | collective-permute-start | bytes 24584 | tf_op jit(solution)/shard_map/ppermute | solution.py:465
  27.4 3.4 %collective-permute-done.4 = f32[1,2048]{1,0:T(1,128)S(1)} collective-permute-done((f32[1,2048]{1,0:T(1,128)S(1)}, f32[1,2048]{1,0:T(1,128)S(1)}, u32[]{:S(2)}, u32[]{:S(2)}) %collective-permute-start.4) | collective-permute-done | bytes 8224 | tf_op jit(solution)/shard_map/ppermute | solution.py:465
  30.8 0.1 collective-permute-start.5
  30.9 1.2 %collective-permute-done.5.other_ref = f32[1,2048]{1,0:T(1,128)S(1)} collective-permute-done((f32[1,2048]{1,0:T(1,128)S(1)}, f32[1,2048]{1,0:T(1,128)S(1)}, u32[]{:S(2)}, u32[]{:S(2)}) %collective-permute-start.5) | collective-permute-done | bytes 8224 | tf_op jit(solution)/shard_map/ppermute | solution.py:465
  32.0 2.8 %collective-permute-done.6.upstream_hbm = bf16[64,2048]{1,0:T(8,128)(2,1)S(1)} collective-permute-done((bf16[64,2048]{1,0:T(8,128)(2,1)S(1)}, bf16[64,2048]{1,0:T(8,128)(2,1)S(1)}, u32[]{:S(2)}, u32[]{:S(2)}) %collective-permute-start.6) | collective-permute-done | bytes 262176 | tf_op jit(solution)/shard_map/ppermute | solution.py:40
  34.9 0.0 collective-permute-done.both_ref
  34.9 0.0 collective-permute-done.3.halo_ref
  34.9 1.9 %project.1 = (bf16[64,1024]{1,0:T(8,128)(2,1)}, f32[1,2048]{1,0:T(1,128)}, bf16[64,2048]{1,0:T(8,128)(2,1)}) custom-call(bf16[2560,128]{1,0:T(8,128)(2,1)S(1)} %collective-permute-done.both_ref, bf16[40,2048]{1,0:T(8,128)(2,1)S(1)} %collective-permute-done.3.halo_ref, f32[1,2048]{1,0:T(1,128)S(1)} %copy-done.1, bf16[2048,1024]{1,0:T(8,128)(2,1)S(1)} %bitcast.12, ...), custom_call_target="tpu_custom_call" | custom-call | flops 268435456 | bytes 4194304 | tf_op jit(solution)/shard_map/project/pallas_call | solution.py:448
  (3 shorter events, 0.0 us)
Async XLA Ops:
  0.6 10.1 %copy-start = (bf16[1,2048,1024]{2,1,0:T(8,128)(2,1)S(1)}, bf16[1,2048,1024]{2,1,0:T(8,128)(2,1)}, u32[]{:S(2)}) copy-start(bf16[1,2048,1024]{2,1,0:T(8,128)(2,1)} %param.13) | copy-start | bytes 12582916
  0.6 10.1 %copy-start.1 = (f32[1,2048]{1,0:T(1,128)S(1)}, f32[1,2048]{1,0:T(1,128)}, u32[]{:S(2)}) copy-start(f32[1,2048]{1,0:T(1,128)} %gain_ref.3) | copy-start | bytes 24580
  4.3 14.4 %collective-permute-start.1 = (bf16[136,2048]{1,0:T(8,128)(2,1)S(1)}, bf16[136,2048]{1,0:T(8,128)(2,1)S(1)}, u32[]{:S(2)}, u32[]{:S(2)}) collective-permute-start(bf16[136,2048]{1,0:T(8,128)(2,1)S(1)} %get-tuple-element.24), channel_id=1, source_target_pairs={{2,0},{4,2},{6,4},{3,1},{5,3},{7,5},{10,8},{12,10},{14,12},{11,9},... | collective-permute-start | bytes 1671176 | tf_op jit(solution)/shard_map/ppermute | solution.py:35
  8.6 26.3 %collective-permute-start = (bf16[2560,128]{1,0:T(8,128)(2,1)S(1)}, bf16[2560,128]{1,0:T(8,128)(2,1)S(1)}, u32[]{:S(2)}, u32[]{:S(2)}) collective-permute-start(bf16[2560,128]{1,0:T(8,128)(2,1)S(1)} %attend_late.1.after_ref), channel_id=1, source_target_pairs={{0,8},{8,16},{16,24},{24,0},{1,9},{9,17},{17,25},{25,1},{2,10},{10... | collective-permute-start | bytes 1966088 | tf_op jit(solution)/shard_map/ppermute | solution.py:40
  12.3 22.5 %collective-permute-start.6 = (bf16[64,2048]{1,0:T(8,128)(2,1)S(1)}, bf16[64,2048]{1,0:T(8,128)(2,1)S(1)}, u32[]{:S(2)}, u32[]{:S(2)}) collective-permute-start(bf16[64,2048]{1,0:T(8,128)(2,1)S(1)} %get-tuple-element.29), channel_id=1, source_target_pairs={{0,24},{8,0},{16,8},{24,16},{1,25},{9,1},{17,9},{25,17},{2,26},{10... | collective-permute-start | bytes 786440 | tf_op jit(solution)/shard_map/ppermute | solution.py:40
  12.9 5.8 %collective-permute-start.2 = (f32[1,2048]{1,0:T(1,128)S(1)}, f32[1,2048]{1,0:T(1,128)S(1)}, u32[]{:S(2)}, u32[]{:S(2)}) collective-permute-start(f32[1,2048]{1,0:T(1,128)S(1)} %get-tuple-element.28), channel_id=1, source_target_pairs={{0,2},{2,0},{4,6},{6,4},{1,3},{3,1},{5,7},{7,5},{8,10},{10,8},{12,... | collective-permute-start | bytes 24584 | tf_op jit(solution)/shard_map/ppermute | solution.py:465
  20.5 14.4 %collective-permute-start.3 = (bf16[40,2048]{1,0:T(8,128)(2,1)S(1)}, bf16[40,2048]{1,0:T(8,128)(2,1)S(1)}, u32[]{:S(2)}, u32[]{:S(2)}) collective-permute-start(bf16[40,2048]{1,0:T(8,128)(2,1)S(1)} %attend_halo.1), channel_id=1, source_target_pairs={{0,10},{2,12},{4,14},{8,18},{10,20},{12,22},{16,26},{18,28},{20,30... | collective-permute-start | bytes 491528 | tf_op jit(solution)/shard_map/ppermute | solution.py:485
  21.8 8.9 %collective-permute-start.4 = (f32[1,2048]{1,0:T(1,128)S(1)}, f32[1,2048]{1,0:T(1,128)S(1)}, u32[]{:S(2)}, u32[]{:S(2)}) collective-permute-start(f32[1,2048]{1,0:T(1,128)S(1)} %add.6.after_ref), channel_id=1, source_target_pairs={{0,4},{2,6},{4,0},{6,2},{1,5},{3,7},{5,1},{7,3},{8,12},{10,14},{12... | collective-permute-start | bytes 24584 | tf_op jit(solution)/shard_map/ppermute | solution.py:465
  30.8 1.2 %collective-permute-start.5 = (f32[1,2048]{1,0:T(1,128)S(1)}, f32[1,2048]{1,0:T(1,128)S(1)}, u32[]{:S(2)}, u32[]{:S(2)}) collective-permute-start(f32[1,2048]{1,0:T(1,128)S(1)} %add.7.term_ref), channel_id=1, source_target_pairs={{0,1},{1,0},{2,3},{3,2},{4,5},{5,4},{6,7},{7,6},{8,9},{9,8},{10,11... | collective-permute-start | bytes 24584 | tf_op jit(solution)/shard_map/ppermute | solution.py:465

commit v8 on v7

--- a/solution.py
+++ b/solution.py
@@ -134,27 +134,36 @@
 
 def early_kernel(
     rows, chunks, offsets_hbm, q_hbm, k_hbm, v_hbm, cotangent_hbm, stashed_hbm,
-    sent_ref, early_ref, q_late_ref, k_ref, v_ref, own_ref, other_ref, next_ref, cotangent_ref, stashed_ref,
-    offsets_ref, bias, sems, offsets_sem,
+    sent_ref, early_ref, q_own_ref, q_late_ref, k_ref, v_ref, forward_ref,
+    first_ref, own_ref, other_ref, next_ref, last_ref, cotangent_ref, stashed_ref,
+    offsets_ref, sems, rest_sems,
 ):
     half = rows // 2
     head, tail = pl.ds(0, half), pl.ds(half, half)
-    offsets_copy = load(offsets_hbm, offsets_ref, offsets_sem.at[0])
+    width = sent_ref.shape[1]
+    back, kept = pl.ds(0, width), pl.ds(width, k_ref.shape[1] - width)
+    offsets_copy = load(offsets_hbm, offsets_ref, rest_sems.at[0])
     arrays = (
-        (k_hbm.at[head], k_ref.at[head]),
-        (q_hbm.at[head], sent_ref.at[head]),
-        (v_hbm.at[head], v_ref.at[head]),
+        (k_hbm.at[head, back], k_ref.at[head, back]),
+        (q_hbm.at[head, back], sent_ref.at[head]),
+        (v_hbm.at[head, back], v_ref.at[head, back]),
     )
     copies = load_chunks(arrays, chunks, sems)
     rest = [
-        load(k_hbm.at[tail], k_ref.at[tail], offsets_sem.at[1]),
-        load(v_hbm.at[tail], v_ref.at[tail], offsets_sem.at[2]),
-        load(q_hbm.at[tail], q_late_ref, offsets_sem.at[3]),
-        load(cotangent_hbm, cotangent_ref, offsets_sem.at[4]),
-        load(stashed_hbm, stashed_ref, offsets_sem.at[5]),
+        (k_hbm.at[tail, kept], forward_ref.at[head]),
+        (v_hbm.at[tail, kept], forward_ref.at[tail]),
+        (k_hbm.at[tail], k_ref.at[tail]),
+        (v_hbm.at[tail], v_ref.at[tail]),
+        (q_hbm.at[tail], q_late_ref),
+        (k_hbm.at[head, kept], k_ref.at[head, kept]),
+        (v_hbm.at[head, kept], v_ref.at[head, kept]),
+        (q_hbm.at[head, kept], q_own_ref),
+        (cotangent_hbm, cotangent_ref),
+        (stashed_hbm, stashed_ref),
     ]
+    rest = [load(source, target, rest_sems.at[i + 1]) for i, (source, target) in enumerate(rest)]
     start = lax.axis_index("seq") * rows
-    pairs = k_ref.shape[1] // LANES
+    pairs = width // LANES
 
     def arrive(pair):
         per_chunk = pairs // chunks
@@ -163,14 +172,14 @@
                 copy.wait()
         if pair == 1:
             offsets_copy.wait()
-            bias[...] = mask_bias(offsets_ref, start, start, lambda key, query: key <= query)
+            first_ref[...] = mask_bias(offsets_ref, start, start, lambda key, query: key <= query)
 
     def score(pair):
         scores = dot_nt(k_ref[head, at(pair)], split_heads(sent_ref[head, at(pair)]))
         return scores, with_ones(jnp.transpose(v_ref[head, at(pair)]))
 
     def top(pair, scores, values_t):
-        scores = scores + bias[...]
+        scores = scores + first_ref[...]
         return scores, tops(scores), values_t
 
     def weigh(pair, scores, top, values_t):
@@ -189,50 +198,86 @@
     own_ref[...] = mask_bias(offsets_ref, start + half, start + half, lambda key, query: key <= query)
     other_ref[...] = mask_bias(offsets_ref, start + half, start, lambda key, query: key > query)
     next_ref[...] = mask_bias(offsets_ref, start + rows, start + half, lambda key, query: key > query)
+    last_ref[...] = mask_bias(offsets_ref, start, start - half, lambda key, query: key > query)
     for copy in rest:
         copy.wait()
 
 
-def late_kernel(
-    q_ref, k_ref, v_ref, own_bias, other_bias, early_ref, both_ref, own, other
-):
+def window_pairs(pairs, q_ref, blocks, biases, shares, emit):
     half = q_ref.shape[0]
+    before_bias, own_bias = biases
+    before, own = shares
     key = lax.broadcasted_iota(jnp.int32, own.shape, 0)
     query = lax.broadcasted_iota(jnp.int32, own.shape, 1) % half
     own[...] = jnp.where(key <= query, 1.0, 0.0).astype(jnp.bfloat16)
-    other[...] = jnp.where(key <= query, 0.0, 1.0).astype(jnp.bfloat16)
+    before[...] = jnp.where(key <= query, 0.0, 1.0).astype(jnp.bfloat16)
     pooling = pool_matrix(half)
-    molecules = half // POOL
-    features = early_ref.shape[0]
-    both_ref[pl.ds(0, features), :] = early_ref[...]
-    pairs = k_ref.shape[1] // LANES
     parts = []
 
     def score(pair):
-        scores = dot_nt(k_ref[:, at(pair)], split_heads(q_ref[:, at(pair)]))
-        return scores, with_ones(jnp.transpose(v_ref[:, at(pair)]))
+        keys, values = blocks(pair)
+        return dot_nt(keys, split_heads(q_ref[:, at(pair)])), with_ones(jnp.transpose(values))
 
     def top(pair, scores, values_t):
-        scores = jnp.maximum(scores[:half] + other_bias[...], scores[half:] + own_bias[...])
+        scores = jnp.maximum(scores[:half] + before_bias[...], scores[half:] + own_bias[...])
         return scores, tops(scores), values_t
 
     def weigh(pair, scores, top, values_t):
         weights = jnp.exp(scores - top).astype(jnp.bfloat16)
-        weights = jnp.concatenate([weights * other[...], weights * own[...]], axis=0)
+        weights = jnp.concatenate([weights * before[...], weights * own[...]], axis=0)
         return (dot_nn(values_t, weights),)
 
     def finish(pair, mixed):
         inverse = 1.0 / mixed[LANES : LANES + 1]
         parts.append(own_heads(mixed, inverse).astype(jnp.bfloat16))
         if len(parts) == 4:
-            pooled = dot_nt(pooling, jnp.concatenate(parts, axis=0)).astype(jnp.bfloat16)
-            for i in range(4):
-                place = features + (pair - 3 + i) * molecules
-                both_ref[pl.ds(place, molecules), :] = pooled[:, i * LANES : (i + 1) * LANES]
+            emit(pair, dot_nt(pooling, jnp.concatenate(parts, axis=0)).astype(jnp.bfloat16))
             parts.clear()
         return ()
 
     over_pairs(pairs, (score, top, weigh, finish), LAGS, lambda pair: None)
+
+
+def late_kernel(q_ref, k_ref, v_ref, own_bias, other_bias, early_ref, both_ref, own, other):
+    half = q_ref.shape[0]
+    molecules = half // POOL
+    features = early_ref.shape[0]
+    both_ref[pl.ds(0, features), :] = early_ref[...]
+
+    def emit(pair, pooled):
+        for i in range(4):
+            place = features + (pair - 3 + i) * molecules
+            both_ref[pl.ds(place, molecules), :] = pooled[:, i * LANES : (i + 1) * LANES]
+
+    window_pairs(
+        q_ref.shape[1] // LANES,
+        q_ref,
+        lambda pair: (k_ref[:, at(pair)], v_ref[:, at(pair)]),
+        (other_bias, own_bias),
+        (other, own),
+        emit,
+    )
+
+
+def kept_kernel(
+    q_ref, k_ref, v_ref, arrived_ref, first_bias, last_bias, after_ref, out_ref, own, other
+):
+    half = q_ref.shape[0]
+    head, tail = pl.ds(0, half), pl.ds(half, half)
+    begin = k_ref.shape[1] - q_ref.shape[1]
+
+    def blocks(pair):
+        columns = pl.ds(begin + pair * LANES, LANES)
+        return (
+            jnp.concatenate([arrived_ref[head, at(pair)], k_ref[head, columns]], axis=0),
+            jnp.concatenate([arrived_ref[tail, at(pair)], v_ref[head, columns]], axis=0),
+        )
+
+    def emit(pair, pooled):
+        out_ref[:, pl.ds((pair - 3) * LANES, 4 * LANES)] = pooled
+
+    pairs = q_ref.shape[1] // LANES
+    window_pairs(pairs, q_ref, blocks, (last_bias, first_bias), (other, own), emit)
 
 
 def halo_kernel(q_ref, k_ref, v_ref, bias, after_ref, out_ref):
@@ -240,7 +285,7 @@
     molecules = half // POOL
     tail = pl.ds(half, half)
     pooling = pool_matrix(half)
-    pairs = k_ref.shape[1] // LANES
+    pairs = q_ref.shape[1] // LANES
     parts = []
 
     def score(pair):
@@ -307,7 +352,7 @@
 
 
 def project_kernel(
-    both_ref, halo_ref, gain_ref, weight_ref, term_ref, other_ref, upstream_hbm,
+    both_ref, halo_ref, kept_ref, gain_ref, weight_ref, term_ref, other_ref, upstream_hbm,
     out_ref, update_ref, passed_hbm, pooled, sem,
 ):
     passing = load(upstream_hbm, passed_hbm, sem)
@@ -317,13 +362,16 @@
     pooling = pool_matrix(half)
     first = lax.axis_index("seq") == 0
     parts = []
+    width = halo_ref.shape[1]
     for pair in range(features // LANES):
+        place = pl.ds(width + pair * molecules, molecules)
+        pooled[pl.ds(molecules, molecules), at(pair)] = both_ref[place, :]
+        if pair * LANES >= width:
+            continue
         shares = halo_ref[molecules:, at(pair)].astype(jnp.float32)
         share_a = jnp.where(first, 1.0, shares[0:1] + shares[1:2])
         share_b = jnp.where(first, 1.0, shares[2:3] + shares[3:4])
         early = both_ref[at(pair), :].astype(jnp.float32)
-        place = pl.ds(features + pair * molecules, molecules)
-        pooled[pl.ds(molecules, molecules), at(pair)] = both_ref[place, :]
         parts += [early[:HEAD_DIM] * share_a, early[HEAD_DIM:] * share_b]
         if len(parts) == 8:
             columns = pl.ds((pair - 3) * LANES, 4 * LANES)
@@ -331,6 +379,7 @@
             arrived = halo_ref[:molecules, columns].astype(jnp.float32)
             pooled[pl.ds(0, molecules), columns] = (mean + arrived).astype(jnp.bfloat16)
             parts = []
+    pooled[pl.ds(0, molecules), pl.ds(width, features - width)] = kept_ref[...]
     arrived = pooled[...].astype(jnp.float32)
     mean = jnp.sum(arrived * arrived, axis=1, keepdims=True) / features
     normed = (arrived * lax.rsqrt(mean + EPS_NORM) * gain_ref[...]).astype(jnp.bfloat16)
@@ -359,36 +408,39 @@
     return pltpu.CompilerParams(vmem_limit_bytes=24 * 2**20)
 
 
-def attend_early(queries, keys, values, offsets, cotangent, stashed, chunks):
+def attend_early(queries, keys, values, offsets, cotangent, stashed, kept):
     rows, width = queries.shape
-    half = rows // 2
-    masks = [jax.ShapeDtypeStruct((half, 2 * half), jnp.float32)] * 3
+    half, back = rows // 2, width - kept
+    chunks = back // (4 * LANES)
+    bf16 = lambda *shape: jax.ShapeDtypeStruct(shape, jnp.bfloat16)
     return pl.pallas_call(
         functools.partial(early_kernel, rows, chunks),
         in_specs=[HBM] * 6,
-        out_specs=[VMEM] * 10,
+        out_specs=[VMEM] * 14,
         out_shape=[
-            jax.ShapeDtypeStruct((half + EXTRA, width), jnp.bfloat16),
-            jax.ShapeDtypeStruct((width, half), jnp.bfloat16),
-            jax.ShapeDtypeStruct((half, width), jnp.bfloat16),
-            jax.ShapeDtypeStruct((rows, width), jnp.bfloat16),
-            jax.ShapeDtypeStruct((rows, width), jnp.bfloat16),
+            bf16(half + EXTRA, back),
+            bf16(back, half),
+            bf16(half, kept),
+            bf16(half, width),
+            bf16(rows, width),
+            bf16(rows, width),
+            bf16(rows, kept),
         ]
-        + masks
-        + [
-            jax.ShapeDtypeStruct(cotangent.shape, cotangent.dtype),
-            jax.ShapeDtypeStruct(stashed.shape, stashed.dtype),
-        ],
+        + [jax.ShapeDtypeStruct((half, 2 * half), jnp.float32)] * 5
+        + [bf16(*cotangent.shape), bf16(*stashed.shape)],
         scratch_shapes=[
             pltpu.SMEM(offsets.shape, jnp.int32),
-            pltpu.VMEM((half, 2 * half), jnp.float32),
             pltpu.SemaphoreType.DMA((3, chunks)),
-            pltpu.SemaphoreType.DMA((6,)),
+            pltpu.SemaphoreType.DMA((11,)),
         ],
-        cost_estimate=cost(4 * half * half * width, 6 * rows * width, half * half * width // 64),
+        cost_estimate=cost(4 * half * half * back, 6 * rows * width, half * half * back // 64),
         compiler_params=params(),
         name="attend_early",
     )(*in_hbm(offsets, queries, keys, values, cotangent, stashed))
+
+
+def share_masks(half):
+    return [pltpu.VMEM((half, 2 * half), jnp.bfloat16)] * 2
 
 
 def attend_late(queries, keys, values, own_bias, other_bias, early):
@@ -397,19 +449,30 @@
         late_kernel,
         in_specs=[VMEM] * 6,
         out_specs=VMEM,
-        out_shape=jax.ShapeDtypeStruct((width + width // POOL, half), jnp.bfloat16),
-        scratch_shapes=[
-            pltpu.VMEM((half, 2 * half), jnp.bfloat16),
-            pltpu.VMEM((half, 2 * half), jnp.bfloat16),
-        ],
+        out_shape=jax.ShapeDtypeStruct((early.shape[0] + width // POOL, half), jnp.bfloat16),
+        scratch_shapes=share_masks(half),
         cost_estimate=cost(8 * half * half * width, 10 * half * width, half * half * width // 64),
         compiler_params=params(),
         name="attend_late",
     )(queries, keys, values, own_bias, other_bias, early)
 
 
+def attend_kept(queries, keys, values, arrived, first_bias, last_bias, after):
+    half, width = queries.shape
+    return pl.pallas_call(
+        kept_kernel,
+        in_specs=[VMEM] * 6 + [ANY],
+        out_specs=VMEM,
+        out_shape=jax.ShapeDtypeStruct((half // POOL, width), jnp.bfloat16),
+        scratch_shapes=share_masks(half),
+        cost_estimate=cost(8 * half * half * width, 10 * half * width, half * half * width // 64),
+        compiler_params=params(),
+        name="attend_kept",
+    )(queries, keys, values, arrived, first_bias, last_bias, after)
+
+
 def attend_halo(sent, keys, values, bias, after):
-    half, width = bias.shape[0], keys.shape[1]
+    half, width = bias.shape[0], sent.shape[1]
     return pl.pallas_call(
         halo_kernel,
         in_specs=[VMEM] * 4 + [ANY],
@@ -442,12 +505,12 @@
     )(slot, cotangent, weight, gain, stashed, after)
 
 
-def project(both, halo, gain, weight, term, other, upstream):
+def project(both, halo, kept, gain, weight, term, other, upstream):
     rows = upstream.shape[0]
     width, depth = weight.shape
     return pl.pallas_call(
         project_kernel,
-        in_specs=[VMEM] * 6 + [ANY],
+        in_specs=[VMEM] * 7 + [ANY],
         out_specs=[VMEM, VMEM, HBM],
         out_shape=[
             jax.ShapeDtypeStruct((rows, depth), jnp.bfloat16),
@@ -458,7 +521,7 @@
         cost_estimate=cost(2 * rows * width * depth, 2 * width * depth),
         compiler_params=params(),
         name="project",
-    )(both, halo, gain, weight, term, other, upstream)
+    )(both, halo, kept, gain, weight, term, other, upstream)
 
 
 def swapped(value, axis, distance):
@@ -492,10 +555,13 @@
     def partner(term, index):
         return swapped(term, *rounds[index]) if rounds else jnp.zeros_like(term)
 
-    sent, early, q_late, keys, values, own_bias, other_bias, next_bias, cotangent, stashed = (
-        attend_early(queries, keys, values, offsets, cotangent[0, 0], stashed[0, 0], 4)
+    kept = queries.shape[1] // LANES // 4 * LANES
+    sent, early, q_own, q_late, keys, values, forward, *rest = attend_early(
+        queries, keys, values, offsets, cotangent[0, 0], stashed[0, 0], kept
     )
+    first_bias, own_bias, other_bias, next_bias, last_bias, cotangent, stashed = rest
     arrived = shifted(sent, "seq", -1)
+    forward = shifted(forward, "seq", 1)
     both = attend_late(q_late, keys, values, own_bias, other_bias, early)
     slot = jnp.broadcast_to(slot, (1, LANES))
     dinput, term = backward(slot, cotangent, weight[0], gain, stashed, both)
@@ -503,10 +569,13 @@
     upstream = passed_along(dinput, "section", -1)
     term = term if rounds else lax.psum(term, ("rep", "seq"))
     term = term + partner(term, 0)
-    halo = onward(attend_halo(arrived, keys, values, next_bias, term))
+    halo = attend_halo(arrived, keys, values, next_bias, term)
+    own = attend_kept(q_own, keys, values, forward, first_bias, last_bias, halo)
+    halo = onward(halo)
+    own = passed_along(own, "section", 1)
     term = term + partner(term, 1)
     mol_keys, update, upstream = project(
-        both, halo, gain, weight[0], term, partner(term, 2), upstream
+        both, halo, own, gain, weight[0], term, partner(term, 2), upstream
     )
     return mol_keys[None, None], upstream[None, None], update
 

time: 36.9 us -> 38 us (1.030)
  the two profiles are of different devices: /device:TPU:26 before, /device:TPU:0 now
where the time goes in v8:
time: 38 us; the launch traced here: 37.8 us
  starting transfers between devices  19.6 us (52%)
  Pallas kernels  10.7 us (28%)
  waiting for transfers between devices  6.11 us (16%)
  between operations  1.41 us (4%)
    ppermute x3, starting transfers between devices, passed_along(): lax.ppermute(value, axis, [(i, (i + steps) % count) for i in range(count)])  6.44 us
    ppermute x3, waiting for transfers between devices, swapped(): lax.ppermute(value, axis, [(i, i ^ distance) for i in range(lax.axis_size...  6.09 us
    ppermute x2, starting transfers between devices, shifted(): lax.ppermute(value, axis, [(i, i + steps) for i in range(first, last)])  5.84 us
    ppermute x1, starting transfers between devices, onward(): return lax.ppermute(value, ('section', 'seq'), route)  3.95 us
    ppermute x3, starting transfers between devices, swapped(): lax.ppermute(value, axis, [(i, i ^ distance) for i in range(lax.axis_size...  3.34 us
    pallas_call x1, Pallas kernels, attend_early(): pl.pallas_call(functools.partial(early_kernel, rows, chunks), in_specs=[H...  3.16 us
    pallas_call x1, Pallas kernels, attend_late(): pl.pallas_call(late_kernel, in_specs=[VMEM] * 6, out_specs=VMEM, out_shap...  1.89 us
    pallas_call x1, Pallas kernels, project(): pl.pallas_call(project_kernel, in_specs=[VMEM] * 7 + [ANY], out_specs=[VM...  1.85 us
  transfers between devices with their start and end apart: 9, of which 3 were waited for; matrix products, arithmetic and copies ran while one was open for 0% of the time, Pallas kernels for 15%

profile of v8, /device:TPU:0, one launch (start us, length us, event | category | flops | bytes accessed | tf_op | source)
XLA Modules:
  0.0 37.8 jit_solution(9125313096213071647)
XLA Ops:
  0.6 0.0 copy-start
  0.6 0.0 copy-start.1
  0.7 3.2 %attend_early.1 = (bf16[136,1536]{1,0:T(8,128)(2,1)S(1)}, bf16[1536,128]{1,0:T(8,128)(2,1)S(1)}, bf16[128,512]{1,0:T(8,128)(2,1)S(1)}, bf16[128,2048]{1,0:T(8,12...) custom-call(s32[1,8]{1,0:T(1,128)} %bitcast.18, ...), custom_call_target="tpu_custom_call" | custom-call | flops 100663296 | bytes 3145728 | tf_op jit(solution)/shard_map/attend_early/pallas_call | solution.py:416
  3.8 1.3 %collective-permute-start.1 = (bf16[136,1536]{1,0:T(8,128)(2,1)S(1)}, bf16[136,1536]{1,0:T(8,128)(2,1)S(1)}, u32[]{:S(2)}, u32[]{:S(2)}) collective-permute-start(bf16[136,1536]{1,0:T(8,128)(2,1)S(1)} %get-tuple-element.28), channel_id=1, source_target_pairs={{2,0},{4,2},{6,4},{3,1},{5,3},{7,5},{10,8},{12,10},{14,12},{11,9},... | collective-permute-start | bytes 1253384 | tf_op jit(solution)/shard_map/ppermute | solution.py:35
  5.1 1.9 %attend_late.1.after_ref = bf16[2048,128]{1,0:T(8,128)(2,1)S(1)} custom-call(bf16[128,2048]{1,0:T(8,128)(2,1)S(1)} %get-tuple-element.22.q_ref, bf16[256,2048]{1,0:T(8,128)(2,1)S(1)} %get-tuple-element.23.k_ref, bf16[256,2048]{1,0:T(8,128)(2,1)S(1)} %get-tuple-element.24.v_ref, f32[128,256]{1,0:T(8,128)S(1)} %get-tuple-element.25.own_bias, ...), custom_call_target="tpu_custom_call" | custom-call | flops 268435456 | bytes 2621440 | tf_op jit(solution)/shard_map/attend_late/pallas_call | solution.py:448
  7.0 3.0 %collective-permute-start = (bf16[2048,128]{1,0:T(8,128)(2,1)S(1)}, bf16[2048,128]{1,0:T(8,128)(2,1)S(1)}, u32[]{:S(2)}, u32[]{:S(2)}) collective-permute-start(bf16[2048,128]{1,0:T(8,128)(2,1)S(1)} %attend_late.1.after_ref), channel_id=1, source_target_pairs={{0,8},{8,16},{16,24},{24,0},{1,9},{9,17},{17,25},{25,1},{2,10},{10... | collective-permute-start | bytes 1572872 | tf_op jit(solution)/shard_map/ppermute | solution.py:40
  10.0 4.5 %collective-permute-start.4 = (bf16[256,512]{1,0:T(8,128)(2,1)S(1)}, bf16[256,512]{1,0:T(8,128)(2,1)S(1)}, u32[]{:S(2)}, u32[]{:S(2)}) collective-permute-start(bf16[256,512]{1,0:T(8,128)(2,1)S(1)} %get-tuple-element.34), channel_id=1, source_target_pairs={{0,2},{2,4},{4,6},{1,3},{3,5},{5,7},{8,10},{10,12},{12,14},{9,11},... | collective-permute-start | bytes 786440 | tf_op jit(solution)/shard_map/ppermute | solution.py:35
  15.2 0.0 copy-done
  15.2 0.0 copy-done.1
  15.2 1.6 %backward.1 = (bf16[64,2048]{1,0:T(8,128)(2,1)S(1)}, f32[1,2048]{1,0:T(1,128)S(1)}) custom-call(s32[1,128]{1,0:T(1,128)S(1)} %broadcast_in_dim.14.slot_ref, bf16[64,1024]{1,0:T(8,128)(2,1)S(1)} %get-tuple-element.30.cotangent_ref, bf16[2048,1024]{1,0:T(8,128)(2,1)S(1)} %bitcast.11, f32[1,2048]{1,0:T(1,128)S(1)} %copy-done.1, ...), custom_call_target="tpu_custom_call" | custom-call | flops 268435456 | bytes 4194304 | tf_op jit(solution)/shard_map/backward/pallas_call | solution.py:490
  16.8 1.1 %collective-permute-start.8 = (bf16[64,2048]{1,0:T(8,128)(2,1)S(1)}, bf16[64,2048]{1,0:T(8,128)(2,1)S(1)}, u32[]{:S(2)}, u32[]{:S(2)}) collective-permute-start(bf16[64,2048]{1,0:T(8,128)(2,1)S(1)} %get-tuple-element.37), channel_id=1, source_target_pairs={{0,24},{8,0},{16,8},{24,16},{1,25},{9,1},{17,9},{25,17},{2,26},{10... | collective-permute-start | bytes 786440 | tf_op jit(solution)/shard_map/ppermute | solution.py:40
  17.8 2.0 %collective-permute-start.2 = (f32[1,2048]{1,0:T(1,128)S(1)}, f32[1,2048]{1,0:T(1,128)S(1)}, u32[]{:S(2)}, u32[]{:S(2)}) collective-permute-start(f32[1,2048]{1,0:T(1,128)S(1)} %get-tuple-element.32), channel_id=1, source_target_pairs={{0,2},{2,0},{4,6},{6,4},{1,3},{3,1},{5,7},{7,5},{8,10},{10,8},{12,... | collective-permute-start | bytes 24584 | tf_op jit(solution)/shard_map/ppermute | solution.py:528
  19.8 1.7 %collective-permute-done.2 = f32[1,2048]{1,0:T(1,128)S(1)} collective-permute-done((f32[1,2048]{1,0:T(1,128)S(1)}, f32[1,2048]{1,0:T(1,128)S(1)}, u32[]{:S(2)}, u32[]{:S(2)}) %collective-permute-start.2) | collective-permute-done | bytes 8224 | tf_op jit(solution)/shard_map/ppermute | solution.py:528
  21.5 0.0 collective-permute-done.1.q_ref
  21.5 1.5 %attend_halo.1.after_ref = bf16[40,1536]{1,0:T(8,128)(2,1)S(1)} custom-call(bf16[136,1536]{1,0:T(8,128)(2,1)S(1)} %collective-permute-done.1.q_ref, bf16[256,2048]{1,0:T(8,128)(2,1)S(1)} %get-tuple-element.23.k_ref, bf16[256,2048]{1,0:T(8,128)(2,1)S(1)} %get-tuple-element.24.v_ref, f32[128,256]{1,0:T(8,128)S(1)} %get-tuple-element.29.bias, ...), custom_call_target="tpu_custom_call" | custom-call | flops 100663296 | bytes 1179648 | tf_op jit(solution)/shard_map/attend_halo/pallas_call | solution.py:476
  23.0 4.0 %collective-permute-start.3 = (bf16[40,1536]{1,0:T(8,128)(2,1)S(1)}, bf16[40,1536]{1,0:T(8,128)(2,1)S(1)}, u32[]{:S(2)}, u32[]{:S(2)}) collective-permute-start(bf16[40,1536]{1,0:T(8,128)(2,1)S(1)} %attend_halo.1.after_ref), channel_id=1, source_target_pairs={{0,10},{2,12},{4,14},{8,18},{10,20},{12,22},{16,26},{18,28},{20,30... | collective-permute-start | bytes 368648 | tf_op jit(solution)/shard_map/ppermute | solution.py:548
  27.0 0.0 collective-permute-done.4.arrived_ref
  27.0 0.7 %attend_kept.1 = bf16[32,512]{1,0:T(8,128)(2,1)S(1)} custom-call(bf16[128,512]{1,0:T(8,128)(2,1)S(1)} %get-tuple-element.33.q_ref, bf16[256,2048]{1,0:T(8,128)(2,1)S(1)} %get-tuple-element.23.k_ref, bf16[256,2048]{1,0:T(8,128)(2,1)S(1)} %get-tuple-element.24.v_ref, bf16[256,512]{1,0:T(8,128)(2,1)S(1)} %collective-permute-done.4.arrived_ref, ...), custom_call_target="tpu_custom_call" | custom-call | flops 67108864 | bytes 655360 | tf_op jit(solution)/shard_map/attend_kept/pallas_call | solution.py:462
  27.7 2.4 %collective-permute-start.5 = (bf16[32,512]{1,0:T(8,128)(2,1)S(1)}, bf16[32,512]{1,0:T(8,128)(2,1)S(1)}, u32[]{:S(2)}, u32[]{:S(2)}) collective-permute-start(bf16[32,512]{1,0:T(8,128)(2,1)S(1)} %attend_kept.1), channel_id=1, source_target_pairs={{0,8},{8,16},{16,24},{24,0},{1,9},{9,17},{17,25},{25,1},{2,10},{10... | collective-permute-start | bytes 98312 | tf_op jit(solution)/shard_map/ppermute | solution.py:40
  30.1 1.3 %collective-permute-start.6 = (f32[1,2048]{1,0:T(1,128)S(1)}, f32[1,2048]{1,0:T(1,128)S(1)}, u32[]{:S(2)}, u32[]{:S(2)}) collective-permute-start(f32[1,2048]{1,0:T(1,128)S(1)} %add.6.after_ref), channel_id=1, source_target_pairs={{0,4},{2,6},{4,0},{6,2},{1,5},{3,7},{5,1},{7,3},{8,12},{10,14},{12... | collective-permute-start | bytes 24584 | tf_op jit(solution)/shard_map/ppermute | solution.py:528
  31.4 3.3 %collective-permute-done.6 = f32[1,2048]{1,0:T(1,128)S(1)} collective-permute-done((f32[1,2048]{1,0:T(1,128)S(1)}, f32[1,2048]{1,0:T(1,128)S(1)}, u32[]{:S(2)}, u32[]{:S(2)}) %collective-permute-start.6) | collective-permute-done | bytes 8224 | tf_op jit(solution)/shard_map/ppermute | solution.py:528
  34.7 0.1 collective-permute-start.7
  34.8 1.2 %collective-permute-done.7.other_ref = f32[1,2048]{1,0:T(1,128)S(1)} collective-permute-done((f32[1,2048]{1,0:T(1,128)S(1)}, f32[1,2048]{1,0:T(1,128)S(1)}, u32[]{:S(2)}, u32[]{:S(2)}) %collective-permute-start.7) | collective-permute-done | bytes 8224 | tf_op jit(solution)/shard_map/ppermute | solution.py:528
  35.9 0.0 collective-permute-done.8.upstream_hbm
  35.9 0.0 collective-permute-done.5.kept_ref
  35.9 0.0 collective-permute-done.both_ref
  36.0 0.0 collective-permute-done.3.halo_ref
  36.0 1.9 %project.1 = (bf16[64,1024]{1,0:T(8,128)(2,1)}, f32[1,2048]{1,0:T(1,128)}, bf16[64,2048]{1,0:T(8,128)(2,1)}) custom-call(bf16[2048,128]{1,0:T(8,128)(2,1)S(1)} %collective-permute-done.both_ref, bf16[40,1536]{1,0:T(8,128)(2,1)S(1)} %collective-permute-done.3.halo_ref, bf16[32,512]{1,0:T(8,128)(2,1)S(1)} %collective-permute-done.5.kept_ref, ...), custom_call_target="tpu_custom_call" | custom-call | flops 268435456 | bytes 4194304 | tf_op jit(solution)/shard_map/project/pallas_call | solution.py:511
  (3 shorter events, 0.0 us)
Async XLA Ops:
  0.6 14.6 %copy-start = (bf16[1,2048,1024]{2,1,0:T(8,128)(2,1)S(1)}, bf16[1,2048,1024]{2,1,0:T(8,128)(2,1)}, u32[]{:S(2)}) copy-start(bf16[1,2048,1024]{2,1,0:T(8,128)(2,1)} %param.13) | copy-start | bytes 12582916
  0.6 14.6 %copy-start.1 = (f32[1,2048]{1,0:T(1,128)S(1)}, f32[1,2048]{1,0:T(1,128)}, u32[]{:S(2)}) copy-start(f32[1,2048]{1,0:T(1,128)} %gain_ref.3) | copy-start | bytes 24580
  3.8 17.7 %collective-permute-start.1 = (bf16[136,1536]{1,0:T(8,128)(2,1)S(1)}, bf16[136,1536]{1,0:T(8,128)(2,1)S(1)}, u32[]{:S(2)}, u32[]{:S(2)}) collective-permute-start(bf16[136,1536]{1,0:T(8,128)(2,1)S(1)} %get-tuple-element.28), channel_id=1, source_target_pairs={{2,0},{4,2},{6,4},{3,1},{5,3},{7,5},{10,8},{12,10},{14,12},{11,9},... | collective-permute-start | bytes 1253384 | tf_op jit(solution)/shard_map/ppermute | solution.py:35
  7.0 28.9 %collective-permute-start = (bf16[2048,128]{1,0:T(8,128)(2,1)S(1)}, bf16[2048,128]{1,0:T(8,128)(2,1)S(1)}, u32[]{:S(2)}, u32[]{:S(2)}) collective-permute-start(bf16[2048,128]{1,0:T(8,128)(2,1)S(1)} %attend_late.1.after_ref), channel_id=1, source_target_pairs={{0,8},{8,16},{16,24},{24,0},{1,9},{9,17},{17,25},{25,1},{2,10},{10... | collective-permute-start | bytes 1572872 | tf_op jit(solution)/shard_map/ppermute | solution.py:40
  10.0 17.0 %collective-permute-start.4 = (bf16[256,512]{1,0:T(8,128)(2,1)S(1)}, bf16[256,512]{1,0:T(8,128)(2,1)S(1)}, u32[]{:S(2)}, u32[]{:S(2)}) collective-permute-start(bf16[256,512]{1,0:T(8,128)(2,1)S(1)} %get-tuple-element.34), channel_id=1, source_target_pairs={{0,2},{2,4},{4,6},{1,3},{3,5},{5,7},{8,10},{10,12},{12,14},{9,11},... | collective-permute-start | bytes 786440 | tf_op jit(solution)/shard_map/ppermute | solution.py:35
  16.8 19.2 %collective-permute-start.8 = (bf16[64,2048]{1,0:T(8,128)(2,1)S(1)}, bf16[64,2048]{1,0:T(8,128)(2,1)S(1)}, u32[]{:S(2)}, u32[]{:S(2)}) collective-permute-start(bf16[64,2048]{1,0:T(8,128)(2,1)S(1)} %get-tuple-element.37), channel_id=1, source_target_pairs={{0,24},{8,0},{16,8},{24,16},{1,25},{9,1},{17,9},{25,17},{2,26},{10... | collective-permute-start | bytes 786440 | tf_op jit(solution)/shard_map/ppermute | solution.py:40
  17.8 3.7 %collective-permute-start.2 = (f32[1,2048]{1,0:T(1,128)S(1)}, f32[1,2048]{1,0:T(1,128)S(1)}, u32[]{:S(2)}, u32[]{:S(2)}) collective-permute-start(f32[1,2048]{1,0:T(1,128)S(1)} %get-tuple-element.32), channel_id=1, source_target_pairs={{0,2},{2,0},{4,6},{6,4},{1,3},{3,1},{5,7},{7,5},{8,10},{10,8},{12,... | collective-permute-start | bytes 24584 | tf_op jit(solution)/shard_map/ppermute | solution.py:528
  23.0 12.9 %collective-permute-start.3 = (bf16[40,1536]{1,0:T(8,128)(2,1)S(1)}, bf16[40,1536]{1,0:T(8,128)(2,1)S(1)}, u32[]{:S(2)}, u32[]{:S(2)}) collective-permute-start(bf16[40,1536]{1,0:T(8,128)(2,1)S(1)} %attend_halo.1.after_ref), channel_id=1, source_target_pairs={{0,10},{2,12},{4,14},{8,18},{10,20},{12,22},{16,26},{18,28},{20,30... | collective-permute-start | bytes 368648 | tf_op jit(solution)/shard_map/ppermute | solution.py:548
  27.7 8.2 %collective-permute-start.5 = (bf16[32,512]{1,0:T(8,128)(2,1)S(1)}, bf16[32,512]{1,0:T(8,128)(2,1)S(1)}, u32[]{:S(2)}, u32[]{:S(2)}) collective-permute-start(bf16[32,512]{1,0:T(8,128)(2,1)S(1)} %attend_kept.1), channel_id=1, source_target_pairs={{0,8},{8,16},{16,24},{24,0},{1,9},{9,17},{17,25},{25,1},{2,10},{10... | collective-permute-start | bytes 98312 | tf_op jit(solution)/shard_map/ppermute | solution.py:40
  30.1 4.5 %collective-permute-start.6 = (f32[1,2048]{1,0:T(1,128)S(1)}, f32[1,2048]{1,0:T(1,128)S(1)}, u32[]{:S(2)}, u32[]{:S(2)}) collective-permute-start(f32[1,2048]{1,0:T(1,128)S(1)} %add.6.after_ref), channel_id=1, source_target_pairs={{0,4},{2,6},{4,0},{6,2},{1,5},{3,7},{5,1},{7,3},{8,12},{10,14},{12... | collective-permute-start | bytes 24584 | tf_op jit(solution)/shard_map/ppermute | solution.py:528
  34.7 1.2 %collective-permute-start.7 = (f32[1,2048]{1,0:T(1,128)S(1)}, f32[1,2048]{1,0:T(1,128)S(1)}, u32[]{:S(2)}, u32[]{:S(2)}) collective-permute-start(f32[1,2048]{1,0:T(1,128)S(1)} %add.7.term_ref), channel_id=1, source_target_pairs={{0,1},{1,0},{2,3},{3,2},{4,5},{5,4},{6,7},{7,6},{8,9},{9,8},{10,11... | collective-permute-start | bytes 24584 | tf_op jit(solution)/shard_map/ppermute | solution.py:528

commit v9 on v7

--- a/solution.py
+++ b/solution.py
@@ -134,7 +134,7 @@
 
 def early_kernel(
     rows, chunks, offsets_hbm, q_hbm, k_hbm, v_hbm, cotangent_hbm, stashed_hbm,
-    sent_ref, early_ref, q_late_ref, k_ref, v_ref, own_ref, other_ref, next_ref, cotangent_ref, stashed_ref,
+    sent_ref, early_ref, more_ref, q_late_ref, k_ref, v_ref, own_ref, other_ref, next_ref, cotangent_ref, stashed_ref,
     offsets_ref, bias, sems, offsets_sem,
 ):
     half = rows // 2
@@ -155,6 +155,7 @@
     ]
     start = lax.axis_index("seq") * rows
     pairs = k_ref.shape[1] // LANES
+    split = early_ref.shape[0] // LANES
 
     def arrive(pair):
         per_chunk = pairs // chunks
@@ -178,7 +179,8 @@
 
     def finish(pair, top, mixed):
         total = mixed[LANES : LANES + 1]
-        early_ref[at(pair), :] = own_heads(mixed, 1.0 / total).astype(jnp.bfloat16)
+        target, place = (early_ref, pair) if pair < split else (more_ref, pair - split)
+        target[at(place), :] = own_heads(mixed, 1.0 / total).astype(jnp.bfloat16)
         lse = top + jnp.log(total)
         terms = three_terms(lse[:, :half]) + three_terms(lse[:, half:])
         terms.append(jnp.zeros((EXTRA - 6, LANES), jnp.float32))
@@ -307,38 +309,47 @@
 
 
 def project_kernel(
-    both_ref, halo_ref, gain_ref, weight_ref, term_ref, other_ref, upstream_hbm,
-    out_ref, update_ref, passed_hbm, pooled, sem,
+    early_ref, both_ref, halo_ref, gain_ref, weight_ref, upstream_hbm, out_ref, passed_hbm, squares_ref, sem
 ):
     passing = load(upstream_hbm, passed_hbm, sem)
     half = both_ref.shape[1]
     features = gain_ref.shape[1]
+    first_part = early_ref.shape[0]
     molecules = half // POOL
     pooling = pool_matrix(half)
     first = lax.axis_index("seq") == 0
-    parts = []
+    squares, product, parts = 0.0, 0.0, []
     for pair in range(features // LANES):
         shares = halo_ref[molecules:, at(pair)].astype(jnp.float32)
         share_a = jnp.where(first, 1.0, shares[0:1] + shares[1:2])
         share_b = jnp.where(first, 1.0, shares[2:3] + shares[3:4])
-        early = both_ref[at(pair), :].astype(jnp.float32)
-        place = pl.ds(features + pair * molecules, molecules)
-        pooled[pl.ds(molecules, molecules), at(pair)] = both_ref[place, :]
+        begin = pair * LANES
+        if begin < first_part:
+            early = early_ref[pl.ds(begin, LANES), :].astype(jnp.float32)
+        else:
+            early = both_ref[pl.ds(begin - first_part, LANES), :].astype(jnp.float32)
         parts += [early[:HEAD_DIM] * share_a, early[HEAD_DIM:] * share_b]
         if len(parts) == 8:
             columns = pl.ds((pair - 3) * LANES, 4 * LANES)
             mean = dot_nt(pooling, jnp.concatenate(parts, axis=0).astype(jnp.bfloat16))
-            arrived = halo_ref[:molecules, columns].astype(jnp.float32)
-            pooled[pl.ds(0, molecules), columns] = (mean + arrived).astype(jnp.bfloat16)
+            upper = mean + halo_ref[:molecules, columns].astype(jnp.float32)
+            place = features - first_part + (pair - 3) * molecules
+            lower = [both_ref[pl.ds(place + i * molecules, molecules), :] for i in range(4)]
+            lower = jnp.concatenate(lower, axis=1)
+            arrived = jnp.concatenate([upper.astype(jnp.bfloat16), lower], axis=0).astype(jnp.float32)
+            squares += jnp.sum(arrived * arrived, axis=1, keepdims=True)
+            scaled = (arrived * gain_ref[:, columns]).astype(jnp.bfloat16)
+            product += dot_nn(scaled, weight_ref[columns, :])
             parts = []
-    arrived = pooled[...].astype(jnp.float32)
-    mean = jnp.sum(arrived * arrived, axis=1, keepdims=True) / features
-    normed = (arrived * lax.rsqrt(mean + EPS_NORM) * gain_ref[...]).astype(jnp.bfloat16)
-    out_ref[...] = dot_nn(normed, weight_ref[...]).astype(jnp.bfloat16)
+    squares_ref[...] = squares
+    out_ref[...] = (product * lax.rsqrt(squares / features + EPS_NORM)).astype(jnp.bfloat16)
+    passing.wait()
+
+
+def update_kernel(term_ref, other_ref, after_ref, update_ref):
     total = term_ref[...] + other_ref[...]
-    mean = jnp.sum(total * total, axis=1, keepdims=True) / features
+    mean = jnp.sum(total * total, axis=1, keepdims=True) / total.shape[1]
     update_ref[...] = total / jnp.sqrt(mean + EPS_STEP)
-    passing.wait()
 
 
 def cost(flops, read, exps=0):
@@ -362,14 +373,16 @@
 def attend_early(queries, keys, values, offsets, cotangent, stashed, chunks):
     rows, width = queries.shape
     half = rows // 2
+    soon = width // (4 * LANES) * 3 // 4 * 4 * LANES
     masks = [jax.ShapeDtypeStruct((half, 2 * half), jnp.float32)] * 3
     return pl.pallas_call(
         functools.partial(early_kernel, rows, chunks),
         in_specs=[HBM] * 6,
-        out_specs=[VMEM] * 10,
+        out_specs=[VMEM] * 11,
         out_shape=[
             jax.ShapeDtypeStruct((half + EXTRA, width), jnp.bfloat16),
-            jax.ShapeDtypeStruct((width, half), jnp.bfloat16),
+            jax.ShapeDtypeStruct((soon, half), jnp.bfloat16),
+            jax.ShapeDtypeStruct((width - soon, half), jnp.bfloat16),
             jax.ShapeDtypeStruct((half, width), jnp.bfloat16),
             jax.ShapeDtypeStruct((rows, width), jnp.bfloat16),
             jax.ShapeDtypeStruct((rows, width), jnp.bfloat16),
@@ -397,7 +410,7 @@
         late_kernel,
         in_specs=[VMEM] * 6,
         out_specs=VMEM,
-        out_shape=jax.ShapeDtypeStruct((width + width // POOL, half), jnp.bfloat16),
+        out_shape=jax.ShapeDtypeStruct((early.shape[0] + width // POOL, half), jnp.bfloat16),
         scratch_shapes=[
             pltpu.VMEM((half, 2 * half), jnp.bfloat16),
             pltpu.VMEM((half, 2 * half), jnp.bfloat16),
@@ -442,23 +455,34 @@
     )(slot, cotangent, weight, gain, stashed, after)
 
 
-def project(both, halo, gain, weight, term, other, upstream):
+def project(early, both, halo, gain, weight, upstream):
     rows = upstream.shape[0]
     width, depth = weight.shape
     return pl.pallas_call(
         project_kernel,
-        in_specs=[VMEM] * 6 + [ANY],
-        out_specs=[VMEM, VMEM, HBM],
+        in_specs=[VMEM] * 5 + [ANY],
+        out_specs=[VMEM, HBM, VMEM],
         out_shape=[
             jax.ShapeDtypeStruct((rows, depth), jnp.bfloat16),
-            jax.ShapeDtypeStruct((1, width), jnp.float32),
             jax.ShapeDtypeStruct(upstream.shape, upstream.dtype),
-        ],
-        scratch_shapes=[pltpu.VMEM((rows, width), jnp.bfloat16), pltpu.SemaphoreType.DMA],
+            jax.ShapeDtypeStruct((rows, 1), jnp.float32),
+        ],
+        scratch_shapes=[pltpu.SemaphoreType.DMA],
         cost_estimate=cost(2 * rows * width * depth, 2 * width * depth),
         compiler_params=params(),
         name="project",
-    )(both, halo, gain, weight, term, other, upstream)
+    )(early, both, halo, gain, weight, upstream)
+
+
+def updated(term, other, after):
+    return pl.pallas_call(
+        update_kernel,
+        in_specs=[VMEM] * 2 + [ANY],
+        out_specs=VMEM,
+        out_shape=jax.ShapeDtypeStruct(term.shape, term.dtype),
+        cost_estimate=cost(8 * term.size, 12 * term.size),
+        name="update",
+    )(term, other, after)
 
 
 def swapped(value, axis, distance):
@@ -467,7 +491,7 @@
 
 def sum_rounds():
     rounds = []
-    for axis in ("seq", "rep"):
+    for axis in ("rep", "seq"):
         count = lax.axis_size(axis)
         if count & (count - 1):
             return []
@@ -492,22 +516,23 @@
     def partner(term, index):
         return swapped(term, *rounds[index]) if rounds else jnp.zeros_like(term)
 
-    sent, early, q_late, keys, values, own_bias, other_bias, next_bias, cotangent, stashed = (
-        attend_early(queries, keys, values, offsets, cotangent[0, 0], stashed[0, 0], 4)
+    sent, early, more, q_late, keys, values, *rest = attend_early(
+        queries, keys, values, offsets, cotangent[0, 0], stashed[0, 0], 4
     )
+    own_bias, other_bias, next_bias, cotangent, stashed = rest
     arrived = shifted(sent, "seq", -1)
-    both = attend_late(q_late, keys, values, own_bias, other_bias, early)
+    early = passed_along(early, "section", 1)
+    both = attend_late(q_late, keys, values, own_bias, other_bias, more)
     slot = jnp.broadcast_to(slot, (1, LANES))
     dinput, term = backward(slot, cotangent, weight[0], gain, stashed, both)
     both = passed_along(both, "section", 1)
     upstream = passed_along(dinput, "section", -1)
     term = term if rounds else lax.psum(term, ("rep", "seq"))
     term = term + partner(term, 0)
+    term = term + partner(term, 1)
     halo = onward(attend_halo(arrived, keys, values, next_bias, term))
-    term = term + partner(term, 1)
-    mol_keys, update, upstream = project(
-        both, halo, gain, weight[0], term, partner(term, 2), upstream
-    )
+    mol_keys, upstream, squares = project(early, both, halo, gain, weight[0], upstream)
+    update = updated(term, partner(term, 2), squares)
     return mol_keys[None, None], upstream[None, None], update
 
 

time: 36.9 us -> 37.8 us (1.024)
  the two profiles are of different devices: /device:TPU:26 before, /device:TPU:24 now
where the time goes in v9:
time: 37.8 us; the launch traced here: 37.5 us
  starting transfers between devices  12.8 us (34%)
  Pallas kernels  12.1 us (32%)
  waiting for transfers between devices  9.97 us (26%)
  between operations  1.41 us (4%)
  local copies, waits for them, and re-layouts  1.2 us (3%)
    ppermute x3, waiting for transfers between devices, passed_along(): lax.ppermute(value, axis, [(i, (i + steps) % count) for i in range(count)])  5.57 us
    ppermute x3, starting transfers between devices, swapped(): lax.ppermute(value, axis, [(i, i ^ distance) for i in range(lax.axis_size...  5.47 us
    ppermute x3, waiting for transfers between devices, swapped(): lax.ppermute(value, axis, [(i, i ^ distance) for i in range(lax.axis_size...  4.4 us
    pallas_call x1, Pallas kernels, attend_early(): pl.pallas_call(functools.partial(early_kernel, rows, chunks), in_specs=[H...  3.63 us
    ppermute x3, starting transfers between devices, passed_along(): lax.ppermute(value, axis, [(i, (i + steps) % count) for i in range(count)])  3.62 us
    ppermute x1, starting transfers between devices, shifted(): lax.ppermute(value, axis, [(i, i + steps) for i in range(first, last)])  2.39 us
    pallas_call x1, Pallas kernels, project(): pl.pallas_call(project_kernel, in_specs=[VMEM] * 5 + [ANY], out_specs=[VM...  1.94 us
    pallas_call x1, Pallas kernels, attend_halo(): pl.pallas_call(halo_kernel, in_specs=[VMEM] * 4 + [ANY], out_specs=VMEM,...  1.8 us
  transfers between devices with their start and end apart: 8, of which 3 were waited for; matrix products, arithmetic and copies ran while one was open for 0% of the time, Pallas kernels for 19%

profile of v9, /device:TPU:24, one launch (start us, length us, event | category | flops | bytes accessed | tf_op | source)
XLA Modules:
  0.0 37.5 jit_solution(1216400400980910846)
XLA Ops:
  0.6 0.0 copy-start
  0.6 0.0 copy-start.2
  0.7 3.6 %attend_early.1 = (bf16[136,2048]{1,0:T(8,128)(2,1)S(1)}, bf16[1536,128]{1,0:T(8,128)(2,1)S(1)}, bf16[512,128]{1,0:T(8,128)(2,1)S(1)}, bf16[128,2048]{1,0:T(8,12...) custom-call(s32[1,8]{1,0:T(1,128)} %bitcast.18, ...), custom_call_target="tpu_custom_call" | custom-call | flops 134217728 | bytes 3145728 | tf_op jit(solution)/shard_map/attend_early/pallas_call | solution.py:378
  4.3 2.4 %collective-permute-start.2 = (bf16[136,2048]{1,0:T(8,128)(2,1)S(1)}, bf16[136,2048]{1,0:T(8,128)(2,1)S(1)}, u32[]{:S(2)}, u32[]{:S(2)}) collective-permute-start(bf16[136,2048]{1,0:T(8,128)(2,1)S(1)} %get-tuple-element.26), channel_id=1, source_target_pairs={{2,0},{4,2},{6,4},{3,1},{5,3},{7,5},{10,8},{12,10},{14,12},{11,9},... | collective-permute-start | bytes 1671176 | tf_op jit(solution)/shard_map/ppermute | solution.py:35
  6.7 1.5 %collective-permute-start = (bf16[1536,128]{1,0:T(8,128)(2,1)S(1)}, bf16[1536,128]{1,0:T(8,128)(2,1)S(1)}, u32[]{:S(2)}, u32[]{:S(2)}) collective-permute-start(bf16[1536,128]{1,0:T(8,128)(2,1)S(1)} %get-tuple-element.19), channel_id=1, source_target_pairs={{0,8},{8,16},{16,24},{24,0},{1,9},{9,17},{17,25},{25,1},{2,10},{10... | collective-permute-start | bytes 1179656 | tf_op jit(solution)/shard_map/ppermute | solution.py:40
  8.9 1.8 %attend_late.1.after_ref = bf16[1024,128]{1,0:T(8,128)(2,1)S(1)} custom-call(bf16[128,2048]{1,0:T(8,128)(2,1)S(1)} %get-tuple-element.20.q_ref, bf16[256,2048]{1,0:T(8,128)(2,1)S(1)} %get-tuple-element.21.k_ref, bf16[256,2048]{1,0:T(8,128)(2,1)S(1)} %get-tuple-element.22.v_ref, f32[128,256]{1,0:T(8,128)S(1)} %get-tuple-element.23.own_bias, ...), custom_call_target="tpu_custom_call" | custom-call | flops 268435456 | bytes 2621440 | tf_op jit(solution)/shard_map/attend_late/pallas_call | solution.py:409
  10.7 0.0 copy-done
  10.7 0.0 copy-done.2
  10.7 1.6 %backward.1 = (bf16[64,2048]{1,0:T(8,128)(2,1)S(1)}, f32[1,2048]{1,0:T(1,128)S(1)}) custom-call(s32[1,128]{1,0:T(1,128)S(1)} %broadcast_in_dim.14.slot_ref, bf16[64,1024]{1,0:T(8,128)(2,1)S(1)} %get-tuple-element.28.cotangent_ref, bf16[2048,1024]{1,0:T(8,128)(2,1)S(1)} %bitcast.11, f32[1,2048]{1,0:T(1,128)S(1)} %copy-done.2, ...), custom_call_target="tpu_custom_call" | custom-call | flops 268435456 | bytes 4194304 | tf_op jit(solution)/shard_map/backward/pallas_call | solution.py:440
  12.3 1.5 %collective-permute-start.6 = (bf16[64,2048]{1,0:T(8,128)(2,1)S(1)}, bf16[64,2048]{1,0:T(8,128)(2,1)S(1)}, u32[]{:S(2)}, u32[]{:S(2)}) collective-permute-start(bf16[64,2048]{1,0:T(8,128)(2,1)S(1)} %get-tuple-element.31), channel_id=1, source_target_pairs={{0,24},{8,0},{16,8},{24,16},{1,25},{9,1},{17,9},{25,17},{2,26},{10... | collective-permute-start | bytes 786440 | tf_op jit(solution)/shard_map/ppermute | solution.py:40
  13.8 0.6 %collective-permute-start.1 = (bf16[1024,128]{1,0:T(8,128)(2,1)S(1)}, bf16[1024,128]{1,0:T(8,128)(2,1)S(1)}, u32[]{:S(2)}, u32[]{:S(2)}) collective-permute-start(bf16[1024,128]{1,0:T(8,128)(2,1)S(1)} %attend_late.1.after_ref), channel_id=1, source_target_pairs={{0,8},{8,16},{16,24},{24,0},{1,9},{9,17},{17,25},{25,1},{2,10},{10... | collective-permute-start | bytes 786440 | tf_op jit(solution)/shard_map/ppermute | solution.py:40
  14.4 0.0 collective-permute-start.3
  14.4 1.2 %collective-permute-done.3 = f32[1,2048]{1,0:T(1,128)S(1)} collective-permute-done((f32[1,2048]{1,0:T(1,128)S(1)}, f32[1,2048]{1,0:T(1,128)S(1)}, u32[]{:S(2)}, u32[]{:S(2)}) %collective-permute-start.3) | collective-permute-done | bytes 8224 | tf_op jit(solution)/shard_map/ppermute | solution.py:489
  15.5 0.5 %collective-permute-start.4 = (f32[1,2048]{1,0:T(1,128)S(1)}, f32[1,2048]{1,0:T(1,128)S(1)}, u32[]{:S(2)}, u32[]{:S(2)}) collective-permute-start(f32[1,2048]{1,0:T(1,128)S(1)} %add.6), channel_id=1, source_target_pairs={{0,2},{2,0},{4,6},{6,4},{1,3},{3,1},{5,7},{7,5},{8,10},{10,8},{12,... | collective-permute-start | bytes 24584 | tf_op jit(solution)/shard_map/ppermute | solution.py:489
  16.0 3.2 %collective-permute-done.4 = f32[1,2048]{1,0:T(1,128)S(1)} collective-permute-done((f32[1,2048]{1,0:T(1,128)S(1)}, f32[1,2048]{1,0:T(1,128)S(1)}, u32[]{:S(2)}, u32[]{:S(2)}) %collective-permute-start.4) | collective-permute-done | bytes 8224 | tf_op jit(solution)/shard_map/ppermute | solution.py:489
  19.3 0.0 copy-start.1
  19.3 0.0 collective-permute-done.2.q_ref
  19.3 1.8 %attend_halo.1 = bf16[40,2048]{1,0:T(8,128)(2,1)S(1)} custom-call(bf16[136,2048]{1,0:T(8,128)(2,1)S(1)} %collective-permute-done.2.q_ref, bf16[256,2048]{1,0:T(8,128)(2,1)S(1)} %get-tuple-element.21.k_ref, bf16[256,2048]{1,0:T(8,128)(2,1)S(1)} %get-tuple-element.22.v_ref, f32[128,256]{1,0:T(8,128)S(1)} %get-tuple-element.27.bias, ...), custom_call_target="tpu_custom_call" | custom-call | flops 134217728 | bytes 1572864 | tf_op jit(solution)/shard_map/attend_halo/pallas_call | solution.py:426
  21.1 1.3 %collective-permute-start.5 = (bf16[40,2048]{1,0:T(8,128)(2,1)S(1)}, bf16[40,2048]{1,0:T(8,128)(2,1)S(1)}, u32[]{:S(2)}, u32[]{:S(2)}) collective-permute-start(bf16[40,2048]{1,0:T(8,128)(2,1)S(1)} %attend_halo.1), channel_id=1, source_target_pairs={{0,10},{2,12},{4,14},{8,18},{10,20},{12,22},{16,26},{18,28},{20,30... | collective-permute-start | bytes 491528 | tf_op jit(solution)/shard_map/ppermute | solution.py:509
  22.4 5.0 %collective-permute-start.7 = (f32[1,2048]{1,0:T(1,128)S(1)}, f32[1,2048]{1,0:T(1,128)S(1)}, u32[]{:S(2)}, u32[]{:S(2)}) collective-permute-start(f32[1,2048]{1,0:T(1,128)S(1)} %add.7.after_ref.term_ref), channel_id=1, source_target_pairs={{0,4},{2,6},{4,0},{6,2},{1,5},{3,7},{5,1},{7,3},{8,12},{10,14},{12... | collective-permute-start | bytes 24584 | tf_op jit(solution)/shard_map/ppermute | solution.py:489
  27.4 0.0 collective-permute-done.6.upstream_hbm
  27.4 5.6 %collective-permute-done.1.both_ref = bf16[1024,128]{1,0:T(8,128)(2,1)S(1)} collective-permute-done((bf16[1024,128]{1,0:T(8,128)(2,1)S(1)}, bf16[1024,128]{1,0:T(8,128)(2,1)S(1)}, u32[]{:S(2)}, u32[]{:S(2)}) %collective-permute-start.1) | collective-permute-done | bytes 262176 | tf_op jit(solution)/shard_map/ppermute | solution.py:40
  33.0 0.0 collective-permute-done.early_ref
  33.0 0.0 collective-permute-done.5.halo_ref
  33.0 1.9 %project.1 = (bf16[64,1024]{1,0:T(8,128)(2,1)}, bf16[64,2048]{1,0:T(8,128)(2,1)}, f32[64,1]{1,0:T(8,128)S(1)}) custom-call(bf16[1536,128]{1,0:T(8,128)(2,1)S(1)} %collective-permute-done.early_ref, bf16[1024,128]{1,0:T(8,128)(2,1)S(1)} %collective-permute-done.1.both_ref, bf16[40,2048]{1,0:T(8,128)(2,1)S(1)} %collective-permute-done.5.halo_ref, ...), custom_call_target="tpu_custom_call" | custom-call | flops 268435456 | bytes 4194304 | tf_op jit(solution)/shard_map/project/pallas_call | solution.py:461
  34.9 0.0 copy-start.3
  34.9 0.6 %copy-done.3 = f32[64,1]{1,0:T(8,128)} copy-done((f32[64,1]{1,0:T(8,128)}, f32[64,1]{1,0:T(8,128)S(1)}, u32[]{:S(2)}) %copy-start.3) | copy-done | bytes 280
  35.5 0.0 collective-permute-done.7.other_ref
  35.5 0.0 copy-start.4
  35.5 0.0 copy-done.1
  35.5 0.6 %copy-done.4 = f32[1,2048]{1,0:T(1,128)} copy-done((f32[1,2048]{1,0:T(1,128)}, f32[1,2048]{1,0:T(1,128)S(1)}, u32[]{:S(2)}) %copy-start.4) | copy-done | bytes 8216
  36.1 1.4 %update.1 = f32[1,2048]{1,0:T(1,128)} custom-call(f32[1,2048]{1,0:T(1,128)} %copy-done.1, f32[1,2048]{1,0:T(1,128)} %copy-done.4, f32[64,1]{1,0:T(8,128)} %copy-done.3), custom_call_target="tpu_custom_call" | custom-call | flops 16384 | bytes 24576 | tf_op jit(solution)/shard_map/update/pallas_call | solution.py:478
  (3 shorter events, 0.0 us)
Async XLA Ops:
  0.6 10.1 %copy-start = (bf16[1,2048,1024]{2,1,0:T(8,128)(2,1)S(1)}, bf16[1,2048,1024]{2,1,0:T(8,128)(2,1)}, u32[]{:S(2)}) copy-start(bf16[1,2048,1024]{2,1,0:T(8,128)(2,1)} %param.13) | copy-start | bytes 12582916
  0.6 10.1 %copy-start.2 = (f32[1,2048]{1,0:T(1,128)S(1)}, f32[1,2048]{1,0:T(1,128)}, u32[]{:S(2)}) copy-start(f32[1,2048]{1,0:T(1,128)} %gain_ref.3) | copy-start | bytes 24580
  4.3 15.0 %collective-permute-start.2 = (bf16[136,2048]{1,0:T(8,128)(2,1)S(1)}, bf16[136,2048]{1,0:T(8,128)(2,1)S(1)}, u32[]{:S(2)}, u32[]{:S(2)}) collective-permute-start(bf16[136,2048]{1,0:T(8,128)(2,1)S(1)} %get-tuple-element.26), channel_id=1, source_target_pairs={{2,0},{4,2},{6,4},{3,1},{5,3},{7,5},{10,8},{12,10},{14,12},{11,9},... | collective-permute-start | bytes 1671176 | tf_op jit(solution)/shard_map/ppermute | solution.py:35
  6.7 26.3 %collective-permute-start = (bf16[1536,128]{1,0:T(8,128)(2,1)S(1)}, bf16[1536,128]{1,0:T(8,128)(2,1)S(1)}, u32[]{:S(2)}, u32[]{:S(2)}) collective-permute-start(bf16[1536,128]{1,0:T(8,128)(2,1)S(1)} %get-tuple-element.19), channel_id=1, source_target_pairs={{0,8},{8,16},{16,24},{24,0},{1,9},{9,17},{17,25},{25,1},{2,10},{10... | collective-permute-start | bytes 1179656 | tf_op jit(solution)/shard_map/ppermute | solution.py:40
  12.3 15.1 %collective-permute-start.6 = (bf16[64,2048]{1,0:T(8,128)(2,1)S(1)}, bf16[64,2048]{1,0:T(8,128)(2,1)S(1)}, u32[]{:S(2)}, u32[]{:S(2)}) collective-permute-start(bf16[64,2048]{1,0:T(8,128)(2,1)S(1)} %get-tuple-element.31), channel_id=1, source_target_pairs={{0,24},{8,0},{16,8},{24,16},{1,25},{9,1},{17,9},{25,17},{2,26},{10... | collective-permute-start | bytes 786440 | tf_op jit(solution)/shard_map/ppermute | solution.py:40
  13.8 19.2 %collective-permute-start.1 = (bf16[1024,128]{1,0:T(8,128)(2,1)S(1)}, bf16[1024,128]{1,0:T(8,128)(2,1)S(1)}, u32[]{:S(2)}, u32[]{:S(2)}) collective-permute-start(bf16[1024,128]{1,0:T(8,128)(2,1)S(1)} %attend_late.1.after_ref), channel_id=1, source_target_pairs={{0,8},{8,16},{16,24},{24,0},{1,9},{9,17},{17,25},{25,1},{2,10},{10... | collective-permute-start | bytes 786440 | tf_op jit(solution)/shard_map/ppermute | solution.py:40
  14.4 1.2 %collective-permute-start.3 = (f32[1,2048]{1,0:T(1,128)S(1)}, f32[1,2048]{1,0:T(1,128)S(1)}, u32[]{:S(2)}, u32[]{:S(2)}) collective-permute-start(f32[1,2048]{1,0:T(1,128)S(1)} %get-tuple-element.30), channel_id=1, source_target_pairs={{0,1},{1,0},{2,3},{3,2},{4,5},{5,4},{6,7},{7,6},{8,9},{9,8},{10,11... | collective-permute-start | bytes 24584 | tf_op jit(solution)/shard_map/ppermute | solution.py:489
  15.5 3.7 %collective-permute-start.4 = (f32[1,2048]{1,0:T(1,128)S(1)}, f32[1,2048]{1,0:T(1,128)S(1)}, u32[]{:S(2)}, u32[]{:S(2)}) collective-permute-start(f32[1,2048]{1,0:T(1,128)S(1)} %add.6), channel_id=1, source_target_pairs={{0,2},{2,0},{4,6},{6,4},{1,3},{3,1},{5,7},{7,5},{8,10},{10,8},{12,... | collective-permute-start | bytes 24584 | tf_op jit(solution)/shard_map/ppermute | solution.py:489
  19.3 16.2 %copy-start.1 = (f32[1,2048]{1,0:T(1,128)}, f32[1,2048]{1,0:T(1,128)S(1)}, u32[]{:S(2)}) copy-start(f32[1,2048]{1,0:T(1,128)S(1)} %add.7.after_ref.term_ref) | copy-start | bytes 24580
  21.1 11.9 %collective-permute-start.5 = (bf16[40,2048]{1,0:T(8,128)(2,1)S(1)}, bf16[40,2048]{1,0:T(8,128)(2,1)S(1)}, u32[]{:S(2)}, u32[]{:S(2)}) collective-permute-start(bf16[40,2048]{1,0:T(8,128)(2,1)S(1)} %attend_halo.1), channel_id=1, source_target_pairs={{0,10},{2,12},{4,14},{8,18},{10,20},{12,22},{16,26},{18,28},{20,30... | collective-permute-start | bytes 491528 | tf_op jit(solution)/shard_map/ppermute | solution.py:509
  22.4 13.1 %collective-permute-start.7 = (f32[1,2048]{1,0:T(1,128)S(1)}, f32[1,2048]{1,0:T(1,128)S(1)}, u32[]{:S(2)}, u32[]{:S(2)}) collective-permute-start(f32[1,2048]{1,0:T(1,128)S(1)} %add.7.after_ref.term_ref), channel_id=1, source_target_pairs={{0,4},{2,6},{4,0},{6,2},{1,5},{3,7},{5,1},{7,3},{8,12},{10,14},{12... | collective-permute-start | bytes 24584 | tf_op jit(solution)/shard_map/ppermute | solution.py:489
  34.9 0.6 %copy-start.3 = (f32[64,1]{1,0:T(8,128)}, f32[64,1]{1,0:T(8,128)S(1)}, u32[]{:S(2)}) copy-start(f32[64,1]{1,0:T(8,128)S(1)} %get-tuple-element.34.after_ref) | copy-start | bytes 772
  35.5 0.6 %copy-start.4 = (f32[1,2048]{1,0:T(1,128)}, f32[1,2048]{1,0:T(1,128)S(1)}, u32[]{:S(2)}) copy-start(f32[1,2048]{1,0:T(1,128)S(1)} %collective-permute-done.7.other_ref) | copy-start | bytes 24580

commit v10 on v9

--- a/solution.py
+++ b/solution.py
@@ -134,7 +134,7 @@
 
 def early_kernel(
     rows, chunks, offsets_hbm, q_hbm, k_hbm, v_hbm, cotangent_hbm, stashed_hbm,
-    sent_ref, early_ref, more_ref, q_late_ref, k_ref, v_ref, own_ref, other_ref, next_ref, cotangent_ref, stashed_ref,
+    sent_ref, early_ref, more_ref, q_late_ref, k_ref, v_ref, cotangent_ref, stashed_ref,
     offsets_ref, bias, sems, offsets_sem,
 ):
     half = rows // 2
@@ -146,14 +146,17 @@
         (v_hbm.at[head], v_ref.at[head]),
     )
     copies = load_chunks(arrays, chunks, sems)
-    rest = [
-        load(k_hbm.at[tail], k_ref.at[tail], offsets_sem.at[1]),
-        load(v_hbm.at[tail], v_ref.at[tail], offsets_sem.at[2]),
-        load(q_hbm.at[tail], q_late_ref, offsets_sem.at[3]),
-        load(cotangent_hbm, cotangent_ref, offsets_sem.at[4]),
-        load(stashed_hbm, stashed_ref, offsets_sem.at[5]),
-    ]
+    later = (
+        (k_hbm.at[tail], k_ref.at[tail]),
+        (v_hbm.at[tail], v_ref.at[tail]),
+        (q_hbm.at[tail], q_late_ref),
+        (cotangent_hbm, cotangent_ref),
+        (stashed_hbm, stashed_ref),
+    )
+    rest = []
+    offsets_copy.wait()
     start = lax.axis_index("seq") * rows
+    bias[...] = mask_bias(offsets_ref, start, start, lambda key, query: key <= query)
     pairs = k_ref.shape[1] // LANES
     split = early_ref.shape[0] // LANES
 
@@ -162,20 +165,20 @@
         if pair % per_chunk == 0:
             for copy in copies[pair // per_chunk]:
                 copy.wait()
-        if pair == 1:
-            offsets_copy.wait()
-            bias[...] = mask_bias(offsets_ref, start, start, lambda key, query: key <= query)
+        if pair == per_chunk:
+            for i, (source, target) in enumerate(later):
+                rest.append(load(source, target, offsets_sem.at[i + 1]))
 
     def score(pair):
         scores = dot_nt(k_ref[head, at(pair)], split_heads(sent_ref[head, at(pair)]))
         return scores, with_ones(jnp.transpose(v_ref[head, at(pair)]))
 
     def top(pair, scores, values_t):
-        scores = scores + bias[...]
-        return scores, tops(scores), values_t
+        return scores, tops(scores + bias[...]), values_t
 
     def weigh(pair, scores, top, values_t):
-        return top, dot_nn(values_t, jnp.exp(scores - top).astype(jnp.bfloat16))
+        weights = jnp.exp((scores + bias[...]) - top).astype(jnp.bfloat16)
+        return top, dot_nn(values_t, weights)
 
     def finish(pair, top, mixed):
         total = mixed[LANES : LANES + 1]
@@ -188,16 +191,20 @@
         return ()
 
     over_pairs(pairs, (score, top, weigh, finish), LAGS, arrive)
-    own_ref[...] = mask_bias(offsets_ref, start + half, start + half, lambda key, query: key <= query)
-    other_ref[...] = mask_bias(offsets_ref, start + half, start, lambda key, query: key > query)
-    next_ref[...] = mask_bias(offsets_ref, start + rows, start + half, lambda key, query: key > query)
     for copy in rest:
         copy.wait()
 
 
 def late_kernel(
-    q_ref, k_ref, v_ref, own_bias, other_bias, early_ref, both_ref, own, other
+    rows, offsets_hbm, weight_hbm, q_ref, k_ref, v_ref, early_ref, both_ref, next_ref, weight_ref,
+    offsets_ref, own_bias, other_bias, own, other, sems,
 ):
+    offsets_copy = load(offsets_hbm, offsets_ref, sems.at[8])
+    block = weight_ref.shape[0] // 8
+    copies = []
+    for i in range(8):
+        place = pl.ds(i * block, block)
+        copies.append(load(weight_hbm.at[place], weight_ref.at[place], sems.at[i]))
     half = q_ref.shape[0]
     key = lax.broadcasted_iota(jnp.int32, own.shape, 0)
     query = lax.broadcasted_iota(jnp.int32, own.shape, 1) % half
@@ -208,6 +215,11 @@
     features = early_ref.shape[0]
     both_ref[pl.ds(0, features), :] = early_ref[...]
     pairs = k_ref.shape[1] // LANES
+    offsets_copy.wait()
+    start = lax.axis_index("seq") * rows
+    own_bias[...] = mask_bias(offsets_ref, start + half, start + half, lambda key, query: key <= query)
+    other_bias[...] = mask_bias(offsets_ref, start + half, start, lambda key, query: key > query)
+    next_ref[...] = mask_bias(offsets_ref, start + rows, start + half, lambda key, query: key > query)
     parts = []
 
     def score(pair):
@@ -235,6 +247,8 @@
         return ()
 
     over_pairs(pairs, (score, top, weigh, finish), LAGS, lambda pair: None)
+    for copy in copies:
+        copy.wait()
 
 
 def halo_kernel(q_ref, k_ref, v_ref, bias, after_ref, out_ref):
@@ -255,11 +269,11 @@
         lse = jnp.concatenate(
             [terms[0:1] + terms[1:2] + terms[2:3], terms[3:4] + terms[4:5] + terms[5:6]], axis=1
         )
-        scores = scores + bias[...]
-        return scores, jnp.maximum(tops(scores), lse), lse, values_t
+        return scores, jnp.maximum(tops(scores + bias[...]), lse), lse, values_t
 
     def weigh(pair, scores, top, lse, values_t):
-        mixed = dot_nn(values_t, jnp.exp(scores - top).astype(jnp.bfloat16))
+        weights = jnp.exp((scores + bias[...]) - top).astype(jnp.bfloat16)
+        mixed = dot_nn(values_t, weights)
         return mixed, jnp.exp(lse - top)
 
     def finish(pair, mixed, kept):
@@ -309,7 +323,8 @@
 
 
 def project_kernel(
-    early_ref, both_ref, halo_ref, gain_ref, weight_ref, upstream_hbm, out_ref, passed_hbm, squares_ref, sem
+    early_ref, both_ref, halo_ref, gain_ref, weight_ref, term_ref, other_ref, upstream_hbm,
+    out_ref, update_ref, passed_hbm, sem,
 ):
     passing = load(upstream_hbm, passed_hbm, sem)
     half = both_ref.shape[1]
@@ -341,15 +356,11 @@
             scaled = (arrived * gain_ref[:, columns]).astype(jnp.bfloat16)
             product += dot_nn(scaled, weight_ref[columns, :])
             parts = []
-    squares_ref[...] = squares
     out_ref[...] = (product * lax.rsqrt(squares / features + EPS_NORM)).astype(jnp.bfloat16)
+    total = term_ref[...] + other_ref[...]
+    mean = jnp.sum(total * total, axis=1, keepdims=True) / features
+    update_ref[...] = total / jnp.sqrt(mean + EPS_STEP)
     passing.wait()
-
-
-def update_kernel(term_ref, other_ref, after_ref, update_ref):
-    total = term_ref[...] + other_ref[...]
-    mean = jnp.sum(total * total, axis=1, keepdims=True) / total.shape[1]
-    update_ref[...] = total / jnp.sqrt(mean + EPS_STEP)
 
 
 def cost(flops, read, exps=0):
@@ -374,23 +385,20 @@
     rows, width = queries.shape
     half = rows // 2
     soon = width // (4 * LANES) * 3 // 4 * 4 * LANES
-    masks = [jax.ShapeDtypeStruct((half, 2 * half), jnp.float32)] * 3
+    bf16 = lambda *shape: jax.ShapeDtypeStruct(shape, jnp.bfloat16)
     return pl.pallas_call(
         functools.partial(early_kernel, rows, chunks),
         in_specs=[HBM] * 6,
-        out_specs=[VMEM] * 11,
+        out_specs=[VMEM] * 8,
         out_shape=[
-            jax.ShapeDtypeStruct((half + EXTRA, width), jnp.bfloat16),
-            jax.ShapeDtypeStruct((soon, half), jnp.bfloat16),
-            jax.ShapeDtypeStruct((width - soon, half), jnp.bfloat16),
-            jax.ShapeDtypeStruct((half, width), jnp.bfloat16),
-            jax.ShapeDtypeStruct((rows, width), jnp.bfloat16),
-            jax.ShapeDtypeStruct((rows, width), jnp.bfloat16),
-        ]
-        + masks
-        + [
-            jax.ShapeDtypeStruct(cotangent.shape, cotangent.dtype),
-            jax.ShapeDtypeStruct(stashed.shape, stashed.dtype),
+            bf16(half + EXTRA, width),
+            bf16(soon, half),
+            bf16(width - soon, half),
+            bf16(half, width),
+            bf16(rows, width),
+            bf16(rows, width),
+            bf16(*cotangent.shape),
+            bf16(*stashed.shape),
         ],
         scratch_shapes=[
             pltpu.SMEM(offsets.shape, jnp.int32),
@@ -404,21 +412,30 @@
     )(*in_hbm(offsets, queries, keys, values, cotangent, stashed))
 
 
-def attend_late(queries, keys, values, own_bias, other_bias, early):
+def attend_late(queries, keys, values, offsets, weight, early):
     half, width = queries.shape
+    rows = 2 * half
     return pl.pallas_call(
-        late_kernel,
-        in_specs=[VMEM] * 6,
-        out_specs=VMEM,
-        out_shape=jax.ShapeDtypeStruct((early.shape[0] + width // POOL, half), jnp.bfloat16),
+        functools.partial(late_kernel, rows),
+        in_specs=[HBM] * 2 + [VMEM] * 4,
+        out_specs=[VMEM] * 3,
+        out_shape=[
+            jax.ShapeDtypeStruct((early.shape[0] + width // POOL, half), jnp.bfloat16),
+            jax.ShapeDtypeStruct((half, rows), jnp.float32),
+            jax.ShapeDtypeStruct(weight.shape, weight.dtype),
+        ],
         scratch_shapes=[
-            pltpu.VMEM((half, 2 * half), jnp.bfloat16),
-            pltpu.VMEM((half, 2 * half), jnp.bfloat16),
+            pltpu.SMEM(offsets.shape, jnp.int32),
+            pltpu.VMEM((half, rows), jnp.float32),
+            pltpu.VMEM((half, rows), jnp.float32),
+            pltpu.VMEM((half, rows), jnp.bfloat16),
+            pltpu.VMEM((half, rows), jnp.bfloat16),
+            pltpu.SemaphoreType.DMA((9,)),
         ],
         cost_estimate=cost(8 * half * half * width, 10 * half * width, half * half * width // 64),
         compiler_params=params(),
         name="attend_late",
-    )(queries, keys, values, own_bias, other_bias, early)
+    )(*in_hbm(offsets, weight), queries, keys, values, early)
 
 
 def attend_halo(sent, keys, values, bias, after):
@@ -455,34 +472,23 @@
     )(slot, cotangent, weight, gain, stashed, after)
 
 
-def project(early, both, halo, gain, weight, upstream):
+def project(early, both, halo, gain, weight, term, other, upstream):
     rows = upstream.shape[0]
     width, depth = weight.shape
     return pl.pallas_call(
         project_kernel,
-        in_specs=[VMEM] * 5 + [ANY],
-        out_specs=[VMEM, HBM, VMEM],
+        in_specs=[VMEM] * 7 + [ANY],
+        out_specs=[VMEM, VMEM, HBM],
         out_shape=[
             jax.ShapeDtypeStruct((rows, depth), jnp.bfloat16),
+            jax.ShapeDtypeStruct(term.shape, term.dtype),
             jax.ShapeDtypeStruct(upstream.shape, upstream.dtype),
-            jax.ShapeDtypeStruct((rows, 1), jnp.float32),
         ],
         scratch_shapes=[pltpu.SemaphoreType.DMA],
         cost_estimate=cost(2 * rows * width * depth, 2 * width * depth),
         compiler_params=params(),
         name="project",
-    )(early, both, halo, gain, weight, upstream)
-
-
-def updated(term, other, after):
-    return pl.pallas_call(
-        update_kernel,
-        in_specs=[VMEM] * 2 + [ANY],
-        out_specs=VMEM,
-        out_shape=jax.ShapeDtypeStruct(term.shape, term.dtype),
-        cost_estimate=cost(8 * term.size, 12 * term.size),
-        name="update",
-    )(term, other, after)
+    )(early, both, halo, gain, weight, term, other, upstream)
 
 
 def swapped(value, axis, distance):
@@ -516,23 +522,23 @@
     def partner(term, index):
         return swapped(term, *rounds[index]) if rounds else jnp.zeros_like(term)
 
-    sent, early, more, q_late, keys, values, *rest = attend_early(
+    sent, early, more, q_late, keys, values, cotangent, stashed = attend_early(
         queries, keys, values, offsets, cotangent[0, 0], stashed[0, 0], 4
     )
-    own_bias, other_bias, next_bias, cotangent, stashed = rest
     arrived = shifted(sent, "seq", -1)
     early = passed_along(early, "section", 1)
-    both = attend_late(q_late, keys, values, own_bias, other_bias, more)
+    both, next_bias, weight = attend_late(q_late, keys, values, offsets, weight[0], more)
     slot = jnp.broadcast_to(slot, (1, LANES))
-    dinput, term = backward(slot, cotangent, weight[0], gain, stashed, both)
+    dinput, term = backward(slot, cotangent, weight, gain, stashed, both)
     both = passed_along(both, "section", 1)
     upstream = passed_along(dinput, "section", -1)
     term = term if rounds else lax.psum(term, ("rep", "seq"))
     term = term + partner(term, 0)
     term = term + partner(term, 1)
     halo = onward(attend_halo(arrived, keys, values, next_bias, term))
-    mol_keys, upstream, squares = project(early, both, halo, gain, weight[0], upstream)
-    update = updated(term, partner(term, 2), squares)
+    mol_keys, update, upstream = project(
+        early, both, halo, gain, weight, term, partner(term, 2), upstream
+    )
     return mol_keys[None, None], upstream[None, None], update
 
 

time: 37.8 us -> 34.7 us (0.918)
  the two profiles are of different devices: /device:TPU:24 before, /device:TPU:0 now
where the time goes in v10:
time: 34.7 us; the launch traced here: 34.5 us
  starting transfers between devices  16.5 us (48%)
  Pallas kernels  10.8 us (31%)
  waiting for transfers between devices  5.74 us (17%)
  between operations  1.38 us (4%)
    ppermute x3, waiting for transfers between devices, swapped(): lax.ppermute(value, axis, [(i, i ^ distance) for i in range(lax.axis_size...  5.73 us
    ppermute x3, starting transfers between devices, swapped(): lax.ppermute(value, axis, [(i, i ^ distance) for i in range(lax.axis_size...  5.38 us
    ppermute x3, starting transfers between devices, passed_along(): lax.ppermute(value, axis, [(i, (i + steps) % count) for i in range(count)])  5.07 us
    ppermute x1, starting transfers between devices, onward(): return lax.ppermute(value, ('section', 'seq'), route)  4.8 us
    pallas_call x1, Pallas kernels, attend_early(): pl.pallas_call(functools.partial(early_kernel, rows, chunks), in_specs=[H...  3.16 us
    pallas_call x1, Pallas kernels, attend_late(): pl.pallas_call(functools.partial(late_kernel, rows), in_specs=[HBM] * 2 +...  2.6 us
    pallas_call x1, Pallas kernels, project(): pl.pallas_call(project_kernel, in_specs=[VMEM] * 7 + [ANY], out_specs=[VM...  1.95 us
    pallas_call x1, Pallas kernels, backward(): pl.pallas_call(back_kernel, in_specs=[VMEM] * 5 + [ANY], out_specs=[VMEM]...  1.56 us
  transfers between devices with their start and end apart: 8, of which 3 were waited for; matrix products, arithmetic and copies ran while one was open for 0% of the time, Pallas kernels for 16%

profile of v10, /device:TPU:0, one launch (start us, length us, event | category | flops | bytes accessed | tf_op | source)
XLA Modules:
  0.0 34.5 jit_solution(17220289905776500846)
XLA Ops:
  0.6 3.2 %attend_early.1 = (bf16[136,2048]{1,0:T(8,128)(2,1)S(1)}, bf16[1536,128]{1,0:T(8,128)(2,1)S(1)}, bf16[512,128]{1,0:T(8,128)(2,1)S(1)}, bf16[128,2048]{1,0:T(8,12...) custom-call(s32[1,8]{1,0:T(1,128)} %bitcast.17, ...), custom_call_target="tpu_custom_call" | custom-call | flops 134217728 | bytes 3145728 | tf_op jit(solution)/shard_map/attend_early/pallas_call | solution.py:389
  3.8 0.0 copy-start
  3.8 1.3 %collective-permute-start.2 = (bf16[136,2048]{1,0:T(8,128)(2,1)S(1)}, bf16[136,2048]{1,0:T(8,128)(2,1)S(1)}, u32[]{:S(2)}, u32[]{:S(2)}) collective-permute-start(bf16[136,2048]{1,0:T(8,128)(2,1)S(1)} %get-tuple-element.25), channel_id=1, source_target_pairs={{2,0},{4,2},{6,4},{3,1},{5,3},{7,5},{10,8},{12,10},{14,12},{11,9},... | collective-permute-start | bytes 1671176 | tf_op jit(solution)/shard_map/ppermute | solution.py:35
  5.1 3.0 %collective-permute-start = (bf16[1536,128]{1,0:T(8,128)(2,1)S(1)}, bf16[1536,128]{1,0:T(8,128)(2,1)S(1)}, u32[]{:S(2)}, u32[]{:S(2)}) collective-permute-start(bf16[1536,128]{1,0:T(8,128)(2,1)S(1)} %get-tuple-element.19), channel_id=1, source_target_pairs={{0,8},{8,16},{16,24},{24,0},{1,9},{9,17},{17,25},{25,1},{2,10},{10... | collective-permute-start | bytes 1179656 | tf_op jit(solution)/shard_map/ppermute | solution.py:40
  8.8 2.6 %attend_late.1 = (bf16[1024,128]{1,0:T(8,128)(2,1)S(1)}, f32[128,256]{1,0:T(8,128)S(1)}, bf16[2048,1024]{1,0:T(8,128)(2,1)S(1)}) custom-call(s32[1,8]{1,0:T(1,128)} %bitcast.18, bf16[2048,1024]{1,0:T(8,128)(2,1)} %bitcast.11, bf16[128,2048]{1,0:T(8,128)(2,1)S(1)} %get-tuple-element.20.q_ref, bf16[256,2048]{1,0:T(8,128)(2,1)S(1)} %get-tuple-element.21.k_ref, ...), custom_call_target="tpu_custom_call" | custom-call | flops 268435456 | bytes 2621440 | tf_op jit(solution)/shard_map/attend_late/pallas_call | solution.py:418
  11.4 0.0 copy-done
  11.4 1.6 %backward.1 = (bf16[64,2048]{1,0:T(8,128)(2,1)S(1)}, f32[1,2048]{1,0:T(1,128)S(1)}) custom-call(s32[1,128]{1,0:T(1,128)S(1)} %broadcast_in_dim.14.slot_ref, bf16[64,1024]{1,0:T(8,128)(2,1)S(1)} %get-tuple-element.27.cotangent_ref, bf16[2048,1024]{1,0:T(8,128)(2,1)S(1)} %get-tuple-element.28.weight_ref, f32[1,2048]{1,0:T(1,128)S(1)} %copy-done, ...), custom_call_target="tpu_custom_call" | custom-call | flops 268435456 | bytes 4194304 | tf_op jit(solution)/shard_map/backward/pallas_call | solution.py:457
  12.9 1.0 %collective-permute-start.7 = (bf16[64,2048]{1,0:T(8,128)(2,1)S(1)}, bf16[64,2048]{1,0:T(8,128)(2,1)S(1)}, u32[]{:S(2)}, u32[]{:S(2)}) collective-permute-start(bf16[64,2048]{1,0:T(8,128)(2,1)S(1)} %get-tuple-element.31), channel_id=1, source_target_pairs={{0,24},{8,0},{16,8},{24,16},{1,25},{9,1},{17,9},{25,17},{2,26},{10... | collective-permute-start | bytes 786440 | tf_op jit(solution)/shard_map/ppermute | solution.py:40
  14.0 1.1 %collective-permute-start.1 = (bf16[1024,128]{1,0:T(8,128)(2,1)S(1)}, bf16[1024,128]{1,0:T(8,128)(2,1)S(1)}, u32[]{:S(2)}, u32[]{:S(2)}) collective-permute-start(bf16[1024,128]{1,0:T(8,128)(2,1)S(1)} %get-tuple-element.24.after_ref), channel_id=1, source_target_pairs={{0,8},{8,16},{16,24},{24,0},{1,9},{9,17},{17,25},{25,1},{2,10},{10... | collective-permute-start | bytes 786440 | tf_op jit(solution)/shard_map/ppermute | solution.py:40
  15.0 0.0 collective-permute-start.3
  15.0 1.2 %collective-permute-done.3 = f32[1,2048]{1,0:T(1,128)S(1)} collective-permute-done((f32[1,2048]{1,0:T(1,128)S(1)}, f32[1,2048]{1,0:T(1,128)S(1)}, u32[]{:S(2)}, u32[]{:S(2)}) %collective-permute-start.3) | collective-permute-done | bytes 8224 | tf_op jit(solution)/shard_map/ppermute | solution.py:495
  16.2 2.7 %collective-permute-start.4 = (f32[1,2048]{1,0:T(1,128)S(1)}, f32[1,2048]{1,0:T(1,128)S(1)}, u32[]{:S(2)}, u32[]{:S(2)}) collective-permute-start(f32[1,2048]{1,0:T(1,128)S(1)} %add.6), channel_id=1, source_target_pairs={{0,2},{2,0},{4,6},{6,4},{1,3},{3,1},{5,7},{7,5},{8,10},{10,8},{12,... | collective-permute-start | bytes 24584 | tf_op jit(solution)/shard_map/ppermute | solution.py:495
  18.9 2.6 %collective-permute-done.4 = f32[1,2048]{1,0:T(1,128)S(1)} collective-permute-done((f32[1,2048]{1,0:T(1,128)S(1)}, f32[1,2048]{1,0:T(1,128)S(1)}, u32[]{:S(2)}, u32[]{:S(2)}) %collective-permute-start.4) | collective-permute-done | bytes 8224 | tf_op jit(solution)/shard_map/ppermute | solution.py:495
  21.6 0.0 collective-permute-done.2.q_ref
  21.6 1.5 %attend_halo.1 = bf16[40,2048]{1,0:T(8,128)(2,1)S(1)} custom-call(bf16[136,2048]{1,0:T(8,128)(2,1)S(1)} %collective-permute-done.2.q_ref, bf16[256,2048]{1,0:T(8,128)(2,1)S(1)} %get-tuple-element.21.k_ref, bf16[256,2048]{1,0:T(8,128)(2,1)S(1)} %get-tuple-element.22.v_ref, f32[128,256]{1,0:T(8,128)S(1)} %get-tuple-element.26.bias, ...), custom_call_target="tpu_custom_call" | custom-call | flops 134217728 | bytes 1572864 | tf_op jit(solution)/shard_map/attend_halo/pallas_call | solution.py:443
  23.1 4.8 %collective-permute-start.5 = (bf16[40,2048]{1,0:T(8,128)(2,1)S(1)}, bf16[40,2048]{1,0:T(8,128)(2,1)S(1)}, u32[]{:S(2)}, u32[]{:S(2)}) collective-permute-start(bf16[40,2048]{1,0:T(8,128)(2,1)S(1)} %attend_halo.1), channel_id=1, source_target_pairs={{0,10},{2,12},{4,14},{8,18},{10,20},{12,22},{16,26},{18,28},{20,30... | collective-permute-start | bytes 491528 | tf_op jit(solution)/shard_map/ppermute | solution.py:515
  27.9 2.7 %collective-permute-start.6 = (f32[1,2048]{1,0:T(1,128)S(1)}, f32[1,2048]{1,0:T(1,128)S(1)}, u32[]{:S(2)}, u32[]{:S(2)}) collective-permute-start(f32[1,2048]{1,0:T(1,128)S(1)} %add.7.after_ref.term_ref), channel_id=1, source_target_pairs={{0,4},{2,6},{4,0},{6,2},{1,5},{3,7},{5,1},{7,3},{8,12},{10,14},{12... | collective-permute-start | bytes 24584 | tf_op jit(solution)/shard_map/ppermute | solution.py:495
  30.5 1.9 %collective-permute-done.6.other_ref = f32[1,2048]{1,0:T(1,128)S(1)} collective-permute-done((f32[1,2048]{1,0:T(1,128)S(1)}, f32[1,2048]{1,0:T(1,128)S(1)}, u32[]{:S(2)}, u32[]{:S(2)}) %collective-permute-start.6) | collective-permute-done | bytes 8224 | tf_op jit(solution)/shard_map/ppermute | solution.py:495
  32.5 0.0 collective-permute-done.7.upstream_hbm
  32.5 0.0 collective-permute-done.1.both_ref
  32.5 0.0 collective-permute-done.early_ref
  32.5 0.0 collective-permute-done.5.halo_ref
  32.5 1.9 %project.1 = (bf16[64,1024]{1,0:T(8,128)(2,1)}, f32[1,2048]{1,0:T(1,128)}, bf16[64,2048]{1,0:T(8,128)(2,1)}) custom-call(bf16[1536,128]{1,0:T(8,128)(2,1)S(1)} %collective-permute-done.early_ref, bf16[1024,128]{1,0:T(8,128)(2,1)S(1)} %collective-permute-done.1.both_ref, bf16[40,2048]{1,0:T(8,128)(2,1)S(1)} %collective-permute-done.5.halo_ref, ...), custom_call_target="tpu_custom_call" | custom-call | flops 268435456 | bytes 4194304 | tf_op jit(solution)/shard_map/project/pallas_call | solution.py:478
  (3 shorter events, 0.0 us)
Async XLA Ops:
  3.8 7.6 %copy-start = (f32[1,2048]{1,0:T(1,128)S(1)}, f32[1,2048]{1,0:T(1,128)}, u32[]{:S(2)}) copy-start(f32[1,2048]{1,0:T(1,128)} %gain_ref.3) | copy-start | bytes 24580
  3.8 17.7 %collective-permute-start.2 = (bf16[136,2048]{1,0:T(8,128)(2,1)S(1)}, bf16[136,2048]{1,0:T(8,128)(2,1)S(1)}, u32[]{:S(2)}, u32[]{:S(2)}) collective-permute-start(bf16[136,2048]{1,0:T(8,128)(2,1)S(1)} %get-tuple-element.25), channel_id=1, source_target_pairs={{2,0},{4,2},{6,4},{3,1},{5,3},{7,5},{10,8},{12,10},{14,12},{11,9},... | collective-permute-start | bytes 1671176 | tf_op jit(solution)/shard_map/ppermute | solution.py:35
  5.1 27.4 %collective-permute-start = (bf16[1536,128]{1,0:T(8,128)(2,1)S(1)}, bf16[1536,128]{1,0:T(8,128)(2,1)S(1)}, u32[]{:S(2)}, u32[]{:S(2)}) collective-permute-start(bf16[1536,128]{1,0:T(8,128)(2,1)S(1)} %get-tuple-element.19), channel_id=1, source_target_pairs={{0,8},{8,16},{16,24},{24,0},{1,9},{9,17},{17,25},{25,1},{2,10},{10... | collective-permute-start | bytes 1179656 | tf_op jit(solution)/shard_map/ppermute | solution.py:40
  12.9 19.5 %collective-permute-start.7 = (bf16[64,2048]{1,0:T(8,128)(2,1)S(1)}, bf16[64,2048]{1,0:T(8,128)(2,1)S(1)}, u32[]{:S(2)}, u32[]{:S(2)}) collective-permute-start(bf16[64,2048]{1,0:T(8,128)(2,1)S(1)} %get-tuple-element.31), channel_id=1, source_target_pairs={{0,24},{8,0},{16,8},{24,16},{1,25},{9,1},{17,9},{25,17},{2,26},{10... | collective-permute-start | bytes 786440 | tf_op jit(solution)/shard_map/ppermute | solution.py:40
  14.0 18.5 %collective-permute-start.1 = (bf16[1024,128]{1,0:T(8,128)(2,1)S(1)}, bf16[1024,128]{1,0:T(8,128)(2,1)S(1)}, u32[]{:S(2)}, u32[]{:S(2)}) collective-permute-start(bf16[1024,128]{1,0:T(8,128)(2,1)S(1)} %get-tuple-element.24.after_ref), channel_id=1, source_target_pairs={{0,8},{8,16},{16,24},{24,0},{1,9},{9,17},{17,25},{25,1},{2,10},{10... | collective-permute-start | bytes 786440 | tf_op jit(solution)/shard_map/ppermute | solution.py:40
  15.0 1.2 %collective-permute-start.3 = (f32[1,2048]{1,0:T(1,128)S(1)}, f32[1,2048]{1,0:T(1,128)S(1)}, u32[]{:S(2)}, u32[]{:S(2)}) collective-permute-start(f32[1,2048]{1,0:T(1,128)S(1)} %get-tuple-element.30), channel_id=1, source_target_pairs={{0,1},{1,0},{2,3},{3,2},{4,5},{5,4},{6,7},{7,6},{8,9},{9,8},{10,11... | collective-permute-start | bytes 24584 | tf_op jit(solution)/shard_map/ppermute | solution.py:495
  16.2 5.3 %collective-permute-start.4 = (f32[1,2048]{1,0:T(1,128)S(1)}, f32[1,2048]{1,0:T(1,128)S(1)}, u32[]{:S(2)}, u32[]{:S(2)}) collective-permute-start(f32[1,2048]{1,0:T(1,128)S(1)} %add.6), channel_id=1, source_target_pairs={{0,2},{2,0},{4,6},{6,4},{1,3},{3,1},{5,7},{7,5},{8,10},{10,8},{12,... | collective-permute-start | bytes 24584 | tf_op jit(solution)/shard_map/ppermute | solution.py:495
  23.1 9.4 %collective-permute-start.5 = (bf16[40,2048]{1,0:T(8,128)(2,1)S(1)}, bf16[40,2048]{1,0:T(8,128)(2,1)S(1)}, u32[]{:S(2)}, u32[]{:S(2)}) collective-permute-start(bf16[40,2048]{1,0:T(8,128)(2,1)S(1)} %attend_halo.1), channel_id=1, source_target_pairs={{0,10},{2,12},{4,14},{8,18},{10,20},{12,22},{16,26},{18,28},{20,30... | collective-permute-start | bytes 491528 | tf_op jit(solution)/shard_map/ppermute | solution.py:515
  27.9 4.6 %collective-permute-start.6 = (f32[1,2048]{1,0:T(1,128)S(1)}, f32[1,2048]{1,0:T(1,128)S(1)}, u32[]{:S(2)}, u32[]{:S(2)}) collective-permute-start(f32[1,2048]{1,0:T(1,128)S(1)} %add.7.after_ref.term_ref), channel_id=1, source_target_pairs={{0,4},{2,6},{4,0},{6,2},{1,5},{3,7},{5,1},{7,3},{8,12},{10,14},{12... | collective-permute-start | bytes 24584 | tf_op jit(solution)/shard_map/ppermute | solution.py:495

commit v11 on v10

--- a/solution.py
+++ b/solution.py
@@ -177,7 +177,7 @@
         return scores, tops(scores + bias[...]), values_t
 
     def weigh(pair, scores, top, values_t):
-        weights = jnp.exp((scores + bias[...]) - top).astype(jnp.bfloat16)
+        weights = jnp.exp(((scores + bias[...]) - top).astype(jnp.bfloat16))
         return top, dot_nn(values_t, weights)
 
     def finish(pair, top, mixed):
@@ -231,7 +231,7 @@
         return scores, tops(scores), values_t
 
     def weigh(pair, scores, top, values_t):
-        weights = jnp.exp(scores - top).astype(jnp.bfloat16)
+        weights = jnp.exp((scores - top).astype(jnp.bfloat16))
         weights = jnp.concatenate([weights * other[...], weights * own[...]], axis=0)
         return (dot_nn(values_t, weights),)
 
@@ -272,7 +272,7 @@
         return scores, jnp.maximum(tops(scores + bias[...]), lse), lse, values_t
 
     def weigh(pair, scores, top, lse, values_t):
-        weights = jnp.exp((scores + bias[...]) - top).astype(jnp.bfloat16)
+        weights = jnp.exp(((scores + bias[...]) - top).astype(jnp.bfloat16))
         mixed = dot_nn(values_t, weights)
         return mixed, jnp.exp(lse - top)
 
@@ -333,29 +333,33 @@
     molecules = half // POOL
     pooling = pool_matrix(half)
     first = lax.axis_index("seq") == 0
-    squares, product, parts = 0.0, 0.0, []
-    for pair in range(features // LANES):
-        shares = halo_ref[molecules:, at(pair)].astype(jnp.float32)
-        share_a = jnp.where(first, 1.0, shares[0:1] + shares[1:2])
-        share_b = jnp.where(first, 1.0, shares[2:3] + shares[3:4])
-        begin = pair * LANES
-        if begin < first_part:
-            early = early_ref[pl.ds(begin, LANES), :].astype(jnp.float32)
-        else:
-            early = both_ref[pl.ds(begin - first_part, LANES), :].astype(jnp.float32)
-        parts += [early[:HEAD_DIM] * share_a, early[HEAD_DIM:] * share_b]
-        if len(parts) == 8:
-            columns = pl.ds((pair - 3) * LANES, 4 * LANES)
+    squares, product, ready = 0.0, 0.0, None
+    group = 4
+    for begin in range(0, features + group * LANES, group * LANES):
+        following = ready
+        if begin < features:
+            parts = []
+            for pair in range(begin // LANES, begin // LANES + group):
+                shares = halo_ref[molecules:, at(pair)].astype(jnp.float32)
+                share_a = jnp.where(first, 1.0, shares[0:1] + shares[1:2])
+                share_b = jnp.where(first, 1.0, shares[2:3] + shares[3:4])
+                if pair * LANES < first_part:
+                    early = early_ref[at(pair), :].astype(jnp.float32)
+                else:
+                    early = both_ref[at(pair - first_part // LANES), :].astype(jnp.float32)
+                parts += [early[:HEAD_DIM] * share_a, early[HEAD_DIM:] * share_b]
+            columns = pl.ds(begin, group * LANES)
             mean = dot_nt(pooling, jnp.concatenate(parts, axis=0).astype(jnp.bfloat16))
             upper = mean + halo_ref[:molecules, columns].astype(jnp.float32)
-            place = features - first_part + (pair - 3) * molecules
-            lower = [both_ref[pl.ds(place + i * molecules, molecules), :] for i in range(4)]
+            place = features - first_part + begin // LANES * molecules
+            lower = [both_ref[pl.ds(place + i * molecules, molecules), :] for i in range(group)]
             lower = jnp.concatenate(lower, axis=1)
             arrived = jnp.concatenate([upper.astype(jnp.bfloat16), lower], axis=0).astype(jnp.float32)
             squares += jnp.sum(arrived * arrived, axis=1, keepdims=True)
-            scaled = (arrived * gain_ref[:, columns]).astype(jnp.bfloat16)
+            ready = (arrived * gain_ref[:, columns]).astype(jnp.bfloat16), columns
+        if following is not None:
+            scaled, columns = following
             product += dot_nn(scaled, weight_ref[columns, :])
-            parts = []
     out_ref[...] = (product * lax.rsqrt(squares / features + EPS_NORM)).astype(jnp.bfloat16)
     total = term_ref[...] + other_ref[...]
     mean = jnp.sum(total * total, axis=1, keepdims=True) / features

time: 34.7 us -> 34.9 us (level)
  no operation moved by 1% of the time
where the time goes in v11:
time: 34.9 us; the launch traced here: 34.6 us
  starting transfers between devices  16.5 us (47%)
  Pallas kernels  10.9 us (31%)
  waiting for transfers between devices  5.73 us (16%)
  between operations  1.38 us (4%)
    ppermute x3, waiting for transfers between devices, swapped(): lax.ppermute(value, axis, [(i, i ^ distance) for i in range(lax.axis_size...  5.72 us
    ppermute x3, starting transfers between devices, swapped(): lax.ppermute(value, axis, [(i, i ^ distance) for i in range(lax.axis_size...  5.4 us
    ppermute x3, starting transfers between devices, passed_along(): lax.ppermute(value, axis, [(i, (i + steps) % count) for i in range(count)])  5.07 us
    ppermute x1, starting transfers between devices, onward(): return lax.ppermute(value, ('section', 'seq'), route)  4.79 us
    pallas_call x1, Pallas kernels, attend_early(): pl.pallas_call(functools.partial(early_kernel, rows, chunks), in_specs=[H...  3.16 us
    pallas_call x1, Pallas kernels, attend_late(): pl.pallas_call(functools.partial(late_kernel, rows), in_specs=[HBM] * 2 +...  2.59 us
    pallas_call x1, Pallas kernels, project(): pl.pallas_call(project_kernel, in_specs=[VMEM] * 7 + [ANY], out_specs=[VM...  2.15 us
    pallas_call x1, Pallas kernels, backward(): pl.pallas_call(back_kernel, in_specs=[VMEM] * 5 + [ANY], out_specs=[VMEM]...  1.56 us
  transfers between devices with their start and end apart: 8, of which 3 were waited for; matrix products, arithmetic and copies ran while one was open for 0% of the time, Pallas kernels for 16%

profile of v11, /device:TPU:0, one launch (start us, length us, event | category | flops | bytes accessed | tf_op | source)
XLA Modules:
  0.0 34.6 jit_solution(5190998446102379440)
XLA Ops:
  0.6 3.2 %attend_early.1 = (bf16[136,2048]{1,0:T(8,128)(2,1)S(1)}, bf16[1536,128]{1,0:T(8,128)(2,1)S(1)}, bf16[512,128]{1,0:T(8,128)(2,1)S(1)}, bf16[128,2048]{1,0:T(8,12...) custom-call(s32[1,8]{1,0:T(1,128)} %bitcast.17, ...), custom_call_target="tpu_custom_call" | custom-call | flops 134217728 | bytes 3145728 | tf_op jit(solution)/shard_map/attend_early/pallas_call | solution.py:393
  3.8 0.0 copy-start
  3.8 1.3 %collective-permute-start.2 = (bf16[136,2048]{1,0:T(8,128)(2,1)S(1)}, bf16[136,2048]{1,0:T(8,128)(2,1)S(1)}, u32[]{:S(2)}, u32[]{:S(2)}) collective-permute-start(bf16[136,2048]{1,0:T(8,128)(2,1)S(1)} %get-tuple-element.25), channel_id=1, source_target_pairs={{2,0},{4,2},{6,4},{3,1},{5,3},{7,5},{10,8},{12,10},{14,12},{11,9},... | collective-permute-start | bytes 1671176 | tf_op jit(solution)/shard_map/ppermute | solution.py:35
  5.1 3.0 %collective-permute-start = (bf16[1536,128]{1,0:T(8,128)(2,1)S(1)}, bf16[1536,128]{1,0:T(8,128)(2,1)S(1)}, u32[]{:S(2)}, u32[]{:S(2)}) collective-permute-start(bf16[1536,128]{1,0:T(8,128)(2,1)S(1)} %get-tuple-element.19), channel_id=1, source_target_pairs={{0,8},{8,16},{16,24},{24,0},{1,9},{9,17},{17,25},{25,1},{2,10},{10... | collective-permute-start | bytes 1179656 | tf_op jit(solution)/shard_map/ppermute | solution.py:40
  8.8 2.6 %attend_late.1 = (bf16[1024,128]{1,0:T(8,128)(2,1)S(1)}, f32[128,256]{1,0:T(8,128)S(1)}, bf16[2048,1024]{1,0:T(8,128)(2,1)S(1)}) custom-call(s32[1,8]{1,0:T(1,128)} %bitcast.18, bf16[2048,1024]{1,0:T(8,128)(2,1)} %bitcast.11, bf16[128,2048]{1,0:T(8,128)(2,1)S(1)} %get-tuple-element.20.q_ref, bf16[256,2048]{1,0:T(8,128)(2,1)S(1)} %get-tuple-element.21.k_ref, ...), custom_call_target="tpu_custom_call" | custom-call | flops 268435456 | bytes 2621440 | tf_op jit(solution)/shard_map/attend_late/pallas_call | solution.py:422
  11.4 0.0 copy-done
  11.4 1.6 %backward.1 = (bf16[64,2048]{1,0:T(8,128)(2,1)S(1)}, f32[1,2048]{1,0:T(1,128)S(1)}) custom-call(s32[1,128]{1,0:T(1,128)S(1)} %broadcast_in_dim.14.slot_ref, bf16[64,1024]{1,0:T(8,128)(2,1)S(1)} %get-tuple-element.27.cotangent_ref, bf16[2048,1024]{1,0:T(8,128)(2,1)S(1)} %get-tuple-element.28.weight_ref, f32[1,2048]{1,0:T(1,128)S(1)} %copy-done, ...), custom_call_target="tpu_custom_call" | custom-call | flops 268435456 | bytes 4194304 | tf_op jit(solution)/shard_map/backward/pallas_call | solution.py:461
  12.9 1.0 %collective-permute-start.7 = (bf16[64,2048]{1,0:T(8,128)(2,1)S(1)}, bf16[64,2048]{1,0:T(8,128)(2,1)S(1)}, u32[]{:S(2)}, u32[]{:S(2)}) collective-permute-start(bf16[64,2048]{1,0:T(8,128)(2,1)S(1)} %get-tuple-element.31), channel_id=1, source_target_pairs={{0,24},{8,0},{16,8},{24,16},{1,25},{9,1},{17,9},{25,17},{2,26},{10... | collective-permute-start | bytes 786440 | tf_op jit(solution)/shard_map/ppermute | solution.py:40
  14.0 1.1 %collective-permute-start.1 = (bf16[1024,128]{1,0:T(8,128)(2,1)S(1)}, bf16[1024,128]{1,0:T(8,128)(2,1)S(1)}, u32[]{:S(2)}, u32[]{:S(2)}) collective-permute-start(bf16[1024,128]{1,0:T(8,128)(2,1)S(1)} %get-tuple-element.24.after_ref), channel_id=1, source_target_pairs={{0,8},{8,16},{16,24},{24,0},{1,9},{9,17},{17,25},{25,1},{2,10},{10... | collective-permute-start | bytes 786440 | tf_op jit(solution)/shard_map/ppermute | solution.py:40
  15.0 0.0 collective-permute-start.3
  15.0 1.2 %collective-permute-done.3 = f32[1,2048]{1,0:T(1,128)S(1)} collective-permute-done((f32[1,2048]{1,0:T(1,128)S(1)}, f32[1,2048]{1,0:T(1,128)S(1)}, u32[]{:S(2)}, u32[]{:S(2)}) %collective-permute-start.3) | collective-permute-done | bytes 8224 | tf_op jit(solution)/shard_map/ppermute | solution.py:499
  16.2 2.7 %collective-permute-start.4 = (f32[1,2048]{1,0:T(1,128)S(1)}, f32[1,2048]{1,0:T(1,128)S(1)}, u32[]{:S(2)}, u32[]{:S(2)}) collective-permute-start(f32[1,2048]{1,0:T(1,128)S(1)} %add.6), channel_id=1, source_target_pairs={{0,2},{2,0},{4,6},{6,4},{1,3},{3,1},{5,7},{7,5},{8,10},{10,8},{12,... | collective-permute-start | bytes 24584 | tf_op jit(solution)/shard_map/ppermute | solution.py:499
  18.9 2.6 %collective-permute-done.4 = f32[1,2048]{1,0:T(1,128)S(1)} collective-permute-done((f32[1,2048]{1,0:T(1,128)S(1)}, f32[1,2048]{1,0:T(1,128)S(1)}, u32[]{:S(2)}, u32[]{:S(2)}) %collective-permute-start.4) | collective-permute-done | bytes 8224 | tf_op jit(solution)/shard_map/ppermute | solution.py:499
  21.6 0.0 collective-permute-done.2.q_ref
  21.6 1.5 %attend_halo.1 = bf16[40,2048]{1,0:T(8,128)(2,1)S(1)} custom-call(bf16[136,2048]{1,0:T(8,128)(2,1)S(1)} %collective-permute-done.2.q_ref, bf16[256,2048]{1,0:T(8,128)(2,1)S(1)} %get-tuple-element.21.k_ref, bf16[256,2048]{1,0:T(8,128)(2,1)S(1)} %get-tuple-element.22.v_ref, f32[128,256]{1,0:T(8,128)S(1)} %get-tuple-element.26.bias, ...), custom_call_target="tpu_custom_call" | custom-call | flops 134217728 | bytes 1572864 | tf_op jit(solution)/shard_map/attend_halo/pallas_call | solution.py:447
  23.0 4.8 %collective-permute-start.5 = (bf16[40,2048]{1,0:T(8,128)(2,1)S(1)}, bf16[40,2048]{1,0:T(8,128)(2,1)S(1)}, u32[]{:S(2)}, u32[]{:S(2)}) collective-permute-start(bf16[40,2048]{1,0:T(8,128)(2,1)S(1)} %attend_halo.1), channel_id=1, source_target_pairs={{0,10},{2,12},{4,14},{8,18},{10,20},{12,22},{16,26},{18,28},{20,30... | collective-permute-start | bytes 491528 | tf_op jit(solution)/shard_map/ppermute | solution.py:519
  27.8 2.7 %collective-permute-start.6 = (f32[1,2048]{1,0:T(1,128)S(1)}, f32[1,2048]{1,0:T(1,128)S(1)}, u32[]{:S(2)}, u32[]{:S(2)}) collective-permute-start(f32[1,2048]{1,0:T(1,128)S(1)} %add.7.after_ref.term_ref), channel_id=1, source_target_pairs={{0,4},{2,6},{4,0},{6,2},{1,5},{3,7},{5,1},{7,3},{8,12},{10,14},{12... | collective-permute-start | bytes 24584 | tf_op jit(solution)/shard_map/ppermute | solution.py:499
  30.5 1.9 %collective-permute-done.6.other_ref = f32[1,2048]{1,0:T(1,128)S(1)} collective-permute-done((f32[1,2048]{1,0:T(1,128)S(1)}, f32[1,2048]{1,0:T(1,128)S(1)}, u32[]{:S(2)}, u32[]{:S(2)}) %collective-permute-start.6) | collective-permute-done | bytes 8224 | tf_op jit(solution)/shard_map/ppermute | solution.py:499
  32.5 0.0 collective-permute-done.7.upstream_hbm
  32.5 0.0 collective-permute-done.1.both_ref
  32.5 0.0 collective-permute-done.early_ref
  32.5 0.0 collective-permute-done.5.halo_ref
  32.5 2.1 %project.1 = (bf16[64,1024]{1,0:T(8,128)(2,1)}, f32[1,2048]{1,0:T(1,128)}, bf16[64,2048]{1,0:T(8,128)(2,1)}) custom-call(bf16[1536,128]{1,0:T(8,128)(2,1)S(1)} %collective-permute-done.early_ref, bf16[1024,128]{1,0:T(8,128)(2,1)S(1)} %collective-permute-done.1.both_ref, bf16[40,2048]{1,0:T(8,128)(2,1)S(1)} %collective-permute-done.5.halo_ref, ...), custom_call_target="tpu_custom_call" | custom-call | flops 268435456 | bytes 4194304 | tf_op jit(solution)/shard_map/project/pallas_call | solution.py:482
  (3 shorter events, 0.0 us)
Async XLA Ops:
  3.8 7.6 %copy-start = (f32[1,2048]{1,0:T(1,128)S(1)}, f32[1,2048]{1,0:T(1,128)}, u32[]{:S(2)}) copy-start(f32[1,2048]{1,0:T(1,128)} %gain_ref.3) | copy-start | bytes 24580
  3.8 17.7 %collective-permute-start.2 = (bf16[136,2048]{1,0:T(8,128)(2,1)S(1)}, bf16[136,2048]{1,0:T(8,128)(2,1)S(1)}, u32[]{:S(2)}, u32[]{:S(2)}) collective-permute-start(bf16[136,2048]{1,0:T(8,128)(2,1)S(1)} %get-tuple-element.25), channel_id=1, source_target_pairs={{2,0},{4,2},{6,4},{3,1},{5,3},{7,5},{10,8},{12,10},{14,12},{11,9},... | collective-permute-start | bytes 1671176 | tf_op jit(solution)/shard_map/ppermute | solution.py:35
  5.1 27.4 %collective-permute-start = (bf16[1536,128]{1,0:T(8,128)(2,1)S(1)}, bf16[1536,128]{1,0:T(8,128)(2,1)S(1)}, u32[]{:S(2)}, u32[]{:S(2)}) collective-permute-start(bf16[1536,128]{1,0:T(8,128)(2,1)S(1)} %get-tuple-element.19), channel_id=1, source_target_pairs={{0,8},{8,16},{16,24},{24,0},{1,9},{9,17},{17,25},{25,1},{2,10},{10... | collective-permute-start | bytes 1179656 | tf_op jit(solution)/shard_map/ppermute | solution.py:40
  12.9 19.5 %collective-permute-start.7 = (bf16[64,2048]{1,0:T(8,128)(2,1)S(1)}, bf16[64,2048]{1,0:T(8,128)(2,1)S(1)}, u32[]{:S(2)}, u32[]{:S(2)}) collective-permute-start(bf16[64,2048]{1,0:T(8,128)(2,1)S(1)} %get-tuple-element.31), channel_id=1, source_target_pairs={{0,24},{8,0},{16,8},{24,16},{1,25},{9,1},{17,9},{25,17},{2,26},{10... | collective-permute-start | bytes 786440 | tf_op jit(solution)/shard_map/ppermute | solution.py:40
  14.0 18.5 %collective-permute-start.1 = (bf16[1024,128]{1,0:T(8,128)(2,1)S(1)}, bf16[1024,128]{1,0:T(8,128)(2,1)S(1)}, u32[]{:S(2)}, u32[]{:S(2)}) collective-permute-start(bf16[1024,128]{1,0:T(8,128)(2,1)S(1)} %get-tuple-element.24.after_ref), channel_id=1, source_target_pairs={{0,8},{8,16},{16,24},{24,0},{1,9},{9,17},{17,25},{25,1},{2,10},{10... | collective-permute-start | bytes 786440 | tf_op jit(solution)/shard_map/ppermute | solution.py:40
  15.0 1.2 %collective-permute-start.3 = (f32[1,2048]{1,0:T(1,128)S(1)}, f32[1,2048]{1,0:T(1,128)S(1)}, u32[]{:S(2)}, u32[]{:S(2)}) collective-permute-start(f32[1,2048]{1,0:T(1,128)S(1)} %get-tuple-element.30), channel_id=1, source_target_pairs={{0,1},{1,0},{2,3},{3,2},{4,5},{5,4},{6,7},{7,6},{8,9},{9,8},{10,11... | collective-permute-start | bytes 24584 | tf_op jit(solution)/shard_map/ppermute | solution.py:499
  16.2 5.3 %collective-permute-start.4 = (f32[1,2048]{1,0:T(1,128)S(1)}, f32[1,2048]{1,0:T(1,128)S(1)}, u32[]{:S(2)}, u32[]{:S(2)}) collective-permute-start(f32[1,2048]{1,0:T(1,128)S(1)} %add.6), channel_id=1, source_target_pairs={{0,2},{2,0},{4,6},{6,4},{1,3},{3,1},{5,7},{7,5},{8,10},{10,8},{12,... | collective-permute-start | bytes 24584 | tf_op jit(solution)/shard_map/ppermute | solution.py:499
  23.0 9.4 %collective-permute-start.5 = (bf16[40,2048]{1,0:T(8,128)(2,1)S(1)}, bf16[40,2048]{1,0:T(8,128)(2,1)S(1)}, u32[]{:S(2)}, u32[]{:S(2)}) collective-permute-start(bf16[40,2048]{1,0:T(8,128)(2,1)S(1)} %attend_halo.1), channel_id=1, source_target_pairs={{0,10},{2,12},{4,14},{8,18},{10,20},{12,22},{16,26},{18,28},{20,30... | collective-permute-start | bytes 491528 | tf_op jit(solution)/shard_map/ppermute | solution.py:519
  27.8 4.6 %collective-permute-start.6 = (f32[1,2048]{1,0:T(1,128)S(1)}, f32[1,2048]{1,0:T(1,128)S(1)}, u32[]{:S(2)}, u32[]{:S(2)}) collective-permute-start(f32[1,2048]{1,0:T(1,128)S(1)} %add.7.after_ref.term_ref), channel_id=1, source_target_pairs={{0,4},{2,6},{4,0},{6,2},{1,5},{3,7},{5,1},{7,3},{8,12},{10,14},{12... | collective-permute-start | bytes 24584 | tf_op jit(solution)/shard_map/ppermute | solution.py:499

commit v12 on v10

--- a/solution.py
+++ b/solution.py
@@ -132,46 +132,11 @@
     return [high, middle, value - high - middle]
 
 
-def early_kernel(
-    rows, chunks, offsets_hbm, q_hbm, k_hbm, v_hbm, cotangent_hbm, stashed_hbm,
-    sent_ref, early_ref, more_ref, q_late_ref, k_ref, v_ref, cotangent_ref, stashed_ref,
-    offsets_ref, bias, sems, offsets_sem,
-):
-    half = rows // 2
-    head, tail = pl.ds(0, half), pl.ds(half, half)
-    offsets_copy = load(offsets_hbm, offsets_ref, offsets_sem.at[0])
-    arrays = (
-        (k_hbm.at[head], k_ref.at[head]),
-        (q_hbm.at[head], sent_ref.at[head]),
-        (v_hbm.at[head], v_ref.at[head]),
-    )
-    copies = load_chunks(arrays, chunks, sems)
-    later = (
-        (k_hbm.at[tail], k_ref.at[tail]),
-        (v_hbm.at[tail], v_ref.at[tail]),
-        (q_hbm.at[tail], q_late_ref),
-        (cotangent_hbm, cotangent_ref),
-        (stashed_hbm, stashed_ref),
-    )
-    rest = []
-    offsets_copy.wait()
-    start = lax.axis_index("seq") * rows
-    bias[...] = mask_bias(offsets_ref, start, start, lambda key, query: key <= query)
-    pairs = k_ref.shape[1] // LANES
-    split = early_ref.shape[0] // LANES
-
-    def arrive(pair):
-        per_chunk = pairs // chunks
-        if pair % per_chunk == 0:
-            for copy in copies[pair // per_chunk]:
-                copy.wait()
-        if pair == per_chunk:
-            for i, (source, target) in enumerate(later):
-                rest.append(load(source, target, offsets_sem.at[i + 1]))
+def early_pairs(pairs, arrive, q_at, k_at, v_at, bias, sent_ref, early_ref):
+    half = bias.shape[0]
 
     def score(pair):
-        scores = dot_nt(k_ref[head, at(pair)], split_heads(sent_ref[head, at(pair)]))
-        return scores, with_ones(jnp.transpose(v_ref[head, at(pair)]))
+        return dot_nt(k_at(pair), split_heads(q_at(pair))), with_ones(jnp.transpose(v_at(pair)))
 
     def top(pair, scores, values_t):
         return scores, tops(scores + bias[...]), values_t
@@ -182,8 +147,7 @@
 
     def finish(pair, top, mixed):
         total = mixed[LANES : LANES + 1]
-        target, place = (early_ref, pair) if pair < split else (more_ref, pair - split)
-        target[at(place), :] = own_heads(mixed, 1.0 / total).astype(jnp.bfloat16)
+        early_ref[at(pair), :] = own_heads(mixed, 1.0 / total).astype(jnp.bfloat16)
         lse = top + jnp.log(total)
         terms = three_terms(lse[:, :half]) + three_terms(lse[:, half:])
         terms.append(jnp.zeros((EXTRA - 6, LANES), jnp.float32))
@@ -191,12 +155,85 @@
         return ()
 
     over_pairs(pairs, (score, top, weigh, finish), LAGS, arrive)
-    for copy in rest:
+
+
+def early_kernel(
+    rows, chunk, offsets_hbm, q_hbm, k_hbm, v_hbm,
+    sent_ref, early_ref, q_more_ref, k_ref, v_ref, bias,
+    offsets_ref, sems, offsets_sem,
+):
+    half = rows // 2
+    head = pl.ds(0, half)
+    width = sent_ref.shape[1]
+    offsets_copy = load(offsets_hbm, offsets_ref, offsets_sem)
+    copies = []
+    for i, begin in enumerate(range(0, k_ref.shape[1], chunk)):
+        columns = pl.ds(begin, chunk)
+        q_ref = sent_ref.at[head, columns] if begin < width else q_more_ref.at[:, pl.ds(begin - width, chunk)]
+        copies.append(
+            [
+                load(k_hbm.at[head, columns], k_ref.at[:, columns], sems.at[0, i]),
+                load(q_hbm.at[head, columns], q_ref, sems.at[1, i]),
+                load(v_hbm.at[head, columns], v_ref.at[:, columns], sems.at[2, i]),
+            ]
+        )
+    offsets_copy.wait()
+    start = lax.axis_index("seq") * rows
+    bias[...] = mask_bias(offsets_ref, start, start, lambda key, query: key <= query)
+
+    def arrive(pair):
+        if pair * LANES % chunk == 0:
+            for copy in copies[pair * LANES // chunk]:
+                copy.wait()
+
+    early_pairs(
+        width // LANES,
+        arrive,
+        lambda pair: sent_ref[head, at(pair)],
+        lambda pair: k_ref[:, at(pair)],
+        lambda pair: v_ref[:, at(pair)],
+        bias,
+        sent_ref,
+        early_ref,
+    )
+    for group in copies[width // chunk :]:
+        for copy in group:
+            copy.wait()
+
+
+def more_kernel(
+    q_ref, k_ref, v_ref, bias, q_hbm, k_hbm, v_hbm, cotangent_hbm, stashed_hbm, after_ref,
+    sent_ref, early_ref, q_late_ref, k_tail_ref, v_tail_ref, cotangent_ref, stashed_ref, sems,
+):
+    half, width = q_ref.shape
+    tail = pl.ds(half, half)
+    later = (
+        (k_hbm.at[tail], k_tail_ref),
+        (v_hbm.at[tail], v_tail_ref),
+        (q_hbm.at[tail], q_late_ref),
+        (cotangent_hbm, cotangent_ref),
+        (stashed_hbm, stashed_ref),
+    )
+    copies = [load(source, target, sems.at[i]) for i, (source, target) in enumerate(later)]
+    begin = k_ref.shape[1] - width
+    sent_ref[pl.ds(0, half), :] = q_ref[...]
+    early_pairs(
+        width // LANES,
+        lambda pair: None,
+        lambda pair: q_ref[:, at(pair)],
+        lambda pair: k_ref[:, pl.ds(begin + pair * LANES, LANES)],
+        lambda pair: v_ref[:, pl.ds(begin + pair * LANES, LANES)],
+        bias,
+        sent_ref,
+        early_ref,
+    )
+    for copy in copies:
         copy.wait()
 
 
 def late_kernel(
-    rows, offsets_hbm, weight_hbm, q_ref, k_ref, v_ref, early_ref, both_ref, next_ref, weight_ref,
+    rows, offsets_hbm, weight_hbm, q_ref, k_ref, v_ref, k_tail_ref, v_tail_ref, early_ref,
+    both_ref, next_ref, weight_ref,
     offsets_ref, own_bias, other_bias, own, other, sems,
 ):
     offsets_copy = load(offsets_hbm, offsets_ref, sems.at[8])
@@ -223,8 +260,9 @@
     parts = []
 
     def score(pair):
-        scores = dot_nt(k_ref[:, at(pair)], split_heads(q_ref[:, at(pair)]))
-        return scores, with_ones(jnp.transpose(v_ref[:, at(pair)]))
+        keys = jnp.concatenate([k_ref[:, at(pair)], k_tail_ref[:, at(pair)]], axis=0)
+        values = jnp.concatenate([v_ref[:, at(pair)], v_tail_ref[:, at(pair)]], axis=0)
+        return dot_nt(keys, split_heads(q_ref[:, at(pair)])), with_ones(jnp.transpose(values))
 
     def top(pair, scores, values_t):
         scores = jnp.maximum(scores[:half] + other_bias[...], scores[half:] + own_bias[...])
@@ -251,21 +289,24 @@
         copy.wait()
 
 
-def halo_kernel(q_ref, k_ref, v_ref, bias, after_ref, out_ref):
+def halo_kernel(q_ref, q_more_ref, k_ref, v_ref, bias, term_ref, other_ref, out_ref, sum_ref):
+    sum_ref[...] = term_ref[...] + other_ref[...]
     half = bias.shape[0]
     molecules = half // POOL
-    tail = pl.ds(half, half)
     pooling = pool_matrix(half)
     pairs = k_ref.shape[1] // LANES
-    parts = []
+    split = q_ref.shape[1] // LANES
+    parts, shares = [], []
+
+    def sent(pair, rows):
+        return q_ref[rows, at(pair)] if pair < split else q_more_ref[rows, at(pair - split)]
 
     def score(pair):
-        queries = split_heads(q_ref[pl.ds(0, half), at(pair)])
-        scores = dot_nt(k_ref[tail, at(pair)], queries)
-        return scores, with_ones(jnp.transpose(v_ref[tail, at(pair)]))
+        scores = dot_nt(k_ref[:, at(pair)], split_heads(sent(pair, pl.ds(0, half))))
+        return scores, with_ones(jnp.transpose(v_ref[:, at(pair)]))
 
     def top(pair, scores, values_t):
-        terms = q_ref[pl.ds(half, EXTRA), at(pair)].astype(jnp.float32)
+        terms = sent(pair, pl.ds(half, EXTRA)).astype(jnp.float32)
         lse = jnp.concatenate(
             [terms[0:1] + terms[1:2] + terms[2:3], terms[3:4] + terms[4:5] + terms[5:6]], axis=1
         )
@@ -273,22 +314,24 @@
 
     def weigh(pair, scores, top, lse, values_t):
         weights = jnp.exp((scores + bias[...]) - top).astype(jnp.bfloat16)
-        mixed = dot_nn(values_t, weights)
-        return mixed, jnp.exp(lse - top)
+        return dot_nn(values_t, weights), jnp.exp(lse - top)
 
     def finish(pair, mixed, kept):
         inverse = 1.0 / (mixed[LANES : LANES + 1] + kept)
         parts.append(own_heads(mixed, inverse).astype(jnp.bfloat16))
-        if len(parts) == 4:
-            pooled = dot_nt(pooling, jnp.concatenate(parts, axis=0)).astype(jnp.bfloat16)
-            out_ref[pl.ds(0, molecules), pl.ds((pair - 3) * LANES, 4 * LANES)] = pooled
-            parts.clear()
         share = kept * inverse
         high = share.astype(jnp.bfloat16).astype(jnp.float32)
         low = share - high
-        shares = [high[:, :half], low[:, :half], high[:, half:], low[:, half:]]
-        shares.append(jnp.zeros((EXTRA - 4, LANES), jnp.float32))
-        out_ref[pl.ds(molecules, EXTRA), at(pair)] = jnp.concatenate(shares, axis=0).astype(jnp.bfloat16)
+        shares.extend([high[:, :half], low[:, :half], high[:, half:], low[:, half:]])
+        if len(parts) == 4:
+            pooled = dot_nt(pooling, jnp.concatenate(parts, axis=0)).astype(jnp.bfloat16)
+            for i in range(4):
+                place = pl.ds((pair - 3 + i) * molecules, molecules)
+                out_ref[place, :] = pooled[:, i * LANES : (i + 1) * LANES]
+            place = pl.ds(pairs * molecules + (pair - 3) * 4, 16)
+            out_ref[place, :] = jnp.concatenate(shares, axis=0).astype(jnp.bfloat16)
+            parts.clear()
+            shares.clear()
         return ()
 
     over_pairs(pairs, (score, top, weigh, finish), LAGS, lambda pair: None)
@@ -335,9 +378,12 @@
     first = lax.axis_index("seq") == 0
     squares, product, parts = 0.0, 0.0, []
     for pair in range(features // LANES):
-        shares = halo_ref[molecules:, at(pair)].astype(jnp.float32)
-        share_a = jnp.where(first, 1.0, shares[0:1] + shares[1:2])
-        share_b = jnp.where(first, 1.0, shares[2:3] + shares[3:4])
+        if pair % 4 == 0:
+            place = pl.ds(features // LANES * molecules + pair * 4, 16)
+            shares = halo_ref[place, :].astype(jnp.float32)
+        row = pair % 4 * 4
+        share_a = jnp.where(first, 1.0, shares[row : row + 1] + shares[row + 1 : row + 2])
+        share_b = jnp.where(first, 1.0, shares[row + 2 : row + 3] + shares[row + 3 : row + 4])
         begin = pair * LANES
         if begin < first_part:
             early = early_ref[pl.ds(begin, LANES), :].astype(jnp.float32)
@@ -347,7 +393,10 @@
         if len(parts) == 8:
             columns = pl.ds((pair - 3) * LANES, 4 * LANES)
             mean = dot_nt(pooling, jnp.concatenate(parts, axis=0).astype(jnp.bfloat16))
-            upper = mean + halo_ref[:molecules, columns].astype(jnp.float32)
+            place = pl.ds((pair - 3) * molecules, 4 * molecules)
+            halo = halo_ref[place, :].astype(jnp.float32)
+            halo = [halo[i * molecules : (i + 1) * molecules] for i in range(4)]
+            upper = mean + jnp.concatenate(halo, axis=1)
             place = features - first_part + (pair - 3) * molecules
             lower = [both_ref[pl.ds(place + i * molecules, molecules), :] for i in range(4)]
             lower = jnp.concatenate(lower, axis=1)
@@ -381,48 +430,70 @@
     return pltpu.CompilerParams(vmem_limit_bytes=24 * 2**20)
 
 
-def attend_early(queries, keys, values, offsets, cotangent, stashed, chunks):
-    rows, width = queries.shape
-    half = rows // 2
-    soon = width // (4 * LANES) * 3 // 4 * 4 * LANES
-    bf16 = lambda *shape: jax.ShapeDtypeStruct(shape, jnp.bfloat16)
+def bf16(*shape):
+    return jax.ShapeDtypeStruct(shape, jnp.bfloat16)
+
+
+def attend_early(queries, keys, values, offsets, width):
+    rows, features = queries.shape
+    half, chunk = rows // 2, 2 * LANES
     return pl.pallas_call(
-        functools.partial(early_kernel, rows, chunks),
-        in_specs=[HBM] * 6,
-        out_specs=[VMEM] * 8,
+        functools.partial(early_kernel, rows, chunk),
+        in_specs=[HBM] * 4,
+        out_specs=[VMEM] * 6,
         out_shape=[
             bf16(half + EXTRA, width),
-            bf16(soon, half),
-            bf16(width - soon, half),
-            bf16(half, width),
-            bf16(rows, width),
-            bf16(rows, width),
+            bf16(width, half),
+            bf16(half, features - width),
+            bf16(half, features),
+            bf16(half, features),
+            jax.ShapeDtypeStruct((half, rows), jnp.float32),
+        ],
+        scratch_shapes=[
+            pltpu.SMEM(offsets.shape, jnp.int32),
+            pltpu.SemaphoreType.DMA((3, features // chunk)),
+            pltpu.SemaphoreType.DMA,
+        ],
+        cost_estimate=cost(4 * half * half * width, 6 * half * features, half * half * width // 64),
+        compiler_params=params(),
+        name="attend_early",
+    )(*in_hbm(offsets, queries, keys, values))
+
+
+def attend_more(q_more, k_head, v_head, bias, queries, keys, values, cotangent, stashed, after):
+    half, width = q_more.shape
+    features = keys.shape[1]
+    return pl.pallas_call(
+        more_kernel,
+        in_specs=[VMEM] * 4 + [HBM] * 5 + [ANY],
+        out_specs=[VMEM] * 7,
+        out_shape=[
+            bf16(half + EXTRA, width),
+            bf16(width, half),
+            bf16(half, features),
+            bf16(half, features),
+            bf16(half, features),
             bf16(*cotangent.shape),
             bf16(*stashed.shape),
         ],
-        scratch_shapes=[
-            pltpu.SMEM(offsets.shape, jnp.int32),
-            pltpu.VMEM((half, 2 * half), jnp.float32),
-            pltpu.SemaphoreType.DMA((3, chunks)),
-            pltpu.SemaphoreType.DMA((6,)),
-        ],
-        cost_estimate=cost(4 * half * half * width, 6 * rows * width, half * half * width // 64),
+        scratch_shapes=[pltpu.SemaphoreType.DMA((5,))],
+        cost_estimate=cost(4 * half * half * width, 6 * half * features, half * half * width // 64),
         compiler_params=params(),
-        name="attend_early",
-    )(*in_hbm(offsets, queries, keys, values, cotangent, stashed))
-
-
-def attend_late(queries, keys, values, offsets, weight, early):
+        name="attend_more",
+    )(q_more, k_head, v_head, bias, *in_hbm(queries, keys, values, cotangent, stashed), after)
+
+
+def attend_late(queries, k_head, v_head, k_tail, v_tail, offsets, weight, early):
     half, width = queries.shape
     rows = 2 * half
     return pl.pallas_call(
         functools.partial(late_kernel, rows),
-        in_specs=[HBM] * 2 + [VMEM] * 4,
+        in_specs=[HBM] * 2 + [VMEM] * 6,
         out_specs=[VMEM] * 3,
         out_shape=[
-            jax.ShapeDtypeStruct((early.shape[0] + width // POOL, half), jnp.bfloat16),
+            bf16(early.shape[0] + width // POOL, half),
             jax.ShapeDtypeStruct((half, rows), jnp.float32),
-            jax.ShapeDtypeStruct(weight.shape, weight.dtype),
+            bf16(*weight.shape),
         ],
         scratch_shapes=[
             pltpu.SMEM(offsets.shape, jnp.int32),
@@ -435,20 +506,23 @@
         cost_estimate=cost(8 * half * half * width, 10 * half * width, half * half * width // 64),
         compiler_params=params(),
         name="attend_late",
-    )(*in_hbm(offsets, weight), queries, keys, values, early)
-
-
-def attend_halo(sent, keys, values, bias, after):
-    half, width = bias.shape[0], keys.shape[1]
+    )(*in_hbm(offsets, weight), queries, k_head, v_head, k_tail, v_tail, early)
+
+
+def attend_halo(sent, sent_more, keys, values, bias, term, other):
+    half, width = keys.shape
     return pl.pallas_call(
         halo_kernel,
-        in_specs=[VMEM] * 4 + [ANY],
-        out_specs=VMEM,
-        out_shape=jax.ShapeDtypeStruct((half // POOL + EXTRA, width), jnp.bfloat16),
+        in_specs=[VMEM] * 7,
+        out_specs=[VMEM] * 2,
+        out_shape=[
+            bf16(width // LANES * (half // POOL + 4), LANES),
+            jax.ShapeDtypeStruct(term.shape, term.dtype),
+        ],
         cost_estimate=cost(4 * half * half * width, 6 * half * width, half * half * width // 64),
         compiler_params=params(),
         name="attend_halo",
-    )(sent, keys, values, bias, after)
+    )(sent, sent_more, keys, values, bias, term, other)
 
 
 def backward(slot, cotangent, weight, gain, stashed, after):
@@ -497,7 +571,7 @@
 
 def sum_rounds():
     rounds = []
-    for axis in ("rep", "seq"):
+    for axis in ("seq", "rep"):
         count = lax.axis_size(axis)
         if count & (count - 1):
             return []
@@ -522,20 +596,28 @@
     def partner(term, index):
         return swapped(term, *rounds[index]) if rounds else jnp.zeros_like(term)
 
-    sent, early, more, q_late, keys, values, cotangent, stashed = attend_early(
-        queries, keys, values, offsets, cotangent[0, 0], stashed[0, 0], 4
-    )
+    features = queries.shape[1]
+    width = features // LANES * 12 // 16 * LANES
+    sent, early, q_more, k_head, v_head, bias = attend_early(queries, keys, values, offsets, width)
     arrived = shifted(sent, "seq", -1)
     early = passed_along(early, "section", 1)
-    both, next_bias, weight = attend_late(q_late, keys, values, offsets, weight[0], more)
+    sent, more, q_late, k_tail, v_tail, cotangent, stashed = attend_more(
+        q_more, k_head, v_head, bias, queries, keys, values, cotangent[0, 0], stashed[0, 0], sent
+    )
+    arrived_more = shifted(sent, "seq", -1)
+    both, next_bias, weight = attend_late(
+        q_late, k_head, v_head, k_tail, v_tail, offsets, weight[0], more
+    )
     slot = jnp.broadcast_to(slot, (1, LANES))
     dinput, term = backward(slot, cotangent, weight, gain, stashed, both)
     both = passed_along(both, "section", 1)
     upstream = passed_along(dinput, "section", -1)
     term = term if rounds else lax.psum(term, ("rep", "seq"))
-    term = term + partner(term, 0)
+    halo, term = attend_halo(
+        arrived, arrived_more, k_tail, v_tail, next_bias, term, partner(term, 0)
+    )
+    halo = onward(halo)
     term = term + partner(term, 1)
-    halo = onward(attend_halo(arrived, keys, values, next_bias, term))
     mol_keys, update, upstream = project(
         early, both, halo, gain, weight, term, partner(term, 2), upstream
     )

time: 34.7 us -> 37 us (1.066)
  the two profiles are of different devices: /device:TPU:0 before, /device:TPU:16 now
where the time goes in v12:
time: 37 us; the launch traced here: 36.7 us
  starting transfers between devices  14.5 us (39%)
  Pallas kernels  12.8 us (35%)
  waiting for transfers between devices  7.96 us (22%)
  between operations  1.39 us (4%)
    ppermute x3, starting transfers between devices, passed_along(): lax.ppermute(value, axis, [(i, (i + steps) % count) for i in range(count)])  5.42 us
    ppermute x3, waiting for transfers between devices, swapped(): lax.ppermute(value, axis, [(i, i ^ distance) for i in range(lax.axis_size...  5.1 us
    ppermute x2, starting transfers between devices, shifted(): lax.ppermute(value, axis, [(i, i + steps) for i in range(first, last)])  4.71 us
    pallas_call x1, Pallas kernels, attend_early(): pl.pallas_call(functools.partial(early_kernel, rows, chunk), in_specs=[HB...  2.99 us
    ppermute x3, waiting for transfers between devices, passed_along(): lax.ppermute(value, axis, [(i, (i + steps) % count) for i in range(count)])  2.86 us
    ppermute x1, starting transfers between devices, onward(): return lax.ppermute(value, ('section', 'seq'), route)  2.6 us
    pallas_call x1, Pallas kernels, attend_late(): pl.pallas_call(functools.partial(late_kernel, rows), in_specs=[HBM] * 2 +...  2.56 us
    pallas_call x1, Pallas kernels, attend_halo(): pl.pallas_call(halo_kernel, in_specs=[VMEM] * 7, out_specs=[VMEM] * 2, ou...  2.04 us
  transfers between devices with their start and end apart: 9, of which 3 were waited for; matrix products, arithmetic and copies ran while one was open for 0% of the time, Pallas kernels for 21%

profile of v12, /device:TPU:16, one launch (start us, length us, event | category | flops | bytes accessed | tf_op | source)
XLA Modules:
  0.0 36.7 jit_solution(3905761191523177969)
XLA Ops:
  0.6 3.0 %attend_early.1 = (bf16[136,1536]{1,0:T(8,128)(2,1)S(1)}, bf16[1536,128]{1,0:T(8,128)(2,1)S(1)}, bf16[128,512]{1,0:T(8,128)(2,1)S(1)}, bf16[128,2048]{1,0:T(8,12...) custom-call(s32[1,8]{1,0:T(1,128)} %bitcast.20, bf16[256,2048]{1,0:T(8,128)(2,1)} %bitcast.12, ...), custom_call_target="tpu_custom_call" | custom-call | flops 100663296 | bytes 1572864 | tf_op jit(solution)/shard_map/attend_early/pallas_call | solution.py:440
  3.6 2.4 %collective-permute-start.2 = (bf16[136,1536]{1,0:T(8,128)(2,1)S(1)}, bf16[136,1536]{1,0:T(8,128)(2,1)S(1)}, u32[]{:S(2)}, u32[]{:S(2)}) collective-permute-start(bf16[136,1536]{1,0:T(8,128)(2,1)S(1)} %get-tuple-element.31.after_ref), channel_id=1, source_target_pairs={{2,0},{4,2},{6,4},{3,1},{5,3},{7,5},{10,8},{12,10},{14,12},{11,9},... | collective-permute-start | bytes 1253384 | tf_op jit(solution)/shard_map/ppermute | solution.py:35
  6.0 1.5 %collective-permute-start = (bf16[1536,128]{1,0:T(8,128)(2,1)S(1)}, bf16[1536,128]{1,0:T(8,128)(2,1)S(1)}, u32[]{:S(2)}, u32[]{:S(2)}) collective-permute-start(bf16[1536,128]{1,0:T(8,128)(2,1)S(1)} %get-tuple-element.26), channel_id=1, source_target_pairs={{0,8},{8,16},{16,24},{24,0},{1,9},{9,17},{17,25},{25,1},{2,10},{10... | collective-permute-start | bytes 1179656 | tf_op jit(solution)/shard_map/ppermute | solution.py:40
  7.5 1.7 %attend_more.1 = (bf16[136,512]{1,0:T(8,128)(2,1)S(1)}, bf16[512,128]{1,0:T(8,128)(2,1)S(1)}, bf16[128,2048]{1,0:T(8,128)(2,1)S(1)}, bf16[128,2048]{1,0:T(8,128)...) custom-call(bf16[128,512]{1,0:T(8,128)(2,1)S(1)} %get-tuple-element.27.q_re, ...), custom_call_target="tpu_custom_call" | custom-call | flops 33554432 | bytes 1572864 | tf_op jit(solution)/shard_map/attend_more/pallas_call | solution.py:466
  9.2 0.0 copy-start
  9.2 2.4 %collective-permute-start.3 = (bf16[136,512]{1,0:T(8,128)(2,1)S(1)}, bf16[136,512]{1,0:T(8,128)(2,1)S(1)}, u32[]{:S(2)}, u32[]{:S(2)}) collective-permute-start(bf16[136,512]{1,0:T(8,128)(2,1)S(1)} %get-tuple-element.37), channel_id=1, source_target_pairs={{2,0},{4,2},{6,4},{3,1},{5,3},{7,5},{10,8},{12,10},{14,12},{11,9},... | collective-permute-start | bytes 417800 | tf_op jit(solution)/shard_map/ppermute | solution.py:35
  11.6 2.6 %attend_late.1 = (bf16[1024,128]{1,0:T(8,128)(2,1)S(1)}, f32[128,256]{1,0:T(8,128)S(1)}, bf16[2048,1024]{1,0:T(8,128)(2,1)S(1)}) custom-call(s32[1,8]{1,0:T(1,128)} %bitcast.21, bf16[2048,1024]{1,0:T(8,128)(2,1)} %bitcast.11, bf16[128,2048]{1,0:T(8,128)(2,1)S(1)} %get-tuple-element.32.q_ref, bf16[128,2048]{1,0:T(8,128)(2,1)S(1)} %get-tuple-element.28.k_ref, ...), custom_call_target="tpu_custom_call" | custom-call | flops 268435456 | bytes 2621440 | tf_op jit(solution)/shard_map/attend_late/pallas_call | solution.py:489
  14.8 0.0 copy-done
  14.8 1.6 %backward.1 = (bf16[64,2048]{1,0:T(8,128)(2,1)S(1)}, f32[1,2048]{1,0:T(1,128)S(1)}) custom-call(s32[1,128]{1,0:T(1,128)S(1)} %broadcast_in_dim.14.slot_ref, bf16[64,1024]{1,0:T(8,128)(2,1)S(1)} %get-tuple-element.39.cotangent_ref, bf16[2048,1024]{1,0:T(8,128)(2,1)S(1)} %get-tuple-element.40.weight_ref, f32[1,2048]{1,0:T(1,128)S(1)} %copy-done, ...), custom_call_target="tpu_custom_call" | custom-call | flops 268435456 | bytes 4194304 | tf_op jit(solution)/shard_map/backward/pallas_call | solution.py:531
  16.4 1.7 %collective-permute-start.4 = (f32[1,2048]{1,0:T(1,128)S(1)}, f32[1,2048]{1,0:T(1,128)S(1)}, u32[]{:S(2)}, u32[]{:S(2)}) collective-permute-start(f32[1,2048]{1,0:T(1,128)S(1)} %get-tuple-element.42.term_ref), channel_id=1, source_target_pairs={{0,2},{2,0},{4,6},{6,4},{1,3},{3,1},{5,7},{7,5},{8,10},{10,8},{12,... | collective-permute-start | bytes 24584 | tf_op jit(solution)/shard_map/ppermute | solution.py:569
  18.1 1.5 %collective-permute-start.1 = (bf16[1024,128]{1,0:T(8,128)(2,1)S(1)}, bf16[1024,128]{1,0:T(8,128)(2,1)S(1)}, u32[]{:S(2)}, u32[]{:S(2)}) collective-permute-start(bf16[1024,128]{1,0:T(8,128)(2,1)S(1)} %get-tuple-element.36.after_ref), channel_id=1, source_target_pairs={{0,8},{8,16},{16,24},{24,0},{1,9},{9,17},{17,25},{25,1},{2,10},{10... | collective-permute-start | bytes 786440 | tf_op jit(solution)/shard_map/ppermute | solution.py:40
  19.6 0.6 %collective-permute-done.4.other_ref = f32[1,2048]{1,0:T(1,128)S(1)} collective-permute-done((f32[1,2048]{1,0:T(1,128)S(1)}, f32[1,2048]{1,0:T(1,128)S(1)}, u32[]{:S(2)}, u32[]{:S(2)}) %collective-permute-start.4) | collective-permute-done | bytes 8224 | tf_op jit(solution)/shard_map/ppermute | solution.py:569
  20.1 2.4 %collective-permute-start.8 = (bf16[64,2048]{1,0:T(8,128)(2,1)S(1)}, bf16[64,2048]{1,0:T(8,128)(2,1)S(1)}, u32[]{:S(2)}, u32[]{:S(2)}) collective-permute-start(bf16[64,2048]{1,0:T(8,128)(2,1)S(1)} %get-tuple-element.45), channel_id=1, source_target_pairs={{0,24},{8,0},{16,8},{24,16},{1,25},{9,1},{17,9},{25,17},{2,26},{10... | collective-permute-start | bytes 786440 | tf_op jit(solution)/shard_map/ppermute | solution.py:40
  22.5 0.0 collective-permute-done.3.q_more_ref
  22.5 0.0 collective-permute-done.2.q_ref
  22.5 2.0 %attend_halo.1 = (bf16[576,128]{1,0:T(8,128)(2,1)S(1)}, f32[1,2048]{1,0:T(1,128)S(1)}) custom-call(bf16[136,1536]{1,0:T(8,128)(2,1)S(1)} %collective-permute-done.2.q_ref, bf16[136,512]{1,0:T(8,128)(2,1)S(1)} %collective-permute-done.3.q_more_ref, bf16[128,2048]{1,0:T(8,128)(2,1)S(1)} %get-tuple-element.33.k_tail_ref.k_ref, ...), custom_call_target="tpu_custom_call" | custom-call | flops 134217728 | bytes 1572864 | tf_op jit(solution)/shard_map/attend_halo/pallas_call | solution.py:514
  24.6 2.6 %collective-permute-start.5 = (bf16[576,128]{1,0:T(8,128)(2,1)S(1)}, bf16[576,128]{1,0:T(8,128)(2,1)S(1)}, u32[]{:S(2)}, u32[]{:S(2)}) collective-permute-start(bf16[576,128]{1,0:T(8,128)(2,1)S(1)} %get-tuple-element.43), channel_id=1, source_target_pairs={{0,10},{2,12},{4,14},{8,18},{10,20},{12,22},{16,26},{18,28},{20,30... | collective-permute-start | bytes 442376 | tf_op jit(solution)/shard_map/ppermute | solution.py:589
  27.2 0.1 collective-permute-start.6
  27.2 4.5 %collective-permute-done.6 = f32[1,2048]{1,0:T(1,128)S(1)} collective-permute-done((f32[1,2048]{1,0:T(1,128)S(1)}, f32[1,2048]{1,0:T(1,128)S(1)}, u32[]{:S(2)}, u32[]{:S(2)}) %collective-permute-start.6) | collective-permute-done | bytes 8224 | tf_op jit(solution)/shard_map/ppermute | solution.py:569
  31.8 0.1 collective-permute-start.7
  31.9 0.0 collective-permute-done.1.both_ref
  31.9 2.9 %collective-permute-done.8.upstream_hbm = bf16[64,2048]{1,0:T(8,128)(2,1)S(1)} collective-permute-done((bf16[64,2048]{1,0:T(8,128)(2,1)S(1)}, bf16[64,2048]{1,0:T(8,128)(2,1)S(1)}, u32[]{:S(2)}, u32[]{:S(2)}) %collective-permute-start.8) | collective-permute-done | bytes 262176 | tf_op jit(solution)/shard_map/ppermute | solution.py:40
  34.7 0.0 collective-permute-done.early_ref
  34.7 0.0 collective-permute-done.7.other_ref
  34.7 0.0 collective-permute-done.5.halo_ref
  34.7 1.9 %project.1 = (bf16[64,1024]{1,0:T(8,128)(2,1)}, f32[1,2048]{1,0:T(1,128)}, bf16[64,2048]{1,0:T(8,128)(2,1)}) custom-call(bf16[1536,128]{1,0:T(8,128)(2,1)S(1)} %collective-permute-done.early_ref, bf16[1024,128]{1,0:T(8,128)(2,1)S(1)} %collective-permute-done.1.both_ref, bf16[576,128]{1,0:T(8,128)(2,1)S(1)} %collective-permute-done.5.halo_ref, ...), custom_call_target="tpu_custom_call" | custom-call | flops 268435456 | bytes 4194304 | tf_op jit(solution)/shard_map/project/pallas_call | solution.py:552
  (2 shorter events, 0.0 us)
Async XLA Ops:
  3.6 18.9 %collective-permute-start.2 = (bf16[136,1536]{1,0:T(8,128)(2,1)S(1)}, bf16[136,1536]{1,0:T(8,128)(2,1)S(1)}, u32[]{:S(2)}, u32[]{:S(2)}) collective-permute-start(bf16[136,1536]{1,0:T(8,128)(2,1)S(1)} %get-tuple-element.31.after_ref), channel_id=1, source_target_pairs={{2,0},{4,2},{6,4},{3,1},{5,3},{7,5},{10,8},{12,10},{14,12},{11,9},... | collective-permute-start | bytes 1253384 | tf_op jit(solution)/shard_map/ppermute | solution.py:35
  6.0 28.7 %collective-permute-start = (bf16[1536,128]{1,0:T(8,128)(2,1)S(1)}, bf16[1536,128]{1,0:T(8,128)(2,1)S(1)}, u32[]{:S(2)}, u32[]{:S(2)}) collective-permute-start(bf16[1536,128]{1,0:T(8,128)(2,1)S(1)} %get-tuple-element.26), channel_id=1, source_target_pairs={{0,8},{8,16},{16,24},{24,0},{1,9},{9,17},{17,25},{25,1},{2,10},{10... | collective-permute-start | bytes 1179656 | tf_op jit(solution)/shard_map/ppermute | solution.py:40
  9.2 5.6 %copy-start = (f32[1,2048]{1,0:T(1,128)S(1)}, f32[1,2048]{1,0:T(1,128)}, u32[]{:S(2)}) copy-start(f32[1,2048]{1,0:T(1,128)} %gain_ref.3) | copy-start | bytes 24580
  9.2 13.3 %collective-permute-start.3 = (bf16[136,512]{1,0:T(8,128)(2,1)S(1)}, bf16[136,512]{1,0:T(8,128)(2,1)S(1)}, u32[]{:S(2)}, u32[]{:S(2)}) collective-permute-start(bf16[136,512]{1,0:T(8,128)(2,1)S(1)} %get-tuple-element.37), channel_id=1, source_target_pairs={{2,0},{4,2},{6,4},{3,1},{5,3},{7,5},{10,8},{12,10},{14,12},{11,9},... | collective-permute-start | bytes 417800 | tf_op jit(solution)/shard_map/ppermute | solution.py:35
  16.4 3.7 %collective-permute-start.4 = (f32[1,2048]{1,0:T(1,128)S(1)}, f32[1,2048]{1,0:T(1,128)S(1)}, u32[]{:S(2)}, u32[]{:S(2)}) collective-permute-start(f32[1,2048]{1,0:T(1,128)S(1)} %get-tuple-element.42.term_ref), channel_id=1, source_target_pairs={{0,2},{2,0},{4,6},{6,4},{1,3},{3,1},{5,7},{7,5},{8,10},{10,8},{12,... | collective-permute-start | bytes 24584 | tf_op jit(solution)/shard_map/ppermute | solution.py:569
  18.1 13.8 %collective-permute-start.1 = (bf16[1024,128]{1,0:T(8,128)(2,1)S(1)}, bf16[1024,128]{1,0:T(8,128)(2,1)S(1)}, u32[]{:S(2)}, u32[]{:S(2)}) collective-permute-start(bf16[1024,128]{1,0:T(8,128)(2,1)S(1)} %get-tuple-element.36.after_ref), channel_id=1, source_target_pairs={{0,8},{8,16},{16,24},{24,0},{1,9},{9,17},{17,25},{25,1},{2,10},{10... | collective-permute-start | bytes 786440 | tf_op jit(solution)/shard_map/ppermute | solution.py:40
  20.1 14.6 %collective-permute-start.8 = (bf16[64,2048]{1,0:T(8,128)(2,1)S(1)}, bf16[64,2048]{1,0:T(8,128)(2,1)S(1)}, u32[]{:S(2)}, u32[]{:S(2)}) collective-permute-start(bf16[64,2048]{1,0:T(8,128)(2,1)S(1)} %get-tuple-element.45), channel_id=1, source_target_pairs={{0,24},{8,0},{16,8},{24,16},{1,25},{9,1},{17,9},{25,17},{2,26},{10... | collective-permute-start | bytes 786440 | tf_op jit(solution)/shard_map/ppermute | solution.py:40
  24.6 10.2 %collective-permute-start.5 = (bf16[576,128]{1,0:T(8,128)(2,1)S(1)}, bf16[576,128]{1,0:T(8,128)(2,1)S(1)}, u32[]{:S(2)}, u32[]{:S(2)}) collective-permute-start(bf16[576,128]{1,0:T(8,128)(2,1)S(1)} %get-tuple-element.43), channel_id=1, source_target_pairs={{0,10},{2,12},{4,14},{8,18},{10,20},{12,22},{16,26},{18,28},{20,30... | collective-permute-start | bytes 442376 | tf_op jit(solution)/shard_map/ppermute | solution.py:589
  27.2 4.6 %collective-permute-start.6 = (f32[1,2048]{1,0:T(1,128)S(1)}, f32[1,2048]{1,0:T(1,128)S(1)}, u32[]{:S(2)}, u32[]{:S(2)}) collective-permute-start(f32[1,2048]{1,0:T(1,128)S(1)} %get-tuple-element.44), channel_id=1, source_target_pairs={{0,4},{2,6},{4,0},{6,2},{1,5},{3,7},{5,1},{7,3},{8,12},{10,14},{12... | collective-permute-start | bytes 24584 | tf_op jit(solution)/shard_map/ppermute | solution.py:569
  31.8 2.9 %collective-permute-start.7 = (f32[1,2048]{1,0:T(1,128)S(1)}, f32[1,2048]{1,0:T(1,128)S(1)}, u32[]{:S(2)}, u32[]{:S(2)}) collective-permute-start(f32[1,2048]{1,0:T(1,128)S(1)} %add.3.term_ref), channel_id=1, source_target_pairs={{0,1},{1,0},{2,3},{3,2},{4,5},{5,4},{6,7},{7,6},{8,9},{9,8},{10,11... | collective-permute-start | bytes 24584 | tf_op jit(solution)/shard_map/ppermute | solution.py:569

commit v13 on v10

--- a/solution.py
+++ b/solution.py
@@ -132,10 +132,28 @@
     return [high, middle, value - high - middle]
 
 
+def put_terms(rows_ref, terms):
+    blocks = [term[i : i + 8] for term in terms for i in range(0, term.shape[0], 8)]
+    blocks.append(jnp.zeros((8, rows_ref.shape[1] - 256 * len(blocks)), jnp.float32))
+    rows_ref[...] = jnp.concatenate(blocks, axis=1).astype(jnp.bfloat16)
+
+
+def get_terms(rows_ref, pairs, count):
+    per_term = pairs // 8
+    sums = []
+    for i in range(per_term):
+        parts = [rows_ref[:, pl.ds((j * per_term + i) * 256, 256)] for j in range(count)]
+        total = parts[0].astype(jnp.float32)
+        for part in parts[1:]:
+            total = total + part.astype(jnp.float32)
+        sums.append(total)
+    return jnp.concatenate(sums, axis=0)
+
+
 def early_kernel(
     rows, chunks, offsets_hbm, q_hbm, k_hbm, v_hbm, cotangent_hbm, stashed_hbm,
     sent_ref, early_ref, more_ref, q_late_ref, k_ref, v_ref, cotangent_ref, stashed_ref,
-    offsets_ref, bias, sems, offsets_sem,
+    offsets_ref, bias, lse_ref, sems, offsets_sem,
 ):
     half = rows // 2
     head, tail = pl.ds(0, half), pl.ds(half, half)
@@ -154,9 +172,7 @@
         (stashed_hbm, stashed_ref),
     )
     rest = []
-    offsets_copy.wait()
     start = lax.axis_index("seq") * rows
-    bias[...] = mask_bias(offsets_ref, start, start, lambda key, query: key <= query)
     pairs = k_ref.shape[1] // LANES
     split = early_ref.shape[0] // LANES
 
@@ -165,6 +181,9 @@
         if pair % per_chunk == 0:
             for copy in copies[pair // per_chunk]:
                 copy.wait()
+        if pair == 1:
+            offsets_copy.wait()
+            bias[...] = mask_bias(offsets_ref, start, start, lambda key, query: key <= query)
         if pair == per_chunk:
             for i, (source, target) in enumerate(later):
                 rest.append(load(source, target, offsets_sem.at[i + 1]))
@@ -184,13 +203,11 @@
         total = mixed[LANES : LANES + 1]
         target, place = (early_ref, pair) if pair < split else (more_ref, pair - split)
         target[at(place), :] = own_heads(mixed, 1.0 / total).astype(jnp.bfloat16)
-        lse = top + jnp.log(total)
-        terms = three_terms(lse[:, :half]) + three_terms(lse[:, half:])
-        terms.append(jnp.zeros((EXTRA - 6, LANES), jnp.float32))
-        sent_ref[pl.ds(half, EXTRA), at(pair)] = jnp.concatenate(terms, axis=0).astype(jnp.bfloat16)
+        lse_ref[pl.ds(pair, 1), :] = top + jnp.log(total)
         return ()
 
     over_pairs(pairs, (score, top, weigh, finish), LAGS, arrive)
+    put_terms(sent_ref.at[pl.ds(half, EXTRA)], three_terms(lse_ref[...]))
     for copy in rest:
         copy.wait()
 
@@ -251,13 +268,14 @@
         copy.wait()
 
 
-def halo_kernel(q_ref, k_ref, v_ref, bias, after_ref, out_ref):
+def halo_kernel(q_ref, k_ref, v_ref, bias, after_ref, out_ref, lse_ref, share_ref):
     half = bias.shape[0]
     molecules = half // POOL
     tail = pl.ds(half, half)
     pooling = pool_matrix(half)
     pairs = k_ref.shape[1] // LANES
     parts = []
+    lse_ref[...] = get_terms(q_ref.at[pl.ds(half, EXTRA)], pairs, 3)
 
     def score(pair):
         queries = split_heads(q_ref[pl.ds(0, half), at(pair)])
@@ -265,10 +283,7 @@
         return scores, with_ones(jnp.transpose(v_ref[tail, at(pair)]))
 
     def top(pair, scores, values_t):
-        terms = q_ref[pl.ds(half, EXTRA), at(pair)].astype(jnp.float32)
-        lse = jnp.concatenate(
-            [terms[0:1] + terms[1:2] + terms[2:3], terms[3:4] + terms[4:5] + terms[5:6]], axis=1
-        )
+        lse = lse_ref[pl.ds(pair, 1), :]
         return scores, jnp.maximum(tops(scores + bias[...]), lse), lse, values_t
 
     def weigh(pair, scores, top, lse, values_t):
@@ -283,15 +298,13 @@
             pooled = dot_nt(pooling, jnp.concatenate(parts, axis=0)).astype(jnp.bfloat16)
             out_ref[pl.ds(0, molecules), pl.ds((pair - 3) * LANES, 4 * LANES)] = pooled
             parts.clear()
-        share = kept * inverse
-        high = share.astype(jnp.bfloat16).astype(jnp.float32)
-        low = share - high
-        shares = [high[:, :half], low[:, :half], high[:, half:], low[:, half:]]
-        shares.append(jnp.zeros((EXTRA - 4, LANES), jnp.float32))
-        out_ref[pl.ds(molecules, EXTRA), at(pair)] = jnp.concatenate(shares, axis=0).astype(jnp.bfloat16)
+        share_ref[pl.ds(pair, 1), :] = kept * inverse
         return ()
 
     over_pairs(pairs, (score, top, weigh, finish), LAGS, lambda pair: None)
+    share = share_ref[...]
+    high = share.astype(jnp.bfloat16).astype(jnp.float32)
+    put_terms(out_ref.at[pl.ds(molecules, EXTRA)], [high, share - high])
 
 
 def back_kernel(
@@ -324,7 +337,7 @@
 
 def project_kernel(
     early_ref, both_ref, halo_ref, gain_ref, weight_ref, term_ref, other_ref, upstream_hbm,
-    out_ref, update_ref, passed_hbm, sem,
+    out_ref, update_ref, passed_hbm, share_ref, sem,
 ):
     passing = load(upstream_hbm, passed_hbm, sem)
     half = both_ref.shape[1]
@@ -333,11 +346,12 @@
     molecules = half // POOL
     pooling = pool_matrix(half)
     first = lax.axis_index("seq") == 0
+    shares = get_terms(halo_ref.at[pl.ds(molecules, EXTRA)], features // LANES, 2)
+    share_ref[...] = jnp.where(first, 1.0, shares)
     squares, product, parts = 0.0, 0.0, []
     for pair in range(features // LANES):
-        shares = halo_ref[molecules:, at(pair)].astype(jnp.float32)
-        share_a = jnp.where(first, 1.0, shares[0:1] + shares[1:2])
-        share_b = jnp.where(first, 1.0, shares[2:3] + shares[3:4])
+        share_a = share_ref[pl.ds(pair, 1), pl.ds(0, half)]
+        share_b = share_ref[pl.ds(pair, 1), pl.ds(half, half)]
         begin = pair * LANES
         if begin < first_part:
             early = early_ref[pl.ds(begin, LANES), :].astype(jnp.float32)
@@ -403,6 +417,7 @@
         scratch_shapes=[
             pltpu.SMEM(offsets.shape, jnp.int32),
             pltpu.VMEM((half, 2 * half), jnp.float32),
+            pltpu.VMEM((width // LANES, rows), jnp.float32),
             pltpu.SemaphoreType.DMA((3, chunks)),
             pltpu.SemaphoreType.DMA((6,)),
         ],
@@ -445,6 +460,7 @@
         in_specs=[VMEM] * 4 + [ANY],
         out_specs=VMEM,
         out_shape=jax.ShapeDtypeStruct((half // POOL + EXTRA, width), jnp.bfloat16),
+        scratch_shapes=[pltpu.VMEM((width // LANES, 2 * half), jnp.float32)] * 2,
         cost_estimate=cost(4 * half * half * width, 6 * half * width, half * half * width // 64),
         compiler_params=params(),
         name="attend_halo",
@@ -484,7 +500,10 @@
             jax.ShapeDtypeStruct(term.shape, term.dtype),
             jax.ShapeDtypeStruct(upstream.shape, upstream.dtype),
         ],
-        scratch_shapes=[pltpu.SemaphoreType.DMA],
+        scratch_shapes=[
+            pltpu.VMEM((width // LANES, 2 * WINDOW), jnp.float32),
+            pltpu.SemaphoreType.DMA,
+        ],
         cost_estimate=cost(2 * rows * width * depth, 2 * width * depth),
         compiler_params=params(),
         name="project",

time: 34.7 us -> 34.8 us (level)
  no operation moved by 1% of the time
where the time goes in v13:
time: 34.8 us; the launch traced here: 34.5 us
  starting transfers between devices  16.5 us (47%)
  Pallas kernels  10.9 us (31%)
  waiting for transfers between devices  5.74 us (16%)
  between operations  1.38 us (4%)
    ppermute x3, waiting for transfers between devices, swapped(): lax.ppermute(value, axis, [(i, i ^ distance) for i in range(lax.axis_size...  5.73 us
    ppermute x3, starting transfers between devices, swapped(): lax.ppermute(value, axis, [(i, i ^ distance) for i in range(lax.axis_size...  5.38 us
    ppermute x3, starting transfers between devices, passed_along(): lax.ppermute(value, axis, [(i, (i + steps) % count) for i in range(count)])  5.07 us
    ppermute x1, starting transfers between devices, onward(): return lax.ppermute(value, ('section', 'seq'), route)  4.79 us
    pallas_call x1, Pallas kernels, attend_early(): pl.pallas_call(functools.partial(early_kernel, rows, chunks), in_specs=[H...  3.25 us
    pallas_call x1, Pallas kernels, attend_late(): pl.pallas_call(functools.partial(late_kernel, rows), in_specs=[HBM] * 2 +...  2.6 us
    pallas_call x1, Pallas kernels, project(): pl.pallas_call(project_kernel, in_specs=[VMEM] * 7 + [ANY], out_specs=[VM...  1.96 us
    pallas_call x1, Pallas kernels, backward(): pl.pallas_call(back_kernel, in_specs=[VMEM] * 5 + [ANY], out_specs=[VMEM]...  1.56 us
  transfers between devices with their start and end apart: 8, of which 3 were waited for; matrix products, arithmetic and copies ran while one was open for 0% of the time, Pallas kernels for 16%

profile of v13, /device:TPU:0, one launch (start us, length us, event | category | flops | bytes accessed | tf_op | source)
XLA Modules:
  0.0 34.5 jit_solution(8546653034909579480)
XLA Ops:
  0.6 3.3 %attend_early.1 = (bf16[136,2048]{1,0:T(8,128)(2,1)S(1)}, bf16[1536,128]{1,0:T(8,128)(2,1)S(1)}, bf16[512,128]{1,0:T(8,128)(2,1)S(1)}, bf16[128,2048]{1,0:T(8,12...) custom-call(s32[1,8]{1,0:T(1,128)} %bitcast.17, ...), custom_call_target="tpu_custom_call" | custom-call | flops 134217728 | bytes 3145728 | tf_op jit(solution)/shard_map/attend_early/pallas_call | solution.py:403
  3.9 0.0 copy-start
  3.9 1.3 %collective-permute-start.2 = (bf16[136,2048]{1,0:T(8,128)(2,1)S(1)}, bf16[136,2048]{1,0:T(8,128)(2,1)S(1)}, u32[]{:S(2)}, u32[]{:S(2)}) collective-permute-start(bf16[136,2048]{1,0:T(8,128)(2,1)S(1)} %get-tuple-element.25), channel_id=1, source_target_pairs={{2,0},{4,2},{6,4},{3,1},{5,3},{7,5},{10,8},{12,10},{14,12},{11,9},... | collective-permute-start | bytes 1671176 | tf_op jit(solution)/shard_map/ppermute | solution.py:35
  5.2 3.0 %collective-permute-start = (bf16[1536,128]{1,0:T(8,128)(2,1)S(1)}, bf16[1536,128]{1,0:T(8,128)(2,1)S(1)}, u32[]{:S(2)}, u32[]{:S(2)}) collective-permute-start(bf16[1536,128]{1,0:T(8,128)(2,1)S(1)} %get-tuple-element.19), channel_id=1, source_target_pairs={{0,8},{8,16},{16,24},{24,0},{1,9},{9,17},{17,25},{25,1},{2,10},{10... | collective-permute-start | bytes 1179656 | tf_op jit(solution)/shard_map/ppermute | solution.py:40
  8.8 2.6 %attend_late.1 = (bf16[1024,128]{1,0:T(8,128)(2,1)S(1)}, f32[128,256]{1,0:T(8,128)S(1)}, bf16[2048,1024]{1,0:T(8,128)(2,1)S(1)}) custom-call(s32[1,8]{1,0:T(1,128)} %bitcast.18, bf16[2048,1024]{1,0:T(8,128)(2,1)} %bitcast.11, bf16[128,2048]{1,0:T(8,128)(2,1)S(1)} %get-tuple-element.20.q_ref, bf16[256,2048]{1,0:T(8,128)(2,1)S(1)} %get-tuple-element.21.k_ref, ...), custom_call_target="tpu_custom_call" | custom-call | flops 268435456 | bytes 2621440 | tf_op jit(solution)/shard_map/attend_late/pallas_call | solution.py:433
  11.5 0.0 copy-done
  11.5 1.6 %backward.1 = (bf16[64,2048]{1,0:T(8,128)(2,1)S(1)}, f32[1,2048]{1,0:T(1,128)S(1)}) custom-call(s32[1,128]{1,0:T(1,128)S(1)} %broadcast_in_dim.14.slot_ref, bf16[64,1024]{1,0:T(8,128)(2,1)S(1)} %get-tuple-element.27.cotangent_ref, bf16[2048,1024]{1,0:T(8,128)(2,1)S(1)} %get-tuple-element.28.weight_ref, f32[1,2048]{1,0:T(1,128)S(1)} %copy-done, ...), custom_call_target="tpu_custom_call" | custom-call | flops 268435456 | bytes 4194304 | tf_op jit(solution)/shard_map/backward/pallas_call | solution.py:473
  13.0 1.0 %collective-permute-start.7 = (bf16[64,2048]{1,0:T(8,128)(2,1)S(1)}, bf16[64,2048]{1,0:T(8,128)(2,1)S(1)}, u32[]{:S(2)}, u32[]{:S(2)}) collective-permute-start(bf16[64,2048]{1,0:T(8,128)(2,1)S(1)} %get-tuple-element.31), channel_id=1, source_target_pairs={{0,24},{8,0},{16,8},{24,16},{1,25},{9,1},{17,9},{25,17},{2,26},{10... | collective-permute-start | bytes 786440 | tf_op jit(solution)/shard_map/ppermute | solution.py:40
  14.1 1.1 %collective-permute-start.1 = (bf16[1024,128]{1,0:T(8,128)(2,1)S(1)}, bf16[1024,128]{1,0:T(8,128)(2,1)S(1)}, u32[]{:S(2)}, u32[]{:S(2)}) collective-permute-start(bf16[1024,128]{1,0:T(8,128)(2,1)S(1)} %get-tuple-element.24.after_ref), channel_id=1, source_target_pairs={{0,8},{8,16},{16,24},{24,0},{1,9},{9,17},{17,25},{25,1},{2,10},{10... | collective-permute-start | bytes 786440 | tf_op jit(solution)/shard_map/ppermute | solution.py:40
  15.1 0.0 collective-permute-start.3
  15.1 1.2 %collective-permute-done.3 = f32[1,2048]{1,0:T(1,128)S(1)} collective-permute-done((f32[1,2048]{1,0:T(1,128)S(1)}, f32[1,2048]{1,0:T(1,128)S(1)}, u32[]{:S(2)}, u32[]{:S(2)}) %collective-permute-start.3) | collective-permute-done | bytes 8224 | tf_op jit(solution)/shard_map/ppermute | solution.py:514
  16.3 2.7 %collective-permute-start.4 = (f32[1,2048]{1,0:T(1,128)S(1)}, f32[1,2048]{1,0:T(1,128)S(1)}, u32[]{:S(2)}, u32[]{:S(2)}) collective-permute-start(f32[1,2048]{1,0:T(1,128)S(1)} %add.6), channel_id=1, source_target_pairs={{0,2},{2,0},{4,6},{6,4},{1,3},{3,1},{5,7},{7,5},{8,10},{10,8},{12,... | collective-permute-start | bytes 24584 | tf_op jit(solution)/shard_map/ppermute | solution.py:514
  19.0 2.6 %collective-permute-done.4 = f32[1,2048]{1,0:T(1,128)S(1)} collective-permute-done((f32[1,2048]{1,0:T(1,128)S(1)}, f32[1,2048]{1,0:T(1,128)S(1)}, u32[]{:S(2)}, u32[]{:S(2)}) %collective-permute-start.4) | collective-permute-done | bytes 8224 | tf_op jit(solution)/shard_map/ppermute | solution.py:514
  21.6 0.0 collective-permute-done.2.q_ref
  21.7 1.5 %attend_halo.1 = bf16[40,2048]{1,0:T(8,128)(2,1)S(1)} custom-call(bf16[136,2048]{1,0:T(8,128)(2,1)S(1)} %collective-permute-done.2.q_ref, bf16[256,2048]{1,0:T(8,128)(2,1)S(1)} %get-tuple-element.21.k_ref, bf16[256,2048]{1,0:T(8,128)(2,1)S(1)} %get-tuple-element.22.v_ref, f32[128,256]{1,0:T(8,128)S(1)} %get-tuple-element.26.bias, ...), custom_call_target="tpu_custom_call" | custom-call | flops 134217728 | bytes 1572864 | tf_op jit(solution)/shard_map/attend_halo/pallas_call | solution.py:458
  23.2 4.8 %collective-permute-start.5 = (bf16[40,2048]{1,0:T(8,128)(2,1)S(1)}, bf16[40,2048]{1,0:T(8,128)(2,1)S(1)}, u32[]{:S(2)}, u32[]{:S(2)}) collective-permute-start(bf16[40,2048]{1,0:T(8,128)(2,1)S(1)} %attend_halo.1), channel_id=1, source_target_pairs={{0,10},{2,12},{4,14},{8,18},{10,20},{12,22},{16,26},{18,28},{20,30... | collective-permute-start | bytes 491528 | tf_op jit(solution)/shard_map/ppermute | solution.py:534
  28.0 2.7 %collective-permute-start.6 = (f32[1,2048]{1,0:T(1,128)S(1)}, f32[1,2048]{1,0:T(1,128)S(1)}, u32[]{:S(2)}, u32[]{:S(2)}) collective-permute-start(f32[1,2048]{1,0:T(1,128)S(1)} %add.7.after_ref.term_ref), channel_id=1, source_target_pairs={{0,4},{2,6},{4,0},{6,2},{1,5},{3,7},{5,1},{7,3},{8,12},{10,14},{12... | collective-permute-start | bytes 24584 | tf_op jit(solution)/shard_map/ppermute | solution.py:514
  30.6 1.9 %collective-permute-done.6.other_ref = f32[1,2048]{1,0:T(1,128)S(1)} collective-permute-done((f32[1,2048]{1,0:T(1,128)S(1)}, f32[1,2048]{1,0:T(1,128)S(1)}, u32[]{:S(2)}, u32[]{:S(2)}) %collective-permute-start.6) | collective-permute-done | bytes 8224 | tf_op jit(solution)/shard_map/ppermute | solution.py:514
  32.6 0.0 collective-permute-done.7.upstream_hbm
  32.6 0.0 collective-permute-done.1.both_ref
  32.6 0.0 collective-permute-done.early_ref
  32.6 0.0 collective-permute-done.5.halo_ref
  32.6 2.0 %project.1 = (bf16[64,1024]{1,0:T(8,128)(2,1)}, f32[1,2048]{1,0:T(1,128)}, bf16[64,2048]{1,0:T(8,128)(2,1)}) custom-call(bf16[1536,128]{1,0:T(8,128)(2,1)S(1)} %collective-permute-done.early_ref, bf16[1024,128]{1,0:T(8,128)(2,1)S(1)} %collective-permute-done.1.both_ref, bf16[40,2048]{1,0:T(8,128)(2,1)S(1)} %collective-permute-done.5.halo_ref, ...), custom_call_target="tpu_custom_call" | custom-call | flops 268435456 | bytes 4194304 | tf_op jit(solution)/shard_map/project/pallas_call | solution.py:494
  (3 shorter events, 0.0 us)
Async XLA Ops:
  3.9 7.6 %copy-start = (f32[1,2048]{1,0:T(1,128)S(1)}, f32[1,2048]{1,0:T(1,128)}, u32[]{:S(2)}) copy-start(f32[1,2048]{1,0:T(1,128)} %gain_ref.3) | copy-start | bytes 24580
  3.9 17.7 %collective-permute-start.2 = (bf16[136,2048]{1,0:T(8,128)(2,1)S(1)}, bf16[136,2048]{1,0:T(8,128)(2,1)S(1)}, u32[]{:S(2)}, u32[]{:S(2)}) collective-permute-start(bf16[136,2048]{1,0:T(8,128)(2,1)S(1)} %get-tuple-element.25), channel_id=1, source_target_pairs={{2,0},{4,2},{6,4},{3,1},{5,3},{7,5},{10,8},{12,10},{14,12},{11,9},... | collective-permute-start | bytes 1671176 | tf_op jit(solution)/shard_map/ppermute | solution.py:35
  5.2 27.4 %collective-permute-start = (bf16[1536,128]{1,0:T(8,128)(2,1)S(1)}, bf16[1536,128]{1,0:T(8,128)(2,1)S(1)}, u32[]{:S(2)}, u32[]{:S(2)}) collective-permute-start(bf16[1536,128]{1,0:T(8,128)(2,1)S(1)} %get-tuple-element.19), channel_id=1, source_target_pairs={{0,8},{8,16},{16,24},{24,0},{1,9},{9,17},{17,25},{25,1},{2,10},{10... | collective-permute-start | bytes 1179656 | tf_op jit(solution)/shard_map/ppermute | solution.py:40
  13.0 19.5 %collective-permute-start.7 = (bf16[64,2048]{1,0:T(8,128)(2,1)S(1)}, bf16[64,2048]{1,0:T(8,128)(2,1)S(1)}, u32[]{:S(2)}, u32[]{:S(2)}) collective-permute-start(bf16[64,2048]{1,0:T(8,128)(2,1)S(1)} %get-tuple-element.31), channel_id=1, source_target_pairs={{0,24},{8,0},{16,8},{24,16},{1,25},{9,1},{17,9},{25,17},{2,26},{10... | collective-permute-start | bytes 786440 | tf_op jit(solution)/shard_map/ppermute | solution.py:40
  14.1 18.5 %collective-permute-start.1 = (bf16[1024,128]{1,0:T(8,128)(2,1)S(1)}, bf16[1024,128]{1,0:T(8,128)(2,1)S(1)}, u32[]{:S(2)}, u32[]{:S(2)}) collective-permute-start(bf16[1024,128]{1,0:T(8,128)(2,1)S(1)} %get-tuple-element.24.after_ref), channel_id=1, source_target_pairs={{0,8},{8,16},{16,24},{24,0},{1,9},{9,17},{17,25},{25,1},{2,10},{10... | collective-permute-start | bytes 786440 | tf_op jit(solution)/shard_map/ppermute | solution.py:40
  15.1 1.2 %collective-permute-start.3 = (f32[1,2048]{1,0:T(1,128)S(1)}, f32[1,2048]{1,0:T(1,128)S(1)}, u32[]{:S(2)}, u32[]{:S(2)}) collective-permute-start(f32[1,2048]{1,0:T(1,128)S(1)} %get-tuple-element.30), channel_id=1, source_target_pairs={{0,1},{1,0},{2,3},{3,2},{4,5},{5,4},{6,7},{7,6},{8,9},{9,8},{10,11... | collective-permute-start | bytes 24584 | tf_op jit(solution)/shard_map/ppermute | solution.py:514
  16.3 5.3 %collective-permute-start.4 = (f32[1,2048]{1,0:T(1,128)S(1)}, f32[1,2048]{1,0:T(1,128)S(1)}, u32[]{:S(2)}, u32[]{:S(2)}) collective-permute-start(f32[1,2048]{1,0:T(1,128)S(1)} %add.6), channel_id=1, source_target_pairs={{0,2},{2,0},{4,6},{6,4},{1,3},{3,1},{5,7},{7,5},{8,10},{10,8},{12,... | collective-permute-start | bytes 24584 | tf_op jit(solution)/shard_map/ppermute | solution.py:514
  23.2 9.4 %collective-permute-start.5 = (bf16[40,2048]{1,0:T(8,128)(2,1)S(1)}, bf16[40,2048]{1,0:T(8,128)(2,1)S(1)}, u32[]{:S(2)}, u32[]{:S(2)}) collective-permute-start(bf16[40,2048]{1,0:T(8,128)(2,1)S(1)} %attend_halo.1), channel_id=1, source_target_pairs={{0,10},{2,12},{4,14},{8,18},{10,20},{12,22},{16,26},{18,28},{20,30... | collective-permute-start | bytes 491528 | tf_op jit(solution)/shard_map/ppermute | solution.py:534
  28.0 4.6 %collective-permute-start.6 = (f32[1,2048]{1,0:T(1,128)S(1)}, f32[1,2048]{1,0:T(1,128)S(1)}, u32[]{:S(2)}, u32[]{:S(2)}) collective-permute-start(f32[1,2048]{1,0:T(1,128)S(1)} %add.7.after_ref.term_ref), channel_id=1, source_target_pairs={{0,4},{2,6},{4,0},{6,2},{1,5},{3,7},{5,1},{7,3},{8,12},{10,14},{12... | collective-permute-start | bytes 24584 | tf_op jit(solution)/shard_map/ppermute | solution.py:514

commit v14 on v10

--- a/solution.py
+++ b/solution.py
@@ -15,7 +15,7 @@
 EPS_NORM = 1e-05
 EPS_STEP = 1e-06
 MASKED = -1e30
-LAGS = (0, 2, 3, 4)
+LAGS = (0, 2, 3, 4, 5)
 EXTRA = 8
 
 NT = (((1,), (1,)), ((), ()))
@@ -177,7 +177,9 @@
         return scores, tops(scores + bias[...]), values_t
 
     def weigh(pair, scores, top, values_t):
-        weights = jnp.exp((scores + bias[...]) - top).astype(jnp.bfloat16)
+        return top, jnp.exp((scores + bias[...]) - top).astype(jnp.bfloat16), values_t
+
+    def mix(pair, top, weights, values_t):
         return top, dot_nn(values_t, weights)
 
     def finish(pair, top, mixed):
@@ -190,7 +192,7 @@
         sent_ref[pl.ds(half, EXTRA), at(pair)] = jnp.concatenate(terms, axis=0).astype(jnp.bfloat16)
         return ()
 
-    over_pairs(pairs, (score, top, weigh, finish), LAGS, arrive)
+    over_pairs(pairs, (score, top, weigh, mix, finish), LAGS, arrive)
     for copy in rest:
         copy.wait()
 
@@ -232,7 +234,9 @@
 
     def weigh(pair, scores, top, values_t):
         weights = jnp.exp(scores - top).astype(jnp.bfloat16)
-        weights = jnp.concatenate([weights * other[...], weights * own[...]], axis=0)
+        return jnp.concatenate([weights * other[...], weights * own[...]], axis=0), values_t
+
+    def mix(pair, weights, values_t):
         return (dot_nn(values_t, weights),)
 
     def finish(pair, mixed):
@@ -246,7 +250,7 @@
             parts.clear()
         return ()
 
-    over_pairs(pairs, (score, top, weigh, finish), LAGS, lambda pair: None)
+    over_pairs(pairs, (score, top, weigh, mix, finish), LAGS, lambda pair: None)
     for copy in copies:
         copy.wait()
 
@@ -273,8 +277,10 @@
 
     def weigh(pair, scores, top, lse, values_t):
         weights = jnp.exp((scores + bias[...]) - top).astype(jnp.bfloat16)
-        mixed = dot_nn(values_t, weights)
-        return mixed, jnp.exp(lse - top)
+        return weights, jnp.exp(lse - top), values_t
+
+    def mix(pair, weights, kept, values_t):
+        return dot_nn(values_t, weights), kept
 
     def finish(pair, mixed, kept):
         inverse = 1.0 / (mixed[LANES : LANES + 1] + kept)
@@ -291,7 +297,7 @@
         out_ref[pl.ds(molecules, EXTRA), at(pair)] = jnp.concatenate(shares, axis=0).astype(jnp.bfloat16)
         return ()
 
-    over_pairs(pairs, (score, top, weigh, finish), LAGS, lambda pair: None)
+    over_pairs(pairs, (score, top, weigh, mix, finish), LAGS, lambda pair: None)
 
 
 def back_kernel(

time: 34.7 us -> 34.6 us (level)
  transfers between devices with their start and end apart: 8 -> 8, of which waited for: 3 -> 3; matrix products, arithmetic and copies ran while one was open for 0% -> 0% of each run, Pallas kernels for 16% -> 17%
where the time goes in v14:
time: 34.6 us; the launch traced here: 34.3 us
  starting transfers between devices  16.5 us (48%)
  Pallas kernels  10.7 us (31%)
  waiting for transfers between devices  5.74 us (17%)
  between operations  1.38 us (4%)
    ppermute x3, waiting for transfers between devices, swapped(): lax.ppermute(value, axis, [(i, i ^ distance) for i in range(lax.axis_size...  5.73 us
    ppermute x3, starting transfers between devices, swapped(): lax.ppermute(value, axis, [(i, i ^ distance) for i in range(lax.axis_size...  5.38 us
    ppermute x3, starting transfers between devices, passed_along(): lax.ppermute(value, axis, [(i, (i + steps) % count) for i in range(count)])  5.07 us
    ppermute x1, starting transfers between devices, onward(): return lax.ppermute(value, ('section', 'seq'), route)  4.8 us
    pallas_call x1, Pallas kernels, attend_early(): pl.pallas_call(functools.partial(early_kernel, rows, chunks), in_specs=[H...  3.04 us
    pallas_call x1, Pallas kernels, attend_late(): pl.pallas_call(functools.partial(late_kernel, rows), in_specs=[HBM] * 2 +...  2.6 us
    pallas_call x1, Pallas kernels, project(): pl.pallas_call(project_kernel, in_specs=[VMEM] * 7 + [ANY], out_specs=[VM...  1.95 us
    pallas_call x1, Pallas kernels, backward(): pl.pallas_call(back_kernel, in_specs=[VMEM] * 5 + [ANY], out_specs=[VMEM]...  1.56 us
  transfers between devices with their start and end apart: 8, of which 3 were waited for; matrix products, arithmetic and copies ran while one was open for 0% of the time, Pallas kernels for 17%

profile of v14, /device:TPU:0, one launch (start us, length us, event | category | flops | bytes accessed | tf_op | source)
XLA Modules:
  0.0 34.3 jit_solution(3580027481218500181)
XLA Ops:
  0.6 3.0 %attend_early.1 = (bf16[136,2048]{1,0:T(8,128)(2,1)S(1)}, bf16[1536,128]{1,0:T(8,128)(2,1)S(1)}, bf16[512,128]{1,0:T(8,128)(2,1)S(1)}, bf16[128,2048]{1,0:T(8,12...) custom-call(s32[1,8]{1,0:T(1,128)} %bitcast.17, ...), custom_call_target="tpu_custom_call" | custom-call | flops 134217728 | bytes 3145728 | tf_op jit(solution)/shard_map/attend_early/pallas_call | solution.py:395
  3.7 0.0 copy-start
  3.7 1.3 %collective-permute-start.2 = (bf16[136,2048]{1,0:T(8,128)(2,1)S(1)}, bf16[136,2048]{1,0:T(8,128)(2,1)S(1)}, u32[]{:S(2)}, u32[]{:S(2)}) collective-permute-start(bf16[136,2048]{1,0:T(8,128)(2,1)S(1)} %get-tuple-element.25), channel_id=1, source_target_pairs={{2,0},{4,2},{6,4},{3,1},{5,3},{7,5},{10,8},{12,10},{14,12},{11,9},... | collective-permute-start | bytes 1671176 | tf_op jit(solution)/shard_map/ppermute | solution.py:35
  5.0 3.0 %collective-permute-start = (bf16[1536,128]{1,0:T(8,128)(2,1)S(1)}, bf16[1536,128]{1,0:T(8,128)(2,1)S(1)}, u32[]{:S(2)}, u32[]{:S(2)}) collective-permute-start(bf16[1536,128]{1,0:T(8,128)(2,1)S(1)} %get-tuple-element.19), channel_id=1, source_target_pairs={{0,8},{8,16},{16,24},{24,0},{1,9},{9,17},{17,25},{25,1},{2,10},{10... | collective-permute-start | bytes 1179656 | tf_op jit(solution)/shard_map/ppermute | solution.py:40
  8.6 2.6 %attend_late.1 = (bf16[1024,128]{1,0:T(8,128)(2,1)S(1)}, f32[128,256]{1,0:T(8,128)S(1)}, bf16[2048,1024]{1,0:T(8,128)(2,1)S(1)}) custom-call(s32[1,8]{1,0:T(1,128)} %bitcast.18, bf16[2048,1024]{1,0:T(8,128)(2,1)} %bitcast.11, bf16[128,2048]{1,0:T(8,128)(2,1)S(1)} %get-tuple-element.20.q_ref, bf16[256,2048]{1,0:T(8,128)(2,1)S(1)} %get-tuple-element.21.k_ref, ...), custom_call_target="tpu_custom_call" | custom-call | flops 268435456 | bytes 2621440 | tf_op jit(solution)/shard_map/attend_late/pallas_call | solution.py:424
  11.3 0.0 copy-done
  11.3 1.6 %backward.1 = (bf16[64,2048]{1,0:T(8,128)(2,1)S(1)}, f32[1,2048]{1,0:T(1,128)S(1)}) custom-call(s32[1,128]{1,0:T(1,128)S(1)} %broadcast_in_dim.14.slot_ref, bf16[64,1024]{1,0:T(8,128)(2,1)S(1)} %get-tuple-element.27.cotangent_ref, bf16[2048,1024]{1,0:T(8,128)(2,1)S(1)} %get-tuple-element.28.weight_ref, f32[1,2048]{1,0:T(1,128)S(1)} %copy-done, ...), custom_call_target="tpu_custom_call" | custom-call | flops 268435456 | bytes 4194304 | tf_op jit(solution)/shard_map/backward/pallas_call | solution.py:463
  12.8 1.0 %collective-permute-start.7 = (bf16[64,2048]{1,0:T(8,128)(2,1)S(1)}, bf16[64,2048]{1,0:T(8,128)(2,1)S(1)}, u32[]{:S(2)}, u32[]{:S(2)}) collective-permute-start(bf16[64,2048]{1,0:T(8,128)(2,1)S(1)} %get-tuple-element.31), channel_id=1, source_target_pairs={{0,24},{8,0},{16,8},{24,16},{1,25},{9,1},{17,9},{25,17},{2,26},{10... | collective-permute-start | bytes 786440 | tf_op jit(solution)/shard_map/ppermute | solution.py:40
  13.9 1.1 %collective-permute-start.1 = (bf16[1024,128]{1,0:T(8,128)(2,1)S(1)}, bf16[1024,128]{1,0:T(8,128)(2,1)S(1)}, u32[]{:S(2)}, u32[]{:S(2)}) collective-permute-start(bf16[1024,128]{1,0:T(8,128)(2,1)S(1)} %get-tuple-element.24.after_ref), channel_id=1, source_target_pairs={{0,8},{8,16},{16,24},{24,0},{1,9},{9,17},{17,25},{25,1},{2,10},{10... | collective-permute-start | bytes 786440 | tf_op jit(solution)/shard_map/ppermute | solution.py:40
  14.9 0.0 collective-permute-start.3
  14.9 1.2 %collective-permute-done.3 = f32[1,2048]{1,0:T(1,128)S(1)} collective-permute-done((f32[1,2048]{1,0:T(1,128)S(1)}, f32[1,2048]{1,0:T(1,128)S(1)}, u32[]{:S(2)}, u32[]{:S(2)}) %collective-permute-start.3) | collective-permute-done | bytes 8224 | tf_op jit(solution)/shard_map/ppermute | solution.py:501
  16.1 2.7 %collective-permute-start.4 = (f32[1,2048]{1,0:T(1,128)S(1)}, f32[1,2048]{1,0:T(1,128)S(1)}, u32[]{:S(2)}, u32[]{:S(2)}) collective-permute-start(f32[1,2048]{1,0:T(1,128)S(1)} %add.6), channel_id=1, source_target_pairs={{0,2},{2,0},{4,6},{6,4},{1,3},{3,1},{5,7},{7,5},{8,10},{10,8},{12,... | collective-permute-start | bytes 24584 | tf_op jit(solution)/shard_map/ppermute | solution.py:501
  18.8 2.6 %collective-permute-done.4 = f32[1,2048]{1,0:T(1,128)S(1)} collective-permute-done((f32[1,2048]{1,0:T(1,128)S(1)}, f32[1,2048]{1,0:T(1,128)S(1)}, u32[]{:S(2)}, u32[]{:S(2)}) %collective-permute-start.4) | collective-permute-done | bytes 8224 | tf_op jit(solution)/shard_map/ppermute | solution.py:501
  21.4 0.0 collective-permute-done.2.q_ref
  21.4 1.5 %attend_halo.1 = bf16[40,2048]{1,0:T(8,128)(2,1)S(1)} custom-call(bf16[136,2048]{1,0:T(8,128)(2,1)S(1)} %collective-permute-done.2.q_ref, bf16[256,2048]{1,0:T(8,128)(2,1)S(1)} %get-tuple-element.21.k_ref, bf16[256,2048]{1,0:T(8,128)(2,1)S(1)} %get-tuple-element.22.v_ref, f32[128,256]{1,0:T(8,128)S(1)} %get-tuple-element.26.bias, ...), custom_call_target="tpu_custom_call" | custom-call | flops 134217728 | bytes 1572864 | tf_op jit(solution)/shard_map/attend_halo/pallas_call | solution.py:449
  22.9 4.8 %collective-permute-start.5 = (bf16[40,2048]{1,0:T(8,128)(2,1)S(1)}, bf16[40,2048]{1,0:T(8,128)(2,1)S(1)}, u32[]{:S(2)}, u32[]{:S(2)}) collective-permute-start(bf16[40,2048]{1,0:T(8,128)(2,1)S(1)} %attend_halo.1), channel_id=1, source_target_pairs={{0,10},{2,12},{4,14},{8,18},{10,20},{12,22},{16,26},{18,28},{20,30... | collective-permute-start | bytes 491528 | tf_op jit(solution)/shard_map/ppermute | solution.py:521
  27.8 2.7 %collective-permute-start.6 = (f32[1,2048]{1,0:T(1,128)S(1)}, f32[1,2048]{1,0:T(1,128)S(1)}, u32[]{:S(2)}, u32[]{:S(2)}) collective-permute-start(f32[1,2048]{1,0:T(1,128)S(1)} %add.7.after_ref.term_ref), channel_id=1, source_target_pairs={{0,4},{2,6},{4,0},{6,2},{1,5},{3,7},{5,1},{7,3},{8,12},{10,14},{12... | collective-permute-start | bytes 24584 | tf_op jit(solution)/shard_map/ppermute | solution.py:501
  30.4 1.9 %collective-permute-done.6.other_ref = f32[1,2048]{1,0:T(1,128)S(1)} collective-permute-done((f32[1,2048]{1,0:T(1,128)S(1)}, f32[1,2048]{1,0:T(1,128)S(1)}, u32[]{:S(2)}, u32[]{:S(2)}) %collective-permute-start.6) | collective-permute-done | bytes 8224 | tf_op jit(solution)/shard_map/ppermute | solution.py:501
  32.4 0.0 collective-permute-done.7.upstream_hbm
  32.4 0.0 collective-permute-done.1.both_ref
  32.4 0.0 collective-permute-done.early_ref
  32.4 0.0 collective-permute-done.5.halo_ref
  32.4 1.9 %project.1 = (bf16[64,1024]{1,0:T(8,128)(2,1)}, f32[1,2048]{1,0:T(1,128)}, bf16[64,2048]{1,0:T(8,128)(2,1)}) custom-call(bf16[1536,128]{1,0:T(8,128)(2,1)S(1)} %collective-permute-done.early_ref, bf16[1024,128]{1,0:T(8,128)(2,1)S(1)} %collective-permute-done.1.both_ref, bf16[40,2048]{1,0:T(8,128)(2,1)S(1)} %collective-permute-done.5.halo_ref, ...), custom_call_target="tpu_custom_call" | custom-call | flops 268435456 | bytes 4194304 | tf_op jit(solution)/shard_map/project/pallas_call | solution.py:484
  (3 shorter events, 0.0 us)
Async XLA Ops:
  3.7 7.6 %copy-start = (f32[1,2048]{1,0:T(1,128)S(1)}, f32[1,2048]{1,0:T(1,128)}, u32[]{:S(2)}) copy-start(f32[1,2048]{1,0:T(1,128)} %gain_ref.3) | copy-start | bytes 24580
  3.7 17.7 %collective-permute-start.2 = (bf16[136,2048]{1,0:T(8,128)(2,1)S(1)}, bf16[136,2048]{1,0:T(8,128)(2,1)S(1)}, u32[]{:S(2)}, u32[]{:S(2)}) collective-permute-start(bf16[136,2048]{1,0:T(8,128)(2,1)S(1)} %get-tuple-element.25), channel_id=1, source_target_pairs={{2,0},{4,2},{6,4},{3,1},{5,3},{7,5},{10,8},{12,10},{14,12},{11,9},... | collective-permute-start | bytes 1671176 | tf_op jit(solution)/shard_map/ppermute | solution.py:35
  5.0 27.4 %collective-permute-start = (bf16[1536,128]{1,0:T(8,128)(2,1)S(1)}, bf16[1536,128]{1,0:T(8,128)(2,1)S(1)}, u32[]{:S(2)}, u32[]{:S(2)}) collective-permute-start(bf16[1536,128]{1,0:T(8,128)(2,1)S(1)} %get-tuple-element.19), channel_id=1, source_target_pairs={{0,8},{8,16},{16,24},{24,0},{1,9},{9,17},{17,25},{25,1},{2,10},{10... | collective-permute-start | bytes 1179656 | tf_op jit(solution)/shard_map/ppermute | solution.py:40
  12.8 19.5 %collective-permute-start.7 = (bf16[64,2048]{1,0:T(8,128)(2,1)S(1)}, bf16[64,2048]{1,0:T(8,128)(2,1)S(1)}, u32[]{:S(2)}, u32[]{:S(2)}) collective-permute-start(bf16[64,2048]{1,0:T(8,128)(2,1)S(1)} %get-tuple-element.31), channel_id=1, source_target_pairs={{0,24},{8,0},{16,8},{24,16},{1,25},{9,1},{17,9},{25,17},{2,26},{10... | collective-permute-start | bytes 786440 | tf_op jit(solution)/shard_map/ppermute | solution.py:40
  13.9 18.5 %collective-permute-start.1 = (bf16[1024,128]{1,0:T(8,128)(2,1)S(1)}, bf16[1024,128]{1,0:T(8,128)(2,1)S(1)}, u32[]{:S(2)}, u32[]{:S(2)}) collective-permute-start(bf16[1024,128]{1,0:T(8,128)(2,1)S(1)} %get-tuple-element.24.after_ref), channel_id=1, source_target_pairs={{0,8},{8,16},{16,24},{24,0},{1,9},{9,17},{17,25},{25,1},{2,10},{10... | collective-permute-start | bytes 786440 | tf_op jit(solution)/shard_map/ppermute | solution.py:40
  14.9 1.2 %collective-permute-start.3 = (f32[1,2048]{1,0:T(1,128)S(1)}, f32[1,2048]{1,0:T(1,128)S(1)}, u32[]{:S(2)}, u32[]{:S(2)}) collective-permute-start(f32[1,2048]{1,0:T(1,128)S(1)} %get-tuple-element.30), channel_id=1, source_target_pairs={{0,1},{1,0},{2,3},{3,2},{4,5},{5,4},{6,7},{7,6},{8,9},{9,8},{10,11... | collective-permute-start | bytes 24584 | tf_op jit(solution)/shard_map/ppermute | solution.py:501
  16.1 5.3 %collective-permute-start.4 = (f32[1,2048]{1,0:T(1,128)S(1)}, f32[1,2048]{1,0:T(1,128)S(1)}, u32[]{:S(2)}, u32[]{:S(2)}) collective-permute-start(f32[1,2048]{1,0:T(1,128)S(1)} %add.6), channel_id=1, source_target_pairs={{0,2},{2,0},{4,6},{6,4},{1,3},{3,1},{5,7},{7,5},{8,10},{10,8},{12,... | collective-permute-start | bytes 24584 | tf_op jit(solution)/shard_map/ppermute | solution.py:501
  22.9 9.4 %collective-permute-start.5 = (bf16[40,2048]{1,0:T(8,128)(2,1)S(1)}, bf16[40,2048]{1,0:T(8,128)(2,1)S(1)}, u32[]{:S(2)}, u32[]{:S(2)}) collective-permute-start(bf16[40,2048]{1,0:T(8,128)(2,1)S(1)} %attend_halo.1), channel_id=1, source_target_pairs={{0,10},{2,12},{4,14},{8,18},{10,20},{12,22},{16,26},{18,28},{20,30... | collective-permute-start | bytes 491528 | tf_op jit(solution)/shard_map/ppermute | solution.py:521
  27.8 4.6 %collective-permute-start.6 = (f32[1,2048]{1,0:T(1,128)S(1)}, f32[1,2048]{1,0:T(1,128)S(1)}, u32[]{:S(2)}, u32[]{:S(2)}) collective-permute-start(f32[1,2048]{1,0:T(1,128)S(1)} %add.7.after_ref.term_ref), channel_id=1, source_target_pairs={{0,4},{2,6},{4,0},{6,2},{1,5},{3,7},{5,1},{7,3},{8,12},{10,14},{12... | collective-permute-start | bytes 24584 | tf_op jit(solution)/shard_map/ppermute | solution.py:501

commit v15 on v14

--- a/solution.py
+++ b/solution.py
@@ -15,7 +15,7 @@
 EPS_NORM = 1e-05
 EPS_STEP = 1e-06
 MASKED = -1e30
-LAGS = (0, 2, 3, 4, 5)
+LAGS = (0, 3, 5, 6, 8)
 EXTRA = 8
 
 NT = (((1,), (1,)), ((), ()))
@@ -330,7 +330,7 @@
 
 def project_kernel(
     early_ref, both_ref, halo_ref, gain_ref, weight_ref, term_ref, other_ref, upstream_hbm,
-    out_ref, update_ref, passed_hbm, sem,
+    out_ref, update_ref, passed_hbm, scaled_ref, sem,
 ):
     passing = load(upstream_hbm, passed_hbm, sem)
     half = both_ref.shape[1]
@@ -339,7 +339,7 @@
     molecules = half // POOL
     pooling = pool_matrix(half)
     first = lax.axis_index("seq") == 0
-    squares, product, parts = 0.0, 0.0, []
+    squares, parts = 0.0, []
     for pair in range(features // LANES):
         shares = halo_ref[molecules:, at(pair)].astype(jnp.float32)
         share_a = jnp.where(first, 1.0, shares[0:1] + shares[1:2])
@@ -359,9 +359,9 @@
             lower = jnp.concatenate(lower, axis=1)
             arrived = jnp.concatenate([upper.astype(jnp.bfloat16), lower], axis=0).astype(jnp.float32)
             squares += jnp.sum(arrived * arrived, axis=1, keepdims=True)
-            scaled = (arrived * gain_ref[:, columns]).astype(jnp.bfloat16)
-            product += dot_nn(scaled, weight_ref[columns, :])
+            scaled_ref[:, columns] = (arrived * gain_ref[:, columns]).astype(jnp.bfloat16)
             parts = []
+    product = dot_nn(scaled_ref[...], weight_ref[...])
     out_ref[...] = (product * lax.rsqrt(squares / features + EPS_NORM)).astype(jnp.bfloat16)
     total = term_ref[...] + other_ref[...]
     mean = jnp.sum(total * total, axis=1, keepdims=True) / features
@@ -490,7 +490,7 @@
             jax.ShapeDtypeStruct(term.shape, term.dtype),
             jax.ShapeDtypeStruct(upstream.shape, upstream.dtype),
         ],
-        scratch_shapes=[pltpu.SemaphoreType.DMA],
+        scratch_shapes=[pltpu.VMEM((rows, width), jnp.bfloat16), pltpu.SemaphoreType.DMA],
         cost_estimate=cost(2 * rows * width * depth, 2 * width * depth),
         compiler_params=params(),
         name="project",

time: 34.6 us -> 34.3 us (level)
  Pallas kernels: 10.7 us -> 10.3 us
  transfers between devices with their start and end apart: 8 -> 8, of which waited for: 3 -> 3; matrix products, arithmetic and copies ran while one was open for 0% -> 0% of each run, Pallas kernels for 17% -> 16%
where the time goes in v15:
time: 34.3 us; the launch traced here: 34 us
  starting transfers between devices  16.5 us (48%)
  Pallas kernels  10.3 us (30%)
  waiting for transfers between devices  5.8 us (17%)
  between operations  1.38 us (4%)
    ppermute x3, waiting for transfers between devices, swapped(): lax.ppermute(value, axis, [(i, i ^ distance) for i in range(lax.axis_size...  5.79 us
    ppermute x3, starting transfers between devices, swapped(): lax.ppermute(value, axis, [(i, i ^ distance) for i in range(lax.axis_size...  5.39 us
    ppermute x3, starting transfers between devices, passed_along(): lax.ppermute(value, axis, [(i, (i + steps) % count) for i in range(count)])  5.07 us
    ppermute x1, starting transfers between devices, onward(): return lax.ppermute(value, ('section', 'seq'), route)  4.72 us
    pallas_call x1, Pallas kernels, attend_early(): pl.pallas_call(functools.partial(early_kernel, rows, chunks), in_specs=[H...  3.03 us
    pallas_call x1, Pallas kernels, attend_late(): pl.pallas_call(functools.partial(late_kernel, rows), in_specs=[HBM] * 2 +...  2.53 us
    pallas_call x1, Pallas kernels, project(): pl.pallas_call(project_kernel, in_specs=[VMEM] * 7 + [ANY], out_specs=[VM...  1.72 us
    pallas_call x1, Pallas kernels, backward(): pl.pallas_call(back_kernel, in_specs=[VMEM] * 5 + [ANY], out_specs=[VMEM]...  1.56 us
  transfers between devices with their start and end apart: 8, of which 3 were waited for; matrix products, arithmetic and copies ran while one was open for 0% of the time, Pallas kernels for 16%

profile of v15, /device:TPU:0, one launch (start us, length us, event | category | flops | bytes accessed | tf_op | source)
XLA Modules:
  0.0 34.0 jit_solution(254394254056874341)
XLA Ops:
  0.6 3.0 %attend_early.1 = (bf16[136,2048]{1,0:T(8,128)(2,1)S(1)}, bf16[1536,128]{1,0:T(8,128)(2,1)S(1)}, bf16[512,128]{1,0:T(8,128)(2,1)S(1)}, bf16[128,2048]{1,0:T(8,12...) custom-call(s32[1,8]{1,0:T(1,128)} %bitcast.17, ...), custom_call_target="tpu_custom_call" | custom-call | flops 134217728 | bytes 3145728 | tf_op jit(solution)/shard_map/attend_early/pallas_call | solution.py:395
  3.7 0.0 copy-start
  3.7 1.3 %collective-permute-start.2 = (bf16[136,2048]{1,0:T(8,128)(2,1)S(1)}, bf16[136,2048]{1,0:T(8,128)(2,1)S(1)}, u32[]{:S(2)}, u32[]{:S(2)}) collective-permute-start(bf16[136,2048]{1,0:T(8,128)(2,1)S(1)} %get-tuple-element.25), channel_id=1, source_target_pairs={{2,0},{4,2},{6,4},{3,1},{5,3},{7,5},{10,8},{12,10},{14,12},{11,9},... | collective-permute-start | bytes 1671176 | tf_op jit(solution)/shard_map/ppermute | solution.py:35
  5.0 3.0 %collective-permute-start = (bf16[1536,128]{1,0:T(8,128)(2,1)S(1)}, bf16[1536,128]{1,0:T(8,128)(2,1)S(1)}, u32[]{:S(2)}, u32[]{:S(2)}) collective-permute-start(bf16[1536,128]{1,0:T(8,128)(2,1)S(1)} %get-tuple-element.19), channel_id=1, source_target_pairs={{0,8},{8,16},{16,24},{24,0},{1,9},{9,17},{17,25},{25,1},{2,10},{10... | collective-permute-start | bytes 1179656 | tf_op jit(solution)/shard_map/ppermute | solution.py:40
  8.6 2.5 %attend_late.1 = (bf16[1024,128]{1,0:T(8,128)(2,1)S(1)}, f32[128,256]{1,0:T(8,128)S(1)}, bf16[2048,1024]{1,0:T(8,128)(2,1)S(1)}) custom-call(s32[1,8]{1,0:T(1,128)} %bitcast.18, bf16[2048,1024]{1,0:T(8,128)(2,1)} %bitcast.11, bf16[128,2048]{1,0:T(8,128)(2,1)S(1)} %get-tuple-element.20.q_ref, bf16[256,2048]{1,0:T(8,128)(2,1)S(1)} %get-tuple-element.21.k_ref, ...), custom_call_target="tpu_custom_call" | custom-call | flops 268435456 | bytes 2621440 | tf_op jit(solution)/shard_map/attend_late/pallas_call | solution.py:424
  11.2 0.0 copy-done
  11.2 1.6 %backward.1 = (bf16[64,2048]{1,0:T(8,128)(2,1)S(1)}, f32[1,2048]{1,0:T(1,128)S(1)}) custom-call(s32[1,128]{1,0:T(1,128)S(1)} %broadcast_in_dim.14.slot_ref, bf16[64,1024]{1,0:T(8,128)(2,1)S(1)} %get-tuple-element.27.cotangent_ref, bf16[2048,1024]{1,0:T(8,128)(2,1)S(1)} %get-tuple-element.28.weight_ref, f32[1,2048]{1,0:T(1,128)S(1)} %copy-done, ...), custom_call_target="tpu_custom_call" | custom-call | flops 268435456 | bytes 4194304 | tf_op jit(solution)/shard_map/backward/pallas_call | solution.py:463
  12.7 1.0 %collective-permute-start.7 = (bf16[64,2048]{1,0:T(8,128)(2,1)S(1)}, bf16[64,2048]{1,0:T(8,128)(2,1)S(1)}, u32[]{:S(2)}, u32[]{:S(2)}) collective-permute-start(bf16[64,2048]{1,0:T(8,128)(2,1)S(1)} %get-tuple-element.31), channel_id=1, source_target_pairs={{0,24},{8,0},{16,8},{24,16},{1,25},{9,1},{17,9},{25,17},{2,26},{10... | collective-permute-start | bytes 786440 | tf_op jit(solution)/shard_map/ppermute | solution.py:40
  13.8 1.1 %collective-permute-start.1 = (bf16[1024,128]{1,0:T(8,128)(2,1)S(1)}, bf16[1024,128]{1,0:T(8,128)(2,1)S(1)}, u32[]{:S(2)}, u32[]{:S(2)}) collective-permute-start(bf16[1024,128]{1,0:T(8,128)(2,1)S(1)} %get-tuple-element.24.after_ref), channel_id=1, source_target_pairs={{0,8},{8,16},{16,24},{24,0},{1,9},{9,17},{17,25},{25,1},{2,10},{10... | collective-permute-start | bytes 786440 | tf_op jit(solution)/shard_map/ppermute | solution.py:40
  14.8 0.0 collective-permute-start.3
  14.8 1.2 %collective-permute-done.3 = f32[1,2048]{1,0:T(1,128)S(1)} collective-permute-done((f32[1,2048]{1,0:T(1,128)S(1)}, f32[1,2048]{1,0:T(1,128)S(1)}, u32[]{:S(2)}, u32[]{:S(2)}) %collective-permute-start.3) | collective-permute-done | bytes 8224 | tf_op jit(solution)/shard_map/ppermute | solution.py:501
  16.0 2.7 %collective-permute-start.4 = (f32[1,2048]{1,0:T(1,128)S(1)}, f32[1,2048]{1,0:T(1,128)S(1)}, u32[]{:S(2)}, u32[]{:S(2)}) collective-permute-start(f32[1,2048]{1,0:T(1,128)S(1)} %add.6), channel_id=1, source_target_pairs={{0,2},{2,0},{4,6},{6,4},{1,3},{3,1},{5,7},{7,5},{8,10},{10,8},{12,... | collective-permute-start | bytes 24584 | tf_op jit(solution)/shard_map/ppermute | solution.py:501
  18.7 2.7 %collective-permute-done.4 = f32[1,2048]{1,0:T(1,128)S(1)} collective-permute-done((f32[1,2048]{1,0:T(1,128)S(1)}, f32[1,2048]{1,0:T(1,128)S(1)}, u32[]{:S(2)}, u32[]{:S(2)}) %collective-permute-start.4) | collective-permute-done | bytes 8224 | tf_op jit(solution)/shard_map/ppermute | solution.py:501
  21.4 0.0 collective-permute-done.2.q_ref
  21.4 1.4 %attend_halo.1 = bf16[40,2048]{1,0:T(8,128)(2,1)S(1)} custom-call(bf16[136,2048]{1,0:T(8,128)(2,1)S(1)} %collective-permute-done.2.q_ref, bf16[256,2048]{1,0:T(8,128)(2,1)S(1)} %get-tuple-element.21.k_ref, bf16[256,2048]{1,0:T(8,128)(2,1)S(1)} %get-tuple-element.22.v_ref, f32[128,256]{1,0:T(8,128)S(1)} %get-tuple-element.26.bias, ...), custom_call_target="tpu_custom_call" | custom-call | flops 134217728 | bytes 1572864 | tf_op jit(solution)/shard_map/attend_halo/pallas_call | solution.py:449
  22.9 4.7 %collective-permute-start.5 = (bf16[40,2048]{1,0:T(8,128)(2,1)S(1)}, bf16[40,2048]{1,0:T(8,128)(2,1)S(1)}, u32[]{:S(2)}, u32[]{:S(2)}) collective-permute-start(bf16[40,2048]{1,0:T(8,128)(2,1)S(1)} %attend_halo.1), channel_id=1, source_target_pairs={{0,10},{2,12},{4,14},{8,18},{10,20},{12,22},{16,26},{18,28},{20,30... | collective-permute-start | bytes 491528 | tf_op jit(solution)/shard_map/ppermute | solution.py:521
  27.6 2.7 %collective-permute-start.6 = (f32[1,2048]{1,0:T(1,128)S(1)}, f32[1,2048]{1,0:T(1,128)S(1)}, u32[]{:S(2)}, u32[]{:S(2)}) collective-permute-start(f32[1,2048]{1,0:T(1,128)S(1)} %add.7.after_ref.term_ref), channel_id=1, source_target_pairs={{0,4},{2,6},{4,0},{6,2},{1,5},{3,7},{5,1},{7,3},{8,12},{10,14},{12... | collective-permute-start | bytes 24584 | tf_op jit(solution)/shard_map/ppermute | solution.py:501
  30.3 1.9 %collective-permute-done.6.other_ref = f32[1,2048]{1,0:T(1,128)S(1)} collective-permute-done((f32[1,2048]{1,0:T(1,128)S(1)}, f32[1,2048]{1,0:T(1,128)S(1)}, u32[]{:S(2)}, u32[]{:S(2)}) %collective-permute-start.6) | collective-permute-done | bytes 8224 | tf_op jit(solution)/shard_map/ppermute | solution.py:501
  32.2 0.0 collective-permute-done.7.upstream_hbm
  32.2 0.0 collective-permute-done.1.both_ref
  32.2 0.0 collective-permute-done.early_ref
  32.2 0.0 collective-permute-done.5.halo_ref
  32.2 1.7 %project.1 = (bf16[64,1024]{1,0:T(8,128)(2,1)}, f32[1,2048]{1,0:T(1,128)}, bf16[64,2048]{1,0:T(8,128)(2,1)}) custom-call(bf16[1536,128]{1,0:T(8,128)(2,1)S(1)} %collective-permute-done.early_ref, bf16[1024,128]{1,0:T(8,128)(2,1)S(1)} %collective-permute-done.1.both_ref, bf16[40,2048]{1,0:T(8,128)(2,1)S(1)} %collective-permute-done.5.halo_ref, ...), custom_call_target="tpu_custom_call" | custom-call | flops 268435456 | bytes 4194304 | tf_op jit(solution)/shard_map/project/pallas_call | solution.py:484
  (3 shorter events, 0.0 us)
Async XLA Ops:
  3.7 7.5 %copy-start = (f32[1,2048]{1,0:T(1,128)S(1)}, f32[1,2048]{1,0:T(1,128)}, u32[]{:S(2)}) copy-start(f32[1,2048]{1,0:T(1,128)} %gain_ref.3) | copy-start | bytes 24580
  3.7 17.7 %collective-permute-start.2 = (bf16[136,2048]{1,0:T(8,128)(2,1)S(1)}, bf16[136,2048]{1,0:T(8,128)(2,1)S(1)}, u32[]{:S(2)}, u32[]{:S(2)}) collective-permute-start(bf16[136,2048]{1,0:T(8,128)(2,1)S(1)} %get-tuple-element.25), channel_id=1, source_target_pairs={{2,0},{4,2},{6,4},{3,1},{5,3},{7,5},{10,8},{12,10},{14,12},{11,9},... | collective-permute-start | bytes 1671176 | tf_op jit(solution)/shard_map/ppermute | solution.py:35
  5.0 27.3 %collective-permute-start = (bf16[1536,128]{1,0:T(8,128)(2,1)S(1)}, bf16[1536,128]{1,0:T(8,128)(2,1)S(1)}, u32[]{:S(2)}, u32[]{:S(2)}) collective-permute-start(bf16[1536,128]{1,0:T(8,128)(2,1)S(1)} %get-tuple-element.19), channel_id=1, source_target_pairs={{0,8},{8,16},{16,24},{24,0},{1,9},{9,17},{17,25},{25,1},{2,10},{10... | collective-permute-start | bytes 1179656 | tf_op jit(solution)/shard_map/ppermute | solution.py:40
  12.7 19.5 %collective-permute-start.7 = (bf16[64,2048]{1,0:T(8,128)(2,1)S(1)}, bf16[64,2048]{1,0:T(8,128)(2,1)S(1)}, u32[]{:S(2)}, u32[]{:S(2)}) collective-permute-start(bf16[64,2048]{1,0:T(8,128)(2,1)S(1)} %get-tuple-element.31), channel_id=1, source_target_pairs={{0,24},{8,0},{16,8},{24,16},{1,25},{9,1},{17,9},{25,17},{2,26},{10... | collective-permute-start | bytes 786440 | tf_op jit(solution)/shard_map/ppermute | solution.py:40
  13.8 18.5 %collective-permute-start.1 = (bf16[1024,128]{1,0:T(8,128)(2,1)S(1)}, bf16[1024,128]{1,0:T(8,128)(2,1)S(1)}, u32[]{:S(2)}, u32[]{:S(2)}) collective-permute-start(bf16[1024,128]{1,0:T(8,128)(2,1)S(1)} %get-tuple-element.24.after_ref), channel_id=1, source_target_pairs={{0,8},{8,16},{16,24},{24,0},{1,9},{9,17},{17,25},{25,1},{2,10},{10... | collective-permute-start | bytes 786440 | tf_op jit(solution)/shard_map/ppermute | solution.py:40
  14.8 1.2 %collective-permute-start.3 = (f32[1,2048]{1,0:T(1,128)S(1)}, f32[1,2048]{1,0:T(1,128)S(1)}, u32[]{:S(2)}, u32[]{:S(2)}) collective-permute-start(f32[1,2048]{1,0:T(1,128)S(1)} %get-tuple-element.30), channel_id=1, source_target_pairs={{0,1},{1,0},{2,3},{3,2},{4,5},{5,4},{6,7},{7,6},{8,9},{9,8},{10,11... | collective-permute-start | bytes 24584 | tf_op jit(solution)/shard_map/ppermute | solution.py:501
  16.0 5.4 %collective-permute-start.4 = (f32[1,2048]{1,0:T(1,128)S(1)}, f32[1,2048]{1,0:T(1,128)S(1)}, u32[]{:S(2)}, u32[]{:S(2)}) collective-permute-start(f32[1,2048]{1,0:T(1,128)S(1)} %add.6), channel_id=1, source_target_pairs={{0,2},{2,0},{4,6},{6,4},{1,3},{3,1},{5,7},{7,5},{8,10},{10,8},{12,... | collective-permute-start | bytes 24584 | tf_op jit(solution)/shard_map/ppermute | solution.py:501
  22.9 9.4 %collective-permute-start.5 = (bf16[40,2048]{1,0:T(8,128)(2,1)S(1)}, bf16[40,2048]{1,0:T(8,128)(2,1)S(1)}, u32[]{:S(2)}, u32[]{:S(2)}) collective-permute-start(bf16[40,2048]{1,0:T(8,128)(2,1)S(1)} %attend_halo.1), channel_id=1, source_target_pairs={{0,10},{2,12},{4,14},{8,18},{10,20},{12,22},{16,26},{18,28},{20,30... | collective-permute-start | bytes 491528 | tf_op jit(solution)/shard_map/ppermute | solution.py:521
  27.6 4.6 %collective-permute-start.6 = (f32[1,2048]{1,0:T(1,128)S(1)}, f32[1,2048]{1,0:T(1,128)S(1)}, u32[]{:S(2)}, u32[]{:S(2)}) collective-permute-start(f32[1,2048]{1,0:T(1,128)S(1)} %add.7.after_ref.term_ref), channel_id=1, source_target_pairs={{0,4},{2,6},{4,0},{6,2},{1,5},{3,7},{5,1},{7,3},{8,12},{10,14},{12... | collective-permute-start | bytes 24584 | tf_op jit(solution)/shard_map/ppermute | solution.py:501

commit v16 on v15

--- a/solution.py
+++ b/solution.py
@@ -255,7 +255,7 @@
         copy.wait()
 
 
-def halo_kernel(q_ref, k_ref, v_ref, bias, after_ref, out_ref):
+def halo_kernel(q_ref, k_ref, v_ref, bias, after_ref, out_ref, share_ref):
     half = bias.shape[0]
     molecules = half // POOL
     tail = pl.ds(half, half)
@@ -287,17 +287,17 @@
         parts.append(own_heads(mixed, inverse).astype(jnp.bfloat16))
         if len(parts) == 4:
             pooled = dot_nt(pooling, jnp.concatenate(parts, axis=0)).astype(jnp.bfloat16)
-            out_ref[pl.ds(0, molecules), pl.ds((pair - 3) * LANES, 4 * LANES)] = pooled
+            for i in range(4):
+                place = pl.ds((pair - 3 + i) * molecules, molecules)
+                out_ref[place, :] = pooled[:, i * LANES : (i + 1) * LANES]
             parts.clear()
-        share = kept * inverse
-        high = share.astype(jnp.bfloat16).astype(jnp.float32)
-        low = share - high
-        shares = [high[:, :half], low[:, :half], high[:, half:], low[:, half:]]
-        shares.append(jnp.zeros((EXTRA - 4, LANES), jnp.float32))
-        out_ref[pl.ds(molecules, EXTRA), at(pair)] = jnp.concatenate(shares, axis=0).astype(jnp.bfloat16)
+        share_ref[pl.ds(pair, 1), :] = kept * inverse
         return ()
 
     over_pairs(pairs, (score, top, weigh, mix, finish), LAGS, lambda pair: None)
+    share = share_ref[...].astype(jnp.bfloat16)
+    out_ref[pl.ds(pairs * molecules, pairs), :] = share[:, :half]
+    out_ref[pl.ds(pairs * (molecules + 1), pairs), :] = share[:, half:]
 
 
 def back_kernel(
@@ -330,7 +330,7 @@
 
 def project_kernel(
     early_ref, both_ref, halo_ref, gain_ref, weight_ref, term_ref, other_ref, upstream_hbm,
-    out_ref, update_ref, passed_hbm, scaled_ref, sem,
+    out_ref, update_ref, passed_hbm, scaled_ref, share_ref, sem,
 ):
     passing = load(upstream_hbm, passed_hbm, sem)
     half = both_ref.shape[1]
@@ -339,11 +339,11 @@
     molecules = half // POOL
     pooling = pool_matrix(half)
     first = lax.axis_index("seq") == 0
-    squares, parts = 0.0, []
-    for pair in range(features // LANES):
-        shares = halo_ref[molecules:, at(pair)].astype(jnp.float32)
-        share_a = jnp.where(first, 1.0, shares[0:1] + shares[1:2])
-        share_b = jnp.where(first, 1.0, shares[2:3] + shares[3:4])
+    squares, parts, pairs = 0.0, [], features // LANES
+    shares = halo_ref[pl.ds(pairs * molecules, 2 * pairs), :].astype(jnp.float32)
+    share_ref[...] = jnp.where(first, 1.0, shares)
+    for pair in range(pairs):
+        share_a, share_b = share_ref[pl.ds(pair, 1), :], share_ref[pl.ds(pairs + pair, 1), :]
         begin = pair * LANES
         if begin < first_part:
             early = early_ref[pl.ds(begin, LANES), :].astype(jnp.float32)
@@ -353,7 +353,8 @@
         if len(parts) == 8:
             columns = pl.ds((pair - 3) * LANES, 4 * LANES)
             mean = dot_nt(pooling, jnp.concatenate(parts, axis=0).astype(jnp.bfloat16))
-            upper = mean + halo_ref[:molecules, columns].astype(jnp.float32)
+            halo = [halo_ref[pl.ds((pair - 3 + i) * molecules, molecules), :] for i in range(4)]
+            upper = mean + jnp.concatenate(halo, axis=1).astype(jnp.float32)
             place = features - first_part + (pair - 3) * molecules
             lower = [both_ref[pl.ds(place + i * molecules, molecules), :] for i in range(4)]
             lower = jnp.concatenate(lower, axis=1)
@@ -450,7 +451,8 @@
         halo_kernel,
         in_specs=[VMEM] * 4 + [ANY],
         out_specs=VMEM,
-        out_shape=jax.ShapeDtypeStruct((half // POOL + EXTRA, width), jnp.bfloat16),
+        out_shape=jax.ShapeDtypeStruct((width // LANES * (half // POOL + 2), LANES), jnp.bfloat16),
+        scratch_shapes=[pltpu.VMEM((width // LANES, 2 * half), jnp.float32)],
         cost_estimate=cost(4 * half * half * width, 6 * half * width, half * half * width // 64),
         compiler_params=params(),
         name="attend_halo",
@@ -490,7 +492,11 @@
             jax.ShapeDtypeStruct(term.shape, term.dtype),
             jax.ShapeDtypeStruct(upstream.shape, upstream.dtype),
         ],
-        scratch_shapes=[pltpu.VMEM((rows, width), jnp.bfloat16), pltpu.SemaphoreType.DMA],
+        scratch_shapes=[
+            pltpu.VMEM((rows, width), jnp.bfloat16),
+            pltpu.VMEM((2 * width // LANES, LANES), jnp.float32),
+            pltpu.SemaphoreType.DMA,
+        ],
         cost_estimate=cost(2 * rows * width * depth, 2 * width * depth),
         compiler_params=params(),
         name="project",

time: 34.3 us -> 34.2 us (level)
  no operation moved by 1% of the time
where the time goes in v16:
time: 34.2 us; the launch traced here: 34 us
  starting transfers between devices  16.5 us (48%)
  Pallas kernels  10.3 us (30%)
  waiting for transfers between devices  5.8 us (17%)
  between operations  1.38 us (4%)
    ppermute x3, waiting for transfers between devices, swapped(): lax.ppermute(value, axis, [(i, i ^ distance) for i in range(lax.axis_size...  5.79 us
    ppermute x3, starting transfers between devices, swapped(): lax.ppermute(value, axis, [(i, i ^ distance) for i in range(lax.axis_size...  5.39 us
    ppermute x3, starting transfers between devices, passed_along(): lax.ppermute(value, axis, [(i, (i + steps) % count) for i in range(count)])  5.07 us
    ppermute x1, starting transfers between devices, onward(): return lax.ppermute(value, ('section', 'seq'), route)  4.73 us
    pallas_call x1, Pallas kernels, attend_early(): pl.pallas_call(functools.partial(early_kernel, rows, chunks), in_specs=[H...  3.03 us
    pallas_call x1, Pallas kernels, attend_late(): pl.pallas_call(functools.partial(late_kernel, rows), in_specs=[HBM] * 2 +...  2.53 us
    pallas_call x1, Pallas kernels, project(): pl.pallas_call(project_kernel, in_specs=[VMEM] * 7 + [ANY], out_specs=[VM...  1.73 us
    pallas_call x1, Pallas kernels, backward(): pl.pallas_call(back_kernel, in_specs=[VMEM] * 5 + [ANY], out_specs=[VMEM]...  1.56 us
  transfers between devices with their start and end apart: 8, of which 3 were waited for; matrix products, arithmetic and copies ran while one was open for 0% of the time, Pallas kernels for 16%

profile of v16, /device:TPU:0, one launch (start us, length us, event | category | flops | bytes accessed | tf_op | source)
XLA Modules:
  0.0 34.0 jit_solution(6667368080662238618)
XLA Ops:
  0.6 3.0 %attend_early.1 = (bf16[136,2048]{1,0:T(8,128)(2,1)S(1)}, bf16[1536,128]{1,0:T(8,128)(2,1)S(1)}, bf16[512,128]{1,0:T(8,128)(2,1)S(1)}, bf16[128,2048]{1,0:T(8,12...) custom-call(s32[1,8]{1,0:T(1,128)} %bitcast.17, ...), custom_call_target="tpu_custom_call" | custom-call | flops 134217728 | bytes 3145728 | tf_op jit(solution)/shard_map/attend_early/pallas_call | solution.py:396
  3.7 0.0 copy-start
  3.7 1.3 %collective-permute-start.2 = (bf16[136,2048]{1,0:T(8,128)(2,1)S(1)}, bf16[136,2048]{1,0:T(8,128)(2,1)S(1)}, u32[]{:S(2)}, u32[]{:S(2)}) collective-permute-start(bf16[136,2048]{1,0:T(8,128)(2,1)S(1)} %get-tuple-element.25), channel_id=1, source_target_pairs={{2,0},{4,2},{6,4},{3,1},{5,3},{7,5},{10,8},{12,10},{14,12},{11,9},... | collective-permute-start | bytes 1671176 | tf_op jit(solution)/shard_map/ppermute | solution.py:35
  5.0 3.0 %collective-permute-start = (bf16[1536,128]{1,0:T(8,128)(2,1)S(1)}, bf16[1536,128]{1,0:T(8,128)(2,1)S(1)}, u32[]{:S(2)}, u32[]{:S(2)}) collective-permute-start(bf16[1536,128]{1,0:T(8,128)(2,1)S(1)} %get-tuple-element.19), channel_id=1, source_target_pairs={{0,8},{8,16},{16,24},{24,0},{1,9},{9,17},{17,25},{25,1},{2,10},{10... | collective-permute-start | bytes 1179656 | tf_op jit(solution)/shard_map/ppermute | solution.py:40
  8.6 2.5 %attend_late.1 = (bf16[1024,128]{1,0:T(8,128)(2,1)S(1)}, f32[128,256]{1,0:T(8,128)S(1)}, bf16[2048,1024]{1,0:T(8,128)(2,1)S(1)}) custom-call(s32[1,8]{1,0:T(1,128)} %bitcast.18, bf16[2048,1024]{1,0:T(8,128)(2,1)} %bitcast.11, bf16[128,2048]{1,0:T(8,128)(2,1)S(1)} %get-tuple-element.20.q_ref, bf16[256,2048]{1,0:T(8,128)(2,1)S(1)} %get-tuple-element.21.k_ref, ...), custom_call_target="tpu_custom_call" | custom-call | flops 268435456 | bytes 2621440 | tf_op jit(solution)/shard_map/attend_late/pallas_call | solution.py:425
  11.2 0.0 copy-done
  11.2 1.6 %backward.1 = (bf16[64,2048]{1,0:T(8,128)(2,1)S(1)}, f32[1,2048]{1,0:T(1,128)S(1)}) custom-call(s32[1,128]{1,0:T(1,128)S(1)} %broadcast_in_dim.14.slot_ref, bf16[64,1024]{1,0:T(8,128)(2,1)S(1)} %get-tuple-element.27.cotangent_ref, bf16[2048,1024]{1,0:T(8,128)(2,1)S(1)} %get-tuple-element.28.weight_ref, f32[1,2048]{1,0:T(1,128)S(1)} %copy-done, ...), custom_call_target="tpu_custom_call" | custom-call | flops 268435456 | bytes 4194304 | tf_op jit(solution)/shard_map/backward/pallas_call | solution.py:465
  12.8 1.0 %collective-permute-start.7 = (bf16[64,2048]{1,0:T(8,128)(2,1)S(1)}, bf16[64,2048]{1,0:T(8,128)(2,1)S(1)}, u32[]{:S(2)}, u32[]{:S(2)}) collective-permute-start(bf16[64,2048]{1,0:T(8,128)(2,1)S(1)} %get-tuple-element.31), channel_id=1, source_target_pairs={{0,24},{8,0},{16,8},{24,16},{1,25},{9,1},{17,9},{25,17},{2,26},{10... | collective-permute-start | bytes 786440 | tf_op jit(solution)/shard_map/ppermute | solution.py:40
  13.8 1.1 %collective-permute-start.1 = (bf16[1024,128]{1,0:T(8,128)(2,1)S(1)}, bf16[1024,128]{1,0:T(8,128)(2,1)S(1)}, u32[]{:S(2)}, u32[]{:S(2)}) collective-permute-start(bf16[1024,128]{1,0:T(8,128)(2,1)S(1)} %get-tuple-element.24.after_ref), channel_id=1, source_target_pairs={{0,8},{8,16},{16,24},{24,0},{1,9},{9,17},{17,25},{25,1},{2,10},{10... | collective-permute-start | bytes 786440 | tf_op jit(solution)/shard_map/ppermute | solution.py:40
  14.8 0.0 collective-permute-start.3
  14.8 1.2 %collective-permute-done.3 = f32[1,2048]{1,0:T(1,128)S(1)} collective-permute-done((f32[1,2048]{1,0:T(1,128)S(1)}, f32[1,2048]{1,0:T(1,128)S(1)}, u32[]{:S(2)}, u32[]{:S(2)}) %collective-permute-start.3) | collective-permute-done | bytes 8224 | tf_op jit(solution)/shard_map/ppermute | solution.py:507
  16.0 2.7 %collective-permute-start.4 = (f32[1,2048]{1,0:T(1,128)S(1)}, f32[1,2048]{1,0:T(1,128)S(1)}, u32[]{:S(2)}, u32[]{:S(2)}) collective-permute-start(f32[1,2048]{1,0:T(1,128)S(1)} %add.6), channel_id=1, source_target_pairs={{0,2},{2,0},{4,6},{6,4},{1,3},{3,1},{5,7},{7,5},{8,10},{10,8},{12,... | collective-permute-start | bytes 24584 | tf_op jit(solution)/shard_map/ppermute | solution.py:507
  18.7 2.7 %collective-permute-done.4 = f32[1,2048]{1,0:T(1,128)S(1)} collective-permute-done((f32[1,2048]{1,0:T(1,128)S(1)}, f32[1,2048]{1,0:T(1,128)S(1)}, u32[]{:S(2)}, u32[]{:S(2)}) %collective-permute-start.4) | collective-permute-done | bytes 8224 | tf_op jit(solution)/shard_map/ppermute | solution.py:507
  21.4 0.0 collective-permute-done.2.q_ref
  21.4 1.5 %attend_halo.1 = bf16[544,128]{1,0:T(8,128)(2,1)S(1)} custom-call(bf16[136,2048]{1,0:T(8,128)(2,1)S(1)} %collective-permute-done.2.q_ref, bf16[256,2048]{1,0:T(8,128)(2,1)S(1)} %get-tuple-element.21.k_ref, bf16[256,2048]{1,0:T(8,128)(2,1)S(1)} %get-tuple-element.22.v_ref, f32[128,256]{1,0:T(8,128)S(1)} %get-tuple-element.26.bias, ...), custom_call_target="tpu_custom_call" | custom-call | flops 134217728 | bytes 1572864 | tf_op jit(solution)/shard_map/attend_halo/pallas_call | solution.py:450
  22.9 4.7 %collective-permute-start.5 = (bf16[544,128]{1,0:T(8,128)(2,1)S(1)}, bf16[544,128]{1,0:T(8,128)(2,1)S(1)}, u32[]{:S(2)}, u32[]{:S(2)}) collective-permute-start(bf16[544,128]{1,0:T(8,128)(2,1)S(1)} %attend_halo.1), channel_id=1, source_target_pairs={{0,10},{2,12},{4,14},{8,18},{10,20},{12,22},{16,26},{18,28},{20,30... | collective-permute-start | bytes 417800 | tf_op jit(solution)/shard_map/ppermute | solution.py:527
  27.6 2.7 %collective-permute-start.6 = (f32[1,2048]{1,0:T(1,128)S(1)}, f32[1,2048]{1,0:T(1,128)S(1)}, u32[]{:S(2)}, u32[]{:S(2)}) collective-permute-start(f32[1,2048]{1,0:T(1,128)S(1)} %add.7.after_ref.term_ref), channel_id=1, source_target_pairs={{0,4},{2,6},{4,0},{6,2},{1,5},{3,7},{5,1},{7,3},{8,12},{10,14},{12... | collective-permute-start | bytes 24584 | tf_op jit(solution)/shard_map/ppermute | solution.py:507
  30.3 1.9 %collective-permute-done.6.other_ref = f32[1,2048]{1,0:T(1,128)S(1)} collective-permute-done((f32[1,2048]{1,0:T(1,128)S(1)}, f32[1,2048]{1,0:T(1,128)S(1)}, u32[]{:S(2)}, u32[]{:S(2)}) %collective-permute-start.6) | collective-permute-done | bytes 8224 | tf_op jit(solution)/shard_map/ppermute | solution.py:507
  32.2 0.0 collective-permute-done.7.upstream_hbm
  32.2 0.0 collective-permute-done.1.both_ref
  32.2 0.0 collective-permute-done.early_ref
  32.3 0.0 collective-permute-done.5.halo_ref
  32.3 1.7 %project.1 = (bf16[64,1024]{1,0:T(8,128)(2,1)}, f32[1,2048]{1,0:T(1,128)}, bf16[64,2048]{1,0:T(8,128)(2,1)}) custom-call(bf16[1536,128]{1,0:T(8,128)(2,1)S(1)} %collective-permute-done.early_ref, bf16[1024,128]{1,0:T(8,128)(2,1)S(1)} %collective-permute-done.1.both_ref, bf16[544,128]{1,0:T(8,128)(2,1)S(1)} %collective-permute-done.5.halo_ref, ...), custom_call_target="tpu_custom_call" | custom-call | flops 268435456 | bytes 4194304 | tf_op jit(solution)/shard_map/project/pallas_call | solution.py:486
  (3 shorter events, 0.0 us)
Async XLA Ops:
  3.7 7.5 %copy-start = (f32[1,2048]{1,0:T(1,128)S(1)}, f32[1,2048]{1,0:T(1,128)}, u32[]{:S(2)}) copy-start(f32[1,2048]{1,0:T(1,128)} %gain_ref.3) | copy-start | bytes 24580
  3.7 17.7 %collective-permute-start.2 = (bf16[136,2048]{1,0:T(8,128)(2,1)S(1)}, bf16[136,2048]{1,0:T(8,128)(2,1)S(1)}, u32[]{:S(2)}, u32[]{:S(2)}) collective-permute-start(bf16[136,2048]{1,0:T(8,128)(2,1)S(1)} %get-tuple-element.25), channel_id=1, source_target_pairs={{2,0},{4,2},{6,4},{3,1},{5,3},{7,5},{10,8},{12,10},{14,12},{11,9},... | collective-permute-start | bytes 1671176 | tf_op jit(solution)/shard_map/ppermute | solution.py:35
  5.0 27.3 %collective-permute-start = (bf16[1536,128]{1,0:T(8,128)(2,1)S(1)}, bf16[1536,128]{1,0:T(8,128)(2,1)S(1)}, u32[]{:S(2)}, u32[]{:S(2)}) collective-permute-start(bf16[1536,128]{1,0:T(8,128)(2,1)S(1)} %get-tuple-element.19), channel_id=1, source_target_pairs={{0,8},{8,16},{16,24},{24,0},{1,9},{9,17},{17,25},{25,1},{2,10},{10... | collective-permute-start | bytes 1179656 | tf_op jit(solution)/shard_map/ppermute | solution.py:40
  12.8 19.5 %collective-permute-start.7 = (bf16[64,2048]{1,0:T(8,128)(2,1)S(1)}, bf16[64,2048]{1,0:T(8,128)(2,1)S(1)}, u32[]{:S(2)}, u32[]{:S(2)}) collective-permute-start(bf16[64,2048]{1,0:T(8,128)(2,1)S(1)} %get-tuple-element.31), channel_id=1, source_target_pairs={{0,24},{8,0},{16,8},{24,16},{1,25},{9,1},{17,9},{25,17},{2,26},{10... | collective-permute-start | bytes 786440 | tf_op jit(solution)/shard_map/ppermute | solution.py:40
  13.8 18.5 %collective-permute-start.1 = (bf16[1024,128]{1,0:T(8,128)(2,1)S(1)}, bf16[1024,128]{1,0:T(8,128)(2,1)S(1)}, u32[]{:S(2)}, u32[]{:S(2)}) collective-permute-start(bf16[1024,128]{1,0:T(8,128)(2,1)S(1)} %get-tuple-element.24.after_ref), channel_id=1, source_target_pairs={{0,8},{8,16},{16,24},{24,0},{1,9},{9,17},{17,25},{25,1},{2,10},{10... | collective-permute-start | bytes 786440 | tf_op jit(solution)/shard_map/ppermute | solution.py:40
  14.8 1.2 %collective-permute-start.3 = (f32[1,2048]{1,0:T(1,128)S(1)}, f32[1,2048]{1,0:T(1,128)S(1)}, u32[]{:S(2)}, u32[]{:S(2)}) collective-permute-start(f32[1,2048]{1,0:T(1,128)S(1)} %get-tuple-element.30), channel_id=1, source_target_pairs={{0,1},{1,0},{2,3},{3,2},{4,5},{5,4},{6,7},{7,6},{8,9},{9,8},{10,11... | collective-permute-start | bytes 24584 | tf_op jit(solution)/shard_map/ppermute | solution.py:507
  16.0 5.4 %collective-permute-start.4 = (f32[1,2048]{1,0:T(1,128)S(1)}, f32[1,2048]{1,0:T(1,128)S(1)}, u32[]{:S(2)}, u32[]{:S(2)}) collective-permute-start(f32[1,2048]{1,0:T(1,128)S(1)} %add.6), channel_id=1, source_target_pairs={{0,2},{2,0},{4,6},{6,4},{1,3},{3,1},{5,7},{7,5},{8,10},{10,8},{12,... | collective-permute-start | bytes 24584 | tf_op jit(solution)/shard_map/ppermute | solution.py:507
  22.9 9.4 %collective-permute-start.5 = (bf16[544,128]{1,0:T(8,128)(2,1)S(1)}, bf16[544,128]{1,0:T(8,128)(2,1)S(1)}, u32[]{:S(2)}, u32[]{:S(2)}) collective-permute-start(bf16[544,128]{1,0:T(8,128)(2,1)S(1)} %attend_halo.1), channel_id=1, source_target_pairs={{0,10},{2,12},{4,14},{8,18},{10,20},{12,22},{16,26},{18,28},{20,30... | collective-permute-start | bytes 417800 | tf_op jit(solution)/shard_map/ppermute | solution.py:527
  27.6 4.6 %collective-permute-start.6 = (f32[1,2048]{1,0:T(1,128)S(1)}, f32[1,2048]{1,0:T(1,128)S(1)}, u32[]{:S(2)}, u32[]{:S(2)}) collective-permute-start(f32[1,2048]{1,0:T(1,128)S(1)} %add.7.after_ref.term_ref), channel_id=1, source_target_pairs={{0,4},{2,6},{4,0},{6,2},{1,5},{3,7},{5,1},{7,3},{8,12},{10,14},{12... | collective-permute-start | bytes 24584 | tf_op jit(solution)/shard_map/ppermute | solution.py:507

commit v17 on v16

--- a/solution.py
+++ b/solution.py
@@ -16,7 +16,6 @@
 EPS_STEP = 1e-06
 MASKED = -1e30
 LAGS = (0, 3, 5, 6, 8)
-EXTRA = 8
 
 NT = (((1,), (1,)), ((), ()))
 
@@ -86,17 +85,6 @@
     copy = pltpu.make_async_copy(source, target, sem)
     copy.start()
     return copy
-
-
-def load_chunks(arrays, chunks, sems):
-    block = arrays[0][1].shape[1] // chunks
-    return [
-        [
-            load(source.at[:, pl.ds(chunk * block, block)], target.at[:, pl.ds(chunk * block, block)], sems.at[i, chunk])
-            for i, (source, target) in enumerate(arrays)
-        ]
-        for chunk in range(chunks)
-    ]
 
 
 def at(pair):
@@ -135,17 +123,28 @@
 def early_kernel(
     rows, chunks, offsets_hbm, q_hbm, k_hbm, v_hbm, cotangent_hbm, stashed_hbm,
     sent_ref, early_ref, more_ref, q_late_ref, k_ref, v_ref, cotangent_ref, stashed_ref,
-    offsets_ref, bias, sems, offsets_sem,
+    offsets_ref, bias, lse_ref, sems, offsets_sem,
 ):
     half = rows // 2
     head, tail = pl.ds(0, half), pl.ds(half, half)
     offsets_copy = load(offsets_hbm, offsets_ref, offsets_sem.at[0])
-    arrays = (
-        (k_hbm.at[head], k_ref.at[head]),
-        (q_hbm.at[head], sent_ref.at[head]),
-        (v_hbm.at[head], v_ref.at[head]),
-    )
-    copies = load_chunks(arrays, chunks, sems)
+    block = k_ref.shape[1] // chunks
+    pairs, per_chunk = k_ref.shape[1] // LANES, block // LANES
+    copies = {}
+
+    def fetch(chunk):
+        columns = pl.ds(chunk * block, block)
+        copies[chunk] = [
+            load(k_hbm.at[head, columns], k_ref.at[head, columns], sems.at[0, chunk]),
+            load(v_hbm.at[head, columns], v_ref.at[head, columns], sems.at[1, chunk]),
+        ]
+        for pair in range(chunk * per_chunk, (chunk + 1) * per_chunk):
+            copies[chunk].append(
+                load(q_hbm.at[head, at(pair)], sent_ref.at[pl.ds(pair * half, half)], sems.at[2 + pair % per_chunk, chunk])
+            )
+
+    fetch(0)
+    fetch(1)
     later = (
         (k_hbm.at[tail], k_ref.at[tail]),
         (v_hbm.at[tail], v_ref.at[tail]),
@@ -157,20 +156,21 @@
     offsets_copy.wait()
     start = lax.axis_index("seq") * rows
     bias[...] = mask_bias(offsets_ref, start, start, lambda key, query: key <= query)
-    pairs = k_ref.shape[1] // LANES
     split = early_ref.shape[0] // LANES
 
     def arrive(pair):
-        per_chunk = pairs // chunks
         if pair % per_chunk == 0:
-            for copy in copies[pair // per_chunk]:
+            chunk = pair // per_chunk
+            for copy in copies[chunk]:
                 copy.wait()
+            if chunk + 2 < chunks:
+                fetch(chunk + 2)
         if pair == per_chunk:
             for i, (source, target) in enumerate(later):
                 rest.append(load(source, target, offsets_sem.at[i + 1]))
 
     def score(pair):
-        scores = dot_nt(k_ref[head, at(pair)], split_heads(sent_ref[head, at(pair)]))
+        scores = dot_nt(k_ref[head, at(pair)], split_heads(sent_ref[pl.ds(pair * half, half), :]))
         return scores, with_ones(jnp.transpose(v_ref[head, at(pair)]))
 
     def top(pair, scores, values_t):
@@ -186,13 +186,14 @@
         total = mixed[LANES : LANES + 1]
         target, place = (early_ref, pair) if pair < split else (more_ref, pair - split)
         target[at(place), :] = own_heads(mixed, 1.0 / total).astype(jnp.bfloat16)
-        lse = top + jnp.log(total)
-        terms = three_terms(lse[:, :half]) + three_terms(lse[:, half:])
-        terms.append(jnp.zeros((EXTRA - 6, LANES), jnp.float32))
-        sent_ref[pl.ds(half, EXTRA), at(pair)] = jnp.concatenate(terms, axis=0).astype(jnp.bfloat16)
+        lse_ref[pl.ds(pair, 1), :] = top + jnp.log(total)
         return ()
 
     over_pairs(pairs, (score, top, weigh, mix, finish), LAGS, arrive)
+    for i, term in enumerate(three_terms(lse_ref[...])):
+        for j in range(2):
+            place = pl.ds(pairs * (half + 2 * i + j), pairs)
+            sent_ref[place, :] = term[:, j * half : (j + 1) * half].astype(jnp.bfloat16)
     for copy in rest:
         copy.wait()
 
@@ -255,24 +256,25 @@
         copy.wait()
 
 
-def halo_kernel(q_ref, k_ref, v_ref, bias, after_ref, out_ref, share_ref):
+def halo_kernel(q_ref, k_ref, v_ref, bias, after_ref, out_ref, lse_ref, share_ref):
     half = bias.shape[0]
     molecules = half // POOL
     tail = pl.ds(half, half)
     pooling = pool_matrix(half)
     pairs = k_ref.shape[1] // LANES
     parts = []
+    for j in range(2):
+        places = [pl.ds(pairs * (half + 2 * i + j), pairs) for i in range(3)]
+        high, middle, low = [q_ref[place, :].astype(jnp.float32) for place in places]
+        lse_ref[:, pl.ds(j * half, half)] = high + middle + low
 
     def score(pair):
-        queries = split_heads(q_ref[pl.ds(0, half), at(pair)])
+        queries = split_heads(q_ref[pl.ds(pair * half, half), :])
         scores = dot_nt(k_ref[tail, at(pair)], queries)
         return scores, with_ones(jnp.transpose(v_ref[tail, at(pair)]))
 
     def top(pair, scores, values_t):
-        terms = q_ref[pl.ds(half, EXTRA), at(pair)].astype(jnp.float32)
-        lse = jnp.concatenate(
-            [terms[0:1] + terms[1:2] + terms[2:3], terms[3:4] + terms[4:5] + terms[5:6]], axis=1
-        )
+        lse = lse_ref[pl.ds(pair, 1), :]
         return scores, jnp.maximum(tops(scores + bias[...]), lse), lse, values_t
 
     def weigh(pair, scores, top, lse, values_t):
@@ -398,7 +400,7 @@
         in_specs=[HBM] * 6,
         out_specs=[VMEM] * 8,
         out_shape=[
-            bf16(half + EXTRA, width),
+            bf16(width // LANES * (half + 6), LANES),
             bf16(soon, half),
             bf16(width - soon, half),
             bf16(half, width),
@@ -410,7 +412,8 @@
         scratch_shapes=[
             pltpu.SMEM(offsets.shape, jnp.int32),
             pltpu.VMEM((half, 2 * half), jnp.float32),
-            pltpu.SemaphoreType.DMA((3, chunks)),
+            pltpu.VMEM((width // LANES, 2 * half), jnp.float32),
+            pltpu.SemaphoreType.DMA((2 + width // LANES // chunks, chunks)),
             pltpu.SemaphoreType.DMA((6,)),
         ],
         cost_estimate=cost(4 * half * half * width, 6 * rows * width, half * half * width // 64),
@@ -452,7 +455,7 @@
         in_specs=[VMEM] * 4 + [ANY],
         out_specs=VMEM,
         out_shape=jax.ShapeDtypeStruct((width // LANES * (half // POOL + 2), LANES), jnp.bfloat16),
-        scratch_shapes=[pltpu.VMEM((width // LANES, 2 * half), jnp.float32)],
+        scratch_shapes=[pltpu.VMEM((width // LANES, 2 * half), jnp.float32)] * 2,
         cost_estimate=cost(4 * half * half * width, 6 * half * width, half * half * width // 64),
         compiler_params=params(),
         name="attend_halo",

time: 34.2 us -> 34.5 us (level)
  no operation moved by 1% of the time
where the time goes in v17:
time: 34.5 us; the launch traced here: 34.2 us
  starting transfers between devices  16.7 us (48%)
  Pallas kernels  10.6 us (31%)
  waiting for transfers between devices  5.59 us (16%)
  between operations  1.38 us (4%)
    ppermute x3, waiting for transfers between devices, swapped(): lax.ppermute(value, axis, [(i, i ^ distance) for i in range(lax.axis_size...  5.58 us
    ppermute x3, starting transfers between devices, swapped(): lax.ppermute(value, axis, [(i, i ^ distance) for i in range(lax.axis_size...  5.41 us
    ppermute x3, starting transfers between devices, passed_along(): lax.ppermute(value, axis, [(i, (i + steps) % count) for i in range(count)])  5.07 us
    ppermute x1, starting transfers between devices, onward(): return lax.ppermute(value, ('section', 'seq'), route)  4.91 us
    pallas_call x1, Pallas kernels, attend_early(): pl.pallas_call(functools.partial(early_kernel, rows, chunks), in_specs=[H...  3.25 us
    pallas_call x1, Pallas kernels, attend_late(): pl.pallas_call(functools.partial(late_kernel, rows), in_specs=[HBM] * 2 +...  2.55 us
    pallas_call x1, Pallas kernels, project(): pl.pallas_call(project_kernel, in_specs=[VMEM] * 7 + [ANY], out_specs=[VM...  1.73 us
    pallas_call x1, Pallas kernels, backward(): pl.pallas_call(back_kernel, in_specs=[VMEM] * 5 + [ANY], out_specs=[VMEM]...  1.56 us
  transfers between devices with their start and end apart: 8, of which 3 were waited for; matrix products, arithmetic and copies ran while one was open for 0% of the time, Pallas kernels for 16%

profile of v17, /device:TPU:0, one launch (start us, length us, event | category | flops | bytes accessed | tf_op | source)
XLA Modules:
  0.0 34.2 jit_solution(18195878917357802760)
XLA Ops:
  0.6 3.2 %attend_early.1 = (bf16[2144,128]{1,0:T(8,128)(2,1)S(1)}, bf16[1536,128]{1,0:T(8,128)(2,1)S(1)}, bf16[512,128]{1,0:T(8,128)(2,1)S(1)}, bf16[128,2048]{1,0:T(8,12...) custom-call(s32[1,8]{1,0:T(1,128)} %bitcast.17, ...), custom_call_target="tpu_custom_call" | custom-call | flops 134217728 | bytes 3145728 | tf_op jit(solution)/shard_map/attend_early/pallas_call | solution.py:398
  3.9 0.0 copy-start
  3.9 1.3 %collective-permute-start.2 = (bf16[2144,128]{1,0:T(8,128)(2,1)S(1)}, bf16[2144,128]{1,0:T(8,128)(2,1)S(1)}, u32[]{:S(2)}, u32[]{:S(2)}) collective-permute-start(bf16[2144,128]{1,0:T(8,128)(2,1)S(1)} %get-tuple-element.25), channel_id=1, source_target_pairs={{2,0},{4,2},{6,4},{3,1},{5,3},{7,5},{10,8},{12,10},{14,12},{11,9},... | collective-permute-start | bytes 1646600 | tf_op jit(solution)/shard_map/ppermute | solution.py:34
  5.2 3.0 %collective-permute-start = (bf16[1536,128]{1,0:T(8,128)(2,1)S(1)}, bf16[1536,128]{1,0:T(8,128)(2,1)S(1)}, u32[]{:S(2)}, u32[]{:S(2)}) collective-permute-start(bf16[1536,128]{1,0:T(8,128)(2,1)S(1)} %get-tuple-element.19), channel_id=1, source_target_pairs={{0,8},{8,16},{16,24},{24,0},{1,9},{9,17},{17,25},{25,1},{2,10},{10... | collective-permute-start | bytes 1179656 | tf_op jit(solution)/shard_map/ppermute | solution.py:39
  8.8 2.6 %attend_late.1 = (bf16[1024,128]{1,0:T(8,128)(2,1)S(1)}, f32[128,256]{1,0:T(8,128)S(1)}, bf16[2048,1024]{1,0:T(8,128)(2,1)S(1)}) custom-call(s32[1,8]{1,0:T(1,128)} %bitcast.18, bf16[2048,1024]{1,0:T(8,128)(2,1)} %bitcast.11, bf16[128,2048]{1,0:T(8,128)(2,1)S(1)} %get-tuple-element.20.q_ref, bf16[256,2048]{1,0:T(8,128)(2,1)S(1)} %get-tuple-element.21.k_ref, ...), custom_call_target="tpu_custom_call" | custom-call | flops 268435456 | bytes 2621440 | tf_op jit(solution)/shard_map/attend_late/pallas_call | solution.py:428
  11.4 0.0 copy-done
  11.4 1.6 %backward.1 = (bf16[64,2048]{1,0:T(8,128)(2,1)S(1)}, f32[1,2048]{1,0:T(1,128)S(1)}) custom-call(s32[1,128]{1,0:T(1,128)S(1)} %broadcast_in_dim.14.slot_ref, bf16[64,1024]{1,0:T(8,128)(2,1)S(1)} %get-tuple-element.27.cotangent_ref, bf16[2048,1024]{1,0:T(8,128)(2,1)S(1)} %get-tuple-element.28.weight_ref, f32[1,2048]{1,0:T(1,128)S(1)} %copy-done, ...), custom_call_target="tpu_custom_call" | custom-call | flops 268435456 | bytes 4194304 | tf_op jit(solution)/shard_map/backward/pallas_call | solution.py:468
  13.0 1.0 %collective-permute-start.7 = (bf16[64,2048]{1,0:T(8,128)(2,1)S(1)}, bf16[64,2048]{1,0:T(8,128)(2,1)S(1)}, u32[]{:S(2)}, u32[]{:S(2)}) collective-permute-start(bf16[64,2048]{1,0:T(8,128)(2,1)S(1)} %get-tuple-element.31), channel_id=1, source_target_pairs={{0,24},{8,0},{16,8},{24,16},{1,25},{9,1},{17,9},{25,17},{2,26},{10... | collective-permute-start | bytes 786440 | tf_op jit(solution)/shard_map/ppermute | solution.py:39
  14.0 1.1 %collective-permute-start.1 = (bf16[1024,128]{1,0:T(8,128)(2,1)S(1)}, bf16[1024,128]{1,0:T(8,128)(2,1)S(1)}, u32[]{:S(2)}, u32[]{:S(2)}) collective-permute-start(bf16[1024,128]{1,0:T(8,128)(2,1)S(1)} %get-tuple-element.24.after_ref), channel_id=1, source_target_pairs={{0,8},{8,16},{16,24},{24,0},{1,9},{9,17},{17,25},{25,1},{2,10},{10... | collective-permute-start | bytes 786440 | tf_op jit(solution)/shard_map/ppermute | solution.py:39
  15.1 0.0 collective-permute-start.3
  15.1 1.2 %collective-permute-done.3 = f32[1,2048]{1,0:T(1,128)S(1)} collective-permute-done((f32[1,2048]{1,0:T(1,128)S(1)}, f32[1,2048]{1,0:T(1,128)S(1)}, u32[]{:S(2)}, u32[]{:S(2)}) %collective-permute-start.3) | collective-permute-done | bytes 8224 | tf_op jit(solution)/shard_map/ppermute | solution.py:510
  16.3 2.7 %collective-permute-start.4 = (f32[1,2048]{1,0:T(1,128)S(1)}, f32[1,2048]{1,0:T(1,128)S(1)}, u32[]{:S(2)}, u32[]{:S(2)}) collective-permute-start(f32[1,2048]{1,0:T(1,128)S(1)} %add.6), channel_id=1, source_target_pairs={{0,2},{2,0},{4,6},{6,4},{1,3},{3,1},{5,7},{7,5},{8,10},{10,8},{12,... | collective-permute-start | bytes 24584 | tf_op jit(solution)/shard_map/ppermute | solution.py:510
  19.0 2.5 %collective-permute-done.4 = f32[1,2048]{1,0:T(1,128)S(1)} collective-permute-done((f32[1,2048]{1,0:T(1,128)S(1)}, f32[1,2048]{1,0:T(1,128)S(1)}, u32[]{:S(2)}, u32[]{:S(2)}) %collective-permute-start.4) | collective-permute-done | bytes 8224 | tf_op jit(solution)/shard_map/ppermute | solution.py:510
  21.5 0.0 collective-permute-done.2.q_ref
  21.5 1.5 %attend_halo.1 = bf16[544,128]{1,0:T(8,128)(2,1)S(1)} custom-call(bf16[2144,128]{1,0:T(8,128)(2,1)S(1)} %collective-permute-done.2.q_ref, bf16[256,2048]{1,0:T(8,128)(2,1)S(1)} %get-tuple-element.21.k_ref, bf16[256,2048]{1,0:T(8,128)(2,1)S(1)} %get-tuple-element.22.v_ref, f32[128,256]{1,0:T(8,128)S(1)} %get-tuple-element.26.bias, ...), custom_call_target="tpu_custom_call" | custom-call | flops 134217728 | bytes 1572864 | tf_op jit(solution)/shard_map/attend_halo/pallas_call | solution.py:453
  23.0 4.9 %collective-permute-start.5 = (bf16[544,128]{1,0:T(8,128)(2,1)S(1)}, bf16[544,128]{1,0:T(8,128)(2,1)S(1)}, u32[]{:S(2)}, u32[]{:S(2)}) collective-permute-start(bf16[544,128]{1,0:T(8,128)(2,1)S(1)} %attend_halo.1), channel_id=1, source_target_pairs={{0,10},{2,12},{4,14},{8,18},{10,20},{12,22},{16,26},{18,28},{20,30... | collective-permute-start | bytes 417800 | tf_op jit(solution)/shard_map/ppermute | solution.py:530
  27.9 2.7 %collective-permute-start.6 = (f32[1,2048]{1,0:T(1,128)S(1)}, f32[1,2048]{1,0:T(1,128)S(1)}, u32[]{:S(2)}, u32[]{:S(2)}) collective-permute-start(f32[1,2048]{1,0:T(1,128)S(1)} %add.7.after_ref.term_ref), channel_id=1, source_target_pairs={{0,4},{2,6},{4,0},{6,2},{1,5},{3,7},{5,1},{7,3},{8,12},{10,14},{12... | collective-permute-start | bytes 24584 | tf_op jit(solution)/shard_map/ppermute | solution.py:510
  30.6 1.9 %collective-permute-done.6.other_ref = f32[1,2048]{1,0:T(1,128)S(1)} collective-permute-done((f32[1,2048]{1,0:T(1,128)S(1)}, f32[1,2048]{1,0:T(1,128)S(1)}, u32[]{:S(2)}, u32[]{:S(2)}) %collective-permute-start.6) | collective-permute-done | bytes 8224 | tf_op jit(solution)/shard_map/ppermute | solution.py:510
  32.5 0.0 collective-permute-done.7.upstream_hbm
  32.5 0.0 collective-permute-done.1.both_ref
  32.5 0.0 collective-permute-done.early_ref
  32.5 0.0 collective-permute-done.5.halo_ref
  32.5 1.7 %project.1 = (bf16[64,1024]{1,0:T(8,128)(2,1)}, f32[1,2048]{1,0:T(1,128)}, bf16[64,2048]{1,0:T(8,128)(2,1)}) custom-call(bf16[1536,128]{1,0:T(8,128)(2,1)S(1)} %collective-permute-done.early_ref, bf16[1024,128]{1,0:T(8,128)(2,1)S(1)} %collective-permute-done.1.both_ref, bf16[544,128]{1,0:T(8,128)(2,1)S(1)} %collective-permute-done.5.halo_ref, ...), custom_call_target="tpu_custom_call" | custom-call | flops 268435456 | bytes 4194304 | tf_op jit(solution)/shard_map/project/pallas_call | solution.py:489
  (3 shorter events, 0.0 us)
Async XLA Ops:
  3.9 7.5 %copy-start = (f32[1,2048]{1,0:T(1,128)S(1)}, f32[1,2048]{1,0:T(1,128)}, u32[]{:S(2)}) copy-start(f32[1,2048]{1,0:T(1,128)} %gain_ref.3) | copy-start | bytes 24580
  3.9 17.6 %collective-permute-start.2 = (bf16[2144,128]{1,0:T(8,128)(2,1)S(1)}, bf16[2144,128]{1,0:T(8,128)(2,1)S(1)}, u32[]{:S(2)}, u32[]{:S(2)}) collective-permute-start(bf16[2144,128]{1,0:T(8,128)(2,1)S(1)} %get-tuple-element.25), channel_id=1, source_target_pairs={{2,0},{4,2},{6,4},{3,1},{5,3},{7,5},{10,8},{12,10},{14,12},{11,9},... | collective-permute-start | bytes 1646600 | tf_op jit(solution)/shard_map/ppermute | solution.py:34
  5.2 27.3 %collective-permute-start = (bf16[1536,128]{1,0:T(8,128)(2,1)S(1)}, bf16[1536,128]{1,0:T(8,128)(2,1)S(1)}, u32[]{:S(2)}, u32[]{:S(2)}) collective-permute-start(bf16[1536,128]{1,0:T(8,128)(2,1)S(1)} %get-tuple-element.19), channel_id=1, source_target_pairs={{0,8},{8,16},{16,24},{24,0},{1,9},{9,17},{17,25},{25,1},{2,10},{10... | collective-permute-start | bytes 1179656 | tf_op jit(solution)/shard_map/ppermute | solution.py:39
  13.0 19.5 %collective-permute-start.7 = (bf16[64,2048]{1,0:T(8,128)(2,1)S(1)}, bf16[64,2048]{1,0:T(8,128)(2,1)S(1)}, u32[]{:S(2)}, u32[]{:S(2)}) collective-permute-start(bf16[64,2048]{1,0:T(8,128)(2,1)S(1)} %get-tuple-element.31), channel_id=1, source_target_pairs={{0,24},{8,0},{16,8},{24,16},{1,25},{9,1},{17,9},{25,17},{2,26},{10... | collective-permute-start | bytes 786440 | tf_op jit(solution)/shard_map/ppermute | solution.py:39
  14.0 18.5 %collective-permute-start.1 = (bf16[1024,128]{1,0:T(8,128)(2,1)S(1)}, bf16[1024,128]{1,0:T(8,128)(2,1)S(1)}, u32[]{:S(2)}, u32[]{:S(2)}) collective-permute-start(bf16[1024,128]{1,0:T(8,128)(2,1)S(1)} %get-tuple-element.24.after_ref), channel_id=1, source_target_pairs={{0,8},{8,16},{16,24},{24,0},{1,9},{9,17},{17,25},{25,1},{2,10},{10... | collective-permute-start | bytes 786440 | tf_op jit(solution)/shard_map/ppermute | solution.py:39
  15.1 1.2 %collective-permute-start.3 = (f32[1,2048]{1,0:T(1,128)S(1)}, f32[1,2048]{1,0:T(1,128)S(1)}, u32[]{:S(2)}, u32[]{:S(2)}) collective-permute-start(f32[1,2048]{1,0:T(1,128)S(1)} %get-tuple-element.30), channel_id=1, source_target_pairs={{0,1},{1,0},{2,3},{3,2},{4,5},{5,4},{6,7},{7,6},{8,9},{9,8},{10,11... | collective-permute-start | bytes 24584 | tf_op jit(solution)/shard_map/ppermute | solution.py:510
  16.3 5.2 %collective-permute-start.4 = (f32[1,2048]{1,0:T(1,128)S(1)}, f32[1,2048]{1,0:T(1,128)S(1)}, u32[]{:S(2)}, u32[]{:S(2)}) collective-permute-start(f32[1,2048]{1,0:T(1,128)S(1)} %add.6), channel_id=1, source_target_pairs={{0,2},{2,0},{4,6},{6,4},{1,3},{3,1},{5,7},{7,5},{8,10},{10,8},{12,... | collective-permute-start | bytes 24584 | tf_op jit(solution)/shard_map/ppermute | solution.py:510
  23.0 9.5 %collective-permute-start.5 = (bf16[544,128]{1,0:T(8,128)(2,1)S(1)}, bf16[544,128]{1,0:T(8,128)(2,1)S(1)}, u32[]{:S(2)}, u32[]{:S(2)}) collective-permute-start(bf16[544,128]{1,0:T(8,128)(2,1)S(1)} %attend_halo.1), channel_id=1, source_target_pairs={{0,10},{2,12},{4,14},{8,18},{10,20},{12,22},{16,26},{18,28},{20,30... | collective-permute-start | bytes 417800 | tf_op jit(solution)/shard_map/ppermute | solution.py:530
  27.9 4.6 %collective-permute-start.6 = (f32[1,2048]{1,0:T(1,128)S(1)}, f32[1,2048]{1,0:T(1,128)S(1)}, u32[]{:S(2)}, u32[]{:S(2)}) collective-permute-start(f32[1,2048]{1,0:T(1,128)S(1)} %add.7.after_ref.term_ref), channel_id=1, source_target_pairs={{0,4},{2,6},{4,0},{6,2},{1,5},{3,7},{5,1},{7,3},{8,12},{10,14},{12... | collective-permute-start | bytes 24584 | tf_op jit(solution)/shard_map/ppermute | solution.py:510

commit v18 on v16

--- a/solution.py
+++ b/solution.py
@@ -88,15 +88,20 @@
     return copy
 
 
-def load_chunks(arrays, chunks, sems):
+def load_chunks(arrays, chunks, sems, between):
     block = arrays[0][1].shape[1] // chunks
-    return [
-        [
-            load(source.at[:, pl.ds(chunk * block, block)], target.at[:, pl.ds(chunk * block, block)], sems.at[i, chunk])
-            for i, (source, target) in enumerate(arrays)
-        ]
-        for chunk in range(chunks)
-    ]
+    copies, extra = [], None
+    for chunk in range(chunks):
+        columns = pl.ds(chunk * block, block)
+        copies.append(
+            [
+                load(source.at[:, columns], target.at[:, columns], sems.at[i, chunk])
+                for i, (source, target) in enumerate(arrays)
+            ]
+        )
+        if chunk == 0:
+            extra = between()
+    return copies, extra
 
 
 def at(pair):
@@ -139,13 +144,13 @@
 ):
     half = rows // 2
     head, tail = pl.ds(0, half), pl.ds(half, half)
-    offsets_copy = load(offsets_hbm, offsets_ref, offsets_sem.at[0])
     arrays = (
         (k_hbm.at[head], k_ref.at[head]),
         (q_hbm.at[head], sent_ref.at[head]),
         (v_hbm.at[head], v_ref.at[head]),
     )
-    copies = load_chunks(arrays, chunks, sems)
+    copies = load_chunks(arrays, chunks, sems, lambda: load(offsets_hbm, offsets_ref, offsets_sem.at[0]))
+    copies, offsets_copy = copies
     later = (
         (k_hbm.at[tail], k_ref.at[tail]),
         (v_hbm.at[tail], v_ref.at[tail]),
@@ -154,9 +159,7 @@
         (stashed_hbm, stashed_ref),
     )
     rest = []
-    offsets_copy.wait()
     start = lax.axis_index("seq") * rows
-    bias[...] = mask_bias(offsets_ref, start, start, lambda key, query: key <= query)
     pairs = k_ref.shape[1] // LANES
     split = early_ref.shape[0] // LANES
 
@@ -165,6 +168,9 @@
         if pair % per_chunk == 0:
             for copy in copies[pair // per_chunk]:
                 copy.wait()
+        if pair == 0:
+            offsets_copy.wait()
+            bias[...] = mask_bias(offsets_ref, start, start, lambda key, query: key <= query)
         if pair == per_chunk:
             for i, (source, target) in enumerate(later):
                 rest.append(load(source, target, offsets_sem.at[i + 1]))

time: 34.2 us -> 34.2 us (level)
  no operation moved by 1% of the time
where the time goes in v18:
time: 34.2 us; the launch traced here: 34 us
  starting transfers between devices  16.5 us (48%)
  Pallas kernels  10.3 us (30%)
  waiting for transfers between devices  5.79 us (17%)
  between operations  1.38 us (4%)
    ppermute x3, waiting for transfers between devices, swapped(): lax.ppermute(value, axis, [(i, i ^ distance) for i in range(lax.axis_size...  5.78 us
    ppermute x3, starting transfers between devices, swapped(): lax.ppermute(value, axis, [(i, i ^ distance) for i in range(lax.axis_size...  5.39 us
    ppermute x3, starting transfers between devices, passed_along(): lax.ppermute(value, axis, [(i, (i + steps) % count) for i in range(count)])  5.07 us
    ppermute x1, starting transfers between devices, onward(): return lax.ppermute(value, ('section', 'seq'), route)  4.73 us
    pallas_call x1, Pallas kernels, attend_early(): pl.pallas_call(functools.partial(early_kernel, rows, chunks), in_specs=[H...  3.02 us
    pallas_call x1, Pallas kernels, attend_late(): pl.pallas_call(functools.partial(late_kernel, rows), in_specs=[HBM] * 2 +...  2.53 us
    pallas_call x1, Pallas kernels, project(): pl.pallas_call(project_kernel, in_specs=[VMEM] * 7 + [ANY], out_specs=[VM...  1.73 us
    pallas_call x1, Pallas kernels, backward(): pl.pallas_call(back_kernel, in_specs=[VMEM] * 5 + [ANY], out_specs=[VMEM]...  1.56 us
  transfers between devices with their start and end apart: 8, of which 3 were waited for; matrix products, arithmetic and copies ran while one was open for 0% of the time, Pallas kernels for 16%

profile of v18, /device:TPU:0, one launch (start us, length us, event | category | flops | bytes accessed | tf_op | source)
XLA Modules:
  0.0 34.0 jit_solution(8488713567859488831)
XLA Ops:
  0.6 3.0 %attend_early.1 = (bf16[136,2048]{1,0:T(8,128)(2,1)S(1)}, bf16[1536,128]{1,0:T(8,128)(2,1)S(1)}, bf16[512,128]{1,0:T(8,128)(2,1)S(1)}, bf16[128,2048]{1,0:T(8,12...) custom-call(s32[1,8]{1,0:T(1,128)} %bitcast.17, ...), custom_call_target="tpu_custom_call" | custom-call | flops 134217728 | bytes 3145728 | tf_op jit(solution)/shard_map/attend_early/pallas_call | solution.py:402
  3.7 0.0 copy-start
  3.7 1.3 %collective-permute-start.2 = (bf16[136,2048]{1,0:T(8,128)(2,1)S(1)}, bf16[136,2048]{1,0:T(8,128)(2,1)S(1)}, u32[]{:S(2)}, u32[]{:S(2)}) collective-permute-start(bf16[136,2048]{1,0:T(8,128)(2,1)S(1)} %get-tuple-element.25), channel_id=1, source_target_pairs={{2,0},{4,2},{6,4},{3,1},{5,3},{7,5},{10,8},{12,10},{14,12},{11,9},... | collective-permute-start | bytes 1671176 | tf_op jit(solution)/shard_map/ppermute | solution.py:35
  5.0 3.0 %collective-permute-start = (bf16[1536,128]{1,0:T(8,128)(2,1)S(1)}, bf16[1536,128]{1,0:T(8,128)(2,1)S(1)}, u32[]{:S(2)}, u32[]{:S(2)}) collective-permute-start(bf16[1536,128]{1,0:T(8,128)(2,1)S(1)} %get-tuple-element.19), channel_id=1, source_target_pairs={{0,8},{8,16},{16,24},{24,0},{1,9},{9,17},{17,25},{25,1},{2,10},{10... | collective-permute-start | bytes 1179656 | tf_op jit(solution)/shard_map/ppermute | solution.py:40
  8.6 2.5 %attend_late.1 = (bf16[1024,128]{1,0:T(8,128)(2,1)S(1)}, f32[128,256]{1,0:T(8,128)S(1)}, bf16[2048,1024]{1,0:T(8,128)(2,1)S(1)}) custom-call(s32[1,8]{1,0:T(1,128)} %bitcast.18, bf16[2048,1024]{1,0:T(8,128)(2,1)} %bitcast.11, bf16[128,2048]{1,0:T(8,128)(2,1)S(1)} %get-tuple-element.20.q_ref, bf16[256,2048]{1,0:T(8,128)(2,1)S(1)} %get-tuple-element.21.k_ref, ...), custom_call_target="tpu_custom_call" | custom-call | flops 268435456 | bytes 2621440 | tf_op jit(solution)/shard_map/attend_late/pallas_call | solution.py:431
  11.2 0.0 copy-done
  11.2 1.6 %backward.1 = (bf16[64,2048]{1,0:T(8,128)(2,1)S(1)}, f32[1,2048]{1,0:T(1,128)S(1)}) custom-call(s32[1,128]{1,0:T(1,128)S(1)} %broadcast_in_dim.14.slot_ref, bf16[64,1024]{1,0:T(8,128)(2,1)S(1)} %get-tuple-element.27.cotangent_ref, bf16[2048,1024]{1,0:T(8,128)(2,1)S(1)} %get-tuple-element.28.weight_ref, f32[1,2048]{1,0:T(1,128)S(1)} %copy-done, ...), custom_call_target="tpu_custom_call" | custom-call | flops 268435456 | bytes 4194304 | tf_op jit(solution)/shard_map/backward/pallas_call | solution.py:471
  12.7 1.0 %collective-permute-start.7 = (bf16[64,2048]{1,0:T(8,128)(2,1)S(1)}, bf16[64,2048]{1,0:T(8,128)(2,1)S(1)}, u32[]{:S(2)}, u32[]{:S(2)}) collective-permute-start(bf16[64,2048]{1,0:T(8,128)(2,1)S(1)} %get-tuple-element.31), channel_id=1, source_target_pairs={{0,24},{8,0},{16,8},{24,16},{1,25},{9,1},{17,9},{25,17},{2,26},{10... | collective-permute-start | bytes 786440 | tf_op jit(solution)/shard_map/ppermute | solution.py:40
  13.8 1.1 %collective-permute-start.1 = (bf16[1024,128]{1,0:T(8,128)(2,1)S(1)}, bf16[1024,128]{1,0:T(8,128)(2,1)S(1)}, u32[]{:S(2)}, u32[]{:S(2)}) collective-permute-start(bf16[1024,128]{1,0:T(8,128)(2,1)S(1)} %get-tuple-element.24.after_ref), channel_id=1, source_target_pairs={{0,8},{8,16},{16,24},{24,0},{1,9},{9,17},{17,25},{25,1},{2,10},{10... | collective-permute-start | bytes 786440 | tf_op jit(solution)/shard_map/ppermute | solution.py:40
  14.8 0.0 collective-permute-start.3
  14.8 1.2 %collective-permute-done.3 = f32[1,2048]{1,0:T(1,128)S(1)} collective-permute-done((f32[1,2048]{1,0:T(1,128)S(1)}, f32[1,2048]{1,0:T(1,128)S(1)}, u32[]{:S(2)}, u32[]{:S(2)}) %collective-permute-start.3) | collective-permute-done | bytes 8224 | tf_op jit(solution)/shard_map/ppermute | solution.py:513
  16.0 2.7 %collective-permute-start.4 = (f32[1,2048]{1,0:T(1,128)S(1)}, f32[1,2048]{1,0:T(1,128)S(1)}, u32[]{:S(2)}, u32[]{:S(2)}) collective-permute-start(f32[1,2048]{1,0:T(1,128)S(1)} %add.6), channel_id=1, source_target_pairs={{0,2},{2,0},{4,6},{6,4},{1,3},{3,1},{5,7},{7,5},{8,10},{10,8},{12,... | collective-permute-start | bytes 24584 | tf_op jit(solution)/shard_map/ppermute | solution.py:513
  18.7 2.7 %collective-permute-done.4 = f32[1,2048]{1,0:T(1,128)S(1)} collective-permute-done((f32[1,2048]{1,0:T(1,128)S(1)}, f32[1,2048]{1,0:T(1,128)S(1)}, u32[]{:S(2)}, u32[]{:S(2)}) %collective-permute-start.4) | collective-permute-done | bytes 8224 | tf_op jit(solution)/shard_map/ppermute | solution.py:513
  21.4 0.0 collective-permute-done.2.q_ref
  21.4 1.5 %attend_halo.1 = bf16[544,128]{1,0:T(8,128)(2,1)S(1)} custom-call(bf16[136,2048]{1,0:T(8,128)(2,1)S(1)} %collective-permute-done.2.q_ref, bf16[256,2048]{1,0:T(8,128)(2,1)S(1)} %get-tuple-element.21.k_ref, bf16[256,2048]{1,0:T(8,128)(2,1)S(1)} %get-tuple-element.22.v_ref, f32[128,256]{1,0:T(8,128)S(1)} %get-tuple-element.26.bias, ...), custom_call_target="tpu_custom_call" | custom-call | flops 134217728 | bytes 1572864 | tf_op jit(solution)/shard_map/attend_halo/pallas_call | solution.py:456
  22.9 4.7 %collective-permute-start.5 = (bf16[544,128]{1,0:T(8,128)(2,1)S(1)}, bf16[544,128]{1,0:T(8,128)(2,1)S(1)}, u32[]{:S(2)}, u32[]{:S(2)}) collective-permute-start(bf16[544,128]{1,0:T(8,128)(2,1)S(1)} %attend_halo.1), channel_id=1, source_target_pairs={{0,10},{2,12},{4,14},{8,18},{10,20},{12,22},{16,26},{18,28},{20,30... | collective-permute-start | bytes 417800 | tf_op jit(solution)/shard_map/ppermute | solution.py:533
  27.6 2.7 %collective-permute-start.6 = (f32[1,2048]{1,0:T(1,128)S(1)}, f32[1,2048]{1,0:T(1,128)S(1)}, u32[]{:S(2)}, u32[]{:S(2)}) collective-permute-start(f32[1,2048]{1,0:T(1,128)S(1)} %add.7.after_ref.term_ref), channel_id=1, source_target_pairs={{0,4},{2,6},{4,0},{6,2},{1,5},{3,7},{5,1},{7,3},{8,12},{10,14},{12... | collective-permute-start | bytes 24584 | tf_op jit(solution)/shard_map/ppermute | solution.py:513
  30.3 1.9 %collective-permute-done.6.other_ref = f32[1,2048]{1,0:T(1,128)S(1)} collective-permute-done((f32[1,2048]{1,0:T(1,128)S(1)}, f32[1,2048]{1,0:T(1,128)S(1)}, u32[]{:S(2)}, u32[]{:S(2)}) %collective-permute-start.6) | collective-permute-done | bytes 8224 | tf_op jit(solution)/shard_map/ppermute | solution.py:513
  32.2 0.0 collective-permute-done.7.upstream_hbm
  32.2 0.0 collective-permute-done.1.both_ref
  32.2 0.0 collective-permute-done.early_ref
  32.2 0.0 collective-permute-done.5.halo_ref
  32.2 1.7 %project.1 = (bf16[64,1024]{1,0:T(8,128)(2,1)}, f32[1,2048]{1,0:T(1,128)}, bf16[64,2048]{1,0:T(8,128)(2,1)}) custom-call(bf16[1536,128]{1,0:T(8,128)(2,1)S(1)} %collective-permute-done.early_ref, bf16[1024,128]{1,0:T(8,128)(2,1)S(1)} %collective-permute-done.1.both_ref, bf16[544,128]{1,0:T(8,128)(2,1)S(1)} %collective-permute-done.5.halo_ref, ...), custom_call_target="tpu_custom_call" | custom-call | flops 268435456 | bytes 4194304 | tf_op jit(solution)/shard_map/project/pallas_call | solution.py:492
  (3 shorter events, 0.0 us)
Async XLA Ops:
  3.7 7.5 %copy-start = (f32[1,2048]{1,0:T(1,128)S(1)}, f32[1,2048]{1,0:T(1,128)}, u32[]{:S(2)}) copy-start(f32[1,2048]{1,0:T(1,128)} %gain_ref.3) | copy-start | bytes 24580
  3.7 17.7 %collective-permute-start.2 = (bf16[136,2048]{1,0:T(8,128)(2,1)S(1)}, bf16[136,2048]{1,0:T(8,128)(2,1)S(1)}, u32[]{:S(2)}, u32[]{:S(2)}) collective-permute-start(bf16[136,2048]{1,0:T(8,128)(2,1)S(1)} %get-tuple-element.25), channel_id=1, source_target_pairs={{2,0},{4,2},{6,4},{3,1},{5,3},{7,5},{10,8},{12,10},{14,12},{11,9},... | collective-permute-start | bytes 1671176 | tf_op jit(solution)/shard_map/ppermute | solution.py:35
  5.0 27.3 %collective-permute-start = (bf16[1536,128]{1,0:T(8,128)(2,1)S(1)}, bf16[1536,128]{1,0:T(8,128)(2,1)S(1)}, u32[]{:S(2)}, u32[]{:S(2)}) collective-permute-start(bf16[1536,128]{1,0:T(8,128)(2,1)S(1)} %get-tuple-element.19), channel_id=1, source_target_pairs={{0,8},{8,16},{16,24},{24,0},{1,9},{9,17},{17,25},{25,1},{2,10},{10... | collective-permute-start | bytes 1179656 | tf_op jit(solution)/shard_map/ppermute | solution.py:40
  12.7 19.5 %collective-permute-start.7 = (bf16[64,2048]{1,0:T(8,128)(2,1)S(1)}, bf16[64,2048]{1,0:T(8,128)(2,1)S(1)}, u32[]{:S(2)}, u32[]{:S(2)}) collective-permute-start(bf16[64,2048]{1,0:T(8,128)(2,1)S(1)} %get-tuple-element.31), channel_id=1, source_target_pairs={{0,24},{8,0},{16,8},{24,16},{1,25},{9,1},{17,9},{25,17},{2,26},{10... | collective-permute-start | bytes 786440 | tf_op jit(solution)/shard_map/ppermute | solution.py:40
  13.8 18.5 %collective-permute-start.1 = (bf16[1024,128]{1,0:T(8,128)(2,1)S(1)}, bf16[1024,128]{1,0:T(8,128)(2,1)S(1)}, u32[]{:S(2)}, u32[]{:S(2)}) collective-permute-start(bf16[1024,128]{1,0:T(8,128)(2,1)S(1)} %get-tuple-element.24.after_ref), channel_id=1, source_target_pairs={{0,8},{8,16},{16,24},{24,0},{1,9},{9,17},{17,25},{25,1},{2,10},{10... | collective-permute-start | bytes 786440 | tf_op jit(solution)/shard_map/ppermute | solution.py:40
  14.8 1.2 %collective-permute-start.3 = (f32[1,2048]{1,0:T(1,128)S(1)}, f32[1,2048]{1,0:T(1,128)S(1)}, u32[]{:S(2)}, u32[]{:S(2)}) collective-permute-start(f32[1,2048]{1,0:T(1,128)S(1)} %get-tuple-element.30), channel_id=1, source_target_pairs={{0,1},{1,0},{2,3},{3,2},{4,5},{5,4},{6,7},{7,6},{8,9},{9,8},{10,11... | collective-permute-start | bytes 24584 | tf_op jit(solution)/shard_map/ppermute | solution.py:513
  16.0 5.4 %collective-permute-start.4 = (f32[1,2048]{1,0:T(1,128)S(1)}, f32[1,2048]{1,0:T(1,128)S(1)}, u32[]{:S(2)}, u32[]{:S(2)}) collective-permute-start(f32[1,2048]{1,0:T(1,128)S(1)} %add.6), channel_id=1, source_target_pairs={{0,2},{2,0},{4,6},{6,4},{1,3},{3,1},{5,7},{7,5},{8,10},{10,8},{12,... | collective-permute-start | bytes 24584 | tf_op jit(solution)/shard_map/ppermute | solution.py:513
  22.9 9.4 %collective-permute-start.5 = (bf16[544,128]{1,0:T(8,128)(2,1)S(1)}, bf16[544,128]{1,0:T(8,128)(2,1)S(1)}, u32[]{:S(2)}, u32[]{:S(2)}) collective-permute-start(bf16[544,128]{1,0:T(8,128)(2,1)S(1)} %attend_halo.1), channel_id=1, source_target_pairs={{0,10},{2,12},{4,14},{8,18},{10,20},{12,22},{16,26},{18,28},{20,30... | collective-permute-start | bytes 417800 | tf_op jit(solution)/shard_map/ppermute | solution.py:533
  27.6 4.6 %collective-permute-start.6 = (f32[1,2048]{1,0:T(1,128)S(1)}, f32[1,2048]{1,0:T(1,128)S(1)}, u32[]{:S(2)}, u32[]{:S(2)}) collective-permute-start(f32[1,2048]{1,0:T(1,128)S(1)} %add.7.after_ref.term_ref), channel_id=1, source_target_pairs={{0,4},{2,6},{4,0},{6,2},{1,5},{3,7},{5,1},{7,3},{8,12},{10,14},{12... | collective-permute-start | bytes 24584 | tf_op jit(solution)/shard_map/ppermute | solution.py:513

commit v19 on v18

--- a/solution.py
+++ b/solution.py
@@ -519,7 +519,7 @@
         count = lax.axis_size(axis)
         if count & (count - 1):
             return []
-        rounds += [(axis, 1 << i) for i in range(count.bit_length() - 1)]
+        rounds += [(axis, (2 << i) - 1) for i in range(count.bit_length() - 1)]
     return rounds if len(rounds) == 3 else []
 
 

time: 34.2 us -> 35.1 us (1.026)
  waiting for transfers between devices: 5.79 us -> 9.3 us
  starting transfers between devices: 16.5 us -> 13.9 us
    ppermute x3, waiting for transfers between devices: 5.78 us -> 9.29 us  [swapped(): lax.ppermute(value, axis, [(i, i ^ distance) for i in range(lax.axis_size...]
    ppermute x3, starting transfers between devices: 5.39 us -> 2.78 us  [swapped(): lax.ppermute(value, axis, [(i, i ^ distance) for i in range(lax.axis_size...]
where the time goes in v19:
time: 35.1 us; the launch traced here: 34.9 us
  starting transfers between devices  13.9 us (40%)
  Pallas kernels  10.3 us (29%)
  waiting for transfers between devices  9.3 us (26%)
  between operations  1.39 us (4%)
    ppermute x3, waiting for transfers between devices, swapped(): lax.ppermute(value, axis, [(i, i ^ distance) for i in range(lax.axis_size...  9.29 us
    ppermute x3, starting transfers between devices, passed_along(): lax.ppermute(value, axis, [(i, (i + steps) % count) for i in range(count)])  5.07 us
    ppermute x1, starting transfers between devices, onward(): return lax.ppermute(value, ('section', 'seq'), route)  4.73 us
    pallas_call x1, Pallas kernels, attend_early(): pl.pallas_call(functools.partial(early_kernel, rows, chunks), in_specs=[H...  3.02 us
    ppermute x3, starting transfers between devices, swapped(): lax.ppermute(value, axis, [(i, i ^ distance) for i in range(lax.axis_size...  2.78 us
    pallas_call x1, Pallas kernels, attend_late(): pl.pallas_call(functools.partial(late_kernel, rows), in_specs=[HBM] * 2 +...  2.53 us
    pallas_call x1, Pallas kernels, project(): pl.pallas_call(project_kernel, in_specs=[VMEM] * 7 + [ANY], out_specs=[VM...  1.73 us
    pallas_call x1, Pallas kernels, backward(): pl.pallas_call(back_kernel, in_specs=[VMEM] * 5 + [ANY], out_specs=[VMEM]...  1.56 us
  transfers between devices with their start and end apart: 8, of which 3 were waited for; matrix products, arithmetic and copies ran while one was open for 0% of the time, Pallas kernels for 16%

profile of v19, /device:TPU:0, one launch (start us, length us, event | category | flops | bytes accessed | tf_op | source)
XLA Modules:
  0.0 34.9 jit_solution(16494257186151799064)
XLA Ops:
  0.6 3.0 %attend_early.1 = (bf16[136,2048]{1,0:T(8,128)(2,1)S(1)}, bf16[1536,128]{1,0:T(8,128)(2,1)S(1)}, bf16[512,128]{1,0:T(8,128)(2,1)S(1)}, bf16[128,2048]{1,0:T(8,12...) custom-call(s32[1,8]{1,0:T(1,128)} %bitcast.17, ...), custom_call_target="tpu_custom_call" | custom-call | flops 134217728 | bytes 3145728 | tf_op jit(solution)/shard_map/attend_early/pallas_call | solution.py:402
  3.7 0.0 copy-start
  3.7 1.3 %collective-permute-start.2 = (bf16[136,2048]{1,0:T(8,128)(2,1)S(1)}, bf16[136,2048]{1,0:T(8,128)(2,1)S(1)}, u32[]{:S(2)}, u32[]{:S(2)}) collective-permute-start(bf16[136,2048]{1,0:T(8,128)(2,1)S(1)} %get-tuple-element.25), channel_id=1, source_target_pairs={{2,0},{4,2},{6,4},{3,1},{5,3},{7,5},{10,8},{12,10},{14,12},{11,9},... | collective-permute-start | bytes 1671176 | tf_op jit(solution)/shard_map/ppermute | solution.py:35
  5.0 3.0 %collective-permute-start = (bf16[1536,128]{1,0:T(8,128)(2,1)S(1)}, bf16[1536,128]{1,0:T(8,128)(2,1)S(1)}, u32[]{:S(2)}, u32[]{:S(2)}) collective-permute-start(bf16[1536,128]{1,0:T(8,128)(2,1)S(1)} %get-tuple-element.19), channel_id=1, source_target_pairs={{0,8},{8,16},{16,24},{24,0},{1,9},{9,17},{17,25},{25,1},{2,10},{10... | collective-permute-start | bytes 1179656 | tf_op jit(solution)/shard_map/ppermute | solution.py:40
  8.6 2.5 %attend_late.1 = (bf16[1024,128]{1,0:T(8,128)(2,1)S(1)}, f32[128,256]{1,0:T(8,128)S(1)}, bf16[2048,1024]{1,0:T(8,128)(2,1)S(1)}) custom-call(s32[1,8]{1,0:T(1,128)} %bitcast.18, bf16[2048,1024]{1,0:T(8,128)(2,1)} %bitcast.11, bf16[128,2048]{1,0:T(8,128)(2,1)S(1)} %get-tuple-element.20.q_ref, bf16[256,2048]{1,0:T(8,128)(2,1)S(1)} %get-tuple-element.21.k_ref, ...), custom_call_target="tpu_custom_call" | custom-call | flops 268435456 | bytes 2621440 | tf_op jit(solution)/shard_map/attend_late/pallas_call | solution.py:431
  11.2 0.0 copy-done
  11.2 1.6 %backward.1 = (bf16[64,2048]{1,0:T(8,128)(2,1)S(1)}, f32[1,2048]{1,0:T(1,128)S(1)}) custom-call(s32[1,128]{1,0:T(1,128)S(1)} %broadcast_in_dim.14.slot_ref, bf16[64,1024]{1,0:T(8,128)(2,1)S(1)} %get-tuple-element.27.cotangent_ref, bf16[2048,1024]{1,0:T(8,128)(2,1)S(1)} %get-tuple-element.28.weight_ref, f32[1,2048]{1,0:T(1,128)S(1)} %copy-done, ...), custom_call_target="tpu_custom_call" | custom-call | flops 268435456 | bytes 4194304 | tf_op jit(solution)/shard_map/backward/pallas_call | solution.py:471
  12.7 1.0 %collective-permute-start.7 = (bf16[64,2048]{1,0:T(8,128)(2,1)S(1)}, bf16[64,2048]{1,0:T(8,128)(2,1)S(1)}, u32[]{:S(2)}, u32[]{:S(2)}) collective-permute-start(bf16[64,2048]{1,0:T(8,128)(2,1)S(1)} %get-tuple-element.31), channel_id=1, source_target_pairs={{0,24},{8,0},{16,8},{24,16},{1,25},{9,1},{17,9},{25,17},{2,26},{10... | collective-permute-start | bytes 786440 | tf_op jit(solution)/shard_map/ppermute | solution.py:40
  13.8 1.1 %collective-permute-start.1 = (bf16[1024,128]{1,0:T(8,128)(2,1)S(1)}, bf16[1024,128]{1,0:T(8,128)(2,1)S(1)}, u32[]{:S(2)}, u32[]{:S(2)}) collective-permute-start(bf16[1024,128]{1,0:T(8,128)(2,1)S(1)} %get-tuple-element.24.after_ref), channel_id=1, source_target_pairs={{0,8},{8,16},{16,24},{24,0},{1,9},{9,17},{17,25},{25,1},{2,10},{10... | collective-permute-start | bytes 786440 | tf_op jit(solution)/shard_map/ppermute | solution.py:40
  14.8 0.0 collective-permute-start.3
  14.8 1.2 %collective-permute-done.3 = f32[1,2048]{1,0:T(1,128)S(1)} collective-permute-done((f32[1,2048]{1,0:T(1,128)S(1)}, f32[1,2048]{1,0:T(1,128)S(1)}, u32[]{:S(2)}, u32[]{:S(2)}) %collective-permute-start.3) | collective-permute-done | bytes 8224 | tf_op jit(solution)/shard_map/ppermute | solution.py:513
  16.0 2.7 %collective-permute-start.4 = (f32[1,2048]{1,0:T(1,128)S(1)}, f32[1,2048]{1,0:T(1,128)S(1)}, u32[]{:S(2)}, u32[]{:S(2)}) collective-permute-start(f32[1,2048]{1,0:T(1,128)S(1)} %add.6), channel_id=1, source_target_pairs={{0,2},{2,0},{4,6},{6,4},{1,3},{3,1},{5,7},{7,5},{8,10},{10,8},{12,... | collective-permute-start | bytes 24584 | tf_op jit(solution)/shard_map/ppermute | solution.py:513
  18.7 2.7 %collective-permute-done.4 = f32[1,2048]{1,0:T(1,128)S(1)} collective-permute-done((f32[1,2048]{1,0:T(1,128)S(1)}, f32[1,2048]{1,0:T(1,128)S(1)}, u32[]{:S(2)}, u32[]{:S(2)}) %collective-permute-start.4) | collective-permute-done | bytes 8224 | tf_op jit(solution)/shard_map/ppermute | solution.py:513
  21.4 0.0 collective-permute-done.2.q_ref
  21.4 1.5 %attend_halo.1 = bf16[544,128]{1,0:T(8,128)(2,1)S(1)} custom-call(bf16[136,2048]{1,0:T(8,128)(2,1)S(1)} %collective-permute-done.2.q_ref, bf16[256,2048]{1,0:T(8,128)(2,1)S(1)} %get-tuple-element.21.k_ref, bf16[256,2048]{1,0:T(8,128)(2,1)S(1)} %get-tuple-element.22.v_ref, f32[128,256]{1,0:T(8,128)S(1)} %get-tuple-element.26.bias, ...), custom_call_target="tpu_custom_call" | custom-call | flops 134217728 | bytes 1572864 | tf_op jit(solution)/shard_map/attend_halo/pallas_call | solution.py:456
  22.9 4.7 %collective-permute-start.5 = (bf16[544,128]{1,0:T(8,128)(2,1)S(1)}, bf16[544,128]{1,0:T(8,128)(2,1)S(1)}, u32[]{:S(2)}, u32[]{:S(2)}) collective-permute-start(bf16[544,128]{1,0:T(8,128)(2,1)S(1)} %attend_halo.1), channel_id=1, source_target_pairs={{0,10},{2,12},{4,14},{8,18},{10,20},{12,22},{16,26},{18,28},{20,30... | collective-permute-start | bytes 417800 | tf_op jit(solution)/shard_map/ppermute | solution.py:533
  27.6 0.1 collective-permute-start.6
  27.7 5.4 %collective-permute-done.6.other_ref = f32[1,2048]{1,0:T(1,128)S(1)} collective-permute-done((f32[1,2048]{1,0:T(1,128)S(1)}, f32[1,2048]{1,0:T(1,128)S(1)}, u32[]{:S(2)}, u32[]{:S(2)}) %collective-permute-start.6) | collective-permute-done | bytes 8224 | tf_op jit(solution)/shard_map/ppermute | solution.py:513
  33.1 0.0 collective-permute-done.7.upstream_hbm
  33.1 0.0 collective-permute-done.1.both_ref
  33.1 0.0 collective-permute-done.early_ref
  33.1 0.0 collective-permute-done.5.halo_ref
  33.1 1.7 %project.1 = (bf16[64,1024]{1,0:T(8,128)(2,1)}, f32[1,2048]{1,0:T(1,128)}, bf16[64,2048]{1,0:T(8,128)(2,1)}) custom-call(bf16[1536,128]{1,0:T(8,128)(2,1)S(1)} %collective-permute-done.early_ref, bf16[1024,128]{1,0:T(8,128)(2,1)S(1)} %collective-permute-done.1.both_ref, bf16[544,128]{1,0:T(8,128)(2,1)S(1)} %collective-permute-done.5.halo_ref, ...), custom_call_target="tpu_custom_call" | custom-call | flops 268435456 | bytes 4194304 | tf_op jit(solution)/shard_map/project/pallas_call | solution.py:492
  (3 shorter events, 0.0 us)
Async XLA Ops:
  3.7 7.5 %copy-start = (f32[1,2048]{1,0:T(1,128)S(1)}, f32[1,2048]{1,0:T(1,128)}, u32[]{:S(2)}) copy-start(f32[1,2048]{1,0:T(1,128)} %gain_ref.3) | copy-start | bytes 24580
  3.7 17.7 %collective-permute-start.2 = (bf16[136,2048]{1,0:T(8,128)(2,1)S(1)}, bf16[136,2048]{1,0:T(8,128)(2,1)S(1)}, u32[]{:S(2)}, u32[]{:S(2)}) collective-permute-start(bf16[136,2048]{1,0:T(8,128)(2,1)S(1)} %get-tuple-element.25), channel_id=1, source_target_pairs={{2,0},{4,2},{6,4},{3,1},{5,3},{7,5},{10,8},{12,10},{14,12},{11,9},... | collective-permute-start | bytes 1671176 | tf_op jit(solution)/shard_map/ppermute | solution.py:35
  5.0 28.2 %collective-permute-start = (bf16[1536,128]{1,0:T(8,128)(2,1)S(1)}, bf16[1536,128]{1,0:T(8,128)(2,1)S(1)}, u32[]{:S(2)}, u32[]{:S(2)}) collective-permute-start(bf16[1536,128]{1,0:T(8,128)(2,1)S(1)} %get-tuple-element.19), channel_id=1, source_target_pairs={{0,8},{8,16},{16,24},{24,0},{1,9},{9,17},{17,25},{25,1},{2,10},{10... | collective-permute-start | bytes 1179656 | tf_op jit(solution)/shard_map/ppermute | solution.py:40
  12.7 20.4 %collective-permute-start.7 = (bf16[64,2048]{1,0:T(8,128)(2,1)S(1)}, bf16[64,2048]{1,0:T(8,128)(2,1)S(1)}, u32[]{:S(2)}, u32[]{:S(2)}) collective-permute-start(bf16[64,2048]{1,0:T(8,128)(2,1)S(1)} %get-tuple-element.31), channel_id=1, source_target_pairs={{0,24},{8,0},{16,8},{24,16},{1,25},{9,1},{17,9},{25,17},{2,26},{10... | collective-permute-start | bytes 786440 | tf_op jit(solution)/shard_map/ppermute | solution.py:40
  13.8 19.4 %collective-permute-start.1 = (bf16[1024,128]{1,0:T(8,128)(2,1)S(1)}, bf16[1024,128]{1,0:T(8,128)(2,1)S(1)}, u32[]{:S(2)}, u32[]{:S(2)}) collective-permute-start(bf16[1024,128]{1,0:T(8,128)(2,1)S(1)} %get-tuple-element.24.after_ref), channel_id=1, source_target_pairs={{0,8},{8,16},{16,24},{24,0},{1,9},{9,17},{17,25},{25,1},{2,10},{10... | collective-permute-start | bytes 786440 | tf_op jit(solution)/shard_map/ppermute | solution.py:40
  14.8 1.2 %collective-permute-start.3 = (f32[1,2048]{1,0:T(1,128)S(1)}, f32[1,2048]{1,0:T(1,128)S(1)}, u32[]{:S(2)}, u32[]{:S(2)}) collective-permute-start(f32[1,2048]{1,0:T(1,128)S(1)} %get-tuple-element.30), channel_id=1, source_target_pairs={{0,1},{1,0},{2,3},{3,2},{4,5},{5,4},{6,7},{7,6},{8,9},{9,8},{10,11... | collective-permute-start | bytes 24584 | tf_op jit(solution)/shard_map/ppermute | solution.py:513
  16.0 5.4 %collective-permute-start.4 = (f32[1,2048]{1,0:T(1,128)S(1)}, f32[1,2048]{1,0:T(1,128)S(1)}, u32[]{:S(2)}, u32[]{:S(2)}) collective-permute-start(f32[1,2048]{1,0:T(1,128)S(1)} %add.6), channel_id=1, source_target_pairs={{0,2},{2,0},{4,6},{6,4},{1,3},{3,1},{5,7},{7,5},{8,10},{10,8},{12,... | collective-permute-start | bytes 24584 | tf_op jit(solution)/shard_map/ppermute | solution.py:513
  22.9 10.3 %collective-permute-start.5 = (bf16[544,128]{1,0:T(8,128)(2,1)S(1)}, bf16[544,128]{1,0:T(8,128)(2,1)S(1)}, u32[]{:S(2)}, u32[]{:S(2)}) collective-permute-start(bf16[544,128]{1,0:T(8,128)(2,1)S(1)} %attend_halo.1), channel_id=1, source_target_pairs={{0,10},{2,12},{4,14},{8,18},{10,20},{12,22},{16,26},{18,28},{20,30... | collective-permute-start | bytes 417800 | tf_op jit(solution)/shard_map/ppermute | solution.py:533
  27.6 5.5 %collective-permute-start.6 = (f32[1,2048]{1,0:T(1,128)S(1)}, f32[1,2048]{1,0:T(1,128)S(1)}, u32[]{:S(2)}, u32[]{:S(2)}) collective-permute-start(f32[1,2048]{1,0:T(1,128)S(1)} %add.7.after_ref.term_ref), channel_id=1, source_target_pairs={{0,6},{2,4},{4,2},{6,0},{1,7},{3,5},{5,3},{7,1},{8,14},{10,12},{12... | collective-permute-start | bytes 24584 | tf_op jit(solution)/shard_map/ppermute | solution.py:513

commit v20 on v18

--- a/solution.py
+++ b/solution.py
@@ -88,11 +88,11 @@
     return copy
 
 
-def load_chunks(arrays, chunks, sems, between):
-    block = arrays[0][1].shape[1] // chunks
+def load_chunks(arrays, begins, sems, between):
+    width = arrays[0][1].shape[1]
     copies, extra = [], None
-    for chunk in range(chunks):
-        columns = pl.ds(chunk * block, block)
+    for chunk, (begin, end) in enumerate(zip(begins, begins[1:] + [width])):
+        columns = pl.ds(begin, end - begin)
         copies.append(
             [
                 load(source.at[:, columns], target.at[:, columns], sems.at[i, chunk])
@@ -149,8 +149,10 @@
         (q_hbm.at[head], sent_ref.at[head]),
         (v_hbm.at[head], v_ref.at[head]),
     )
-    copies = load_chunks(arrays, chunks, sems, lambda: load(offsets_hbm, offsets_ref, offsets_sem.at[0]))
-    copies, offsets_copy = copies
+    begins = [0, k_ref.shape[1] // chunks]
+    copies, offsets_copy = load_chunks(
+        arrays, begins, sems, lambda: load(offsets_hbm, offsets_ref, offsets_sem.at[0])
+    )
     later = (
         (k_hbm.at[tail], k_ref.at[tail]),
         (v_hbm.at[tail], v_ref.at[tail]),
@@ -164,14 +166,13 @@
     split = early_ref.shape[0] // LANES
 
     def arrive(pair):
-        per_chunk = pairs // chunks
-        if pair % per_chunk == 0:
-            for copy in copies[pair // per_chunk]:
+        if pair * LANES in begins:
+            for copy in copies[begins.index(pair * LANES)]:
                 copy.wait()
         if pair == 0:
             offsets_copy.wait()
             bias[...] = mask_bias(offsets_ref, start, start, lambda key, query: key <= query)
-        if pair == per_chunk:
+        if pair * LANES == begins[1]:
             for i, (source, target) in enumerate(later):
                 rest.append(load(source, target, offsets_sem.at[i + 1]))
 
@@ -416,7 +417,7 @@
         scratch_shapes=[
             pltpu.SMEM(offsets.shape, jnp.int32),
             pltpu.VMEM((half, 2 * half), jnp.float32),
-            pltpu.SemaphoreType.DMA((3, chunks)),
+            pltpu.SemaphoreType.DMA((3, 2)),
             pltpu.SemaphoreType.DMA((6,)),
         ],
         cost_estimate=cost(4 * half * half * width, 6 * rows * width, half * half * width // 64),

time: 34.2 us -> 34.3 us (level)
  no operation moved by 1% of the time
where the time goes in v20:
time: 34.3 us; the launch traced here: 34.1 us
  starting transfers between devices  16.5 us (48%)
  Pallas kernels  10.4 us (30%)
  waiting for transfers between devices  5.79 us (17%)
  between operations  1.38 us (4%)
    ppermute x3, waiting for transfers between devices, swapped(): lax.ppermute(value, axis, [(i, i ^ distance) for i in range(lax.axis_size...  5.78 us
    ppermute x3, starting transfers between devices, swapped(): lax.ppermute(value, axis, [(i, i ^ distance) for i in range(lax.axis_size...  5.39 us
    ppermute x3, starting transfers between devices, passed_along(): lax.ppermute(value, axis, [(i, (i + steps) % count) for i in range(count)])  5.07 us
    ppermute x1, starting transfers between devices, onward(): return lax.ppermute(value, ('section', 'seq'), route)  4.73 us
    pallas_call x1, Pallas kernels, attend_early(): pl.pallas_call(functools.partial(early_kernel, rows, chunks), in_specs=[H...  3.1 us
    pallas_call x1, Pallas kernels, attend_late(): pl.pallas_call(functools.partial(late_kernel, rows), in_specs=[HBM] * 2 +...  2.53 us
    pallas_call x1, Pallas kernels, project(): pl.pallas_call(project_kernel, in_specs=[VMEM] * 7 + [ANY], out_specs=[VM...  1.73 us
    pallas_call x1, Pallas kernels, backward(): pl.pallas_call(back_kernel, in_specs=[VMEM] * 5 + [ANY], out_specs=[VMEM]...  1.56 us
  transfers between devices with their start and end apart: 8, of which 3 were waited for; matrix products, arithmetic and copies ran while one was open for 0% of the time, Pallas kernels for 16%

profile of v20, /device:TPU:0, one launch (start us, length us, event | category | flops | bytes accessed | tf_op | source)
XLA Modules:
  0.0 34.1 jit_solution(4324395445810327050)
XLA Ops:
  0.6 3.1 %attend_early.1 = (bf16[136,2048]{1,0:T(8,128)(2,1)S(1)}, bf16[1536,128]{1,0:T(8,128)(2,1)S(1)}, bf16[512,128]{1,0:T(8,128)(2,1)S(1)}, bf16[128,2048]{1,0:T(8,12...) custom-call(s32[1,8]{1,0:T(1,128)} %bitcast.17, ...), custom_call_target="tpu_custom_call" | custom-call | flops 134217728 | bytes 3145728 | tf_op jit(solution)/shard_map/attend_early/pallas_call | solution.py:403
  3.7 0.0 copy-start
  3.7 1.3 %collective-permute-start.2 = (bf16[136,2048]{1,0:T(8,128)(2,1)S(1)}, bf16[136,2048]{1,0:T(8,128)(2,1)S(1)}, u32[]{:S(2)}, u32[]{:S(2)}) collective-permute-start(bf16[136,2048]{1,0:T(8,128)(2,1)S(1)} %get-tuple-element.25), channel_id=1, source_target_pairs={{2,0},{4,2},{6,4},{3,1},{5,3},{7,5},{10,8},{12,10},{14,12},{11,9},... | collective-permute-start | bytes 1671176 | tf_op jit(solution)/shard_map/ppermute | solution.py:35
  5.0 3.0 %collective-permute-start = (bf16[1536,128]{1,0:T(8,128)(2,1)S(1)}, bf16[1536,128]{1,0:T(8,128)(2,1)S(1)}, u32[]{:S(2)}, u32[]{:S(2)}) collective-permute-start(bf16[1536,128]{1,0:T(8,128)(2,1)S(1)} %get-tuple-element.19), channel_id=1, source_target_pairs={{0,8},{8,16},{16,24},{24,0},{1,9},{9,17},{17,25},{25,1},{2,10},{10... | collective-permute-start | bytes 1179656 | tf_op jit(solution)/shard_map/ppermute | solution.py:40
  8.7 2.5 %attend_late.1 = (bf16[1024,128]{1,0:T(8,128)(2,1)S(1)}, f32[128,256]{1,0:T(8,128)S(1)}, bf16[2048,1024]{1,0:T(8,128)(2,1)S(1)}) custom-call(s32[1,8]{1,0:T(1,128)} %bitcast.18, bf16[2048,1024]{1,0:T(8,128)(2,1)} %bitcast.11, bf16[128,2048]{1,0:T(8,128)(2,1)S(1)} %get-tuple-element.20.q_ref, bf16[256,2048]{1,0:T(8,128)(2,1)S(1)} %get-tuple-element.21.k_ref, ...), custom_call_target="tpu_custom_call" | custom-call | flops 268435456 | bytes 2621440 | tf_op jit(solution)/shard_map/attend_late/pallas_call | solution.py:432
  11.2 0.0 copy-done
  11.3 1.6 %backward.1 = (bf16[64,2048]{1,0:T(8,128)(2,1)S(1)}, f32[1,2048]{1,0:T(1,128)S(1)}) custom-call(s32[1,128]{1,0:T(1,128)S(1)} %broadcast_in_dim.14.slot_ref, bf16[64,1024]{1,0:T(8,128)(2,1)S(1)} %get-tuple-element.27.cotangent_ref, bf16[2048,1024]{1,0:T(8,128)(2,1)S(1)} %get-tuple-element.28.weight_ref, f32[1,2048]{1,0:T(1,128)S(1)} %copy-done, ...), custom_call_target="tpu_custom_call" | custom-call | flops 268435456 | bytes 4194304 | tf_op jit(solution)/shard_map/backward/pallas_call | solution.py:472
  12.8 1.0 %collective-permute-start.7 = (bf16[64,2048]{1,0:T(8,128)(2,1)S(1)}, bf16[64,2048]{1,0:T(8,128)(2,1)S(1)}, u32[]{:S(2)}, u32[]{:S(2)}) collective-permute-start(bf16[64,2048]{1,0:T(8,128)(2,1)S(1)} %get-tuple-element.31), channel_id=1, source_target_pairs={{0,24},{8,0},{16,8},{24,16},{1,25},{9,1},{17,9},{25,17},{2,26},{10... | collective-permute-start | bytes 786440 | tf_op jit(solution)/shard_map/ppermute | solution.py:40
  13.8 1.1 %collective-permute-start.1 = (bf16[1024,128]{1,0:T(8,128)(2,1)S(1)}, bf16[1024,128]{1,0:T(8,128)(2,1)S(1)}, u32[]{:S(2)}, u32[]{:S(2)}) collective-permute-start(bf16[1024,128]{1,0:T(8,128)(2,1)S(1)} %get-tuple-element.24.after_ref), channel_id=1, source_target_pairs={{0,8},{8,16},{16,24},{24,0},{1,9},{9,17},{17,25},{25,1},{2,10},{10... | collective-permute-start | bytes 786440 | tf_op jit(solution)/shard_map/ppermute | solution.py:40
  14.9 0.0 collective-permute-start.3
  14.9 1.2 %collective-permute-done.3 = f32[1,2048]{1,0:T(1,128)S(1)} collective-permute-done((f32[1,2048]{1,0:T(1,128)S(1)}, f32[1,2048]{1,0:T(1,128)S(1)}, u32[]{:S(2)}, u32[]{:S(2)}) %collective-permute-start.3) | collective-permute-done | bytes 8224 | tf_op jit(solution)/shard_map/ppermute | solution.py:514
  16.1 2.7 %collective-permute-start.4 = (f32[1,2048]{1,0:T(1,128)S(1)}, f32[1,2048]{1,0:T(1,128)S(1)}, u32[]{:S(2)}, u32[]{:S(2)}) collective-permute-start(f32[1,2048]{1,0:T(1,128)S(1)} %add.6), channel_id=1, source_target_pairs={{0,2},{2,0},{4,6},{6,4},{1,3},{3,1},{5,7},{7,5},{8,10},{10,8},{12,... | collective-permute-start | bytes 24584 | tf_op jit(solution)/shard_map/ppermute | solution.py:514
  18.8 2.7 %collective-permute-done.4 = f32[1,2048]{1,0:T(1,128)S(1)} collective-permute-done((f32[1,2048]{1,0:T(1,128)S(1)}, f32[1,2048]{1,0:T(1,128)S(1)}, u32[]{:S(2)}, u32[]{:S(2)}) %collective-permute-start.4) | collective-permute-done | bytes 8224 | tf_op jit(solution)/shard_map/ppermute | solution.py:514
  21.5 0.0 collective-permute-done.2.q_ref
  21.5 1.5 %attend_halo.1 = bf16[544,128]{1,0:T(8,128)(2,1)S(1)} custom-call(bf16[136,2048]{1,0:T(8,128)(2,1)S(1)} %collective-permute-done.2.q_ref, bf16[256,2048]{1,0:T(8,128)(2,1)S(1)} %get-tuple-element.21.k_ref, bf16[256,2048]{1,0:T(8,128)(2,1)S(1)} %get-tuple-element.22.v_ref, f32[128,256]{1,0:T(8,128)S(1)} %get-tuple-element.26.bias, ...), custom_call_target="tpu_custom_call" | custom-call | flops 134217728 | bytes 1572864 | tf_op jit(solution)/shard_map/attend_halo/pallas_call | solution.py:457
  23.0 4.7 %collective-permute-start.5 = (bf16[544,128]{1,0:T(8,128)(2,1)S(1)}, bf16[544,128]{1,0:T(8,128)(2,1)S(1)}, u32[]{:S(2)}, u32[]{:S(2)}) collective-permute-start(bf16[544,128]{1,0:T(8,128)(2,1)S(1)} %attend_halo.1), channel_id=1, source_target_pairs={{0,10},{2,12},{4,14},{8,18},{10,20},{12,22},{16,26},{18,28},{20,30... | collective-permute-start | bytes 417800 | tf_op jit(solution)/shard_map/ppermute | solution.py:534
  27.7 2.7 %collective-permute-start.6 = (f32[1,2048]{1,0:T(1,128)S(1)}, f32[1,2048]{1,0:T(1,128)S(1)}, u32[]{:S(2)}, u32[]{:S(2)}) collective-permute-start(f32[1,2048]{1,0:T(1,128)S(1)} %add.7.after_ref.term_ref), channel_id=1, source_target_pairs={{0,4},{2,6},{4,0},{6,2},{1,5},{3,7},{5,1},{7,3},{8,12},{10,14},{12... | collective-permute-start | bytes 24584 | tf_op jit(solution)/shard_map/ppermute | solution.py:514
  30.4 1.9 %collective-permute-done.6.other_ref = f32[1,2048]{1,0:T(1,128)S(1)} collective-permute-done((f32[1,2048]{1,0:T(1,128)S(1)}, f32[1,2048]{1,0:T(1,128)S(1)}, u32[]{:S(2)}, u32[]{:S(2)}) %collective-permute-start.6) | collective-permute-done | bytes 8224 | tf_op jit(solution)/shard_map/ppermute | solution.py:514
  32.3 0.0 collective-permute-done.7.upstream_hbm
  32.3 0.0 collective-permute-done.1.both_ref
  32.3 0.0 collective-permute-done.early_ref
  32.3 0.0 collective-permute-done.5.halo_ref
  32.3 1.7 %project.1 = (bf16[64,1024]{1,0:T(8,128)(2,1)}, f32[1,2048]{1,0:T(1,128)}, bf16[64,2048]{1,0:T(8,128)(2,1)}) custom-call(bf16[1536,128]{1,0:T(8,128)(2,1)S(1)} %collective-permute-done.early_ref, bf16[1024,128]{1,0:T(8,128)(2,1)S(1)} %collective-permute-done.1.both_ref, bf16[544,128]{1,0:T(8,128)(2,1)S(1)} %collective-permute-done.5.halo_ref, ...), custom_call_target="tpu_custom_call" | custom-call | flops 268435456 | bytes 4194304 | tf_op jit(solution)/shard_map/project/pallas_call | solution.py:493
  (3 shorter events, 0.0 us)
Async XLA Ops:
  3.7 7.5 %copy-start = (f32[1,2048]{1,0:T(1,128)S(1)}, f32[1,2048]{1,0:T(1,128)}, u32[]{:S(2)}) copy-start(f32[1,2048]{1,0:T(1,128)} %gain_ref.3) | copy-start | bytes 24580
  3.7 17.7 %collective-permute-start.2 = (bf16[136,2048]{1,0:T(8,128)(2,1)S(1)}, bf16[136,2048]{1,0:T(8,128)(2,1)S(1)}, u32[]{:S(2)}, u32[]{:S(2)}) collective-permute-start(bf16[136,2048]{1,0:T(8,128)(2,1)S(1)} %get-tuple-element.25), channel_id=1, source_target_pairs={{2,0},{4,2},{6,4},{3,1},{5,3},{7,5},{10,8},{12,10},{14,12},{11,9},... | collective-permute-start | bytes 1671176 | tf_op jit(solution)/shard_map/ppermute | solution.py:35
  5.0 27.3 %collective-permute-start = (bf16[1536,128]{1,0:T(8,128)(2,1)S(1)}, bf16[1536,128]{1,0:T(8,128)(2,1)S(1)}, u32[]{:S(2)}, u32[]{:S(2)}) collective-permute-start(bf16[1536,128]{1,0:T(8,128)(2,1)S(1)} %get-tuple-element.19), channel_id=1, source_target_pairs={{0,8},{8,16},{16,24},{24,0},{1,9},{9,17},{17,25},{25,1},{2,10},{10... | collective-permute-start | bytes 1179656 | tf_op jit(solution)/shard_map/ppermute | solution.py:40
  12.8 19.5 %collective-permute-start.7 = (bf16[64,2048]{1,0:T(8,128)(2,1)S(1)}, bf16[64,2048]{1,0:T(8,128)(2,1)S(1)}, u32[]{:S(2)}, u32[]{:S(2)}) collective-permute-start(bf16[64,2048]{1,0:T(8,128)(2,1)S(1)} %get-tuple-element.31), channel_id=1, source_target_pairs={{0,24},{8,0},{16,8},{24,16},{1,25},{9,1},{17,9},{25,17},{2,26},{10... | collective-permute-start | bytes 786440 | tf_op jit(solution)/shard_map/ppermute | solution.py:40
  13.8 18.5 %collective-permute-start.1 = (bf16[1024,128]{1,0:T(8,128)(2,1)S(1)}, bf16[1024,128]{1,0:T(8,128)(2,1)S(1)}, u32[]{:S(2)}, u32[]{:S(2)}) collective-permute-start(bf16[1024,128]{1,0:T(8,128)(2,1)S(1)} %get-tuple-element.24.after_ref), channel_id=1, source_target_pairs={{0,8},{8,16},{16,24},{24,0},{1,9},{9,17},{17,25},{25,1},{2,10},{10... | collective-permute-start | bytes 786440 | tf_op jit(solution)/shard_map/ppermute | solution.py:40
  14.9 1.2 %collective-permute-start.3 = (f32[1,2048]{1,0:T(1,128)S(1)}, f32[1,2048]{1,0:T(1,128)S(1)}, u32[]{:S(2)}, u32[]{:S(2)}) collective-permute-start(f32[1,2048]{1,0:T(1,128)S(1)} %get-tuple-element.30), channel_id=1, source_target_pairs={{0,1},{1,0},{2,3},{3,2},{4,5},{5,4},{6,7},{7,6},{8,9},{9,8},{10,11... | collective-permute-start | bytes 24584 | tf_op jit(solution)/shard_map/ppermute | solution.py:514
  16.1 5.4 %collective-permute-start.4 = (f32[1,2048]{1,0:T(1,128)S(1)}, f32[1,2048]{1,0:T(1,128)S(1)}, u32[]{:S(2)}, u32[]{:S(2)}) collective-permute-start(f32[1,2048]{1,0:T(1,128)S(1)} %add.6), channel_id=1, source_target_pairs={{0,2},{2,0},{4,6},{6,4},{1,3},{3,1},{5,7},{7,5},{8,10},{10,8},{12,... | collective-permute-start | bytes 24584 | tf_op jit(solution)/shard_map/ppermute | solution.py:514
  23.0 9.4 %collective-permute-start.5 = (bf16[544,128]{1,0:T(8,128)(2,1)S(1)}, bf16[544,128]{1,0:T(8,128)(2,1)S(1)}, u32[]{:S(2)}, u32[]{:S(2)}) collective-permute-start(bf16[544,128]{1,0:T(8,128)(2,1)S(1)} %attend_halo.1), channel_id=1, source_target_pairs={{0,10},{2,12},{4,14},{8,18},{10,20},{12,22},{16,26},{18,28},{20,30... | collective-permute-start | bytes 417800 | tf_op jit(solution)/shard_map/ppermute | solution.py:534
  27.7 4.6 %collective-permute-start.6 = (f32[1,2048]{1,0:T(1,128)S(1)}, f32[1,2048]{1,0:T(1,128)S(1)}, u32[]{:S(2)}, u32[]{:S(2)}) collective-permute-start(f32[1,2048]{1,0:T(1,128)S(1)} %add.7.after_ref.term_ref), channel_id=1, source_target_pairs={{0,4},{2,6},{4,0},{6,2},{1,5},{3,7},{5,1},{7,3},{8,12},{10,14},{12... | collective-permute-start | bytes 24584 | tf_op jit(solution)/shard_map/ppermute | solution.py:514

commit v21 on v18

--- a/solution.py
+++ b/solution.py
@@ -349,16 +349,17 @@
     shares = halo_ref[pl.ds(pairs * molecules, 2 * pairs), :].astype(jnp.float32)
     share_ref[...] = jnp.where(first, 1.0, shares)
     for pair in range(pairs):
-        share_a, share_b = share_ref[pl.ds(pair, 1), :], share_ref[pl.ds(pairs + pair, 1), :]
+        share_a = share_ref[pl.ds(pair, 1), :].astype(jnp.bfloat16)
+        share_b = share_ref[pl.ds(pairs + pair, 1), :].astype(jnp.bfloat16)
         begin = pair * LANES
         if begin < first_part:
-            early = early_ref[pl.ds(begin, LANES), :].astype(jnp.float32)
+            early = early_ref[pl.ds(begin, LANES), :]
         else:
-            early = both_ref[pl.ds(begin - first_part, LANES), :].astype(jnp.float32)
+            early = both_ref[pl.ds(begin - first_part, LANES), :]
         parts += [early[:HEAD_DIM] * share_a, early[HEAD_DIM:] * share_b]
         if len(parts) == 8:
             columns = pl.ds((pair - 3) * LANES, 4 * LANES)
-            mean = dot_nt(pooling, jnp.concatenate(parts, axis=0).astype(jnp.bfloat16))
+            mean = dot_nt(pooling, jnp.concatenate(parts, axis=0))
             halo = [halo_ref[pl.ds((pair - 3 + i) * molecules, molecules), :] for i in range(4)]
             upper = mean + jnp.concatenate(halo, axis=1).astype(jnp.float32)
             place = features - first_part + (pair - 3) * molecules

time: 34.2 us -> 34.2 us (level)
  no operation moved by 1% of the time
where the time goes in v21:
time: 34.2 us; the launch traced here: 34 us
  starting transfers between devices  16.5 us (48%)
  Pallas kernels  10.3 us (30%)
  waiting for transfers between devices  5.79 us (17%)
  between operations  1.38 us (4%)
    ppermute x3, waiting for transfers between devices, swapped(): lax.ppermute(value, axis, [(i, i ^ distance) for i in range(lax.axis_size...  5.78 us
    ppermute x3, starting transfers between devices, swapped(): lax.ppermute(value, axis, [(i, i ^ distance) for i in range(lax.axis_size...  5.39 us
    ppermute x3, starting transfers between devices, passed_along(): lax.ppermute(value, axis, [(i, (i + steps) % count) for i in range(count)])  5.07 us
    ppermute x1, starting transfers between devices, onward(): return lax.ppermute(value, ('section', 'seq'), route)  4.73 us
    pallas_call x1, Pallas kernels, attend_early(): pl.pallas_call(functools.partial(early_kernel, rows, chunks), in_specs=[H...  3.02 us
    pallas_call x1, Pallas kernels, attend_late(): pl.pallas_call(functools.partial(late_kernel, rows), in_specs=[HBM] * 2 +...  2.53 us
    pallas_call x1, Pallas kernels, project(): pl.pallas_call(project_kernel, in_specs=[VMEM] * 7 + [ANY], out_specs=[VM...  1.73 us
    pallas_call x1, Pallas kernels, backward(): pl.pallas_call(back_kernel, in_specs=[VMEM] * 5 + [ANY], out_specs=[VMEM]...  1.56 us
  transfers between devices with their start and end apart: 8, of which 3 were waited for; matrix products, arithmetic and copies ran while one was open for 0% of the time, Pallas kernels for 16%

profile of v21, /device:TPU:0, one launch (start us, length us, event | category | flops | bytes accessed | tf_op | source)
XLA Modules:
  0.0 34.0 jit_solution(14925928423296498068)
XLA Ops:
  0.6 3.0 %attend_early.1 = (bf16[136,2048]{1,0:T(8,128)(2,1)S(1)}, bf16[1536,128]{1,0:T(8,128)(2,1)S(1)}, bf16[512,128]{1,0:T(8,128)(2,1)S(1)}, bf16[128,2048]{1,0:T(8,12...) custom-call(s32[1,8]{1,0:T(1,128)} %bitcast.17, ...), custom_call_target="tpu_custom_call" | custom-call | flops 134217728 | bytes 3145728 | tf_op jit(solution)/shard_map/attend_early/pallas_call | solution.py:403
  3.7 0.0 copy-start
  3.7 1.3 %collective-permute-start.2 = (bf16[136,2048]{1,0:T(8,128)(2,1)S(1)}, bf16[136,2048]{1,0:T(8,128)(2,1)S(1)}, u32[]{:S(2)}, u32[]{:S(2)}) collective-permute-start(bf16[136,2048]{1,0:T(8,128)(2,1)S(1)} %get-tuple-element.25), channel_id=1, source_target_pairs={{2,0},{4,2},{6,4},{3,1},{5,3},{7,5},{10,8},{12,10},{14,12},{11,9},... | collective-permute-start | bytes 1671176 | tf_op jit(solution)/shard_map/ppermute | solution.py:35
  5.0 3.0 %collective-permute-start = (bf16[1536,128]{1,0:T(8,128)(2,1)S(1)}, bf16[1536,128]{1,0:T(8,128)(2,1)S(1)}, u32[]{:S(2)}, u32[]{:S(2)}) collective-permute-start(bf16[1536,128]{1,0:T(8,128)(2,1)S(1)} %get-tuple-element.19), channel_id=1, source_target_pairs={{0,8},{8,16},{16,24},{24,0},{1,9},{9,17},{17,25},{25,1},{2,10},{10... | collective-permute-start | bytes 1179656 | tf_op jit(solution)/shard_map/ppermute | solution.py:40
  8.6 2.5 %attend_late.1 = (bf16[1024,128]{1,0:T(8,128)(2,1)S(1)}, f32[128,256]{1,0:T(8,128)S(1)}, bf16[2048,1024]{1,0:T(8,128)(2,1)S(1)}) custom-call(s32[1,8]{1,0:T(1,128)} %bitcast.18, bf16[2048,1024]{1,0:T(8,128)(2,1)} %bitcast.11, bf16[128,2048]{1,0:T(8,128)(2,1)S(1)} %get-tuple-element.20.q_ref, bf16[256,2048]{1,0:T(8,128)(2,1)S(1)} %get-tuple-element.21.k_ref, ...), custom_call_target="tpu_custom_call" | custom-call | flops 268435456 | bytes 2621440 | tf_op jit(solution)/shard_map/attend_late/pallas_call | solution.py:432
  11.2 0.0 copy-done
  11.2 1.6 %backward.1 = (bf16[64,2048]{1,0:T(8,128)(2,1)S(1)}, f32[1,2048]{1,0:T(1,128)S(1)}) custom-call(s32[1,128]{1,0:T(1,128)S(1)} %broadcast_in_dim.14.slot_ref, bf16[64,1024]{1,0:T(8,128)(2,1)S(1)} %get-tuple-element.27.cotangent_ref, bf16[2048,1024]{1,0:T(8,128)(2,1)S(1)} %get-tuple-element.28.weight_ref, f32[1,2048]{1,0:T(1,128)S(1)} %copy-done, ...), custom_call_target="tpu_custom_call" | custom-call | flops 268435456 | bytes 4194304 | tf_op jit(solution)/shard_map/backward/pallas_call | solution.py:472
  12.7 1.0 %collective-permute-start.7 = (bf16[64,2048]{1,0:T(8,128)(2,1)S(1)}, bf16[64,2048]{1,0:T(8,128)(2,1)S(1)}, u32[]{:S(2)}, u32[]{:S(2)}) collective-permute-start(bf16[64,2048]{1,0:T(8,128)(2,1)S(1)} %get-tuple-element.31), channel_id=1, source_target_pairs={{0,24},{8,0},{16,8},{24,16},{1,25},{9,1},{17,9},{25,17},{2,26},{10... | collective-permute-start | bytes 786440 | tf_op jit(solution)/shard_map/ppermute | solution.py:40
  13.8 1.1 %collective-permute-start.1 = (bf16[1024,128]{1,0:T(8,128)(2,1)S(1)}, bf16[1024,128]{1,0:T(8,128)(2,1)S(1)}, u32[]{:S(2)}, u32[]{:S(2)}) collective-permute-start(bf16[1024,128]{1,0:T(8,128)(2,1)S(1)} %get-tuple-element.24.after_ref), channel_id=1, source_target_pairs={{0,8},{8,16},{16,24},{24,0},{1,9},{9,17},{17,25},{25,1},{2,10},{10... | collective-permute-start | bytes 786440 | tf_op jit(solution)/shard_map/ppermute | solution.py:40
  14.8 0.0 collective-permute-start.3
  14.8 1.2 %collective-permute-done.3 = f32[1,2048]{1,0:T(1,128)S(1)} collective-permute-done((f32[1,2048]{1,0:T(1,128)S(1)}, f32[1,2048]{1,0:T(1,128)S(1)}, u32[]{:S(2)}, u32[]{:S(2)}) %collective-permute-start.3) | collective-permute-done | bytes 8224 | tf_op jit(solution)/shard_map/ppermute | solution.py:514
  16.0 2.7 %collective-permute-start.4 = (f32[1,2048]{1,0:T(1,128)S(1)}, f32[1,2048]{1,0:T(1,128)S(1)}, u32[]{:S(2)}, u32[]{:S(2)}) collective-permute-start(f32[1,2048]{1,0:T(1,128)S(1)} %add.6), channel_id=1, source_target_pairs={{0,2},{2,0},{4,6},{6,4},{1,3},{3,1},{5,7},{7,5},{8,10},{10,8},{12,... | collective-permute-start | bytes 24584 | tf_op jit(solution)/shard_map/ppermute | solution.py:514
  18.7 2.7 %collective-permute-done.4 = f32[1,2048]{1,0:T(1,128)S(1)} collective-permute-done((f32[1,2048]{1,0:T(1,128)S(1)}, f32[1,2048]{1,0:T(1,128)S(1)}, u32[]{:S(2)}, u32[]{:S(2)}) %collective-permute-start.4) | collective-permute-done | bytes 8224 | tf_op jit(solution)/shard_map/ppermute | solution.py:514
  21.4 0.0 collective-permute-done.2.q_ref
  21.4 1.5 %attend_halo.1 = bf16[544,128]{1,0:T(8,128)(2,1)S(1)} custom-call(bf16[136,2048]{1,0:T(8,128)(2,1)S(1)} %collective-permute-done.2.q_ref, bf16[256,2048]{1,0:T(8,128)(2,1)S(1)} %get-tuple-element.21.k_ref, bf16[256,2048]{1,0:T(8,128)(2,1)S(1)} %get-tuple-element.22.v_ref, f32[128,256]{1,0:T(8,128)S(1)} %get-tuple-element.26.bias, ...), custom_call_target="tpu_custom_call" | custom-call | flops 134217728 | bytes 1572864 | tf_op jit(solution)/shard_map/attend_halo/pallas_call | solution.py:457
  22.9 4.7 %collective-permute-start.5 = (bf16[544,128]{1,0:T(8,128)(2,1)S(1)}, bf16[544,128]{1,0:T(8,128)(2,1)S(1)}, u32[]{:S(2)}, u32[]{:S(2)}) collective-permute-start(bf16[544,128]{1,0:T(8,128)(2,1)S(1)} %attend_halo.1), channel_id=1, source_target_pairs={{0,10},{2,12},{4,14},{8,18},{10,20},{12,22},{16,26},{18,28},{20,30... | collective-permute-start | bytes 417800 | tf_op jit(solution)/shard_map/ppermute | solution.py:534
  27.6 2.7 %collective-permute-start.6 = (f32[1,2048]{1,0:T(1,128)S(1)}, f32[1,2048]{1,0:T(1,128)S(1)}, u32[]{:S(2)}, u32[]{:S(2)}) collective-permute-start(f32[1,2048]{1,0:T(1,128)S(1)} %add.7.after_ref.term_ref), channel_id=1, source_target_pairs={{0,4},{2,6},{4,0},{6,2},{1,5},{3,7},{5,1},{7,3},{8,12},{10,14},{12... | collective-permute-start | bytes 24584 | tf_op jit(solution)/shard_map/ppermute | solution.py:514
  30.3 1.9 %collective-permute-done.6.other_ref = f32[1,2048]{1,0:T(1,128)S(1)} collective-permute-done((f32[1,2048]{1,0:T(1,128)S(1)}, f32[1,2048]{1,0:T(1,128)S(1)}, u32[]{:S(2)}, u32[]{:S(2)}) %collective-permute-start.6) | collective-permute-done | bytes 8224 | tf_op jit(solution)/shard_map/ppermute | solution.py:514
  32.2 0.0 collective-permute-done.7.upstream_hbm
  32.2 0.0 collective-permute-done.1.both_ref
  32.2 0.0 collective-permute-done.early_ref
  32.2 0.0 collective-permute-done.5.halo_ref
  32.2 1.7 %project.1 = (bf16[64,1024]{1,0:T(8,128)(2,1)}, f32[1,2048]{1,0:T(1,128)}, bf16[64,2048]{1,0:T(8,128)(2,1)}) custom-call(bf16[1536,128]{1,0:T(8,128)(2,1)S(1)} %collective-permute-done.early_ref, bf16[1024,128]{1,0:T(8,128)(2,1)S(1)} %collective-permute-done.1.both_ref, bf16[544,128]{1,0:T(8,128)(2,1)S(1)} %collective-permute-done.5.halo_ref, ...), custom_call_target="tpu_custom_call" | custom-call | flops 268435456 | bytes 4194304 | tf_op jit(solution)/shard_map/project/pallas_call | solution.py:493
  (3 shorter events, 0.0 us)
Async XLA Ops:
  3.7 7.5 %copy-start = (f32[1,2048]{1,0:T(1,128)S(1)}, f32[1,2048]{1,0:T(1,128)}, u32[]{:S(2)}) copy-start(f32[1,2048]{1,0:T(1,128)} %gain_ref.3) | copy-start | bytes 24580
  3.7 17.7 %collective-permute-start.2 = (bf16[136,2048]{1,0:T(8,128)(2,1)S(1)}, bf16[136,2048]{1,0:T(8,128)(2,1)S(1)}, u32[]{:S(2)}, u32[]{:S(2)}) collective-permute-start(bf16[136,2048]{1,0:T(8,128)(2,1)S(1)} %get-tuple-element.25), channel_id=1, source_target_pairs={{2,0},{4,2},{6,4},{3,1},{5,3},{7,5},{10,8},{12,10},{14,12},{11,9},... | collective-permute-start | bytes 1671176 | tf_op jit(solution)/shard_map/ppermute | solution.py:35
  5.0 27.3 %collective-permute-start = (bf16[1536,128]{1,0:T(8,128)(2,1)S(1)}, bf16[1536,128]{1,0:T(8,128)(2,1)S(1)}, u32[]{:S(2)}, u32[]{:S(2)}) collective-permute-start(bf16[1536,128]{1,0:T(8,128)(2,1)S(1)} %get-tuple-element.19), channel_id=1, source_target_pairs={{0,8},{8,16},{16,24},{24,0},{1,9},{9,17},{17,25},{25,1},{2,10},{10... | collective-permute-start | bytes 1179656 | tf_op jit(solution)/shard_map/ppermute | solution.py:40
  12.7 19.5 %collective-permute-start.7 = (bf16[64,2048]{1,0:T(8,128)(2,1)S(1)}, bf16[64,2048]{1,0:T(8,128)(2,1)S(1)}, u32[]{:S(2)}, u32[]{:S(2)}) collective-permute-start(bf16[64,2048]{1,0:T(8,128)(2,1)S(1)} %get-tuple-element.31), channel_id=1, source_target_pairs={{0,24},{8,0},{16,8},{24,16},{1,25},{9,1},{17,9},{25,17},{2,26},{10... | collective-permute-start | bytes 786440 | tf_op jit(solution)/shard_map/ppermute | solution.py:40
  13.8 18.5 %collective-permute-start.1 = (bf16[1024,128]{1,0:T(8,128)(2,1)S(1)}, bf16[1024,128]{1,0:T(8,128)(2,1)S(1)}, u32[]{:S(2)}, u32[]{:S(2)}) collective-permute-start(bf16[1024,128]{1,0:T(8,128)(2,1)S(1)} %get-tuple-element.24.after_ref), channel_id=1, source_target_pairs={{0,8},{8,16},{16,24},{24,0},{1,9},{9,17},{17,25},{25,1},{2,10},{10... | collective-permute-start | bytes 786440 | tf_op jit(solution)/shard_map/ppermute | solution.py:40
  14.8 1.2 %collective-permute-start.3 = (f32[1,2048]{1,0:T(1,128)S(1)}, f32[1,2048]{1,0:T(1,128)S(1)}, u32[]{:S(2)}, u32[]{:S(2)}) collective-permute-start(f32[1,2048]{1,0:T(1,128)S(1)} %get-tuple-element.30), channel_id=1, source_target_pairs={{0,1},{1,0},{2,3},{3,2},{4,5},{5,4},{6,7},{7,6},{8,9},{9,8},{10,11... | collective-permute-start | bytes 24584 | tf_op jit(solution)/shard_map/ppermute | solution.py:514
  16.0 5.4 %collective-permute-start.4 = (f32[1,2048]{1,0:T(1,128)S(1)}, f32[1,2048]{1,0:T(1,128)S(1)}, u32[]{:S(2)}, u32[]{:S(2)}) collective-permute-start(f32[1,2048]{1,0:T(1,128)S(1)} %add.6), channel_id=1, source_target_pairs={{0,2},{2,0},{4,6},{6,4},{1,3},{3,1},{5,7},{7,5},{8,10},{10,8},{12,... | collective-permute-start | bytes 24584 | tf_op jit(solution)/shard_map/ppermute | solution.py:514
  22.9 9.4 %collective-permute-start.5 = (bf16[544,128]{1,0:T(8,128)(2,1)S(1)}, bf16[544,128]{1,0:T(8,128)(2,1)S(1)}, u32[]{:S(2)}, u32[]{:S(2)}) collective-permute-start(bf16[544,128]{1,0:T(8,128)(2,1)S(1)} %attend_halo.1), channel_id=1, source_target_pairs={{0,10},{2,12},{4,14},{8,18},{10,20},{12,22},{16,26},{18,28},{20,30... | collective-permute-start | bytes 417800 | tf_op jit(solution)/shard_map/ppermute | solution.py:534
  27.6 4.6 %collective-permute-start.6 = (f32[1,2048]{1,0:T(1,128)S(1)}, f32[1,2048]{1,0:T(1,128)S(1)}, u32[]{:S(2)}, u32[]{:S(2)}) collective-permute-start(f32[1,2048]{1,0:T(1,128)S(1)} %add.7.after_ref.term_ref), channel_id=1, source_target_pairs={{0,4},{2,6},{4,0},{6,2},{1,5},{3,7},{5,1},{7,3},{8,12},{10,14},{12... | collective-permute-start | bytes 24584 | tf_op jit(solution)/shard_map/ppermute | solution.py:514

commit v22 on v18

--- a/solution.py
+++ b/solution.py
@@ -336,9 +336,9 @@
 
 def project_kernel(
     early_ref, both_ref, halo_ref, gain_ref, weight_ref, term_ref, other_ref, upstream_hbm,
-    out_ref, update_ref, passed_hbm, scaled_ref, share_ref, sem,
+    out_hbm, update_ref, passed_hbm, scaled_ref, share_ref, out_ref, sems,
 ):
-    passing = load(upstream_hbm, passed_hbm, sem)
+    passing = load(upstream_hbm, passed_hbm, sems.at[0])
     half = both_ref.shape[1]
     features = gain_ref.shape[1]
     first_part = early_ref.shape[0]
@@ -368,12 +368,19 @@
             squares += jnp.sum(arrived * arrived, axis=1, keepdims=True)
             scaled_ref[:, columns] = (arrived * gain_ref[:, columns]).astype(jnp.bfloat16)
             parts = []
-    product = dot_nn(scaled_ref[...], weight_ref[...])
-    out_ref[...] = (product * lax.rsqrt(squares / features + EPS_NORM)).astype(jnp.bfloat16)
+    inverse = lax.rsqrt(squares / features + EPS_NORM)
+    width = out_ref.shape[1] // 2
+    leaving = []
+    for i in range(2):
+        columns = pl.ds(i * width, width)
+        product = dot_nn(scaled_ref[...], weight_ref[:, columns])
+        out_ref[:, columns] = (product * inverse).astype(jnp.bfloat16)
+        leaving.append(load(out_ref.at[:, columns], out_hbm.at[:, columns], sems.at[1 + i]))
     total = term_ref[...] + other_ref[...]
     mean = jnp.sum(total * total, axis=1, keepdims=True) / features
     update_ref[...] = total / jnp.sqrt(mean + EPS_STEP)
-    passing.wait()
+    for copy in (passing, *leaving):
+        copy.wait()
 
 
 def cost(flops, read, exps=0):
@@ -492,7 +499,7 @@
     return pl.pallas_call(
         project_kernel,
         in_specs=[VMEM] * 7 + [ANY],
-        out_specs=[VMEM, VMEM, HBM],
+        out_specs=[HBM, VMEM, HBM],
         out_shape=[
             jax.ShapeDtypeStruct((rows, depth), jnp.bfloat16),
             jax.ShapeDtypeStruct(term.shape, term.dtype),
@@ -501,7 +508,8 @@
         scratch_shapes=[
             pltpu.VMEM((rows, width), jnp.bfloat16),
             pltpu.VMEM((2 * width // LANES, LANES), jnp.float32),
-            pltpu.SemaphoreType.DMA,
+            pltpu.VMEM((rows, depth), jnp.bfloat16),
+            pltpu.SemaphoreType.DMA((3,)),
         ],
         cost_estimate=cost(2 * rows * width * depth, 2 * width * depth),
         compiler_params=params(),

time: 34.2 us -> 34.8 us (1.018)
  Pallas kernels: 10.3 us -> 10.9 us
    pallas_call x1, Pallas kernels: 1.73 us -> 2.31 us  [project(): pl.pallas_call(project_kernel, in_specs=[VMEM] * 7 + [ANY], out_specs=[HB...]
where the time goes in v22:
time: 34.8 us; the launch traced here: 34.6 us
  starting transfers between devices  16.5 us (47%)
  Pallas kernels  10.9 us (31%)
  waiting for transfers between devices  5.79 us (17%)
  between operations  1.38 us (4%)
    ppermute x3, waiting for transfers between devices, swapped(): lax.ppermute(value, axis, [(i, i ^ distance) for i in range(lax.axis_size...  5.78 us
    ppermute x3, starting transfers between devices, swapped(): lax.ppermute(value, axis, [(i, i ^ distance) for i in range(lax.axis_size...  5.39 us
    ppermute x3, starting transfers between devices, passed_along(): lax.ppermute(value, axis, [(i, (i + steps) % count) for i in range(count)])  5.07 us
    ppermute x1, starting transfers between devices, onward(): return lax.ppermute(value, ('section', 'seq'), route)  4.73 us
    pallas_call x1, Pallas kernels, attend_early(): pl.pallas_call(functools.partial(early_kernel, rows, chunks), in_specs=[H...  3.02 us
    pallas_call x1, Pallas kernels, attend_late(): pl.pallas_call(functools.partial(late_kernel, rows), in_specs=[HBM] * 2 +...  2.53 us
    pallas_call x1, Pallas kernels, project(): pl.pallas_call(project_kernel, in_specs=[VMEM] * 7 + [ANY], out_specs=[HB...  2.31 us
    pallas_call x1, Pallas kernels, backward(): pl.pallas_call(back_kernel, in_specs=[VMEM] * 5 + [ANY], out_specs=[VMEM]...  1.56 us
  transfers between devices with their start and end apart: 8, of which 3 were waited for; matrix products, arithmetic and copies ran while one was open for 0% of the time, Pallas kernels for 16%

profile of v22, /device:TPU:0, one launch (start us, length us, event | category | flops | bytes accessed | tf_op | source)
XLA Modules:
  0.0 34.6 jit_solution(8295746923508185444)
XLA Ops:
  0.6 3.0 %attend_early.1 = (bf16[136,2048]{1,0:T(8,128)(2,1)S(1)}, bf16[1536,128]{1,0:T(8,128)(2,1)S(1)}, bf16[512,128]{1,0:T(8,128)(2,1)S(1)}, bf16[128,2048]{1,0:T(8,12...) custom-call(s32[1,8]{1,0:T(1,128)} %bitcast.17, ...), custom_call_target="tpu_custom_call" | custom-call | flops 134217728 | bytes 3145728 | tf_op jit(solution)/shard_map/attend_early/pallas_call | solution.py:409
  3.7 0.0 copy-start
  3.7 1.3 %collective-permute-start.2 = (bf16[136,2048]{1,0:T(8,128)(2,1)S(1)}, bf16[136,2048]{1,0:T(8,128)(2,1)S(1)}, u32[]{:S(2)}, u32[]{:S(2)}) collective-permute-start(bf16[136,2048]{1,0:T(8,128)(2,1)S(1)} %get-tuple-element.25), channel_id=1, source_target_pairs={{2,0},{4,2},{6,4},{3,1},{5,3},{7,5},{10,8},{12,10},{14,12},{11,9},... | collective-permute-start | bytes 1671176 | tf_op jit(solution)/shard_map/ppermute | solution.py:35
  5.0 3.0 %collective-permute-start = (bf16[1536,128]{1,0:T(8,128)(2,1)S(1)}, bf16[1536,128]{1,0:T(8,128)(2,1)S(1)}, u32[]{:S(2)}, u32[]{:S(2)}) collective-permute-start(bf16[1536,128]{1,0:T(8,128)(2,1)S(1)} %get-tuple-element.19), channel_id=1, source_target_pairs={{0,8},{8,16},{16,24},{24,0},{1,9},{9,17},{17,25},{25,1},{2,10},{10... | collective-permute-start | bytes 1179656 | tf_op jit(solution)/shard_map/ppermute | solution.py:40
  8.6 2.5 %attend_late.1 = (bf16[1024,128]{1,0:T(8,128)(2,1)S(1)}, f32[128,256]{1,0:T(8,128)S(1)}, bf16[2048,1024]{1,0:T(8,128)(2,1)S(1)}) custom-call(s32[1,8]{1,0:T(1,128)} %bitcast.18, bf16[2048,1024]{1,0:T(8,128)(2,1)} %bitcast.11, bf16[128,2048]{1,0:T(8,128)(2,1)S(1)} %get-tuple-element.20.q_ref, bf16[256,2048]{1,0:T(8,128)(2,1)S(1)} %get-tuple-element.21.k_ref, ...), custom_call_target="tpu_custom_call" | custom-call | flops 268435456 | bytes 2621440 | tf_op jit(solution)/shard_map/attend_late/pallas_call | solution.py:438
  11.2 0.0 copy-done
  11.2 1.6 %backward.1 = (bf16[64,2048]{1,0:T(8,128)(2,1)S(1)}, f32[1,2048]{1,0:T(1,128)S(1)}) custom-call(s32[1,128]{1,0:T(1,128)S(1)} %broadcast_in_dim.14.slot_ref, bf16[64,1024]{1,0:T(8,128)(2,1)S(1)} %get-tuple-element.27.cotangent_ref, bf16[2048,1024]{1,0:T(8,128)(2,1)S(1)} %get-tuple-element.28.weight_ref, f32[1,2048]{1,0:T(1,128)S(1)} %copy-done, ...), custom_call_target="tpu_custom_call" | custom-call | flops 268435456 | bytes 4194304 | tf_op jit(solution)/shard_map/backward/pallas_call | solution.py:478
  12.7 1.0 %collective-permute-start.7 = (bf16[64,2048]{1,0:T(8,128)(2,1)S(1)}, bf16[64,2048]{1,0:T(8,128)(2,1)S(1)}, u32[]{:S(2)}, u32[]{:S(2)}) collective-permute-start(bf16[64,2048]{1,0:T(8,128)(2,1)S(1)} %get-tuple-element.31), channel_id=1, source_target_pairs={{0,24},{8,0},{16,8},{24,16},{1,25},{9,1},{17,9},{25,17},{2,26},{10... | collective-permute-start | bytes 786440 | tf_op jit(solution)/shard_map/ppermute | solution.py:40
  13.8 1.1 %collective-permute-start.1 = (bf16[1024,128]{1,0:T(8,128)(2,1)S(1)}, bf16[1024,128]{1,0:T(8,128)(2,1)S(1)}, u32[]{:S(2)}, u32[]{:S(2)}) collective-permute-start(bf16[1024,128]{1,0:T(8,128)(2,1)S(1)} %get-tuple-element.24.after_ref), channel_id=1, source_target_pairs={{0,8},{8,16},{16,24},{24,0},{1,9},{9,17},{17,25},{25,1},{2,10},{10... | collective-permute-start | bytes 786440 | tf_op jit(solution)/shard_map/ppermute | solution.py:40
  14.8 0.0 collective-permute-start.3
  14.8 1.2 %collective-permute-done.3 = f32[1,2048]{1,0:T(1,128)S(1)} collective-permute-done((f32[1,2048]{1,0:T(1,128)S(1)}, f32[1,2048]{1,0:T(1,128)S(1)}, u32[]{:S(2)}, u32[]{:S(2)}) %collective-permute-start.3) | collective-permute-done | bytes 8224 | tf_op jit(solution)/shard_map/ppermute | solution.py:521
  16.0 2.7 %collective-permute-start.4 = (f32[1,2048]{1,0:T(1,128)S(1)}, f32[1,2048]{1,0:T(1,128)S(1)}, u32[]{:S(2)}, u32[]{:S(2)}) collective-permute-start(f32[1,2048]{1,0:T(1,128)S(1)} %add.6), channel_id=1, source_target_pairs={{0,2},{2,0},{4,6},{6,4},{1,3},{3,1},{5,7},{7,5},{8,10},{10,8},{12,... | collective-permute-start | bytes 24584 | tf_op jit(solution)/shard_map/ppermute | solution.py:521
  18.7 2.7 %collective-permute-done.4 = f32[1,2048]{1,0:T(1,128)S(1)} collective-permute-done((f32[1,2048]{1,0:T(1,128)S(1)}, f32[1,2048]{1,0:T(1,128)S(1)}, u32[]{:S(2)}, u32[]{:S(2)}) %collective-permute-start.4) | collective-permute-done | bytes 8224 | tf_op jit(solution)/shard_map/ppermute | solution.py:521
  21.4 0.0 collective-permute-done.2.q_ref
  21.4 1.5 %attend_halo.1 = bf16[544,128]{1,0:T(8,128)(2,1)S(1)} custom-call(bf16[136,2048]{1,0:T(8,128)(2,1)S(1)} %collective-permute-done.2.q_ref, bf16[256,2048]{1,0:T(8,128)(2,1)S(1)} %get-tuple-element.21.k_ref, bf16[256,2048]{1,0:T(8,128)(2,1)S(1)} %get-tuple-element.22.v_ref, f32[128,256]{1,0:T(8,128)S(1)} %get-tuple-element.26.bias, ...), custom_call_target="tpu_custom_call" | custom-call | flops 134217728 | bytes 1572864 | tf_op jit(solution)/shard_map/attend_halo/pallas_call | solution.py:463
  22.9 4.7 %collective-permute-start.5 = (bf16[544,128]{1,0:T(8,128)(2,1)S(1)}, bf16[544,128]{1,0:T(8,128)(2,1)S(1)}, u32[]{:S(2)}, u32[]{:S(2)}) collective-permute-start(bf16[544,128]{1,0:T(8,128)(2,1)S(1)} %attend_halo.1), channel_id=1, source_target_pairs={{0,10},{2,12},{4,14},{8,18},{10,20},{12,22},{16,26},{18,28},{20,30... | collective-permute-start | bytes 417800 | tf_op jit(solution)/shard_map/ppermute | solution.py:541
  27.6 2.7 %collective-permute-start.6 = (f32[1,2048]{1,0:T(1,128)S(1)}, f32[1,2048]{1,0:T(1,128)S(1)}, u32[]{:S(2)}, u32[]{:S(2)}) collective-permute-start(f32[1,2048]{1,0:T(1,128)S(1)} %add.7.after_ref.term_ref), channel_id=1, source_target_pairs={{0,4},{2,6},{4,0},{6,2},{1,5},{3,7},{5,1},{7,3},{8,12},{10,14},{12... | collective-permute-start | bytes 24584 | tf_op jit(solution)/shard_map/ppermute | solution.py:521
  30.3 1.9 %collective-permute-done.6.other_ref = f32[1,2048]{1,0:T(1,128)S(1)} collective-permute-done((f32[1,2048]{1,0:T(1,128)S(1)}, f32[1,2048]{1,0:T(1,128)S(1)}, u32[]{:S(2)}, u32[]{:S(2)}) %collective-permute-start.6) | collective-permute-done | bytes 8224 | tf_op jit(solution)/shard_map/ppermute | solution.py:521
  32.2 0.0 collective-permute-done.7.upstream_hbm
  32.2 0.0 collective-permute-done.1.both_ref
  32.2 0.0 collective-permute-done.early_ref
  32.2 0.0 collective-permute-done.5.halo_ref
  32.2 2.3 %project.1 = (bf16[64,1024]{1,0:T(8,128)(2,1)}, f32[1,2048]{1,0:T(1,128)}, bf16[64,2048]{1,0:T(8,128)(2,1)}) custom-call(bf16[1536,128]{1,0:T(8,128)(2,1)S(1)} %collective-permute-done.early_ref, bf16[1024,128]{1,0:T(8,128)(2,1)S(1)} %collective-permute-done.1.both_ref, bf16[544,128]{1,0:T(8,128)(2,1)S(1)} %collective-permute-done.5.halo_ref, ...), custom_call_target="tpu_custom_call" | custom-call | flops 268435456 | bytes 4194304 | tf_op jit(solution)/shard_map/project/pallas_call | solution.py:499
  (3 shorter events, 0.0 us)
Async XLA Ops:
  3.7 7.5 %copy-start = (f32[1,2048]{1,0:T(1,128)S(1)}, f32[1,2048]{1,0:T(1,128)}, u32[]{:S(2)}) copy-start(f32[1,2048]{1,0:T(1,128)} %gain_ref.3) | copy-start | bytes 24580
  3.7 17.7 %collective-permute-start.2 = (bf16[136,2048]{1,0:T(8,128)(2,1)S(1)}, bf16[136,2048]{1,0:T(8,128)(2,1)S(1)}, u32[]{:S(2)}, u32[]{:S(2)}) collective-permute-start(bf16[136,2048]{1,0:T(8,128)(2,1)S(1)} %get-tuple-element.25), channel_id=1, source_target_pairs={{2,0},{4,2},{6,4},{3,1},{5,3},{7,5},{10,8},{12,10},{14,12},{11,9},... | collective-permute-start | bytes 1671176 | tf_op jit(solution)/shard_map/ppermute | solution.py:35
  5.0 27.3 %collective-permute-start = (bf16[1536,128]{1,0:T(8,128)(2,1)S(1)}, bf16[1536,128]{1,0:T(8,128)(2,1)S(1)}, u32[]{:S(2)}, u32[]{:S(2)}) collective-permute-start(bf16[1536,128]{1,0:T(8,128)(2,1)S(1)} %get-tuple-element.19), channel_id=1, source_target_pairs={{0,8},{8,16},{16,24},{24,0},{1,9},{9,17},{17,25},{25,1},{2,10},{10... | collective-permute-start | bytes 1179656 | tf_op jit(solution)/shard_map/ppermute | solution.py:40
  12.7 19.5 %collective-permute-start.7 = (bf16[64,2048]{1,0:T(8,128)(2,1)S(1)}, bf16[64,2048]{1,0:T(8,128)(2,1)S(1)}, u32[]{:S(2)}, u32[]{:S(2)}) collective-permute-start(bf16[64,2048]{1,0:T(8,128)(2,1)S(1)} %get-tuple-element.31), channel_id=1, source_target_pairs={{0,24},{8,0},{16,8},{24,16},{1,25},{9,1},{17,9},{25,17},{2,26},{10... | collective-permute-start | bytes 786440 | tf_op jit(solution)/shard_map/ppermute | solution.py:40
  13.8 18.5 %collective-permute-start.1 = (bf16[1024,128]{1,0:T(8,128)(2,1)S(1)}, bf16[1024,128]{1,0:T(8,128)(2,1)S(1)}, u32[]{:S(2)}, u32[]{:S(2)}) collective-permute-start(bf16[1024,128]{1,0:T(8,128)(2,1)S(1)} %get-tuple-element.24.after_ref), channel_id=1, source_target_pairs={{0,8},{8,16},{16,24},{24,0},{1,9},{9,17},{17,25},{25,1},{2,10},{10... | collective-permute-start | bytes 786440 | tf_op jit(solution)/shard_map/ppermute | solution.py:40
  14.8 1.2 %collective-permute-start.3 = (f32[1,2048]{1,0:T(1,128)S(1)}, f32[1,2048]{1,0:T(1,128)S(1)}, u32[]{:S(2)}, u32[]{:S(2)}) collective-permute-start(f32[1,2048]{1,0:T(1,128)S(1)} %get-tuple-element.30), channel_id=1, source_target_pairs={{0,1},{1,0},{2,3},{3,2},{4,5},{5,4},{6,7},{7,6},{8,9},{9,8},{10,11... | collective-permute-start | bytes 24584 | tf_op jit(solution)/shard_map/ppermute | solution.py:521
  16.0 5.4 %collective-permute-start.4 = (f32[1,2048]{1,0:T(1,128)S(1)}, f32[1,2048]{1,0:T(1,128)S(1)}, u32[]{:S(2)}, u32[]{:S(2)}) collective-permute-start(f32[1,2048]{1,0:T(1,128)S(1)} %add.6), channel_id=1, source_target_pairs={{0,2},{2,0},{4,6},{6,4},{1,3},{3,1},{5,7},{7,5},{8,10},{10,8},{12,... | collective-permute-start | bytes 24584 | tf_op jit(solution)/shard_map/ppermute | solution.py:521
  22.9 9.4 %collective-permute-start.5 = (bf16[544,128]{1,0:T(8,128)(2,1)S(1)}, bf16[544,128]{1,0:T(8,128)(2,1)S(1)}, u32[]{:S(2)}, u32[]{:S(2)}) collective-permute-start(bf16[544,128]{1,0:T(8,128)(2,1)S(1)} %attend_halo.1), channel_id=1, source_target_pairs={{0,10},{2,12},{4,14},{8,18},{10,20},{12,22},{16,26},{18,28},{20,30... | collective-permute-start | bytes 417800 | tf_op jit(solution)/shard_map/ppermute | solution.py:541
  27.6 4.6 %collective-permute-start.6 = (f32[1,2048]{1,0:T(1,128)S(1)}, f32[1,2048]{1,0:T(1,128)S(1)}, u32[]{:S(2)}, u32[]{:S(2)}) collective-permute-start(f32[1,2048]{1,0:T(1,128)S(1)} %add.7.after_ref.term_ref), channel_id=1, source_target_pairs={{0,4},{2,6},{4,0},{6,2},{1,5},{3,7},{5,1},{7,3},{8,12},{10,14},{12... | collective-permute-start | bytes 24584 | tf_op jit(solution)/shard_map/ppermute | solution.py:521
